TPU v7x, 256 devices: a whole 4x4x8 slice. The times are simulated.
256 devices in a mesh: region: 64 (over y_hi, x, z), mp: 4 (over y_lo, core).
Axes of the slice: x: 4, y: 4 (y_hi: 2, y_lo: 2; y = y_hi * 2 + y_lo), z: 8, core: 2. Of those that a mesh axis runs over, the one named last changes fastest.
Arguments:
- tile_data: bfloat16 [256, 256, 2048], P('region', None, 'mp'), may hold values from -6.5 to 6.5
- tile_counts: int32 [64], replicated, may hold values from 0 to 4, as said below
- modulation: bfloat16 [64, 3, 2048], P('region'), may hold values from -4 to 4
- qkv_weight: bfloat16 [2048, 3, 2048], P('region', None, 'mp'), may hold values from -0.92807765 to 0.92807765
- out_weight: bfloat16 [2048, 2048], P('region', 'mp'), may hold values from -0.125 to 0.125
- blend_weights: float32 [6], replicated, may hold values from 0.1 to 0.9
Outputs:
- blended: bfloat16 [256, 256, 2048], P('region', None, 'mp')
Inputs may be any that keep to these rules, and one draw needn't show every extreme that they name: `tile_counts`: groups 2m and 2m + 1 together hold exactly 4 tiles. In every draw some group holds 4 tiles and its partner none.
All inputs are finite; a program needn't handle non-finite values.
Results may differ from a plain program's by a relative error of at most 0.0071.
Values may be sent and summed in bfloat16 or wider, within the bound.
No kernel may reach another device: no remote copies, remote signals or barrier semaphores. Data moves between devices by JAX's collectives and lax.ppermute only.
A program may use at most 64 MiB of HBM per device.

v0:
```python
import math

import jax
import jax.numpy as jnp
from jax import lax
from jax.sharding import PartitionSpec as P

D = 2048
HDIM = 128
S = 16
W = 6
TCOLS = 8
TPD = 2


def from_behind(block, axis, distance):
    devices = range(lax.axis_size(axis))
    route = [(i - distance, i) for i in devices if i - distance in devices]
    return lax.ppermute(block, axis, route)


def normalise(values):
    row_mean = jnp.mean(values, axis=-1, keepdims=True)
    centred = values - row_mean
    spread = jnp.mean(centred * centred, axis=-1, keepdims=True)
    return centred * lax.rsqrt(spread + 1e-06)


def attend(local_rows, modulators, qkv_weight, out_weight):
    tile_count = local_rows.shape[0]
    tokens = local_rows.shape[1]
    narrow = local_rows.shape[2]
    gathered = lax.all_gather(local_rows, "mp", axis=2, tiled=True)
    mod_values = modulators.astype(jnp.float32)
    hidden = (
        normalise(gathered.astype(jnp.float32)) * (1.0 + mod_values[:, 1][:, None, :])
        + mod_values[:, 0][:, None, :]
    )
    hidden = hidden.astype(jnp.bfloat16).reshape(tile_count * tokens, D)
    weight_piece = lax.all_gather(qkv_weight, "region", axis=0, tiled=True)
    flat_piece = weight_piece.reshape(weight_piece.shape[0], 3 * narrow)
    projections = jnp.dot(hidden, flat_piece, preferred_element_type=jnp.float32).astype(
        jnp.bfloat16
    )
    projections = projections.reshape(tile_count, tokens, 3, narrow // HDIM, HDIM)
    scores = jnp.einsum(
        "nqhe,nkhe->nhqk",
        projections[:, :, 0],
        projections[:, :, 1],
        preferred_element_type=jnp.float32,
    )
    scores = scores / math.sqrt(HDIM)
    attention_weights = jax.nn.softmax(scores, axis=-1).astype(jnp.bfloat16)
    attended = jnp.einsum(
        "nhqk,nkhe->nqhe",
        attention_weights,
        projections[:, :, 2],
        preferred_element_type=jnp.float32,
    )
    attended = attended.astype(jnp.bfloat16).reshape(tile_count * tokens, narrow)
    partial_out = jnp.einsum(
        "rd,md->rm",
        attended,
        lax.all_gather(out_weight, "region", axis=0, tiled=True),
        preferred_element_type=jnp.float32,
    )
    summed = lax.psum_scatter(partial_out, "mp", scatter_dimension=1, tiled=True)
    gate_slice = lax.dynamic_slice_in_dim(
        mod_values[:, 2], lax.axis_index("mp") * narrow, narrow, 1
    )
    updated = local_rows.astype(jnp.float32) + gate_slice[:, None, :] * summed.reshape(
        tile_count, tokens, narrow
    )
    return updated.astype(jnp.bfloat16)


def join_edges(tile_grid, earlier_rim, later_rim, has_before, has_after, shares, edge_axis):
    rim_width = shares.shape[0]
    side_len = tile_grid.shape[edge_axis]
    share_shape = [1, 1, 1, 1]
    share_shape[edge_axis] = rim_width
    share_view = shares.reshape(share_shape)
    near_part = lax.slice_in_dim(tile_grid, 0, rim_width, axis=edge_axis)
    middle = lax.slice_in_dim(tile_grid, rim_width, side_len - rim_width, axis=edge_axis)
    far_part = lax.slice_in_dim(tile_grid, side_len - rim_width, side_len, axis=edge_axis)
    near_mix = (1.0 - share_view) * earlier_rim + share_view * near_part
    far_mix = (1.0 - share_view) * far_part + share_view * later_rim
    near_part = jnp.where(has_before[:, None, None, None], near_mix, near_part)
    far_part = jnp.where(has_after[:, None, None, None], far_mix, far_part)
    return jnp.concatenate([near_part, middle, far_part], axis=edge_axis)


def locate(targets, tile_counts, slot_count):
    pair_of = targets // slot_count
    within = targets - pair_of * slot_count
    group_ids = jnp.arange(tile_counts.shape[0], dtype=jnp.int32)
    even_of = jnp.sum(
        jnp.where(group_ids[None, :] == 2 * pair_of[:, None], tile_counts[None, :], 0), axis=1
    )
    in_second = (within >= even_of).astype(jnp.int32)
    return (2 * pair_of + in_second, within - in_second * even_of)


def on_device(tile_data, tile_counts, modulation, qkv_weight, out_weight, blend_weights):
    device_id = lax.axis_index("region")
    parity_bit = device_id % 2
    pair_base = device_id - parity_bit
    group_ids = jnp.arange(tile_counts.shape[0], dtype=jnp.int32)
    even_count = jnp.sum(jnp.where(group_ids == pair_base, tile_counts, 0))
    own_count = jnp.sum(jnp.where(group_ids == device_id, tile_counts, 0))
    tile_total = TPD * tile_counts.shape[0]
    slot_count = tile_data.shape[0]
    narrow = tile_data.shape[2]
    slot_ids = jnp.arange(slot_count, dtype=jnp.int32)
    live_slots = slot_ids < own_count
    modulators = jnp.broadcast_to(modulation, (slot_count, 3, D))
    updated = attend(tile_data, modulators, qkv_weight, out_weight)
    tile_grid = updated.reshape(slot_count, S, S, narrow)
    tile_ids = device_id // 2 * slot_count + parity_bit * even_count + slot_ids
    column_pos = tile_ids % TCOLS
    has_left = live_slots & (column_pos != 0)
    has_right = live_slots & (column_pos != TCOLS - 1)
    right_device, right_slot = locate(tile_ids + 1, tile_counts, slot_count)
    left_device, left_slot = locate(tile_ids - 1, tile_counts, slot_count)
    west_edge = tile_grid[:, :, :W]
    east_edge = tile_grid[:, :, S - W :]
    later_stack = jnp.concatenate(
        [west_edge]
        + [from_behind(west_edge, "region", -offset_step) for offset_step in range(1, 4)],
        axis=0,
    )
    pick_index = jnp.clip(
        (right_device - device_id) * slot_count + right_slot, 0, 4 * slot_count - 1
    )
    later_rim = jnp.take(later_stack, pick_index, axis=0).astype(jnp.float32)
    earlier_stack = jnp.concatenate(
        [east_edge]
        + [from_behind(east_edge, "region", offset_step) for offset_step in range(1, 4)],
        axis=0,
    )
    pick_index = jnp.clip((device_id - left_device) * slot_count + left_slot, 0, 4 * slot_count - 1)
    earlier_rim = jnp.take(earlier_stack, pick_index, axis=0).astype(jnp.float32)
    joined = join_edges(
        tile_grid.astype(jnp.float32), earlier_rim, later_rim, has_left, has_right, blend_weights, 2
    )
    joined = joined.astype(jnp.bfloat16)
    lowest = max(0, 2 * (TCOLS // slot_count) - 1)
    highest = 2 * -(-TCOLS // slot_count) + 1
    offsets = list(range(lowest, highest + 1))
    north_edge = joined[:, :W]
    south_edge = joined[:, S - W :]
    below_device, below_slot = locate(tile_ids + TCOLS, tile_counts, slot_count)
    above_device, above_slot = locate(tile_ids - TCOLS, tile_counts, slot_count)
    has_below = live_slots & (tile_ids + TCOLS < tile_total)
    has_above = live_slots & (tile_ids >= TCOLS)
    rising = [from_behind(north_edge, "region", -offset_step) for offset_step in offsets]
    later_stack = jnp.concatenate(rising, axis=0)
    pick_index = jnp.clip(
        (below_device - device_id - lowest) * slot_count + below_slot,
        0,
        len(offsets) * slot_count - 1,
    )
    later_rim = jnp.take(later_stack, pick_index, axis=0).astype(jnp.float32)
    falling = [from_behind(south_edge, "region", offset_step) for offset_step in offsets]
    earlier_stack = jnp.concatenate(falling, axis=0)
    pick_index = jnp.clip(
        (device_id - above_device - lowest) * slot_count + above_slot,
        0,
        len(offsets) * slot_count - 1,
    )
    earlier_rim = jnp.take(earlier_stack, pick_index, axis=0).astype(jnp.float32)
    finished = join_edges(
        joined.astype(jnp.float32), earlier_rim, later_rim, has_above, has_below, blend_weights, 1
    )
    finished = jnp.where(live_slots[:, None, None, None], finished, 0.0)
    result = finished.astype(jnp.bfloat16).reshape(slot_count, S * S, narrow)
    return result


def solution(mesh):
    return jax.shard_map(
        on_device,
        mesh=mesh,
        in_specs=(
            P("region", None, "mp"),
            P(),
            P("region", None, None),
            P("region", None, "mp"),
            P("region", "mp"),
            P(),
        ),
        out_specs=P("region", None, "mp"),
        check_vma=False,
    )
```

profile of v0, /device:TPU:24, one launch (start us, length us, event | category | flops | bytes accessed | tf_op | source)
XLA Modules:
  0.0 603.8 jit_solution(17825116697051295569)
XLA Ops:
  10.3 49.5 %all-gather.4.cloned.1.call-done = bf16[4,256,2048]{2,1,0:T(8,128)(2,1)} async-done(((bf16[4,256,512]{2,1,0:T(8,128)(2,1)}), bf16[4,256,2048]{2,1,0:T(8,128)(2,1)}) %all-gather.4.cloned.1.call-update) | async-done | bytes 4194320 | tf_op jit(solution)/shard_map/all_gather | solution.py:33
  59.8 3.0 convert_reduce_fusion
  64.5 3.0 fusion.6
  67.5 133.0 %all-gather.6.cloned.1.call-done = bf16[2048,3,512]{2,0,1:T(8,128)(2,1)} async-done(((bf16[32,3,512]{2,0,1:T(8,128)(2,1)}), bf16[2048,3,512]{2,0,1:T(8,128)(2,1)}) %all-gather.6.cloned.1.call-update) | async-done | bytes 6291472 | tf_op jit(solution)/shard_map/all_gather | solution.py:40
  200.5 8.8 %copy.23 = bf16[2048,3,512]{0,2,1:T(8,128)(2,1)} copy(bf16[2048,3,512]{2,0,1:T(8,128)(2,1)} %all-gather.6.cloned.1.call-done) | data formatting | bytes 12582912 | tf_op jit(solution)/shard_map/all_gather | solution.py:40
  209.3 11.3 %convolution_convert_fusion = bf16[1024,1536]{1,0:T(8,128)(2,1)} fusion(bf16[1024,2048]{1,0:T(8,128)(2,1)} %bitcast.34, bf16[2048,1536]{0,1:T(8,128)(2,1)} %bitcast.33), kind=kOutput, calls=%fused_computation.15 | convolution fusion | flops 6444023808 | bytes 13631488 | tf_op jit(solution)/shard_map/dot_general | solution.py:42
  220.6 5.0 reshape.199
  225.6 2.5 fusion.45
  230.7 3.2 fusion.49
  235.1 83.2 %all-gather.8.cloned.1.call-done = bf16[2048,512]{1,0:T(8,128)(2,1)} async-done(((bf16[32,512]{1,0:T(8,128)(2,1)}), bf16[2048,512]{1,0:T(8,128)(2,1)}) %all-gather.8.cloned.1.call-update) | async-done | bytes 2097168 | tf_op jit(solution)/shard_map/all_gather | solution.py:64
  318.2 7.2 %fusion.15 = f32[1024,2048]{1,0:T(8,128)} fusion(bf16[2048,512]{1,0:T(8,128)(2,1)} %all-gather.8.cloned.1.call-done, bf16[128,8,4,128]{3,2,1,0:T(4,128)(2,1)S(1)} %bitcast.36), kind=kOutput, calls=%fused_computation.30 | convolution fusion | flops 2147483648 | bytes 11534336 | tf_op jit(solution)/shard_map/rd,md->rm/dot_general | solution.py:61
  327.7 77.2 %reduce-scatter.2.cloned.1.call-done = f32[1024,512]{1,0:T(8,128)} async-done(((f32[1024,2048]{1,0:T(8,128)}), f32[1024,512]{1,0:T(8,128)}) %reduce-scatter.2.cloned.1.call-update) | async-done | bytes 2097168 | tf_op jit(solution)/shard_map/reduce_scatter | solution.py:67
  407.0 7.9 %collective-permute-start.3 = (bf16[4,16,6,512]{3,2,1,0:T(8,128)(2,1)S(1)}, bf16[4,16,6,512]{3,2,1,0:T(8,128)(2,1)S(1)}, u32[]{:S(2)}, u32[]{:S(2)}) collective-permute-start(bf16[4,16,6,512]{3,2,1,0:T(8,128)(2,1)S(1)} %get-tuple-element.33), channel_id=1, source_target_pairs={{4,0},{8,4},{12,8},{16,12},{20,16},{24,20},{28,24},{32,28},{36,32}... | collective-permute-start | bytes 1179656 | tf_op jit(solution)/shard_map/ppermute | solution.py:19
  414.9 4.1 collective-permute-start.4
  419.0 3.1 collective-permute-start.5
  422.7 3.4 collective-permute-start
  426.2 3.6 collective-permute-start.1
  429.7 9.7 %collective-permute-done.3 = bf16[4,16,6,512]{3,2,1,0:T(8,128)(2,1)S(1)} collective-permute-done((bf16[4,16,6,512]{3,2,1,0:T(8,128)(2,1)S(1)}, bf16[4,16,6,512]{3,2,1,0:T(8,128)(2,1)S(1)}, u32[]{:S(2)}, u32[]{:S(2)}) %collective-permute-start.3) | collective-permute-done | bytes 393248 | tf_op jit(solution)/shard_map/ppermute | solution.py:19
  442.1 16.7 %collective-permute-done.4 = bf16[4,16,6,512]{3,2,1,0:T(8,128)(2,1)S(1)} collective-permute-done((bf16[4,16,6,512]{3,2,1,0:T(8,128)(2,1)S(1)}, bf16[4,16,6,512]{3,2,1,0:T(8,128)(2,1)S(1)}, u32[]{:S(2)}, u32[]{:S(2)}) %collective-permute-start.4) | collective-permute-done | bytes 393248 | tf_op jit(solution)/shard_map/ppermute | solution.py:19
  458.7 23.7 %collective-permute-done.5 = bf16[4,16,6,512]{3,2,1,0:T(8,128)(2,1)S(1)} collective-permute-done((bf16[4,16,6,512]{3,2,1,0:T(8,128)(2,1)S(1)}, bf16[4,16,6,512]{3,2,1,0:T(8,128)(2,1)S(1)}, u32[]{:S(2)}, u32[]{:S(2)}) %collective-permute-start.5) | collective-permute-done | bytes 393248 | tf_op jit(solution)/shard_map/ppermute | solution.py:19
  486.5 9.0 %collective-permute-done.2 = bf16[4,16,6,512]{3,2,1,0:T(8,128)(2,1)} collective-permute-done((bf16[4,16,6,512]{3,2,1,0:T(8,128)(2,1)S(1)}, bf16[4,16,6,512]{3,2,1,0:T(8,128)(2,1)}, u32[]{:S(2)}, u32[]{:S(2)}) %collective-permute-start.2) | collective-permute-done | bytes 393248 | tf_op jit(solution)/shard_map/ppermute | solution.py:19
  495.5 3.2 pad_maximum_fusion
  505.4 5.5 collective-permute-start.11
  510.9 5.5 collective-permute-start.9
  517.6 3.9 collective-permute-start.6
  521.5 5.2 collective-permute-start.7
  526.7 9.1 %collective-permute-done.10 = bf16[4,6,16,512]{3,2,1,0:T(8,128)(2,1)S(1)} collective-permute-done((bf16[4,6,16,512]{3,2,1,0:T(8,128)(2,1)S(1)}, bf16[4,6,16,512]{3,2,1,0:T(8,128)(2,1)S(1)}, u32[]{:S(2)}, u32[]{:S(2)}) %collective-permute-start.10) | collective-permute-done | bytes 393248 | tf_op jit(solution)/shard_map/ppermute | solution.py:19
  539.0 20.2 %collective-permute-done.11 = bf16[4,6,16,512]{3,2,1,0:T(8,128)(2,1)S(1)} collective-permute-done((bf16[4,6,16,512]{3,2,1,0:T(8,128)(2,1)S(1)}, bf16[4,6,16,512]{3,2,1,0:T(8,128)(2,1)S(1)}, u32[]{:S(2)}, u32[]{:S(2)}) %collective-permute-start.11) | collective-permute-done | bytes 393248 | tf_op jit(solution)/shard_map/ppermute | solution.py:19
  559.2 9.0 %collective-permute-done.9 = bf16[4,6,16,512]{3,2,1,0:T(8,128)(2,1)S(1)} collective-permute-done((bf16[4,6,16,512]{3,2,1,0:T(8,128)(2,1)S(1)}, bf16[4,6,16,512]{3,2,1,0:T(8,128)(2,1)S(1)}, u32[]{:S(2)}, u32[]{:S(2)}) %collective-permute-start.9) | collective-permute-done | bytes 393248 | tf_op jit(solution)/shard_map/ppermute | solution.py:19
  569.6 12.6 %collective-permute-done.6 = bf16[4,6,16,512]{3,2,1,0:T(8,128)(2,1)} collective-permute-done((bf16[4,6,16,512]{3,2,1,0:T(8,128)(2,1)}, bf16[4,6,16,512]{3,2,1,0:T(8,128)(2,1)}, u32[]{:S(2)}, u32[]{:S(2)}) %collective-permute-start.6) | collective-permute-done | bytes 393248 | tf_op jit(solution)/shard_map/ppermute | solution.py:19
  582.3 4.6 collective-permute-done.7
  586.9 4.7 collective-permute-done.8
  (74 shorter events, 38.0 us)
Async XLA Ops:
  6.5 53.3 %all-gather.4.cloned.1.call-start = ((), (), s32[]{:S(2)}) async-start(), calls=%async_computation.1 | async-start | bytes 5242880 | tf_op jit(solution)/shard_map/all_gather | solution.py:33
  7.3 193.2 %all-gather.6.cloned.1.call-start = ((), (), s32[]{:S(2)}) async-start(), calls=%async_computation.2 | async-start | bytes 6389760 | tf_op jit(solution)/shard_map/all_gather | solution.py:40
  8.0 310.2 %all-gather.8.cloned.1.call-start = ((), (), s32[]{:S(2)}) async-start(), calls=%async_computation.3 | async-start | bytes 2129920 | tf_op jit(solution)/shard_map/all_gather | solution.py:64
  8.7 396.1 %reduce-scatter.2.cloned.1.call-start = ((), (), s32[]{:S(2)}) async-start(), calls=%async_computation.4 | async-start | bytes 10485760 | tf_op jit(solution)/shard_map/reduce_scatter | solution.py:67
  59.8 3.4 copy-start
  228.1 1.7 copy-start.2
  228.1 1.9 copy-start.3
  325.4 0.7 copy-start.6
  325.4 79.4 %copy-start.1 = (bf16[4,256,512]{2,1,0:T(8,128)(2,1)S(1)}, bf16[4,256,512]{2,1,0:T(8,128)(2,1)}, u32[]{:S(2)}) copy-start(bf16[4,256,512]{2,1,0:T(8,128)(2,1)} %param.10) | copy-start | bytes 3145732
  406.8 34.8 %copy-start.4 = (f32[6]{0:T(128)S(1)}, f32[6]{0:T(128)}, u32[]{:S(2)}) copy-start(f32[6]{0:T(128)} %param.15) | copy-start | bytes 76
  407.0 32.5 %collective-permute-start.3 = (bf16[4,16,6,512]{3,2,1,0:T(8,128)(2,1)S(1)}, bf16[4,16,6,512]{3,2,1,0:T(8,128)(2,1)S(1)}, u32[]{:S(2)}, u32[]{:S(2)}) collective-permute-start(bf16[4,16,6,512]{3,2,1,0:T(8,128)(2,1)S(1)} %get-tuple-element.33), channel_id=1, source_target_pairs={{4,0},{8,4},{12,8},{16,12},{20,16},{24,20},{28,24},{32,28},{36,32}... | collective-permute-start | bytes 1179656 | tf_op jit(solution)/shard_map/ppermute | solution.py:19
  414.9 43.8 %collective-permute-start.4 = (bf16[4,16,6,512]{3,2,1,0:T(8,128)(2,1)S(1)}, bf16[4,16,6,512]{3,2,1,0:T(8,128)(2,1)S(1)}, u32[]{:S(2)}, u32[]{:S(2)}) collective-permute-start(bf16[4,16,6,512]{3,2,1,0:T(8,128)(2,1)S(1)} %get-tuple-element.33), channel_id=1, source_target_pairs={{8,0},{12,4},{16,8},{20,12},{24,16},{28,20},{32,24},{36,28},{40,32... | collective-permute-start | bytes 1179656 | tf_op jit(solution)/shard_map/ppermute | solution.py:19
  419.0 63.5 %collective-permute-start.5 = (bf16[4,16,6,512]{3,2,1,0:T(8,128)(2,1)S(1)}, bf16[4,16,6,512]{3,2,1,0:T(8,128)(2,1)S(1)}, u32[]{:S(2)}, u32[]{:S(2)}) collective-permute-start(bf16[4,16,6,512]{3,2,1,0:T(8,128)(2,1)S(1)} %get-tuple-element.33), channel_id=1, source_target_pairs={{12,0},{16,4},{20,8},{24,12},{28,16},{32,20},{36,24},{40,28},{44,3... | collective-permute-start | bytes 1179656 | tf_op jit(solution)/shard_map/ppermute | solution.py:19
  422.7 63.8 %collective-permute-start = (bf16[4,16,6,512]{3,2,1,0:T(8,128)(2,1)S(1)}, bf16[4,16,6,512]{3,2,1,0:T(8,128)(2,1)}, u32[]{:S(2)}, u32[]{:S(2)}) collective-permute-start(bf16[4,16,6,512]{3,2,1,0:T(8,128)(2,1)S(1)} %get-tuple-element.32), channel_id=1, source_target_pairs={{0,4},{4,8},{8,12},{12,16},{16,20},{20,24},{24,28},{28,32},{32,36}... | collective-permute-start | bytes 1179656 | tf_op jit(solution)/shard_map/ppermute | solution.py:19
  426.2 60.3 %collective-permute-start.1 = (bf16[4,16,6,512]{3,2,1,0:T(8,128)(2,1)S(1)}, bf16[4,16,6,512]{3,2,1,0:T(8,128)(2,1)}, u32[]{:S(2)}, u32[]{:S(2)}) collective-permute-start(bf16[4,16,6,512]{3,2,1,0:T(8,128)(2,1)S(1)} %get-tuple-element.32), channel_id=1, source_target_pairs={{0,8},{4,12},{8,16},{12,20},{16,24},{20,28},{24,32},{28,36},{32,40... | collective-permute-start | bytes 1179656 | tf_op jit(solution)/shard_map/ppermute | solution.py:19
  439.5 56.0 %collective-permute-start.2 = (bf16[4,16,6,512]{3,2,1,0:T(8,128)(2,1)S(1)}, bf16[4,16,6,512]{3,2,1,0:T(8,128)(2,1)}, u32[]{:S(2)}, u32[]{:S(2)}) collective-permute-start(bf16[4,16,6,512]{3,2,1,0:T(8,128)(2,1)S(1)} %get-tuple-element.32), channel_id=1, source_target_pairs={{0,12},{4,16},{8,20},{12,24},{16,28},{20,32},{24,36},{28,40},{32,4... | collective-permute-start | bytes 1179656 | tf_op jit(solution)/shard_map/ppermute | solution.py:19
  502.9 33.0 %collective-permute-start.10 = (bf16[4,6,16,512]{3,2,1,0:T(8,128)(2,1)S(1)}, bf16[4,6,16,512]{3,2,1,0:T(8,128)(2,1)S(1)}, u32[]{:S(2)}, u32[]{:S(2)}) collective-permute-start(bf16[4,6,16,512]{3,2,1,0:T(8,128)(2,1)S(1)} %get-tuple-element.31), channel_id=1, source_target_pairs={{16,0},{20,4},{24,8},{28,12},{32,16},{36,20},{40,24},{44,28},{48,3... | collective-permute-start | bytes 1179656 | tf_op jit(solution)/shard_map/ppermute | solution.py:19
  505.4 53.8 %collective-permute-start.11 = (bf16[4,6,16,512]{3,2,1,0:T(8,128)(2,1)S(1)}, bf16[4,6,16,512]{3,2,1,0:T(8,128)(2,1)S(1)}, u32[]{:S(2)}, u32[]{:S(2)}) collective-permute-start(bf16[4,6,16,512]{3,2,1,0:T(8,128)(2,1)S(1)} %get-tuple-element.31), channel_id=1, source_target_pairs={{20,0},{24,4},{28,8},{32,12},{36,16},{40,20},{44,24},{48,28},{52,3... | collective-permute-start | bytes 1179656 | tf_op jit(solution)/shard_map/ppermute | solution.py:19
  510.9 57.3 %collective-permute-start.9 = (bf16[4,6,16,512]{3,2,1,0:T(8,128)(2,1)S(1)}, bf16[4,6,16,512]{3,2,1,0:T(8,128)(2,1)S(1)}, u32[]{:S(2)}, u32[]{:S(2)}) collective-permute-start(bf16[4,6,16,512]{3,2,1,0:T(8,128)(2,1)S(1)} %get-tuple-element.31), channel_id=1, source_target_pairs={{12,0},{16,4},{20,8},{24,12},{28,16},{32,20},{36,24},{40,28},{44,3... | collective-permute-start | bytes 1179656 | tf_op jit(solution)/shard_map/ppermute | solution.py:19
  517.6 64.7 %collective-permute-start.6 = (bf16[4,6,16,512]{3,2,1,0:T(8,128)(2,1)}, bf16[4,6,16,512]{3,2,1,0:T(8,128)(2,1)}, u32[]{:S(2)}, u32[]{:S(2)}) collective-permute-start(bf16[4,6,16,512]{3,2,1,0:T(8,128)(2,1)} %get-tuple-element.30), channel_id=1, source_target_pairs={{0,12},{4,16},{8,20},{12,24},{16,28},{20,32},{24,36},{28,40},{32,4... | collective-permute-start | bytes 1179656 | tf_op jit(solution)/shard_map/ppermute | solution.py:19
  521.5 65.4 %collective-permute-start.7 = (bf16[4,6,16,512]{3,2,1,0:T(8,128)(2,1)}, bf16[4,6,16,512]{3,2,1,0:T(8,128)(2,1)}, u32[]{:S(2)}, u32[]{:S(2)}) collective-permute-start(bf16[4,6,16,512]{3,2,1,0:T(8,128)(2,1)} %get-tuple-element.30), channel_id=1, source_target_pairs={{0,16},{4,20},{8,24},{12,28},{16,32},{20,36},{24,40},{28,44},{32,4... | collective-permute-start | bytes 1179656 | tf_op jit(solution)/shard_map/ppermute | solution.py:19
  535.9 55.7 %collective-permute-start.8 = (bf16[4,6,16,512]{3,2,1,0:T(8,128)(2,1)}, bf16[4,6,16,512]{3,2,1,0:T(8,128)(2,1)}, u32[]{:S(2)}, u32[]{:S(2)}) collective-permute-start(bf16[4,6,16,512]{3,2,1,0:T(8,128)(2,1)} %get-tuple-element.30), channel_id=1, source_target_pairs={{0,20},{4,24},{8,28},{12,32},{16,36},{20,40},{24,44},{28,48},{32,5... | collective-permute-start | bytes 1179656 | tf_op jit(solution)/shard_map/ppermute | solution.py:19
  569.6 24.6 %copy-start.5 = (pred[4]{0:T(512)(128)(4,1)S(1)}, pred[4]{0:T(512)(128)(4,1)}, u32[]{:S(2)}) copy-start(pred[4]{0:T(512)(128)(4,1)} %get-tuple-element.42) | copy-start | bytes 16
  594.3 1.7 copy-start.7
Sparse Core Ops, SparseCore 0:
  9.2 50.5 all-gather.3
  63.3 137.1 all-gather.5
  204.2 113.9 all-gather.7
  325.6 79.2 reduce-scatter.1
where the time goes:
time: 610 us; the launch traced here: 604 us
  waiting for transfers between devices  464 us (76%)
  starting transfers between devices  48.3 us (8%)
  local copies, waits for them, and re-layouts  28.9 us (5%)
  other arithmetic  28.6 us (5%)
  matrix products  19.7 us (3%)
  between operations  14.2 us (2%)
    all_gather x1, waiting for transfers between devices, attend(): weight_piece = lax.all_gather(qkv_weight, 'region', axis=0, tiled=True)  133 us
    ppermute x12, waiting for transfers between devices, from_behind(): return lax.ppermute(block, axis, route)  119 us
    all_gather x1, waiting for transfers between devices, attend(): lax.all_gather(out_weight, 'region', axis=0, tiled=True)  83.2 us
    reduce_scatter x1, waiting for transfers between devices, attend(): lax.psum_scatter(partial_out, 'mp', scatter_dimension=1, tiled=True)  77.2 us
    all_gather x1, waiting for transfers between devices, attend(): gathered = lax.all_gather(local_rows, 'mp', axis=2, tiled=True)  49.5 us
    ppermute x12, starting transfers between devices, from_behind(): return lax.ppermute(block, axis, route)  48.2 us
  transfers between devices with their start and end apart: 16, of which 14 were waited for; matrix products, arithmetic and copies ran while one was open for 9% of the time, Pallas kernels for 0%

commit v1 on v0

v1 whole, which is shorter than its diff:
```python
import functools
import math

import jax
import jax.numpy as jnp
from jax import lax
from jax.experimental import pallas as pl
from jax.experimental.pallas import tpu as pltpu
from jax.sharding import Mesh, PartitionSpec as P

D = 2048
HDIM = 128
S = 16
W = 6
TOK = 256
NARROW = 512
HALF = 256
REGION = ("h", "x", "z")
MP = ("yl", "c")
BF = jnp.bfloat16
F32 = jnp.float32


def xor_swap(block, axis, bit):
    size = lax.axis_size(axis)
    return lax.ppermute(block, axis, [(i, i ^ bit) for i in range(size)])


def shift(block, distance, allowed):
    route = [(i, i + distance) for i in range(64) if 0 <= i + distance < 64 and allowed(i)]
    return lax.ppermute(block, REGION, route)


def ring_of_four(block, axis, split_axis):
    near = xor_swap(block, axis, 1)
    side = xor_swap(block, axis, 3)
    half = block.shape[split_axis] // 2
    size = block.shape[split_axis]
    first = xor_swap(lax.slice_in_dim(side, 0, half, axis=split_axis), axis, 1)
    second = xor_swap(lax.slice_in_dim(near, half, size, axis=split_axis), axis, 3)
    return block, near, (first, second), side


def hidden_kernel(a_ref, b_ref, c_ref, d_ref, mod_ref, out_ref):
    parts = [r[...].astype(F32) for r in (a_ref, b_ref, c_ref, d_ref)]
    mean = sum(jnp.sum(p, axis=-1, keepdims=True) for p in parts) * (1.0 / D)
    parts = [p - mean for p in parts]
    spread = sum(jnp.sum(p * p, axis=-1, keepdims=True) for p in parts) * (1.0 / D)
    scale = lax.rsqrt(spread + 1e-06)
    mods = mod_ref[0].astype(F32)
    for j, p in enumerate(parts):
        cols = slice(j * NARROW, (j + 1) * NARROW)
        value = p * scale * (1.0 + mods[1:2, cols]) + mods[0:1, cols]
        out_ref[:, cols] = value.astype(BF)


def hidden_of(pieces, mods):
    rows = 128
    piece = pl.BlockSpec((rows, NARROW), lambda i: (i, 0))
    return pl.pallas_call(
        hidden_kernel,
        grid=(512 // rows,),
        in_specs=[piece] * 4 + [pl.BlockSpec((1, 3, D), lambda i: (i * rows // TOK, 0, 0))],
        out_specs=pl.BlockSpec((rows, D), lambda i: (i, 0)),
        out_shape=jax.ShapeDtypeStruct((512, D), BF),
        cost_estimate=pl.CostEstimate(flops=8 * 512 * D, bytes_accessed=4 * 512 * D, transcendentals=512),
        name="hidden",
    )(*pieces, mods)


def attend_kernel(slot_ref, hid_ref, qk_ref, v0, v1, v2, v3, out_ref, w_ref, sem):
    copies = []
    for hr in range(2):
        for xr in range(4):
            slot = slot_ref[hr * 4 + xr]
            copies.append(
                pltpu.make_async_copy(
                    qk_ref.at[:, xr, hr], w_ref.at[slot, :, :, pl.ds(0, 2 * HALF)], sem
                )
            )
            copies.append(
                pltpu.make_async_copy(
                    (v0, v1, v2, v3)[xr].at[:, hr],
                    w_ref.at[slot, :, :, pl.ds(2 * HALF, HALF)],
                    sem,
                )
            )
    for copy in copies:
        copy.start()
    for copy in copies:
        copy.wait()
    weight = w_ref[...].reshape(D, 3 * HALF)
    for t in range(2):
        rows = slice(t * TOK, (t + 1) * TOK)
        proj = jnp.dot(hid_ref[rows, :], weight, preferred_element_type=F32).astype(BF)
        for n in range(2):
            q = proj[:, n * HDIM : (n + 1) * HDIM]
            k = proj[:, HALF + n * HDIM : HALF + (n + 1) * HDIM]
            v = proj[:, 2 * HALF + n * HDIM : 2 * HALF + (n + 1) * HDIM]
            scores = lax.dot_general(
                q, k, (((1,), (1,)), ((), ())), preferred_element_type=F32
            ) * (1.0 / math.sqrt(HDIM))
            top = jnp.max(scores, axis=-1, keepdims=True)
            e = jnp.exp(scores - top)
            probs = (e / jnp.sum(e, axis=-1, keepdims=True)).astype(BF)
            got = jnp.dot(probs, v, preferred_element_type=F32)
            out_ref[rows, n * HDIM : (n + 1) * HDIM] = got.astype(BF)


def attended_of(slots, hidden, qk, vs):
    anywhere = pl.BlockSpec(memory_space=pl.ANY)
    vmem = pl.BlockSpec(memory_space=pltpu.VMEM)
    return pl.pallas_call(
        attend_kernel,
        in_specs=[pl.BlockSpec(memory_space=pltpu.SMEM), vmem] + [anywhere] * 5,
        out_specs=vmem,
        out_shape=jax.ShapeDtypeStruct((512, HALF), BF),
        scratch_shapes=[pltpu.VMEM((8, 8, 32, 3 * HALF), BF), pltpu.SemaphoreType.DMA],
        compiler_params=pltpu.CompilerParams(vmem_limit_bytes=32 * 2**20),
        cost_estimate=pl.CostEstimate(
            flops=2 * 512 * D * 768 + 4 * 4 * TOK * TOK * HDIM,
            bytes_accessed=6 * 2**20,
            transcendentals=4 * TOK * TOK,
        ),
        name="attend",
    )(slots, hidden, qk, *vs)


def project_kernel(slot_ref, own_ref, other_ref, o0, o1, o2, o3, keep_ref, send_ref, w_ref, sem):
    copies = []
    for xr in range(4):
        copies.append(
            pltpu.make_async_copy(
                (o0, o1, o2, o3)[xr].at[:, slot_ref[0]], w_ref.at[slot_ref[1 + xr]], sem
            )
        )
    for copy in copies:
        copy.start()
    for copy in copies:
        copy.wait()
    for b, out_ref in ((1, send_ref), (0, keep_ref)):
        weight = w_ref[2 * b : 2 * b + 2].reshape(NARROW, NARROW)
        total = lax.dot_general(
            own_ref[...], weight[:, :HALF], (((1,), (1,)), ((), ())), preferred_element_type=F32
        ) + lax.dot_general(
            other_ref[...], weight[:, HALF:], (((1,), (1,)), ((), ())), preferred_element_type=F32
        )
        out_ref[...] = total.astype(BF)


def partial_of(slots, own, other, os):
    anywhere = pl.BlockSpec(memory_space=pl.ANY)
    vmem = pl.BlockSpec(memory_space=pltpu.VMEM)
    return pl.pallas_call(
        project_kernel,
        in_specs=[pl.BlockSpec(memory_space=pltpu.SMEM), vmem, vmem] + [anywhere] * 4,
        out_specs=[vmem, vmem],
        out_shape=[jax.ShapeDtypeStruct((512, NARROW), BF)] * 2,
        scratch_shapes=[pltpu.VMEM((4, 8, 32, NARROW), BF), pltpu.SemaphoreType.DMA],
        compiler_params=pltpu.CompilerParams(vmem_limit_bytes=32 * 2**20),
        cost_estimate=pl.CostEstimate(
            flops=2 * 512 * 512 * 1024, bytes_accessed=3 * 2**20, transcendentals=0
        ),
        name="project",
    )(slots, own, other, *os)


def mix(earlier, later, share):
    return (1.0 - share) * earlier.astype(F32) + share * later.astype(F32)


def join_columns(grid, region, shares):
    share = shares.reshape(1, W, 1)
    west, east = grid[:, :, :W], grid[:, :, S - W :]
    later = shift(west[0], -1, lambda i: i % 4 != 0)
    earlier = shift(east[1], 1, lambda i: i % 4 != 3)
    place = region % 4
    inner = mix(east[0], west[1], share).astype(BF)
    left = jnp.where(place != 0, mix(earlier, west[0], share).astype(BF), west[0])
    right = jnp.where(place != 3, mix(east[1], later, share).astype(BF), east[1])
    middle = grid[:, :, W : S - W]
    first = jnp.concatenate([left, middle[0], inner], axis=1)
    second = jnp.concatenate([inner, middle[1], right], axis=1)
    return jnp.stack([first, second])


def join_rows(grid, region, shares):
    share = shares.reshape(1, W, 1, 1)
    north, south = grid[:, :W], grid[:, S - W :]
    later = shift(north, -4, lambda i: True)
    earlier = shift(south, 4, lambda i: True)
    top = jnp.where(region >= 4, mix(earlier, north, share).astype(BF), north)
    bottom = jnp.where(region < 60, mix(south, later, share).astype(BF), south)
    return jnp.concatenate([top, grid[:, W : S - W], bottom], axis=1)


def pick(choices, index):
    return lax.dynamic_index_in_dim(choices, index, 0, keepdims=False)


def on_device(tile_data, tile_counts, modulation, qkv_weight, out_weight, blend_weights):
    h, x, z = (lax.axis_index(a) for a in REGION)
    yl, c = (lax.axis_index(a) for a in MP)
    region = h * 32 + x * 8 + z
    parity = z % 2
    even = jnp.sum(jnp.where(jnp.arange(64) == region - parity, tile_counts, 0))

    own_heads = jnp.where(h == 0, qkv_weight[:, :, :HALF], qkv_weight[:, :, HALF:])
    other_heads = jnp.where(h == 0, qkv_weight[:, :, HALF:], qkv_weight[:, :, :HALF])
    out_cols = jnp.where(
        h == 0, out_weight, jnp.concatenate([out_weight[:, HALF:], out_weight[:, :HALF]], axis=1)
    )
    out_swapped = jnp.concatenate([out_cols[:, HALF:], out_cols[:, :HALF]], axis=1)
    own_block = jnp.concatenate([own_heads.reshape(32, 3 * HALF), out_cols], axis=1)
    sent_block = jnp.concatenate([other_heads.reshape(32, 3 * HALF), out_swapped], axis=1)
    block = jnp.stack([own_block, xor_swap(sent_block, "h", 1)])
    qk_block, vo_block = block[:, :, : 2 * HALF], block[:, :, 2 * HALF :]

    vo_z = lax.all_gather(vo_block, "z", axis=0)
    p0, p1, p2, p3 = ring_of_four(qk_block, "x", 0)
    qk_x = jnp.stack([p0, p1, jnp.concatenate(p2, axis=0), p3])
    qk_all = lax.all_gather(qk_x, "z", axis=0)
    v_x = ring_of_four(vo_z[..., :HALF], "x", 0)
    o_x = ring_of_four(vo_z[..., HALF:], "x", 0)
    v_all = [v_x[0], v_x[1], jnp.concatenate(v_x[2], axis=0), v_x[3]]
    o_all = [o_x[0], o_x[1], jnp.concatenate(o_x[2], axis=0), o_x[3]]

    slots = jnp.arange(2)
    send_slot = jnp.where(parity == 0, 2 + slots, jnp.clip(slots - even, 0, 3))
    keep_slot = jnp.where(parity == 0, slots, jnp.clip(2 + slots - even, 0, 3))
    use_other = jnp.where(parity == 0, slots >= even, 2 + slots < even)
    sent = jnp.stack([pick(tile_data, send_slot[0]), pick(tile_data, send_slot[1])])
    kept = jnp.stack([pick(tile_data, keep_slot[0]), pick(tile_data, keep_slot[1])])
    came = xor_swap(sent, "z", 1)
    other_mod = xor_swap(modulation, "z", 1)
    tiles = jnp.where(use_other[:, None, None], came, kept)
    mods = jnp.where(use_other[:, None, None], other_mod, modulation)

    mine = tiles.reshape(512, NARROW)
    near = lax.ppermute(mine, ("h", "yl"), [(i, i ^ 1) for i in range(4)])
    side = lax.ppermute(mine, ("h", "yl"), [(i, i ^ 3) for i in range(4)])
    across_a = lax.ppermute(side[:HALF], ("h", "yl"), [(i, i ^ 1) for i in range(4)])
    across_b = lax.ppermute(near[HALF:], ("h", "yl"), [(i, i ^ 3) for i in range(4)])
    across = jnp.concatenate([across_a, across_b], axis=0)
    mods_across = xor_swap(mods, "h", 1)

    def in_order(m):
        m = m.reshape(2, 3, 2, 2, NARROW)
        m = jnp.where(yl == 0, m, m[:, :, ::-1])
        m = jnp.where(c == 0, m, m[:, :, :, ::-1])
        return m.reshape(2, 3, D)

    hid_own = hidden_of(
        (mine, xor_swap(mine, "c", 1), near, xor_swap(near, "c", 1)), in_order(mods)
    )
    hid_other = hidden_of(
        (across, xor_swap(across, "c", 1), side, xor_swap(side, "c", 1)), in_order(mods_across)
    )

    hr = jnp.arange(8) // 4
    place_x = (jnp.arange(8) % 4) ^ x
    place = ((hr ^ h) ^ yl) * 4 + ((place_x // 2) ^ c) * 2 + place_x % 2
    place = place.astype(jnp.int32)
    att_sent = attended_of(place, hid_other, qk_all, v_all)
    att_other = xor_swap(att_sent, "h", 1)
    att_own = attended_of(place, hid_own, qk_all, v_all)

    x_slots = place[:4] % 4
    sums = []
    for a in (1, 0):
        rows = jnp.concatenate([((yl ^ a) ^ h)[None], x_slots]).astype(jnp.int32)
        keep, send = partial_of(rows, att_own, att_other, o_all)
        sums.append((keep, xor_swap(send, "c", 1)))
    far = (sums[0][0].astype(F32) + sums[0][1].astype(F32)).astype(BF)
    far = xor_swap(far, "yl", 1)
    gate = mods[:, 2].reshape(2, 4, NARROW)
    gate = lax.dynamic_index_in_dim(gate, yl * 2 + c, 1, keepdims=True).astype(F32)
    summed = sums[1][0].astype(F32) + sums[1][1].astype(F32) + far.astype(F32)
    updated = tiles.astype(F32) + gate * summed.reshape(2, TOK, NARROW)
    grid = updated.astype(BF).reshape(2, S, S, NARROW)

    joined = join_columns(grid, region, blend_weights)
    finished = join_rows(joined, region, blend_weights).reshape(2, TOK, NARROW)

    other = xor_swap(finished, "z", 1)
    both = jnp.where(
        parity == 0,
        jnp.concatenate([finished, other], axis=0),
        jnp.concatenate([other, finished], axis=0),
    )
    outs = []
    for slot in range(4):
        source = jnp.where(parity == 0, slot, slot + even)
        live = jnp.where(parity == 0, slot < even, slot + even < 4)
        outs.append(jnp.where(live, pick(both, jnp.clip(source, 0, 3)), jnp.zeros((), BF)))
    return jnp.stack(outs)


def solution(mesh):
    fine = Mesh(mesh.devices.reshape(2, 4, 8, 2, 2), REGION + MP)
    return jax.shard_map(
        on_device,
        mesh=fine,
        in_specs=(
            P(REGION, None, MP),
            P(),
            P(REGION, None, None),
            P(REGION, None, MP),
            P(REGION, MP),
            P(),
        ),
        out_specs=P(REGION, None, MP),
        check_vma=False,
    )
```

time: 610 us -> 220 us (0.36)
  waiting for transfers between devices: 464 us -> 67.1 us
  blocking collectives: 0 us -> 35.2 us
  Pallas kernels: 0 us -> 21.5 us
  matrix products: 19.7 us -> 0 us
  other arithmetic: 28.6 us -> 9.45 us
  between operations: 14.2 us -> 27.4 us
  local copies, waits for them, and re-layouts: 28.9 us -> 19.1 us
  starting transfers between devices: 48.3 us -> 39.3 us
    all_gather x3 -> x1, waiting for transfers between devices: 266 us -> 0.01 us  [on_device(): qk_all = lax.all_gather(qk_x, 'z', axis=0)]
    reduce_scatter x1 -> x0, waiting for transfers between devices: 77.2 us -> none  [attend(): lax.psum_scatter(partial_out, 'mp', scatter_dimension=1, tiled=True)]
    ppermute x12 -> x33, waiting for transfers between devices: 119 us -> 67.1 us  [the longest x25 33.3 us: xor_swap(): return lax.ppermute(block, axis, [(i, i ^ bit) for i in range(size)])]
    all_gather x0 -> x1, blocking collectives: none -> 35.2 us  [on_device(): vo_z = lax.all_gather(vo_block, 'z', axis=0)]
    pallas_call x0 -> x6, Pallas kernels: none -> 21.5 us  [the longest x2 9.5 us: hidden_of(): pl.pallas_call(hidden_kernel, grid=(512 // rows,), in_specs=[piece] * 4 +...]
    dot_general x4 -> x0, matrix products: 19.7 us -> none  [the longest x1 11.3 us: attend(): jnp.dot(hidden, flat_piece, preferred_element_type=jnp.float32)]
    ppermute x12 -> x33, starting transfers between devices: 48.2 us -> 39.3 us  [the longest x25 23.9 us: xor_swap(): return lax.ppermute(block, axis, [(i, i ^ bit) for i in range(size)])]
    all_gather x1 -> x0, local copies, waits for them, and re-layouts: 8.81 us -> none  [attend(): weight_piece = lax.all_gather(qkv_weight, 'region', axis=0, tiled=True)]
  transfers between devices with their start and end apart: 16 -> 34, of which waited for: 14 -> 12; matrix products, arithmetic and copies ran while one was open for 9% -> 8% of each run, Pallas kernels for 0% -> 9%
where the time goes in v1:
time: 220 us; the launch traced here: 219 us
  waiting for transfers between devices  67.1 us (30%)
  starting transfers between devices  39.3 us (18%)
  blocking collectives  35.2 us (16%)
  between operations  27.4 us (12%)
  Pallas kernels  21.5 us (10%)
  local copies, waits for them, and re-layouts  19.1 us (9%)
  other arithmetic  9.45 us (4%)
    all_gather x1, blocking collectives, on_device(): vo_z = lax.all_gather(vo_block, 'z', axis=0)  35.2 us
    ppermute x25, waiting for transfers between devices, xor_swap(): return lax.ppermute(block, axis, [(i, i ^ bit) for i in range(size)])  33.3 us
    ppermute x4, waiting for transfers between devices, shift(): return lax.ppermute(block, REGION, route)  31.7 us
    ppermute x25, starting transfers between devices, xor_swap(): return lax.ppermute(block, axis, [(i, i ^ bit) for i in range(size)])  23.9 us
    ppermute x4, starting transfers between devices, shift(): return lax.ppermute(block, REGION, route)  10.5 us
    pallas_call x2, Pallas kernels, hidden_of(): pl.pallas_call(hidden_kernel, grid=(512 // rows,), in_specs=[piece] * 4 +...  9.5 us
    pallas_call x2, Pallas kernels, attended_of(): pl.pallas_call(attend_kernel, in_specs=[pl.BlockSpec(memory_space=pltpu.S...  9.29 us
    unnamed x30, local copies, waits for them, and re-layouts  8.07 us
  transfers between devices with their start and end apart: 34, of which 12 were waited for; matrix products, arithmetic and copies ran while one was open for 8% of the time, Pallas kernels for 9%

profile of v1, /device:TPU:24, one launch (start us, length us, event | category | flops | bytes accessed | tf_op | source)
XLA Modules:
  0.0 219.1 jit_solution(6431084147740504845)
XLA Ops:
  8.3 2.1 collective-permute-start.5
  14.4 2.8 %collective-permute-start.7 = (bf16[2,32,512]{2,1,0:T(8,128)(2,1)S(1)}, bf16[2,32,512]{2,1,0:T(8,128)(2,1)S(1)}, u32[]{:S(2)}, u32[]{:S(2)}) collective-permute-start(bf16[2,32,512]{2,1,0:T(8,128)(2,1)S(1)} %pad_maximum_fusion.5), channel_id=1, source_target_pairs={{0,96},{32,64},{64,32},{96,0},{1,97},{33,65},{65,33},{97,1},{2,98}... | collective-permute-start | bytes 196616 | tf_op jit(solution)/shard_map/ppermute | solution.py:26
  24.5 1.9 collective-permute-start.8
  26.9 1.5 collective-permute-done.8
  28.5 3.1 %collective-permute-done.9 = bf16[1,32,512]{2,1,0:T(8,128)(2,1)S(1)} collective-permute-done((bf16[1,32,512]{2,1,0:T(8,128)(2,1)S(1)}, bf16[1,32,512]{2,1,0:T(8,128)(2,1)S(1)}, u32[]{:S(2)}, u32[]{:S(2)}) %collective-permute-start.9) | collective-permute-done | bytes 32800 | tf_op jit(solution)/shard_map/ppermute | solution.py:26
  32.5 2.0 collective-permute-start
  35.4 9.1 %collective-permute-done.1 = bf16[1,3,2048]{2,1,0:T(4,128)(2,1)S(1)} collective-permute-done((bf16[1,3,2048]{2,1,0:T(4,128)(2,1)S(1)}, bf16[1,3,2048]{2,1,0:T(4,128)(2,1)S(1)}, u32[]{:S(2)}, u32[]{:S(2)}) %collective-permute-start.1) | collective-permute-done | bytes 12320 | tf_op jit(solution)/shard_map/ppermute | solution.py:26
  44.6 1.6 collective-permute-start.19
  49.6 35.2 %all-gather.1 = bf16[16,32,768]{2,1,0:T(8,128)(2,1)S(1)} all-gather(bf16[2,32,768]{2,1,0:T(8,128)(2,1)S(1)} %pad_maximum_fusion.3), channel_id=3, replica_groups=mesh['h'=2,'x'=4,'z'=8,'yl'=2,'c'=2] {'z'}, dimensions={0}, use_global_device_ids=true | all-gather | bytes 884736 | tf_op jit(solution)/shard_map/all_gather | solution.py:219
  85.0 3.2 %collective-permute-start.22 = (bf16[8,2,32,512]{3,2,1,0:T(8,128)(2,1)S(1)}, bf16[8,2,32,512]{3,2,1,0:T(8,128)(2,1)S(1)}, u32[]{:S(2)}, u32[]{:S(2)}) collective-permute-start(bf16[8,2,32,512]{3,2,1,0:T(8,128)(2,1)S(1)} %slice.157.o0), channel_id=1, source_target_pairs={{0,96},{32,64},{64,32},{96,0},{1,97},{33,65},{65,33},{97,1},{2,98}... | collective-permute-start | bytes 1572872 | tf_op jit(solution)/shard_map/ppermute | solution.py:26
  91.4 2.1 collective-permute-start.21
  93.5 1.7 slice.156
  95.2 1.6 collective-permute-start.16
  100.9 2.1 collective-permute-done.16
  109.2 4.7 %hidden.3.hid_ref = bf16[512,2048]{1,0:T(8,128)(2,1)} custom-call(bf16[512,512]{1,0:T(8,128)(2,1)} %constant_dynamic-update-slice_fusion.2.a_ref, bf16[512,512]{1,0:T(8,128)(2,1)} %collective-permute-done.17.b_ref, bf16[512,512]{1,0:T(8,128)(2,1)} %collective-permute-done.14.c_ref, bf16[512,512]{1,0:T(8,128)(2,1)} %collective-permute-done.18.d_ref, ...), custom_call_target="tpu_custom_call" | custom-call | flops 8388608 | bytes 4194304 | tf_op jit(solution)/shard_map/hidden/pallas_call | solution.py:60
  113.9 1.6 copy-done.1
  115.5 1.6 copy-done.2
  117.1 5.0 %attend.3 = bf16[512,256]{1,0:T(8,128)(2,1)} custom-call(s32[8]{0:T(128)S(1)} %fusion.15.slot_ref, bf16[512,2048]{1,0:T(8,128)(2,1)S(1)} %copy-done.1, bf16[8,4,2,32,512]{4,3,2,1,0:T(8,128)(2,1)S(1)} %bitcast.66, bf16[8,2,32,256]{3,2,1,0:T(8,128)(2,1)S(1)} %slice.152.v0, bf16[8,2,32,256]{3,2,1,0:T(8,128)(2,1)S(1)} %collective-permute-done.10.v1, ...), custom_call_target="tpu_custom_call" | custom-call | flops 1744830464 | bytes 6291456 | tf_op jit(solution)/shard_map/attend/pallas_call | solution.py:113
  122.1 1.8 collective-permute-start.20
  124.9 4.7 %hidden.2.hid_ref = bf16[512,2048]{1,0:T(8,128)(2,1)} custom-call(bf16[512,512]{1,0:T(8,128)(2,1)} %bitcast.7.a_ref, bf16[512,512]{1,0:T(8,128)(2,1)} %collective-permute-done.2.b_ref, bf16[512,512]{1,0:T(8,128)(2,1)} %collective-permute-done.3.c_ref, bf16[512,512]{1,0:T(8,128)(2,1)} %collective-permute-done.4.d_ref, bf16[2,3,2048]{2,1,0:T(4,128)(2,1)} %copy.11.mod_ref), custom_call_target="tpu_custom_call" | custom-call | flops 8388608 | bytes 4194304 | tf_op jit(solution)/shard_map/hidden/pallas_call | solution.py:60
  129.7 1.6 copy-done
  131.3 1.6 copy-done.3
  132.9 4.3 %attend.2.own_ref = bf16[512,256]{1,0:T(8,128)(2,1)S(1)} custom-call(s32[8]{0:T(128)S(1)} %fusion.15.slot_ref, bf16[512,2048]{1,0:T(8,128)(2,1)S(1)} %copy-done, bf16[8,4,2,32,512]{4,3,2,1,0:T(8,128)(2,1)S(1)} %bitcast.67, bf16[8,2,32,256]{3,2,1,0:T(8,128)(2,1)S(1)} %slice.152.v0, bf16[8,2,32,256]{3,2,1,0:T(8,128)(2,1)S(1)} %collective-permute-done.10.v1, ...), custom_call_target="tpu_custom_call" | custom-call | flops 1744830464 | bytes 6291456 | tf_op jit(solution)/shard_map/attend/pallas_call | solution.py:113
  138.7 1.4 project.2
  142.8 13.1 %collective-permute-done.27 = bf16[512,512]{1,0:T(8,128)(2,1)S(1)} collective-permute-done((bf16[512,512]{1,0:T(8,128)(2,1)}, bf16[512,512]{1,0:T(8,128)(2,1)S(1)}, u32[]{:S(2)}, u32[]{:S(2)}) %collective-permute-start.27) | collective-permute-done | bytes 524320 | tf_op jit(solution)/shard_map/ppermute | solution.py:26
  156.5 2.3 %collective-permute-start.28 = (bf16[16,6,512]{2,1,0:T(8,128)(2,1)S(1)}, bf16[16,6,512]{2,1,0:T(8,128)(2,1)S(1)}, u32[]{:S(2)}, u32[]{:S(2)}) collective-permute-start(bf16[16,6,512]{2,1,0:T(8,128)(2,1)S(1)} %get-tuple-element.28), channel_id=1, source_target_pairs={{0,4},{4,8},{8,12},{16,20},{20,24},{24,28},{32,36},{36,40},{40,44}... | collective-permute-start | bytes 294920 | tf_op jit(solution)/shard_map/ppermute | solution.py:31
  161.3 4.4 %collective-permute-done.29 = bf16[16,6,512]{2,1,0:T(8,128)(2,1)S(1)} collective-permute-done((bf16[16,6,512]{2,1,0:T(8,128)(2,1)S(1)}, bf16[16,6,512]{2,1,0:T(8,128)(2,1)S(1)}, u32[]{:S(2)}, u32[]{:S(2)}) %collective-permute-start.29) | collective-permute-done | bytes 98336 | tf_op jit(solution)/shard_map/ppermute | solution.py:31
  166.1 4.5 %collective-permute-start.30 = (bf16[2,6,16,512]{3,2,1,0:T(8,128)(2,1)S(1)}, bf16[2,6,16,512]{3,2,1,0:T(8,128)(2,1)S(1)}, u32[]{:S(2)}, u32[]{:S(2)}) collective-permute-start(bf16[2,6,16,512]{3,2,1,0:T(8,128)(2,1)S(1)} %fusion.13), channel_id=1, source_target_pairs={{0,16},{4,20},{8,24},{12,28},{16,32},{20,36},{24,40},{28,44},{32,4... | collective-permute-start | bytes 589832 | tf_op jit(solution)/shard_map/ppermute | solution.py:31
  170.6 13.3 %collective-permute-done.30 = bf16[2,6,16,512]{3,2,1,0:T(8,128)(2,1)S(1)} collective-permute-done((bf16[2,6,16,512]{3,2,1,0:T(8,128)(2,1)S(1)}, bf16[2,6,16,512]{3,2,1,0:T(8,128)(2,1)S(1)}, u32[]{:S(2)}, u32[]{:S(2)}) %collective-permute-start.30) | collective-permute-done | bytes 196640 | tf_op jit(solution)/shard_map/ppermute | solution.py:31
  184.1 2.5 %collective-permute-start.31 = (bf16[2,6,16,512]{3,2,1,0:T(8,128)(2,1)S(1)}, bf16[2,6,16,512]{3,2,1,0:T(8,128)(2,1)S(1)}, u32[]{:S(2)}, u32[]{:S(2)}) collective-permute-start(bf16[2,6,16,512]{3,2,1,0:T(8,128)(2,1)S(1)} %get-tuple-element.14), channel_id=1, source_target_pairs={{16,0},{20,4},{24,8},{28,12},{32,16},{36,20},{40,24},{44,28},{48,3... | collective-permute-start | bytes 589832 | tf_op jit(solution)/shard_map/ppermute | solution.py:31
  186.6 13.1 %collective-permute-done.31 = bf16[2,6,16,512]{3,2,1,0:T(8,128)(2,1)S(1)} collective-permute-done((bf16[2,6,16,512]{3,2,1,0:T(8,128)(2,1)S(1)}, bf16[2,6,16,512]{3,2,1,0:T(8,128)(2,1)S(1)}, u32[]{:S(2)}, u32[]{:S(2)}) %collective-permute-start.31) | collective-permute-done | bytes 196640 | tf_op jit(solution)/shard_map/ppermute | solution.py:31
  205.6 5.2 %collective-permute-done.32 = bf16[2,256,512]{2,1,0:T(8,128)(2,1)S(1)} collective-permute-done((bf16[2,256,512]{2,1,0:T(8,128)(2,1)S(1)}, bf16[2,256,512]{2,1,0:T(8,128)(2,1)S(1)}, u32[]{:S(2)}, u32[]{:S(2)}) %collective-permute-start.32) | collective-permute-done | bytes 524320 | tf_op jit(solution)/shard_map/ppermute | solution.py:26
  (145 shorter events, 34.9 us)
Async XLA Ops:
  6.5 107.4 %all-gather.4.cloned.1.call-start = ((), (), s32[]{:S(2)}) async-start(), calls=%async_computation | async-start | bytes 2359296 | tf_op jit(solution)/shard_map/all_gather | solution.py:222
  8.3 6.1 %collective-permute-start.5 = (bf16[32,1280]{1,0:T(8,128)(2,1)S(1)}, bf16[32,1280]{1,0:T(8,128)(2,1)S(1)}, u32[]{:S(2)}, u32[]{:S(2)}) collective-permute-start(bf16[32,1280]{1,0:T(8,128)(2,1)S(1)} %pad_maximum_fusion.4), channel_id=1, source_target_pairs={{0,128},{128,0},{1,129},{129,1},{2,130},{130,2},{3,131},{131,3},{4... | collective-permute-start | bytes 245768 | tf_op jit(solution)/shard_map/ppermute | solution.py:26
  14.4 10.0 %collective-permute-start.7 = (bf16[2,32,512]{2,1,0:T(8,128)(2,1)S(1)}, bf16[2,32,512]{2,1,0:T(8,128)(2,1)S(1)}, u32[]{:S(2)}, u32[]{:S(2)}) collective-permute-start(bf16[2,32,512]{2,1,0:T(8,128)(2,1)S(1)} %pad_maximum_fusion.5), channel_id=1, source_target_pairs={{0,96},{32,64},{64,32},{96,0},{1,97},{33,65},{65,33},{97,1},{2,98}... | collective-permute-start | bytes 196616 | tf_op jit(solution)/shard_map/ppermute | solution.py:26
  17.3 9.1 %collective-permute-start.6 = (bf16[2,32,512]{2,1,0:T(8,128)(2,1)S(1)}, bf16[2,32,512]{2,1,0:T(8,128)(2,1)S(1)}, u32[]{:S(2)}, u32[]{:S(2)}) collective-permute-start(bf16[2,32,512]{2,1,0:T(8,128)(2,1)S(1)} %pad_maximum_fusion.5), channel_id=1, source_target_pairs={{0,32},{32,0},{64,96},{96,64},{1,33},{33,1},{65,97},{97,65},{2,34}... | collective-permute-start | bytes 196616 | tf_op jit(solution)/shard_map/ppermute | solution.py:26
  24.5 4.0 %collective-permute-start.8 = (bf16[1,32,512]{2,1,0:T(8,128)(2,1)S(1)}, bf16[1,32,512]{2,1,0:T(8,128)(2,1)S(1)}, u32[]{:S(2)}, u32[]{:S(2)}) collective-permute-start(bf16[1,32,512]{2,1,0:T(8,128)(2,1)S(1)} %slice.150), channel_id=1, source_target_pairs={{0,32},{32,0},{64,96},{96,64},{1,33},{33,1},{65,97},{97,65},{2,34}... | collective-permute-start | bytes 98312 | tf_op jit(solution)/shard_map/ppermute | solution.py:26
  26.4 5.2 %collective-permute-start.9 = (bf16[1,32,512]{2,1,0:T(8,128)(2,1)S(1)}, bf16[1,32,512]{2,1,0:T(8,128)(2,1)S(1)}, u32[]{:S(2)}, u32[]{:S(2)}) collective-permute-start(bf16[1,32,512]{2,1,0:T(8,128)(2,1)S(1)} %slice.151), channel_id=1, source_target_pairs={{0,96},{32,64},{64,32},{96,0},{1,97},{33,65},{65,33},{97,1},{2,98}... | collective-permute-start | bytes 98312 | tf_op jit(solution)/shard_map/ppermute | solution.py:26
  32.5 13.9 %collective-permute-start = (bf16[2,256,512]{2,1,0:T(8,128)(2,1)S(1)}, bf16[2,256,512]{2,1,0:T(8,128)(2,1)S(1)}, u32[]{:S(2)}, u32[]{:S(2)}) collective-permute-start(bf16[2,256,512]{2,1,0:T(8,128)(2,1)S(1)} %pad_maximum_fusion.1), channel_id=1, source_target_pairs={{0,4},{4,0},{8,12},{12,8},{16,20},{20,16},{24,28},{28,24},{1,5},{5... | collective-permute-start | bytes 1572872 | tf_op jit(solution)/shard_map/ppermute | solution.py:26
  34.5 10.0 %collective-permute-start.1 = (bf16[1,3,2048]{2,1,0:T(4,128)(2,1)S(1)}, bf16[1,3,2048]{2,1,0:T(4,128)(2,1)S(1)}, u32[]{:S(2)}, u32[]{:S(2)}) collective-permute-start(bf16[1,3,2048]{2,1,0:T(4,128)(2,1)S(1)} %copy-done.11), channel_id=1, source_target_pairs={{0,4},{4,0},{8,12},{12,8},{16,20},{20,16},{24,28},{28,24},{1,5},{5... | collective-permute-start | bytes 36872 | tf_op jit(solution)/shard_map/ppermute | solution.py:26
  44.6 44.9 %collective-permute-start.19 = (bf16[2,3,2048]{2,0,1:T(2,128)(2,1)S(1)}, bf16[2,3,2048]{2,0,1:T(2,128)(2,1)S(1)}, u32[]{:S(2)}, u32[]{:S(2)}) collective-permute-start(bf16[2,3,2048]{2,0,1:T(2,128)(2,1)S(1)} %broadcast_select_fusion.5), channel_id=1, source_target_pairs={{0,128},{128,0},{1,129},{129,1},{2,130},{130,2},{3,131},{131,3},{4... | collective-permute-start | bytes 73736 | tf_op jit(solution)/shard_map/ppermute | solution.py:26
  47.4 41.1 %collective-permute-start.14 = (bf16[512,512]{1,0:T(8,128)(2,1)}, bf16[512,512]{1,0:T(8,128)(2,1)}, u32[]{:S(2)}, u32[]{:S(2)}) collective-permute-start(bf16[512,512]{1,0:T(8,128)(2,1)} %bitcast.7.a_ref), channel_id=1, source_target_pairs={{0,130},{2,128},{128,2},{130,0},{1,131},{3,129},{129,3},{131,1},{4... | collective-permute-start | bytes 1572872 | tf_op jit(solution)/shard_map/ppermute | solution.py:241
  48.7 42.7 %collective-permute-start.3 = (bf16[512,512]{1,0:T(8,128)(2,1)}, bf16[512,512]{1,0:T(8,128)(2,1)}, u32[]{:S(2)}, u32[]{:S(2)}) collective-permute-start(bf16[512,512]{1,0:T(8,128)(2,1)} %bitcast.7.a_ref), channel_id=1, source_target_pairs={{0,2},{2,0},{128,130},{130,128},{1,3},{3,1},{129,131},{131,129},{4... | collective-permute-start | bytes 1572872 | tf_op jit(solution)/shard_map/ppermute | solution.py:240
  84.9 10.4 %collective-permute-start.11 = (bf16[8,2,32,256]{3,2,1,0:T(8,128)(2,1)S(1)}, bf16[8,2,32,256]{3,2,1,0:T(8,128)(2,1)S(1)}, u32[]{:S(2)}, u32[]{:S(2)}) collective-permute-start(bf16[8,2,32,256]{3,2,1,0:T(8,128)(2,1)S(1)} %slice.152.v0), channel_id=1, source_target_pairs={{0,96},{32,64},{64,32},{96,0},{1,97},{33,65},{65,33},{97,1},{2,98}... | collective-permute-start | bytes 786440 | tf_op jit(solution)/shard_map/ppermute | solution.py:26
  85.0 13.8 %collective-permute-start.22 = (bf16[8,2,32,512]{3,2,1,0:T(8,128)(2,1)S(1)}, bf16[8,2,32,512]{3,2,1,0:T(8,128)(2,1)S(1)}, u32[]{:S(2)}, u32[]{:S(2)}) collective-permute-start(bf16[8,2,32,512]{3,2,1,0:T(8,128)(2,1)S(1)} %slice.157.o0), channel_id=1, source_target_pairs={{0,96},{32,64},{64,32},{96,0},{1,97},{33,65},{65,33},{97,1},{2,98}... | collective-permute-start | bytes 1572872 | tf_op jit(solution)/shard_map/ppermute | solution.py:26
  88.5 8.6 %collective-permute-start.10 = (bf16[8,2,32,256]{3,2,1,0:T(8,128)(2,1)S(1)}, bf16[8,2,32,256]{3,2,1,0:T(8,128)(2,1)S(1)}, u32[]{:S(2)}, u32[]{:S(2)}) collective-permute-start(bf16[8,2,32,256]{3,2,1,0:T(8,128)(2,1)S(1)} %slice.152.v0), channel_id=1, source_target_pairs={{0,32},{32,0},{64,96},{96,64},{1,33},{33,1},{65,97},{97,65},{2,34}... | collective-permute-start | bytes 786440 | tf_op jit(solution)/shard_map/ppermute | solution.py:26
  89.5 10.0 %collective-permute-start.15 = (bf16[256,512]{1,0:T(8,128)(2,1)S(1)}, bf16[256,512]{1,0:T(8,128)(2,1)S(1)}, u32[]{:S(2)}, u32[]{:S(2)}) collective-permute-start(bf16[256,512]{1,0:T(8,128)(2,1)S(1)} %slice.155), channel_id=1, source_target_pairs={{0,2},{2,0},{128,130},{130,128},{1,3},{3,1},{129,131},{131,129},{4... | collective-permute-start | bytes 786440 | tf_op jit(solution)/shard_map/ppermute | solution.py:242
  91.4 13.8 %collective-permute-start.21 = (bf16[8,2,32,512]{3,2,1,0:T(8,128)(2,1)S(1)}, bf16[8,2,32,512]{3,2,1,0:T(8,128)(2,1)S(1)}, u32[]{:S(2)}, u32[]{:S(2)}) collective-permute-start(bf16[8,2,32,512]{3,2,1,0:T(8,128)(2,1)S(1)} %slice.157.o0), channel_id=1, source_target_pairs={{0,32},{32,0},{64,96},{96,64},{1,33},{33,1},{65,97},{97,65},{2,34}... | collective-permute-start | bytes 1572872 | tf_op jit(solution)/shard_map/ppermute | solution.py:26
  95.2 7.8 %collective-permute-start.16 = (bf16[256,512]{1,0:T(8,128)(2,1)}, bf16[256,512]{1,0:T(8,128)(2,1)S(1)}, u32[]{:S(2)}, u32[]{:S(2)}) collective-permute-start(bf16[256,512]{1,0:T(8,128)(2,1)} %slice.156), channel_id=1, source_target_pairs={{0,130},{2,128},{128,2},{130,0},{1,131},{3,129},{129,3},{131,1},{4... | collective-permute-start | bytes 786440 | tf_op jit(solution)/shard_map/ppermute | solution.py:243
  97.1 6.7 %collective-permute-start.12 = (bf16[4,2,32,256]{3,2,1,0:T(8,128)(2,1)S(1)}, bf16[4,2,32,256]{3,2,1,0:T(8,128)(2,1)}, u32[]{:S(2)}, u32[]{:S(2)}) collective-permute-start(bf16[4,2,32,256]{3,2,1,0:T(8,128)(2,1)S(1)} %slice.153), channel_id=1, source_target_pairs={{0,32},{32,0},{64,96},{96,64},{1,33},{33,1},{65,97},{97,65},{2,34}... | collective-permute-start | bytes 393224 | tf_op jit(solution)/shard_map/ppermute | solution.py:26
  98.7 6.5 %collective-permute-start.13 = (bf16[4,2,32,256]{3,2,1,0:T(8,128)(2,1)}, bf16[4,2,32,256]{3,2,1,0:T(8,128)(2,1)}, u32[]{:S(2)}, u32[]{:S(2)}) collective-permute-start(bf16[4,2,32,256]{3,2,1,0:T(8,128)(2,1)} %slice.154), channel_id=1, source_target_pairs={{0,96},{32,64},{64,32},{96,0},{1,97},{33,65},{65,33},{97,1},{2,98}... | collective-permute-start | bytes 393224 | tf_op jit(solution)/shard_map/ppermute | solution.py:26
  99.6 8.7 %collective-permute-start.23 = (bf16[4,2,32,512]{3,2,1,0:T(8,128)(2,1)S(1)}, bf16[4,2,32,512]{3,2,1,0:T(8,128)(2,1)S(1)}, u32[]{:S(2)}, u32[]{:S(2)}) collective-permute-start(bf16[4,2,32,512]{3,2,1,0:T(8,128)(2,1)S(1)} %slice.158), channel_id=1, source_target_pairs={{0,32},{32,0},{64,96},{96,64},{1,33},{33,1},{65,97},{97,65},{2,34}... | collective-permute-start | bytes 786440 | tf_op jit(solution)/shard_map/ppermute | solution.py:26
  103.0 6.2 %collective-permute-start.18 = (bf16[512,512]{1,0:T(8,128)(2,1)}, bf16[512,512]{1,0:T(8,128)(2,1)}, u32[]{:S(2)}, u32[]{:S(2)}) collective-permute-start(bf16[512,512]{1,0:T(8,128)(2,1)} %collective-permute-done.14.c_ref), channel_id=1, source_target_pairs={{0,1},{1,0},{2,3},{3,2},{4,5},{5,4},{6,7},{7,6},{8,9},{9,8},{10,11... | collective-permute-start | bytes 1572872 | tf_op jit(solution)/shard_map/ppermute | solution.py:26
  103.8 5.4 %collective-permute-start.17 = (bf16[512,512]{1,0:T(8,128)(2,1)}, bf16[512,512]{1,0:T(8,128)(2,1)}, u32[]{:S(2)}, u32[]{:S(2)}) collective-permute-start(bf16[512,512]{1,0:T(8,128)(2,1)} %constant_dynamic-update-slice_fusion.2.a_ref), channel_id=1, source_target_pairs={{0,1},{1,0},{2,3},{3,2},{4,5},{5,4},{6,7},{7,6},{8,9},{9,8},{10,11... | collective-permute-start | bytes 1572872 | tf_op jit(solution)/shard_map/ppermute | solution.py:26
  105.2 19.7 %collective-permute-start.2 = (bf16[512,512]{1,0:T(8,128)(2,1)}, bf16[512,512]{1,0:T(8,128)(2,1)}, u32[]{:S(2)}, u32[]{:S(2)}) collective-permute-start(bf16[512,512]{1,0:T(8,128)(2,1)} %bitcast.7.a_ref), channel_id=1, source_target_pairs={{0,1},{1,0},{2,3},{3,2},{4,5},{5,4},{6,7},{7,6},{8,9},{9,8},{10,11... | collective-permute-start | bytes 1572872 | tf_op jit(solution)/shard_map/ppermute | solution.py:26
  105.2 19.7 %collective-permute-start.4 = (bf16[512,512]{1,0:T(8,128)(2,1)}, bf16[512,512]{1,0:T(8,128)(2,1)}, u32[]{:S(2)}, u32[]{:S(2)}) collective-permute-start(bf16[512,512]{1,0:T(8,128)(2,1)} %collective-permute-done.3.c_ref), channel_id=1, source_target_pairs={{0,1},{1,0},{2,3},{3,2},{4,5},{5,4},{6,7},{7,6},{8,9},{9,8},{10,11... | collective-permute-start | bytes 1572872 | tf_op jit(solution)/shard_map/ppermute | solution.py:26
  108.3 15.6 %collective-permute-start.24 = (bf16[4,2,32,512]{3,2,1,0:T(8,128)(2,1)}, bf16[4,2,32,512]{3,2,1,0:T(8,128)(2,1)}, u32[]{:S(2)}, u32[]{:S(2)}) collective-permute-start(bf16[4,2,32,512]{3,2,1,0:T(8,128)(2,1)} %slice.159), channel_id=1, source_target_pairs={{0,96},{32,64},{64,32},{96,0},{1,97},{33,65},{65,33},{97,1},{2,98}... | collective-permute-start | bytes 786440 | tf_op jit(solution)/shard_map/ppermute | solution.py:26
  122.1 15.0 %collective-permute-start.20 = (bf16[512,256]{1,0:T(8,128)(2,1)}, bf16[512,256]{1,0:T(8,128)(2,1)S(1)}, u32[]{:S(2)}, u32[]{:S(2)}) collective-permute-start(bf16[512,256]{1,0:T(8,128)(2,1)} %attend.3), channel_id=1, source_target_pairs={{0,128},{128,0},{1,129},{129,1},{2,130},{130,2},{3,131},{131,3},{4... | collective-permute-start | bytes 786440 | tf_op jit(solution)/shard_map/ppermute | solution.py:26
  141.8 14.1 %collective-permute-start.27 = (bf16[512,512]{1,0:T(8,128)(2,1)}, bf16[512,512]{1,0:T(8,128)(2,1)S(1)}, u32[]{:S(2)}, u32[]{:S(2)}) collective-permute-start(bf16[512,512]{1,0:T(8,128)(2,1)} %add_convert_fusion.1), channel_id=1, source_target_pairs={{0,2},{2,0},{1,3},{3,1},{4,6},{6,4},{5,7},{7,5},{8,10},{10,8},{9,1... | collective-permute-start | bytes 1572872 | tf_op jit(solution)/shard_map/ppermute | solution.py:26
  156.5 4.8 %collective-permute-start.28 = (bf16[16,6,512]{2,1,0:T(8,128)(2,1)S(1)}, bf16[16,6,512]{2,1,0:T(8,128)(2,1)S(1)}, u32[]{:S(2)}, u32[]{:S(2)}) collective-permute-start(bf16[16,6,512]{2,1,0:T(8,128)(2,1)S(1)} %get-tuple-element.28), channel_id=1, source_target_pairs={{0,4},{4,8},{8,12},{16,20},{20,24},{24,28},{32,36},{36,40},{40,44}... | collective-permute-start | bytes 294920 | tf_op jit(solution)/shard_map/ppermute | solution.py:31
  158.8 6.9 %collective-permute-start.29 = (bf16[16,6,512]{2,1,0:T(8,128)(2,1)S(1)}, bf16[16,6,512]{2,1,0:T(8,128)(2,1)S(1)}, u32[]{:S(2)}, u32[]{:S(2)}) collective-permute-start(bf16[16,6,512]{2,1,0:T(8,128)(2,1)S(1)} %get-tuple-element.27), channel_id=1, source_target_pairs={{4,0},{8,4},{12,8},{20,16},{24,20},{28,24},{36,32},{40,36},{44,40}... | collective-permute-start | bytes 294920 | tf_op jit(solution)/shard_map/ppermute | solution.py:31
  166.1 17.8 %collective-permute-start.30 = (bf16[2,6,16,512]{3,2,1,0:T(8,128)(2,1)S(1)}, bf16[2,6,16,512]{3,2,1,0:T(8,128)(2,1)S(1)}, u32[]{:S(2)}, u32[]{:S(2)}) collective-permute-start(bf16[2,6,16,512]{3,2,1,0:T(8,128)(2,1)S(1)} %fusion.13), channel_id=1, source_target_pairs={{0,16},{4,20},{8,24},{12,28},{16,32},{20,36},{24,40},{28,44},{32,4... | collective-permute-start | bytes 589832 | tf_op jit(solution)/shard_map/ppermute | solution.py:31
  184.1 15.6 %collective-permute-start.31 = (bf16[2,6,16,512]{3,2,1,0:T(8,128)(2,1)S(1)}, bf16[2,6,16,512]{3,2,1,0:T(8,128)(2,1)S(1)}, u32[]{:S(2)}, u32[]{:S(2)}) collective-permute-start(bf16[2,6,16,512]{3,2,1,0:T(8,128)(2,1)S(1)} %get-tuple-element.14), channel_id=1, source_target_pairs={{16,0},{20,4},{24,8},{28,12},{32,16},{36,20},{40,24},{44,28},{48,3... | collective-permute-start | bytes 589832 | tf_op jit(solution)/shard_map/ppermute | solution.py:31
  199.9 11.0 %collective-permute-start.32 = (bf16[2,256,512]{2,1,0:T(8,128)(2,1)S(1)}, bf16[2,256,512]{2,1,0:T(8,128)(2,1)S(1)}, u32[]{:S(2)}, u32[]{:S(2)}) collective-permute-start(bf16[2,256,512]{2,1,0:T(8,128)(2,1)S(1)} %bitcast.75), channel_id=1, source_target_pairs={{0,4},{4,0},{8,12},{12,8},{16,20},{20,16},{24,28},{28,24},{1,5},{5... | collective-permute-start | bytes 1572872 | tf_op jit(solution)/shard_map/ppermute | solution.py:26
  (15 other events, 238.1 us)
Sparse Core Ops, SparseCore 0:
  32.5 43.9 all-gather.3

commit v2 on v1

v2 whole, which is shorter than its diff:
```python
import functools
import math

import jax
import jax.numpy as jnp
from jax import lax
from jax.experimental import pallas as pl
from jax.experimental.pallas import tpu as pltpu
from jax.sharding import Mesh, PartitionSpec as P

D = 2048
HDIM = 128
S = 16
W = 6
TOK = 256
NARROW = 512
HALF = 256
REGION = ("h", "x", "z")
MP = ("yl", "c")
BF = jnp.bfloat16
F32 = jnp.float32


def xor_swap(block, axis, bit):
    size = math.prod(lax.axis_size(a) for a in ((axis,) if isinstance(axis, str) else axis))
    return lax.ppermute(block, axis, [(i, i ^ bit) for i in range(size)])


def rotate(block, axis, step):
    size = lax.axis_size(axis)
    return lax.ppermute(block, axis, [(i, (i + step) % size) for i in range(size)])


def shift(block, distance, allowed):
    route = [(i, i + distance) for i in range(64) if 0 <= i + distance < 64 and allowed(i)]
    return lax.ppermute(block, REGION, route)


def opposite(near, side, axis, split_axis):
    size = near.shape[split_axis]
    first = xor_swap(lax.slice_in_dim(side, 0, size // 2, axis=split_axis), axis, 1)
    second = xor_swap(lax.slice_in_dim(near, size // 2, size, axis=split_axis), axis, 3)
    return jnp.concatenate([first, second], axis=split_axis)


def ring_of_four(block, axis, split_axis):
    near = xor_swap(block, axis, 1)
    side = xor_swap(block, axis, 3)
    return block, near, opposite(near, side, axis, split_axis), side


def ring_of_eight(block, axis):
    up = [rotate(block, axis, 1)]
    down = [rotate(block, axis, -1)]
    for _ in range(2):
        up.append(rotate(up[-1], axis, 1))
        down.append(rotate(down[-1], axis, -1))
    across = jnp.concatenate([rotate(up[2][:1], axis, 1), rotate(down[2][1:], axis, -1)], axis=0)
    return [block] + up + [across] + down[::-1]


def where_am_i():
    h, x, z = (lax.axis_index(a) for a in REGION)
    yl, c = (lax.axis_index(a) for a in MP)
    return h, x, z, yl, c


def even_count(counts_ref):
    h, x, z, _, _ = where_am_i()
    return counts_ref[h * 32 + x * 8 + (z // 2) * 2]


SMEM = pl.BlockSpec(memory_space=pltpu.SMEM)
VMEM = pl.BlockSpec(memory_space=pltpu.VMEM)
HBM = pl.BlockSpec(memory_space=pltpu.HBM)


def cost(flops, size, special=0):
    return pl.CostEstimate(flops=flops, bytes_accessed=size, transcendentals=special)


def pack_kernel(qkv_ref, out_ref, own_qk, own_vo, sent):
    h = lax.axis_index("h")
    mine = pl.ds(pl.multiple_of(h * HALF, HALF), HALF)
    theirs = pl.ds(pl.multiple_of((1 - h) * HALF, HALF), HALF)
    own_qk[:, :HALF] = qkv_ref[0, :, mine]
    own_qk[:, HALF:] = qkv_ref[1, :, mine]
    own_vo[:, :HALF] = qkv_ref[2, :, mine]
    own_vo[:, HALF : 2 * HALF] = out_ref[:, mine]
    own_vo[:, 2 * HALF :] = out_ref[:, theirs]
    for n in range(3):
        sent[:, n * HALF : (n + 1) * HALF] = qkv_ref[n, :, theirs]
    sent[:, 3 * HALF : 4 * HALF] = out_ref[:, theirs]
    sent[:, 4 * HALF :] = out_ref[:, mine]


def packed(qkv, out):
    return pl.pallas_call(
        pack_kernel,
        in_specs=[VMEM, VMEM],
        out_specs=[VMEM] * 3,
        out_shape=[jax.ShapeDtypeStruct((32, n * HALF), BF) for n in (2, 3, 5)],
        cost_estimate=cost(0, 2**18),
        name="pack",
    )(qkv, out)


def split_kernel(counts_ref, data_ref, sent_ref, kept_ref, sem):
    even = even_count(counts_ref)
    odd = lax.axis_index("z") % 2 == 1
    copies = []
    for s in range(2):
        away = jnp.where(odd, jnp.clip(s - even, 0, 3), 2 + s)
        stays = jnp.where(odd, jnp.clip(2 + s - even, 0, 3), s)
        copies.append(pltpu.make_async_copy(data_ref.at[away], sent_ref.at[s], sem))
        copies.append(pltpu.make_async_copy(data_ref.at[stays], kept_ref.at[s], sem))
    for copy in copies:
        copy.start()
    for copy in copies:
        copy.wait()


def split_tiles(counts, data):
    return pl.pallas_call(
        split_kernel,
        in_specs=[SMEM, HBM],
        out_specs=[VMEM, VMEM],
        out_shape=[jax.ShapeDtypeStruct((2, TOK, NARROW), BF)] * 2,
        scratch_shapes=[pltpu.SemaphoreType.DMA],
        cost_estimate=cost(0, 2**21),
        name="split",
    )(counts, data)


def choose_kernel(counts_ref, kept, came, mod, other_mod, tiles, mods, gate):
    even = even_count(counts_ref)
    odd = lax.axis_index("z") % 2 == 1
    place = lax.axis_index("yl") * 2 + lax.axis_index("c")
    cols = pl.ds(pl.multiple_of(place * NARROW, NARROW), NARROW)
    for s in range(2):
        use_other = jnp.where(odd, 2 + s < even, s >= even)

        @pl.when(use_other)
        def _():
            tiles[s] = came[s]
            mods[s] = other_mod[0]
            gate[s] = other_mod[0, 2:3, cols].astype(F32)

        @pl.when(jnp.logical_not(use_other))
        def _():
            tiles[s] = kept[s]
            mods[s] = mod[0]
            gate[s] = mod[0, 2:3, cols].astype(F32)


def choose(counts, kept, came, mod, other_mod):
    return pl.pallas_call(
        choose_kernel,
        in_specs=[SMEM] + [VMEM] * 4,
        out_specs=[VMEM] * 3,
        out_shape=[
            jax.ShapeDtypeStruct((2, TOK, NARROW), BF),
            jax.ShapeDtypeStruct((2, 3, D), BF),
            jax.ShapeDtypeStruct((2, 1, NARROW), F32),
        ],
        cost_estimate=cost(0, 2**21),
        name="choose",
    )(counts, kept, came, mod, other_mod)


def hidden_kernel(a_ref, b_ref, c_ref, d_ref, mod_ref, out_ref):
    place = lax.axis_index("yl") * 2 + lax.axis_index("c")
    parts = [r[...].astype(F32) for r in (a_ref, b_ref, c_ref, d_ref)]
    mean = sum(jnp.sum(p, axis=-1, keepdims=True) for p in parts) * (1.0 / D)
    parts = [p - mean for p in parts]
    spread = sum(jnp.sum(p * p, axis=-1, keepdims=True) for p in parts) * (1.0 / D)
    scale = lax.rsqrt(spread + 1e-06)
    for j, p in enumerate(parts):
        source = pl.ds(pl.multiple_of((place ^ j) * NARROW, NARROW), NARROW)
        gain = 1.0 + mod_ref[0, 1:2, source].astype(F32)
        value = p * scale * gain + mod_ref[0, 0:1, source].astype(F32)
        out_ref[:, j * NARROW : (j + 1) * NARROW] = value.astype(BF)


def hidden_of(pieces, mods):
    rows = 128
    piece = pl.BlockSpec((rows, NARROW), lambda i: (i, 0))
    return pl.pallas_call(
        hidden_kernel,
        grid=(512 // rows,),
        in_specs=[piece] * 4 + [pl.BlockSpec((1, 3, D), lambda i: (i * rows // TOK, 0, 0))],
        out_specs=pl.BlockSpec((rows, D), lambda i: (i, 0)),
        out_shape=jax.ShapeDtypeStruct((512, D), BF),
        cost_estimate=cost(8 * 512 * D, 4 * 512 * D, 512),
        name="hidden",
    )(*pieces, mods)


def slot_of(hr, xr):
    h, x, _, yl, c = where_am_i()
    px = x ^ xr
    return ((h ^ hr ^ yl) * 2 + ((px // 2) ^ c)) * 2 + px % 2


def attend_kernel(hid_hbm, qk_ref, v0, v1, v2, v3, out_ref, hid_ref, w_ref, hid_sem, sem):
    z = lax.axis_index("z")
    load = pltpu.make_async_copy(hid_hbm, hid_ref, hid_sem)
    load.start()
    copies = []
    for hr in range(2):
        for xr, v in enumerate((v0, v1, v2, v3)):
            slot = slot_of(hr, xr)
            copies.append(
                pltpu.make_async_copy(
                    qk_ref.at[:, xr, hr], w_ref.at[slot, :, :, pl.ds(0, 2 * HALF)], sem
                )
            )
            for s in range(8):
                copies.append(
                    pltpu.make_async_copy(
                        v.at[s, hr],
                        w_ref.at[slot, (z + 8 - s) % 8, :, pl.ds(2 * HALF, HALF)],
                        sem,
                    )
                )
    for copy in copies:
        copy.start()
    load.wait()
    for copy in copies:
        copy.wait()
    weight = w_ref[...].reshape(D, 3 * HALF)
    for t in range(2):
        rows = slice(t * TOK, (t + 1) * TOK)
        proj = jnp.dot(hid_ref[rows, :], weight, preferred_element_type=F32).astype(BF)
        for n in range(2):
            q = proj[:, n * HDIM : (n + 1) * HDIM]
            k = proj[:, HALF + n * HDIM : HALF + (n + 1) * HDIM]
            v = proj[:, 2 * HALF + n * HDIM : 2 * HALF + (n + 1) * HDIM]
            scores = lax.dot_general(
                q, k, (((1,), (1,)), ((), ())), preferred_element_type=F32
            ) * (1.0 / math.sqrt(HDIM))
            top = jnp.max(scores, axis=-1, keepdims=True)
            e = jnp.exp(scores - top)
            probs = (e / jnp.sum(e, axis=-1, keepdims=True)).astype(BF)
            got = jnp.dot(probs, v, preferred_element_type=F32)
            out_ref[rows, n * HDIM : (n + 1) * HDIM] = got.astype(BF)


def attended_of(hidden, qk, vs):
    return pl.pallas_call(
        attend_kernel,
        in_specs=[HBM] * 6,
        out_specs=VMEM,
        out_shape=jax.ShapeDtypeStruct((512, HALF), BF),
        scratch_shapes=[
            pltpu.VMEM((512, D), BF),
            pltpu.VMEM((8, 8, 32, 3 * HALF), BF),
            pltpu.SemaphoreType.DMA,
            pltpu.SemaphoreType.DMA,
        ],
        compiler_params=pltpu.CompilerParams(vmem_limit_bytes=32 * 2**20),
        cost_estimate=cost(
            2 * 512 * D * 768 + 4 * 4 * TOK * TOK * HDIM, 6 * 2**20, 4 * TOK * TOK
        ),
        name="attend",
    )(hidden, qk, *vs)


def project_kernel(far, own_ref, other_ref, o0, o1, o2, o3, *rest):
    keep, send, (w_ref, sem) = rest[:2], rest[2:4], rest[4:]
    h, x, z, yl, c = where_am_i()
    copies = []
    for xr, piece in enumerate((o0, o1, o2, o3)):
        px = x ^ xr
        slot = ((px // 2) ^ c) * 2 + px % 2
        for s in range(8):
            copies.append(
                pltpu.make_async_copy(
                    piece.at[s, yl ^ far ^ h], w_ref.at[slot, (z + 8 - s) % 8], sem
                )
            )
    for copy in copies:
        copy.start()
    for copy in copies:
        copy.wait()
    for b, outs in ((1, send), (0, keep)):
        for f in range(2):
            weight = w_ref[2 * b + f].reshape(HALF, NARROW)
            total = lax.dot_general(
                own_ref[...], weight[:, :HALF], (((1,), (1,)), ((), ())), preferred_element_type=F32
            ) + lax.dot_general(
                other_ref[...], weight[:, HALF:], (((1,), (1,)), ((), ())), preferred_element_type=F32
            )
            outs[f][...] = total.astype(BF)


def partial_of(far, own, other, os):
    got = pl.pallas_call(
        functools.partial(project_kernel, far),
        in_specs=[VMEM, VMEM] + [HBM] * 4,
        out_specs=[VMEM] * 4,
        out_shape=[jax.ShapeDtypeStruct((512, HALF), BF)] * 4,
        scratch_shapes=[pltpu.VMEM((4, 8, 32, NARROW), BF), pltpu.SemaphoreType.DMA],
        compiler_params=pltpu.CompilerParams(vmem_limit_bytes=32 * 2**20),
        cost_estimate=cost(2 * 512 * 512 * 1024, 3 * 2**20),
        name="project",
    )(own, other, *os)
    return got[:2], got[2:]


def place_kernel(counts_ref, own0, own1, other0, other1, out_ref, zero_ref, sem):
    even = even_count(counts_ref)
    parity = lax.axis_index("z") % 2
    zero_ref[...] = jnp.zeros_like(zero_ref)
    waits = []
    for slot in range(4):
        tile = slot + parity * even
        live = jnp.where(parity == 1, tile < 4, slot < even)
        ours = tile // 2 == parity
        for f, (own, other) in enumerate(((own0, other0), (own1, other1))):
            target = out_ref.at[slot, :, pl.ds(f * HALF, HALF)]

            @pl.when(live & ours)
            def _():
                pltpu.make_async_copy(own.at[tile % 2], target, sem).start()

            @pl.when(live & jnp.logical_not(ours))
            def _():
                pltpu.make_async_copy(other.at[tile % 2], target, sem).start()

            @pl.when(jnp.logical_not(live))
            def _():
                pltpu.make_async_copy(zero_ref, target, sem).start()

            waits.append(pltpu.make_async_copy(zero_ref, target, sem))
    for wait in waits:
        wait.wait()


def place_tiles(counts, own, other):
    return pl.pallas_call(
        place_kernel,
        in_specs=[SMEM] + [VMEM] * 4,
        out_specs=HBM,
        out_shape=jax.ShapeDtypeStruct((4, TOK, NARROW), BF),
        scratch_shapes=[pltpu.VMEM((TOK, HALF), BF), pltpu.SemaphoreType.DMA],
        cost_estimate=cost(0, 2**21),
        name="place",
    )(counts, *own, *other)


def mix(earlier, later, share):
    return (1.0 - share) * earlier.astype(F32) + share * later.astype(F32)


def join_columns(grid, region, shares):
    share = shares.reshape(1, W, 1)
    west, east = grid[:, :, :W], grid[:, :, S - W :]
    later = shift(west[0], -1, lambda i: i % 4 != 0)
    earlier = shift(east[1], 1, lambda i: i % 4 != 3)
    place = region % 4
    inner = mix(east[0], west[1], share).astype(BF)
    left = jnp.where(place != 0, mix(earlier, west[0], share).astype(BF), west[0])
    right = jnp.where(place != 3, mix(east[1], later, share).astype(BF), east[1])
    middle = grid[:, :, W : S - W]
    first = jnp.concatenate([left, middle[0], inner], axis=1)
    second = jnp.concatenate([inner, middle[1], right], axis=1)
    return jnp.stack([first, second])


def join_rows(grid, region, shares):
    share = shares.reshape(1, W, 1, 1)
    north, south = grid[:, :W], grid[:, S - W :]
    later = shift(north, -4, lambda i: True)
    earlier = shift(south, 4, lambda i: True)
    top = jnp.where(region >= 4, mix(earlier, north, share).astype(BF), north)
    bottom = jnp.where(region < 60, mix(south, later, share).astype(BF), south)
    return jnp.concatenate([top, grid[:, W : S - W], bottom], axis=1)


def on_device(tile_data, tile_counts, modulation, qkv_weight, out_weight, blend_weights):
    h, x, z, _, _ = where_am_i()
    region = h * 32 + x * 8 + z

    own_qk, own_vo, sent = packed(qkv_weight.transpose(1, 0, 2), out_weight)
    came = xor_swap(sent, "h", 1)
    qk_block = jnp.stack([own_qk, came[:, : 2 * HALF]])
    vo_block = jnp.stack([own_vo, came[:, 2 * HALF :]])
    qk_all = lax.all_gather(jnp.stack(ring_of_four(qk_block, "x", 0)), "z", axis=0)
    vo_z = ring_of_eight(vo_block, "z")
    v_all = ring_of_four(jnp.stack([b[..., :HALF] for b in vo_z]), "x", 0)
    o_all = ring_of_four(jnp.stack([b[..., HALF:] for b in vo_z]), "x", 0)

    away, kept = split_tiles(tile_counts, tile_data)
    tiles, mods, gate = choose(
        tile_counts, kept, xor_swap(away, "z", 1), modulation, xor_swap(modulation, "z", 1)
    )

    ring = ("h", "yl")
    mine = tiles.reshape(512, NARROW)
    _, near, across, side = ring_of_four(mine, ring, 0)
    mods_across = xor_swap(mods, "h", 1)
    hid_other = hidden_of(
        (across, xor_swap(across, "c", 1), side, xor_swap(side, "c", 1)), mods_across
    )
    hid_own = hidden_of((mine, xor_swap(mine, "c", 1), near, xor_swap(near, "c", 1)), mods)

    att_sent = attended_of(hid_other, qk_all, v_all)
    att_other = opposite(xor_swap(att_sent, ring, 1), xor_swap(att_sent, ring, 3), ring, 0)
    att_own = attended_of(hid_own, qk_all, v_all)

    far_keep, far_send = partial_of(1, att_own, att_other, o_all)
    far = [
        xor_swap((k.astype(F32) + xor_swap(s, "c", 1).astype(F32)).astype(BF), "yl", 1)
        for k, s in zip(far_keep, far_send)
    ]
    keep, send = partial_of(0, att_own, att_other, o_all)
    own, other = [], []
    for f in range(2):
        cols = slice(f * HALF, (f + 1) * HALF)
        summed = sum(p.astype(F32) for p in (keep[f], xor_swap(send[f], "c", 1), far[f]))
        updated = tiles[:, :, cols].astype(F32) + gate[:, :, cols] * summed.reshape(2, TOK, HALF)
        grid = updated.astype(BF).reshape(2, S, S, HALF)
        grid = join_columns(grid, region, blend_weights)
        grid = join_rows(grid, region, blend_weights).reshape(2, TOK, HALF)
        own.append(grid)
        other.append(xor_swap(grid, "z", 1))
    return place_tiles(tile_counts, own, other)


def solution(mesh):
    fine = Mesh(mesh.devices.reshape(2, 4, 8, 2, 2), REGION + MP)
    return jax.shard_map(
        on_device,
        mesh=fine,
        in_specs=(
            P(REGION, None, MP),
            P(),
            P(REGION, None, None),
            P(REGION, None, MP),
            P(REGION, MP),
            P(),
        ),
        out_specs=P(REGION, None, MP),
        check_vma=False,
    )
```

time: 220 us -> 243 us (1.10)
  the two profiles are of different devices: /device:TPU:24 before, /device:TPU:80 now
where the time goes in v2:
time: 243 us; the launch traced here: 238 us
  starting transfers between devices  98 us (40%)
  waiting for transfers between devices  73.4 us (30%)
  Pallas kernels  31.4 us (13%)
  local copies, waits for them, and re-layouts  15.2 us (6%)
  between operations  14.3 us (6%)
  other arithmetic  6.28 us (3%)
    ppermute x36, starting transfers between devices, xor_swap(): return lax.ppermute(block, axis, [(i, i ^ bit) for i in range(size)])  51.7 us
    ppermute x36, waiting for transfers between devices, xor_swap(): return lax.ppermute(block, axis, [(i, i ^ bit) for i in range(size)])  38.4 us
    ppermute x8, starting transfers between devices, shift(): return lax.ppermute(block, REGION, route)  33.1 us
    ppermute x8, waiting for transfers between devices, shift(): return lax.ppermute(block, REGION, route)  22.1 us
    ppermute x8, starting transfers between devices, rotate(): lax.ppermute(block, axis, [(i, (i + step) % size) for i in range(size)])  13.3 us
    ppermute x8, waiting for transfers between devices, rotate(): lax.ppermute(block, axis, [(i, (i + step) % size) for i in range(size)])  12.9 us
    unnamed x52, local copies, waits for them, and re-layouts  9.74 us
    pallas_call x2, Pallas kernels, hidden_of(): pl.pallas_call(hidden_kernel, grid=(512 // rows,), in_specs=[piece] * 4 +...  9.47 us
  transfers between devices with their start and end apart: 53, of which 26 were waited for; matrix products, arithmetic and copies ran while one was open for 4% of the time, Pallas kernels for 11%

profile of v2, /device:TPU:80, one launch (start us, length us, event | category | flops | bytes accessed | tf_op | source)
XLA Modules:
  0.0 238.5 jit_solution(18252579093374530510)
XLA Ops:
  8.4 2.9 %split.1 = (bf16[2,256,512]{2,1,0:T(8,128)(2,1)}, bf16[2,256,512]{2,1,0:T(8,128)(2,1)}) custom-call(s32[64]{0:T(128)} %counts_ref.5, bf16[4,256,512]{2,1,0:T(8,128)(2,1)} %data_ref.1), custom_call_target="tpu_custom_call" | custom-call | bytes 2097152 | tf_op jit(solution)/shard_map/split/pallas_call | solution.py:124
  15.0 2.8 %collective-permute-start.7 = (bf16[2,32,512]{2,1,0:T(8,128)(2,1)S(1)}, bf16[2,32,512]{2,1,0:T(8,128)(2,1)S(1)}, u32[]{:S(2)}, u32[]{:S(2)}) collective-permute-start(bf16[2,32,512]{2,1,0:T(8,128)(2,1)S(1)} %get-tuple-element.60), channel_id=1, source_target_pairs={{0,96},{32,64},{64,32},{96,0},{1,97},{33,65},{65,33},{97,1},{2,98}... | collective-permute-start | bytes 196616 | tf_op jit(solution)/shard_map/ppermute | solution.py:26
  29.3 2.1 collective-permute-start.11
  32.0 2.6 %collective-permute-done.11 = bf16[2,32,768]{2,1,0:T(8,128)(2,1)S(1)} collective-permute-done((bf16[2,32,768]{2,1,0:T(8,128)(2,1)S(1)}, bf16[2,32,768]{2,1,0:T(8,128)(2,1)S(1)}, u32[]{:S(2)}, u32[]{:S(2)}) %collective-permute-start.11) | collective-permute-done | bytes 98336 | tf_op jit(solution)/shard_map/ppermute | solution.py:31
  34.6 3.6 %collective-permute-start.12 = (bf16[2,32,768]{2,1,0:T(8,128)(2,1)S(1)}, bf16[2,32,768]{2,1,0:T(8,128)(2,1)S(1)}, u32[]{:S(2)}, u32[]{:S(2)}) collective-permute-start(bf16[2,32,768]{2,1,0:T(8,128)(2,1)S(1)} %collective-permute-done.11), channel_id=1, source_target_pairs={{0,4},{4,8},{8,12},{12,16},{16,20},{20,24},{24,28},{28,0},{1,5},{5... | collective-permute-start | bytes 294920 | tf_op jit(solution)/shard_map/ppermute | solution.py:31
  40.4 5.5 %collective-permute-start.13 = (bf16[1,32,768]{2,1,0:T(8,128)(2,1)S(1)}, bf16[1,32,768]{2,1,0:T(8,128)(2,1)S(1)}, u32[]{:S(2)}, u32[]{:S(2)}) collective-permute-start(bf16[1,32,768]{2,1,0:T(8,128)(2,1)S(1)} %slice.243), channel_id=1, source_target_pairs={{0,4},{4,8},{8,12},{12,16},{16,20},{20,24},{24,28},{28,0},{1,5},{5... | collective-permute-start | bytes 147464 | tf_op jit(solution)/shard_map/ppermute | solution.py:31
  48.3 4.0 %collective-permute-done.17 = bf16[1,32,768]{2,1,0:T(8,128)(2,1)S(1)} collective-permute-done((bf16[1,32,768]{2,1,0:T(8,128)(2,1)S(1)}, bf16[1,32,768]{2,1,0:T(8,128)(2,1)S(1)}, u32[]{:S(2)}, u32[]{:S(2)}) %collective-permute-start.17) | collective-permute-done | bytes 49184 | tf_op jit(solution)/shard_map/ppermute | solution.py:31
  61.5 5.7 %collective-permute-done.22.c_ref = bf16[512,512]{1,0:T(8,128)(2,1)S(1)} collective-permute-done((bf16[512,512]{1,0:T(8,128)(2,1)}, bf16[512,512]{1,0:T(8,128)(2,1)S(1)}, u32[]{:S(2)}, u32[]{:S(2)}) %collective-permute-start.22) | collective-permute-done | bytes 524320 | tf_op jit(solution)/shard_map/ppermute | solution.py:26
  70.2 2.7 %collective-permute-start.24 = (bf16[256,512]{1,0:T(8,128)(2,1)S(1)}, bf16[256,512]{1,0:T(8,128)(2,1)S(1)}, u32[]{:S(2)}, u32[]{:S(2)}) collective-permute-start(bf16[256,512]{1,0:T(8,128)(2,1)S(1)} %slice.252), channel_id=1, source_target_pairs={{0,130},{2,128},{128,2},{130,0},{1,131},{3,129},{129,3},{131,1},{4... | collective-permute-start | bytes 786440 | tf_op jit(solution)/shard_map/ppermute | solution.py:26
  75.0 2.3 collective-permute-done.24
  79.2 7.7 %collective-permute-done.20 = bf16[4,2,32,256]{3,2,1,0:T(8,128)(2,1)S(1)} collective-permute-done((bf16[4,2,32,256]{3,2,1,0:T(8,128)(2,1)S(1)}, bf16[4,2,32,256]{3,2,1,0:T(8,128)(2,1)S(1)}, u32[]{:S(2)}, u32[]{:S(2)}) %collective-permute-start.20) | collective-permute-done | bytes 131104 | tf_op jit(solution)/shard_map/ppermute | solution.py:26
  88.1 3.6 %collective-permute-start.27 = (bf16[2,3,2048]{2,1,0:T(4,128)(2,1)S(1)}, bf16[2,3,2048]{2,1,0:T(4,128)(2,1)S(1)}, u32[]{:S(2)}, u32[]{:S(2)}) collective-permute-start(bf16[2,3,2048]{2,1,0:T(4,128)(2,1)S(1)} %copy-done.12), channel_id=1, source_target_pairs={{0,128},{128,0},{1,129},{129,1},{2,130},{130,2},{3,131},{131,3},{4... | collective-permute-start | bytes 73736 | tf_op jit(solution)/shard_map/ppermute | solution.py:26
  96.6 4.7 %hidden.3.hid_hbm = bf16[512,2048]{1,0:T(8,128)(2,1)} custom-call(bf16[512,512]{1,0:T(8,128)(2,1)} %copy-done.5, bf16[512,512]{1,0:T(8,128)(2,1)} %collective-permute-done.25.b_ref, bf16[512,512]{1,0:T(8,128)(2,1)} %copy-done.4, bf16[512,512]{1,0:T(8,128)(2,1)} %copy-done.9, bf16[2,3,2048]{2,1,0:T(4,128)(2,1)} %copy-done.13), custom_call_target="tpu_custom_call" | custom-call | flops 8388608 | bytes 4194304 | tf_op jit(solution)/shard_map/hidden/pallas_call | solution.py:188
  104.5 4.4 %attend.3 = bf16[512,256]{1,0:T(8,128)(2,1)S(1)} custom-call(bf16[512,2048]{1,0:T(8,128)(2,1)S(1)} %copy-done.1, bf16[8,4,2,32,512]{4,3,2,1,0:T(8,128)(2,1)S(1)} %bitcast.141, bf16[8,2,32,256]{3,2,1,0:T(8,128)(2,1)S(1)} %constant_dynamic-update-slice_fusion.2.v0, bf16[8,2,32,256]{3,2,1,0:T(8,128)(2,1)S(1)} %collective-permute-done.18.v1, ...), custom_call_target="tpu_custom_call" | custom-call | flops 1744830464 | bytes 6291456 | tf_op jit(solution)/shard_map/attend/pallas_call | solution.py:250
  108.9 11.5 %collective-permute-start.28 = (bf16[512,256]{1,0:T(8,128)(2,1)S(1)}, bf16[512,256]{1,0:T(8,128)(2,1)}, u32[]{:S(2)}, u32[]{:S(2)}) collective-permute-start(bf16[512,256]{1,0:T(8,128)(2,1)S(1)} %attend.3), channel_id=1, source_target_pairs={{0,130},{2,128},{128,2},{130,0},{1,131},{3,129},{129,3},{131,1},{4... | collective-permute-start | bytes 786440 | tf_op jit(solution)/shard_map/ppermute | solution.py:26
  120.5 2.6 %collective-permute-start.30 = (bf16[512,256]{1,0:T(8,128)(2,1)S(1)}, bf16[512,256]{1,0:T(8,128)(2,1)}, u32[]{:S(2)}, u32[]{:S(2)}) collective-permute-start(bf16[512,256]{1,0:T(8,128)(2,1)S(1)} %attend.3), channel_id=1, source_target_pairs={{0,2},{2,0},{128,130},{130,128},{1,3},{3,1},{129,131},{131,129},{4... | collective-permute-start | bytes 786440 | tf_op jit(solution)/shard_map/ppermute | solution.py:26
  125.1 4.7 %hidden.2.hid_hbm = bf16[512,2048]{1,0:T(8,128)(2,1)} custom-call(bf16[512,512]{1,0:T(8,128)(2,1)} %bitcast.a_ref, bf16[512,512]{1,0:T(8,128)(2,1)} %collective-permute-done.2.b_ref, bf16[512,512]{1,0:T(8,128)(2,1)} %collective-permute-done.3.c_ref, bf16[512,512]{1,0:T(8,128)(2,1)} %collective-permute-done.4.d_ref, bf16[2,3,2048]{2,1,0:T(4,128)(2,1)} %get-tuple-element.25.mod_ref), custom_call_target="tpu_custom_call" | custom-call | flops 8388608 | bytes 4194304 | tf_op jit(solution)/shard_map/hidden/pallas_call | solution.py:188
  131.8 2.4 %collective-permute-start.31 = (bf16[256,256]{1,0:T(8,128)(2,1)S(1)}, bf16[256,256]{1,0:T(8,128)(2,1)S(1)}, u32[]{:S(2)}, u32[]{:S(2)}) collective-permute-start(bf16[256,256]{1,0:T(8,128)(2,1)S(1)} %slice.254), channel_id=1, source_target_pairs={{0,130},{2,128},{128,2},{130,0},{1,131},{3,129},{129,3},{131,1},{4... | collective-permute-start | bytes 393224 | tf_op jit(solution)/shard_map/ppermute | solution.py:26
  137.4 4.4 %attend.2.own_ref = bf16[512,256]{1,0:T(8,128)(2,1)S(1)} custom-call(bf16[512,2048]{1,0:T(8,128)(2,1)S(1)} %copy-done, bf16[8,4,2,32,512]{4,3,2,1,0:T(8,128)(2,1)S(1)} %bitcast.142, bf16[8,2,32,256]{3,2,1,0:T(8,128)(2,1)S(1)} %constant_dynamic-update-slice_fusion.2.v0, bf16[8,2,32,256]{3,2,1,0:T(8,128)(2,1)S(1)} %collective-permute-done.18.v1, ...), custom_call_target="tpu_custom_call" | custom-call | flops 1744830464 | bytes 6291456 | tf_op jit(solution)/shard_map/attend/pallas_call | solution.py:250
  141.9 2.2 project.3
  149.8 7.0 %collective-permute-done.38 = bf16[512,256]{1,0:T(8,128)(2,1)S(1)} collective-permute-done((bf16[512,256]{1,0:T(8,128)(2,1)S(1)}, bf16[512,256]{1,0:T(8,128)(2,1)S(1)}, u32[]{:S(2)}, u32[]{:S(2)}) %collective-permute-start.38) | collective-permute-done | bytes 262176 | tf_op jit(solution)/shard_map/ppermute | solution.py:26
  156.9 4.7 %collective-permute-done.45 = bf16[512,256]{1,0:T(8,128)(2,1)S(1)} collective-permute-done((bf16[512,256]{1,0:T(8,128)(2,1)S(1)}, bf16[512,256]{1,0:T(8,128)(2,1)S(1)}, u32[]{:S(2)}, u32[]{:S(2)}) %collective-permute-start.45) | collective-permute-done | bytes 262176 | tf_op jit(solution)/shard_map/ppermute | solution.py:26
  163.0 5.5 %collective-permute-start.39 = (bf16[16,6,256]{2,1,0:T(8,128)(2,1)S(1)}, bf16[16,6,256]{2,1,0:T(8,128)(2,1)S(1)}, u32[]{:S(2)}, u32[]{:S(2)}) collective-permute-start(bf16[16,6,256]{2,1,0:T(8,128)(2,1)S(1)} %get-tuple-element.54), channel_id=1, source_target_pairs={{0,4},{4,8},{8,12},{16,20},{20,24},{24,28},{32,36},{36,40},{40,44}... | collective-permute-start | bytes 147464 | tf_op jit(solution)/shard_map/ppermute | solution.py:36
  170.5 3.9 %collective-permute-start.46 = (bf16[16,6,256]{2,1,0:T(8,128)(2,1)S(1)}, bf16[16,6,256]{2,1,0:T(8,128)(2,1)S(1)}, u32[]{:S(2)}, u32[]{:S(2)}) collective-permute-start(bf16[16,6,256]{2,1,0:T(8,128)(2,1)S(1)} %get-tuple-element.50), channel_id=1, source_target_pairs={{0,4},{4,8},{8,12},{16,20},{20,24},{24,28},{32,36},{36,40},{40,44}... | collective-permute-start | bytes 147464 | tf_op jit(solution)/shard_map/ppermute | solution.py:36
  176.6 3.9 %collective-permute-done.47 = bf16[16,6,256]{2,1,0:T(8,128)(2,1)S(1)} collective-permute-done((bf16[16,6,256]{2,1,0:T(8,128)(2,1)S(1)}, bf16[16,6,256]{2,1,0:T(8,128)(2,1)S(1)}, u32[]{:S(2)}, u32[]{:S(2)}) %collective-permute-start.47) | collective-permute-done | bytes 49184 | tf_op jit(solution)/shard_map/ppermute | solution.py:36
  183.0 8.7 %collective-permute-start.48 = (bf16[2,6,16,256]{3,2,1,0:T(8,128)(2,1)S(1)}, bf16[2,6,16,256]{3,2,1,0:T(8,128)(2,1)S(1)}, u32[]{:S(2)}, u32[]{:S(2)}) collective-permute-start(bf16[2,6,16,256]{3,2,1,0:T(8,128)(2,1)S(1)} %fusion.20), channel_id=1, source_target_pairs={{0,16},{4,20},{8,24},{12,28},{16,32},{20,36},{24,40},{28,44},{32,4... | collective-permute-start | bytes 294920 | tf_op jit(solution)/shard_map/ppermute | solution.py:36
  191.7 5.8 %collective-permute-done.41 = bf16[2,6,16,256]{3,2,1,0:T(8,128)(2,1)S(1)} collective-permute-done((bf16[2,6,16,256]{3,2,1,0:T(8,128)(2,1)S(1)}, bf16[2,6,16,256]{3,2,1,0:T(8,128)(2,1)S(1)}, u32[]{:S(2)}, u32[]{:S(2)}) %collective-permute-start.41) | collective-permute-done | bytes 98336 | tf_op jit(solution)/shard_map/ppermute | solution.py:36
  199.7 7.3 %collective-permute-start.42 = (bf16[2,6,16,256]{3,2,1,0:T(8,128)(2,1)S(1)}, bf16[2,6,16,256]{3,2,1,0:T(8,128)(2,1)S(1)}, u32[]{:S(2)}, u32[]{:S(2)}) collective-permute-start(bf16[2,6,16,256]{3,2,1,0:T(8,128)(2,1)S(1)} %get-tuple-element.66), channel_id=1, source_target_pairs={{16,0},{20,4},{24,8},{28,12},{32,16},{36,20},{40,24},{44,28},{48,3... | collective-permute-start | bytes 294920 | tf_op jit(solution)/shard_map/ppermute | solution.py:36
  210.3 8.8 %collective-permute-done.49 = bf16[2,6,16,256]{3,2,1,0:T(8,128)(2,1)S(1)} collective-permute-done((bf16[2,6,16,256]{3,2,1,0:T(8,128)(2,1)S(1)}, bf16[2,6,16,256]{3,2,1,0:T(8,128)(2,1)S(1)}, u32[]{:S(2)}, u32[]{:S(2)}) %collective-permute-start.49) | collective-permute-done | bytes 98336 | tf_op jit(solution)/shard_map/ppermute | solution.py:36
  221.5 4.2 %collective-permute-done.51.other1 = bf16[2,256,256]{2,1,0:T(8,128)(2,1)S(1)} collective-permute-done((bf16[2,256,256]{2,1,0:T(8,128)(2,1)S(1)}, bf16[2,256,256]{2,1,0:T(8,128)(2,1)S(1)}, u32[]{:S(2)}, u32[]{:S(2)}) %collective-permute-start.51) | collective-permute-done | bytes 262176 | tf_op jit(solution)/shard_map/ppermute | solution.py:26
  225.7 2.8 %collective-permute-done.50.other0 = bf16[2,256,256]{2,1,0:T(8,128)(2,1)S(1)} collective-permute-done((bf16[2,256,256]{2,1,0:T(8,128)(2,1)S(1)}, bf16[2,256,256]{2,1,0:T(8,128)(2,1)S(1)}, u32[]{:S(2)}, u32[]{:S(2)}) %collective-permute-start.50) | collective-permute-done | bytes 262176 | tf_op jit(solution)/shard_map/ppermute | solution.py:26
  229.2 2.2 place.1
  (185 shorter events, 76.8 us)
Async XLA Ops:
  6.5 94.8 %all-gather.3.cloned.1.call-start = ((), (), s32[]{:S(2)}) async-start(), calls=%async_computation | async-start | bytes 2359296 | tf_op jit(solution)/shard_map/all_gather | solution.py:389
  11.3 41.1 %collective-permute-start = (bf16[2,256,512]{2,1,0:T(8,128)(2,1)}, bf16[2,256,512]{2,1,0:T(8,128)(2,1)S(1)}, u32[]{:S(2)}, u32[]{:S(2)}) collective-permute-start(bf16[2,256,512]{2,1,0:T(8,128)(2,1)} %get-tuple-element.22), channel_id=1, source_target_pairs={{0,4},{4,0},{8,12},{12,8},{16,20},{20,16},{24,28},{28,24},{1,5},{5... | collective-permute-start | bytes 1572872 | tf_op jit(solution)/shard_map/ppermute | solution.py:26
  13.3 39.1 %collective-permute-start.1 = (bf16[1,3,2048]{2,1,0:T(4,128)(2,1)}, bf16[1,3,2048]{2,1,0:T(4,128)(2,1)S(1)}, u32[]{:S(2)}, u32[]{:S(2)}) collective-permute-start(bf16[1,3,2048]{2,1,0:T(4,128)(2,1)} %mod.1), channel_id=1, source_target_pairs={{0,4},{4,0},{8,12},{12,8},{16,20},{20,16},{24,28},{28,24},{1,5},{5... | collective-permute-start | bytes 36872 | tf_op jit(solution)/shard_map/ppermute | solution.py:26
  40.4 7.9 %collective-permute-start.13 = (bf16[1,32,768]{2,1,0:T(8,128)(2,1)S(1)}, bf16[1,32,768]{2,1,0:T(8,128)(2,1)S(1)}, u32[]{:S(2)}, u32[]{:S(2)}) collective-permute-start(bf16[1,32,768]{2,1,0:T(8,128)(2,1)S(1)} %slice.243), channel_id=1, source_target_pairs={{0,4},{4,8},{8,12},{12,16},{16,20},{20,24},{24,28},{28,0},{1,5},{5... | collective-permute-start | bytes 147464 | tf_op jit(solution)/shard_map/ppermute | solution.py:31
  55.3 11.8 %collective-permute-start.22 = (bf16[512,512]{1,0:T(8,128)(2,1)}, bf16[512,512]{1,0:T(8,128)(2,1)S(1)}, u32[]{:S(2)}, u32[]{:S(2)}) collective-permute-start(bf16[512,512]{1,0:T(8,128)(2,1)} %bitcast.a_ref), channel_id=1, source_target_pairs={{0,130},{2,128},{128,2},{130,0},{1,131},{3,129},{129,3},{131,1},{4... | collective-permute-start | bytes 1572872 | tf_op jit(solution)/shard_map/ppermute | solution.py:26
  57.3 19.9 %collective-permute-start.19 = (bf16[8,2,32,256]{3,2,1,0:T(8,128)(2,1)S(1)}, bf16[8,2,32,256]{3,2,1,0:T(8,128)(2,1)S(1)}, u32[]{:S(2)}, u32[]{:S(2)}) collective-permute-start(bf16[8,2,32,256]{3,2,1,0:T(8,128)(2,1)S(1)} %constant_dynamic-update-slice_fusion.2.v0), channel_id=1, source_target_pairs={{0,96},{32,64},{64,32},{96,0},{1,97},{33,65},{65,33},{97,1},{2,98}... | collective-permute-start | bytes 786440 | tf_op jit(solution)/shard_map/ppermute | solution.py:26
  59.3 18.6 %collective-permute-start.18 = (bf16[8,2,32,256]{3,2,1,0:T(8,128)(2,1)S(1)}, bf16[8,2,32,256]{3,2,1,0:T(8,128)(2,1)S(1)}, u32[]{:S(2)}, u32[]{:S(2)}) collective-permute-start(bf16[8,2,32,256]{3,2,1,0:T(8,128)(2,1)S(1)} %constant_dynamic-update-slice_fusion.2.v0), channel_id=1, source_target_pairs={{0,32},{32,0},{64,96},{96,64},{1,33},{33,1},{65,97},{97,65},{2,34}... | collective-permute-start | bytes 786440 | tf_op jit(solution)/shard_map/ppermute | solution.py:26
  59.5 9.7 %collective-permute-start.3 = (bf16[512,512]{1,0:T(8,128)(2,1)}, bf16[512,512]{1,0:T(8,128)(2,1)}, u32[]{:S(2)}, u32[]{:S(2)}) collective-permute-start(bf16[512,512]{1,0:T(8,128)(2,1)} %bitcast.a_ref), channel_id=1, source_target_pairs={{0,2},{2,0},{128,130},{130,128},{1,3},{3,1},{129,131},{131,129},{4... | collective-permute-start | bytes 1572872 | tf_op jit(solution)/shard_map/ppermute | solution.py:26
  67.2 7.8 %collective-permute-start.23 = (bf16[256,512]{1,0:T(8,128)(2,1)S(1)}, bf16[256,512]{1,0:T(8,128)(2,1)S(1)}, u32[]{:S(2)}, u32[]{:S(2)}) collective-permute-start(bf16[256,512]{1,0:T(8,128)(2,1)S(1)} %slice.251), channel_id=1, source_target_pairs={{0,2},{2,0},{128,130},{130,128},{1,3},{3,1},{129,131},{131,129},{4... | collective-permute-start | bytes 786440 | tf_op jit(solution)/shard_map/ppermute | solution.py:26
  72.9 15.2 %collective-permute-start.33 = (bf16[8,2,32,512]{3,2,1,0:T(8,128)(2,1)S(1)}, bf16[8,2,32,512]{3,2,1,0:T(8,128)(2,1)S(1)}, u32[]{:S(2)}, u32[]{:S(2)}) collective-permute-start(bf16[8,2,32,512]{3,2,1,0:T(8,128)(2,1)S(1)} %fusion.26.o0), channel_id=1, source_target_pairs={{0,96},{32,64},{64,32},{96,0},{1,97},{33,65},{65,33},{97,1},{2,98}... | collective-permute-start | bytes 1572872 | tf_op jit(solution)/shard_map/ppermute | solution.py:26
  74.9 18.2 %collective-permute-start.32 = (bf16[8,2,32,512]{3,2,1,0:T(8,128)(2,1)S(1)}, bf16[8,2,32,512]{3,2,1,0:T(8,128)(2,1)S(1)}, u32[]{:S(2)}, u32[]{:S(2)}) collective-permute-start(bf16[8,2,32,512]{3,2,1,0:T(8,128)(2,1)S(1)} %fusion.26.o0), channel_id=1, source_target_pairs={{0,32},{32,0},{64,96},{96,64},{1,33},{33,1},{65,97},{97,65},{2,34}... | collective-permute-start | bytes 1572872 | tf_op jit(solution)/shard_map/ppermute | solution.py:26
  77.2 18.5 %collective-permute-start.26 = (bf16[512,512]{1,0:T(8,128)(2,1)S(1)}, bf16[512,512]{1,0:T(8,128)(2,1)S(1)}, u32[]{:S(2)}, u32[]{:S(2)}) collective-permute-start(bf16[512,512]{1,0:T(8,128)(2,1)S(1)} %collective-permute-done.22.c_ref), channel_id=1, source_target_pairs={{0,1},{1,0},{2,3},{3,2},{4,5},{5,4},{6,7},{7,6},{8,9},{9,8},{10,11... | collective-permute-start | bytes 1572872 | tf_op jit(solution)/shard_map/ppermute | solution.py:26
  77.3 19.3 %collective-permute-start.25 = (bf16[512,512]{1,0:T(8,128)(2,1)S(1)}, bf16[512,512]{1,0:T(8,128)(2,1)}, u32[]{:S(2)}, u32[]{:S(2)}) collective-permute-start(bf16[512,512]{1,0:T(8,128)(2,1)S(1)} %constant_dynamic-update-slice_fusion.12.a_ref), channel_id=1, source_target_pairs={{0,1},{1,0},{2,3},{3,2},{4,5},{5,4},{6,7},{7,6},{8,9},{9,8},{10,11... | collective-permute-start | bytes 1572872 | tf_op jit(solution)/shard_map/ppermute | solution.py:26
  77.9 9.0 %collective-permute-start.20 = (bf16[4,2,32,256]{3,2,1,0:T(8,128)(2,1)S(1)}, bf16[4,2,32,256]{3,2,1,0:T(8,128)(2,1)S(1)}, u32[]{:S(2)}, u32[]{:S(2)}) collective-permute-start(bf16[4,2,32,256]{3,2,1,0:T(8,128)(2,1)S(1)} %slice.249), channel_id=1, source_target_pairs={{0,32},{32,0},{64,96},{96,64},{1,33},{33,1},{65,97},{97,65},{2,34}... | collective-permute-start | bytes 393224 | tf_op jit(solution)/shard_map/ppermute | solution.py:26
  93.1 27.4 %collective-permute-start.34 = (bf16[4,2,32,512]{3,2,1,0:T(8,128)(2,1)}, bf16[4,2,32,512]{3,2,1,0:T(8,128)(2,1)}, u32[]{:S(2)}, u32[]{:S(2)}) collective-permute-start(bf16[4,2,32,512]{3,2,1,0:T(8,128)(2,1)} %slice.264), channel_id=1, source_target_pairs={{0,32},{32,0},{64,96},{96,64},{1,33},{33,1},{65,97},{97,65},{2,34}... | collective-permute-start | bytes 786440 | tf_op jit(solution)/shard_map/ppermute | solution.py:26
  93.1 31.9 %collective-permute-start.2 = (bf16[512,512]{1,0:T(8,128)(2,1)}, bf16[512,512]{1,0:T(8,128)(2,1)}, u32[]{:S(2)}, u32[]{:S(2)}) collective-permute-start(bf16[512,512]{1,0:T(8,128)(2,1)} %bitcast.a_ref), channel_id=1, source_target_pairs={{0,1},{1,0},{2,3},{3,2},{4,5},{5,4},{6,7},{7,6},{8,9},{9,8},{10,11... | collective-permute-start | bytes 1572872 | tf_op jit(solution)/shard_map/ppermute | solution.py:26
  94.0 30.1 %collective-permute-start.35 = (bf16[4,2,32,512]{3,2,1,0:T(8,128)(2,1)}, bf16[4,2,32,512]{3,2,1,0:T(8,128)(2,1)}, u32[]{:S(2)}, u32[]{:S(2)}) collective-permute-start(bf16[4,2,32,512]{3,2,1,0:T(8,128)(2,1)} %slice.265), channel_id=1, source_target_pairs={{0,96},{32,64},{64,32},{96,0},{1,97},{33,65},{65,33},{97,1},{2,98}... | collective-permute-start | bytes 786440 | tf_op jit(solution)/shard_map/ppermute | solution.py:26
  95.7 29.4 %collective-permute-start.4 = (bf16[512,512]{1,0:T(8,128)(2,1)}, bf16[512,512]{1,0:T(8,128)(2,1)}, u32[]{:S(2)}, u32[]{:S(2)}) collective-permute-start(bf16[512,512]{1,0:T(8,128)(2,1)} %collective-permute-done.3.c_ref), channel_id=1, source_target_pairs={{0,1},{1,0},{2,3},{3,2},{4,5},{5,4},{6,7},{7,6},{8,9},{9,8},{10,11... | collective-permute-start | bytes 1572872 | tf_op jit(solution)/shard_map/ppermute | solution.py:26
  108.9 20.9 %collective-permute-start.28 = (bf16[512,256]{1,0:T(8,128)(2,1)S(1)}, bf16[512,256]{1,0:T(8,128)(2,1)}, u32[]{:S(2)}, u32[]{:S(2)}) collective-permute-start(bf16[512,256]{1,0:T(8,128)(2,1)S(1)} %attend.3), channel_id=1, source_target_pairs={{0,130},{2,128},{128,2},{130,0},{1,131},{3,129},{129,3},{131,1},{4... | collective-permute-start | bytes 786440 | tf_op jit(solution)/shard_map/ppermute | solution.py:26
  120.5 10.4 %collective-permute-start.30 = (bf16[512,256]{1,0:T(8,128)(2,1)S(1)}, bf16[512,256]{1,0:T(8,128)(2,1)}, u32[]{:S(2)}, u32[]{:S(2)}) collective-permute-start(bf16[512,256]{1,0:T(8,128)(2,1)S(1)} %attend.3), channel_id=1, source_target_pairs={{0,2},{2,0},{128,130},{130,128},{1,3},{3,1},{129,131},{131,129},{4... | collective-permute-start | bytes 786440 | tf_op jit(solution)/shard_map/ppermute | solution.py:26
  130.7 11.1 %collective-permute-start.29 = (bf16[256,256]{1,0:T(8,128)(2,1)S(1)}, bf16[256,256]{1,0:T(8,128)(2,1)S(1)}, u32[]{:S(2)}, u32[]{:S(2)}) collective-permute-start(bf16[256,256]{1,0:T(8,128)(2,1)S(1)} %slice.253), channel_id=1, source_target_pairs={{0,2},{2,0},{128,130},{130,128},{1,3},{3,1},{129,131},{131,129},{4... | collective-permute-start | bytes 393224 | tf_op jit(solution)/shard_map/ppermute | solution.py:26
  131.8 10.1 %collective-permute-start.31 = (bf16[256,256]{1,0:T(8,128)(2,1)S(1)}, bf16[256,256]{1,0:T(8,128)(2,1)S(1)}, u32[]{:S(2)}, u32[]{:S(2)}) collective-permute-start(bf16[256,256]{1,0:T(8,128)(2,1)S(1)} %slice.254), channel_id=1, source_target_pairs={{0,130},{2,128},{128,2},{130,0},{1,131},{3,129},{129,3},{131,1},{4... | collective-permute-start | bytes 393224 | tf_op jit(solution)/shard_map/ppermute | solution.py:26
  147.0 9.8 %collective-permute-start.43 = (bf16[512,256]{1,0:T(8,128)(2,1)S(1)}, bf16[512,256]{1,0:T(8,128)(2,1)S(1)}, u32[]{:S(2)}, u32[]{:S(2)}) collective-permute-start(bf16[512,256]{1,0:T(8,128)(2,1)S(1)} %get-tuple-element.34), channel_id=1, source_target_pairs={{0,1},{1,0},{2,3},{3,2},{4,5},{5,4},{6,7},{7,6},{8,9},{9,8},{10,11... | collective-permute-start | bytes 786440 | tf_op jit(solution)/shard_map/ppermute | solution.py:26
  147.5 9.2 %collective-permute-start.38 = (bf16[512,256]{1,0:T(8,128)(2,1)S(1)}, bf16[512,256]{1,0:T(8,128)(2,1)S(1)}, u32[]{:S(2)}, u32[]{:S(2)}) collective-permute-start(bf16[512,256]{1,0:T(8,128)(2,1)S(1)} %add_convert_fusion.3), channel_id=1, source_target_pairs={{0,2},{2,0},{1,3},{3,1},{4,6},{6,4},{5,7},{7,5},{8,10},{10,8},{9,1... | collective-permute-start | bytes 786440 | tf_op jit(solution)/shard_map/ppermute | solution.py:26
  148.3 13.2 %collective-permute-start.45 = (bf16[512,256]{1,0:T(8,128)(2,1)S(1)}, bf16[512,256]{1,0:T(8,128)(2,1)S(1)}, u32[]{:S(2)}, u32[]{:S(2)}) collective-permute-start(bf16[512,256]{1,0:T(8,128)(2,1)S(1)} %add_convert_fusion.1), channel_id=1, source_target_pairs={{0,2},{2,0},{1,3},{3,1},{4,6},{6,4},{5,7},{7,5},{8,10},{10,8},{9,1... | collective-permute-start | bytes 786440 | tf_op jit(solution)/shard_map/ppermute | solution.py:26
  163.0 13.4 %collective-permute-start.39 = (bf16[16,6,256]{2,1,0:T(8,128)(2,1)S(1)}, bf16[16,6,256]{2,1,0:T(8,128)(2,1)S(1)}, u32[]{:S(2)}, u32[]{:S(2)}) collective-permute-start(bf16[16,6,256]{2,1,0:T(8,128)(2,1)S(1)} %get-tuple-element.54), channel_id=1, source_target_pairs={{0,4},{4,8},{8,12},{16,20},{20,24},{24,28},{32,36},{36,40},{40,44}... | collective-permute-start | bytes 147464 | tf_op jit(solution)/shard_map/ppermute | solution.py:36
  168.5 7.9 %collective-permute-start.40 = (bf16[16,6,256]{2,1,0:T(8,128)(2,1)S(1)}, bf16[16,6,256]{2,1,0:T(8,128)(2,1)S(1)}, u32[]{:S(2)}, u32[]{:S(2)}) collective-permute-start(bf16[16,6,256]{2,1,0:T(8,128)(2,1)S(1)} %get-tuple-element.53), channel_id=1, source_target_pairs={{4,0},{8,4},{12,8},{20,16},{24,20},{28,24},{36,32},{40,36},{44,40}... | collective-permute-start | bytes 147464 | tf_op jit(solution)/shard_map/ppermute | solution.py:36
  181.0 16.6 %collective-permute-start.41 = (bf16[2,6,16,256]{3,2,1,0:T(8,128)(2,1)S(1)}, bf16[2,6,16,256]{3,2,1,0:T(8,128)(2,1)S(1)}, u32[]{:S(2)}, u32[]{:S(2)}) collective-permute-start(bf16[2,6,16,256]{3,2,1,0:T(8,128)(2,1)S(1)} %fusion.22), channel_id=1, source_target_pairs={{0,16},{4,20},{8,24},{12,28},{16,32},{20,36},{24,40},{28,44},{32,4... | collective-permute-start | bytes 294920 | tf_op jit(solution)/shard_map/ppermute | solution.py:36
  183.0 16.5 %collective-permute-start.48 = (bf16[2,6,16,256]{3,2,1,0:T(8,128)(2,1)S(1)}, bf16[2,6,16,256]{3,2,1,0:T(8,128)(2,1)S(1)}, u32[]{:S(2)}, u32[]{:S(2)}) collective-permute-start(bf16[2,6,16,256]{3,2,1,0:T(8,128)(2,1)S(1)} %fusion.20), channel_id=1, source_target_pairs={{0,16},{4,20},{8,24},{12,28},{16,32},{20,36},{24,40},{28,44},{32,4... | collective-permute-start | bytes 294920 | tf_op jit(solution)/shard_map/ppermute | solution.py:36
  199.7 10.5 %collective-permute-start.42 = (bf16[2,6,16,256]{3,2,1,0:T(8,128)(2,1)S(1)}, bf16[2,6,16,256]{3,2,1,0:T(8,128)(2,1)S(1)}, u32[]{:S(2)}, u32[]{:S(2)}) collective-permute-start(bf16[2,6,16,256]{3,2,1,0:T(8,128)(2,1)S(1)} %get-tuple-element.66), channel_id=1, source_target_pairs={{16,0},{20,4},{24,8},{28,12},{32,16},{36,20},{40,24},{44,28},{48,3... | collective-permute-start | bytes 294920 | tf_op jit(solution)/shard_map/ppermute | solution.py:36
  207.0 12.0 %collective-permute-start.49 = (bf16[2,6,16,256]{3,2,1,0:T(8,128)(2,1)S(1)}, bf16[2,6,16,256]{3,2,1,0:T(8,128)(2,1)S(1)}, u32[]{:S(2)}, u32[]{:S(2)}) collective-permute-start(bf16[2,6,16,256]{3,2,1,0:T(8,128)(2,1)S(1)} %get-tuple-element.38), channel_id=1, source_target_pairs={{16,0},{20,4},{24,8},{28,12},{32,16},{36,20},{40,24},{44,28},{48,3... | collective-permute-start | bytes 294920 | tf_op jit(solution)/shard_map/ppermute | solution.py:36
  219.4 9.1 %collective-permute-start.50 = (bf16[2,256,256]{2,1,0:T(8,128)(2,1)S(1)}, bf16[2,256,256]{2,1,0:T(8,128)(2,1)S(1)}, u32[]{:S(2)}, u32[]{:S(2)}) collective-permute-start(bf16[2,256,256]{2,1,0:T(8,128)(2,1)S(1)} %bitcast.155), channel_id=1, source_target_pairs={{0,4},{4,0},{8,12},{12,8},{16,20},{20,16},{24,28},{28,24},{1,5},{5... | collective-permute-start | bytes 786440 | tf_op jit(solution)/shard_map/ppermute | solution.py:26
  (38 other events, 249.3 us)
Sparse Core Ops, SparseCore 0:
  28.2 42.5 all-gather.2

commit v3 on v2

v3 whole, which is shorter than its diff:
```python
import functools
import math

import jax
import jax.numpy as jnp
from jax import lax
from jax.experimental import pallas as pl
from jax.experimental.pallas import tpu as pltpu
from jax.sharding import Mesh, PartitionSpec as P

D = 2048
HDIM = 128
S = 16
W = 6
TOK = 256
NARROW = 512
HALF = 256
REGION = ("h", "x", "z")
MP = ("yl", "c")
BF = jnp.bfloat16
F32 = jnp.float32


def xor_swap(block, axis, bit):
    size = math.prod(lax.axis_size(a) for a in ((axis,) if isinstance(axis, str) else axis))
    return lax.ppermute(block, axis, [(i, i ^ bit) for i in range(size)])


def rotate(block, axis, step):
    size = lax.axis_size(axis)
    return lax.ppermute(block, axis, [(i, (i + step) % size) for i in range(size)])


def shift(block, distance, allowed):
    route = [(i, i + distance) for i in range(64) if 0 <= i + distance < 64 and allowed(i)]
    return lax.ppermute(block, REGION, route)


def opposite(near, side, axis, split_axis):
    size = near.shape[split_axis]
    first = xor_swap(lax.slice_in_dim(side, 0, size // 2, axis=split_axis), axis, 1)
    second = xor_swap(lax.slice_in_dim(near, size // 2, size, axis=split_axis), axis, 3)
    return jnp.concatenate([first, second], axis=split_axis)


def ring_of_four(block, axis, split_axis):
    near = xor_swap(block, axis, 1)
    side = xor_swap(block, axis, 3)
    return block, near, opposite(near, side, axis, split_axis), side


def where_am_i():
    h, x, z = (lax.axis_index(a) for a in REGION)
    yl, c = (lax.axis_index(a) for a in MP)
    return h, x, z, yl, c


def even_count(counts_ref):
    h, x, z, _, _ = where_am_i()
    return counts_ref[h * 32 + x * 8 + (z // 2) * 2]


SMEM = pl.BlockSpec(memory_space=pltpu.SMEM)
VMEM = pl.BlockSpec(memory_space=pltpu.VMEM)
HBM = pl.BlockSpec(memory_space=pltpu.HBM)


def cost(flops, size, special=0):
    return pl.CostEstimate(flops=flops, bytes_accessed=size, transcendentals=special)


def pack_kernel(qkv_ref, out_ref, own, sent):
    h = lax.axis_index("h")
    mine = pl.ds(pl.multiple_of(h * HALF, HALF), HALF)
    theirs = pl.ds(pl.multiple_of((1 - h) * HALF, HALF), HALF)
    for n in range(3):
        own[n] = qkv_ref[n, :, mine]
        sent[n] = qkv_ref[n, :, theirs]
    own[3] = out_ref[:, mine]
    own[4] = out_ref[:, theirs]
    sent[3] = out_ref[:, theirs]
    sent[4] = out_ref[:, mine]


def packed(qkv, out):
    return pl.pallas_call(
        pack_kernel,
        in_specs=[VMEM, VMEM],
        out_specs=[VMEM] * 2,
        out_shape=[jax.ShapeDtypeStruct((5, 32, HALF), BF)] * 2,
        cost_estimate=cost(0, 2**18),
        name="pack",
    )(qkv, out)


def split_kernel(counts_ref, data_ref, sent_ref, kept_ref, sem):
    even = even_count(counts_ref)
    odd = lax.axis_index("z") % 2 == 1
    copies = []
    for s in range(2):
        away = jnp.where(odd, jnp.clip(s - even, 0, 3), 2 + s)
        stays = jnp.where(odd, jnp.clip(2 + s - even, 0, 3), s)
        copies.append(pltpu.make_async_copy(data_ref.at[away], sent_ref.at[s], sem))
        copies.append(pltpu.make_async_copy(data_ref.at[stays], kept_ref.at[s], sem))
    for copy in copies:
        copy.start()
    for copy in copies:
        copy.wait()


def split_tiles(counts, data):
    return pl.pallas_call(
        split_kernel,
        in_specs=[SMEM, HBM],
        out_specs=[VMEM, VMEM],
        out_shape=[jax.ShapeDtypeStruct((2, TOK, NARROW), BF)] * 2,
        scratch_shapes=[pltpu.SemaphoreType.DMA],
        cost_estimate=cost(0, 2**21),
        name="split",
    )(counts, data)


def choose_kernel(counts_ref, kept, came, mod, other_mod, tiles, mods, gate):
    even = even_count(counts_ref)
    odd = lax.axis_index("z") % 2 == 1
    place = lax.axis_index("yl") * 2 + lax.axis_index("c")
    cols = pl.ds(pl.multiple_of(place * NARROW, NARROW), NARROW)
    for s in range(2):
        use_other = jnp.where(odd, 2 + s < even, s >= even)

        @pl.when(use_other)
        def _():
            tiles[s] = came[s]
            mods[s] = other_mod[0]
            gate[s] = other_mod[0, 2:3, cols].astype(F32)

        @pl.when(jnp.logical_not(use_other))
        def _():
            tiles[s] = kept[s]
            mods[s] = mod[0]
            gate[s] = mod[0, 2:3, cols].astype(F32)


def choose(counts, kept, came, mod, other_mod):
    return pl.pallas_call(
        choose_kernel,
        in_specs=[SMEM] + [VMEM] * 4,
        out_specs=[VMEM] * 3,
        out_shape=[
            jax.ShapeDtypeStruct((2, TOK, NARROW), BF),
            jax.ShapeDtypeStruct((2, 3, D), BF),
            jax.ShapeDtypeStruct((2, 1, NARROW), F32),
        ],
        cost_estimate=cost(0, 2**21),
        name="choose",
    )(counts, kept, came, mod, other_mod)


def slot_of(hr, xr):
    h, x, _, yl, c = where_am_i()
    px = x ^ xr
    return ((h ^ hr ^ yl) * 2 + ((px // 2) ^ c)) * 2 + px % 2


def normalise_rows(rows, part_ref, mod_ref, hid_ref):
    place = lax.axis_index("yl") * 2 + lax.axis_index("c")
    parts = [part_ref[j, rows, :].astype(F32) for j in range(4)]
    mean = sum(jnp.sum(p, axis=-1, keepdims=True) for p in parts) * (1.0 / D)
    parts = [p - mean for p in parts]
    spread = sum(jnp.sum(p * p, axis=-1, keepdims=True) for p in parts) * (1.0 / D)
    scale = lax.rsqrt(spread + 1e-06)
    tile = rows.start // TOK
    for j, p in enumerate(parts):
        source = pl.ds(pl.multiple_of((place ^ j) * NARROW, NARROW), NARROW)
        gain = 1.0 + mod_ref[tile, 1:2, source].astype(F32)
        value = p * scale * gain + mod_ref[tile, 0:1, source].astype(F32)
        hid_ref[rows, j * NARROW : (j + 1) * NARROW] = value.astype(BF)


def attend_kernel(
    a_hbm, b_hbm, c_hbm, d_hbm, mod_ref, g_ref, out_ref, part_ref, hid_ref, w_ref, part_sem, sem
):
    loads = [
        pltpu.make_async_copy(piece, part_ref.at[j], part_sem)
        for j, piece in enumerate((a_hbm, b_hbm, c_hbm, d_hbm))
    ]
    copies = []
    for hr in range(2):
        for xr in range(4):
            slot = slot_of(hr, xr)
            for n in range(3):
                copies.append(
                    pltpu.make_async_copy(
                        g_ref.at[:, (xr * 2 + hr) * 3 + n],
                        w_ref.at[slot, :, :, pl.ds(n * HALF, HALF)],
                        sem,
                    )
                )
    for copy in loads + copies:
        copy.start()
    for load in loads:
        load.wait()
    for r in range(0, 2 * TOK, 64):
        normalise_rows(slice(r, r + 64), part_ref, mod_ref, hid_ref)
    for copy in copies:
        copy.wait()
    weight = w_ref[...].reshape(D, 3 * HALF)
    for t in range(2):
        rows = slice(t * TOK, (t + 1) * TOK)
        proj = jnp.dot(hid_ref[rows, :], weight, preferred_element_type=F32).astype(BF)
        for n in range(2):
            q = proj[:, n * HDIM : (n + 1) * HDIM]
            k = proj[:, HALF + n * HDIM : HALF + (n + 1) * HDIM]
            v = proj[:, 2 * HALF + n * HDIM : 2 * HALF + (n + 1) * HDIM]
            scores = lax.dot_general(
                q, k, (((1,), (1,)), ((), ())), preferred_element_type=F32
            ) * (1.0 / math.sqrt(HDIM))
            top = jnp.max(scores, axis=-1, keepdims=True)
            e = jnp.exp(scores - top)
            probs = (e / jnp.sum(e, axis=-1, keepdims=True)).astype(BF)
            got = jnp.dot(probs, v, preferred_element_type=F32)
            out_ref[rows, n * HDIM : (n + 1) * HDIM] = got.astype(BF)


def attended_of(pieces, mods, gathered):
    return pl.pallas_call(
        attend_kernel,
        in_specs=[HBM] * 4 + [VMEM, HBM],
        out_specs=VMEM,
        out_shape=jax.ShapeDtypeStruct((512, HALF), BF),
        scratch_shapes=[
            pltpu.VMEM((4, 512, NARROW), BF),
            pltpu.VMEM((512, D), BF),
            pltpu.VMEM((8, 8, 32, 3 * HALF), BF),
            pltpu.SemaphoreType.DMA,
            pltpu.SemaphoreType.DMA,
        ],
        compiler_params=pltpu.CompilerParams(vmem_limit_bytes=60 * 2**20),
        cost_estimate=cost(
            2 * 512 * D * 768 + 4 * 4 * TOK * TOK * HDIM, 6 * 2**20, 4 * TOK * TOK
        ),
        name="attend",
    )(*pieces, mods, gathered)


def project_kernel(far, own_ref, other_ref, o0, o1, o2, o3, keep_ref, send_ref, w_ref, sem):
    h, x, _, yl, c = where_am_i()
    copies = []
    for xr, piece in enumerate((o0, o1, o2, o3)):
        px = x ^ xr
        slot = ((px // 2) ^ c) * 2 + px % 2
        for n in range(2):
            copies.append(
                pltpu.make_async_copy(
                    piece.at[:, (yl ^ far ^ h) * 2 + n],
                    w_ref.at[slot, :, :, pl.ds(n * HALF, HALF)],
                    sem,
                )
            )
    for copy in copies:
        copy.start()
    for copy in copies:
        copy.wait()
    for b, out_ref in ((1, send_ref), (0, keep_ref)):
        weight = w_ref[2 * b : 2 * b + 2].reshape(NARROW, NARROW)
        total = lax.dot_general(
            own_ref[...], weight[:, :HALF], (((1,), (1,)), ((), ())), preferred_element_type=F32
        ) + lax.dot_general(
            other_ref[...], weight[:, HALF:], (((1,), (1,)), ((), ())), preferred_element_type=F32
        )
        out_ref[...] = total.astype(BF)


def partial_of(far, own, other, os):
    return pl.pallas_call(
        functools.partial(project_kernel, far),
        in_specs=[VMEM, VMEM] + [HBM] * 4,
        out_specs=[VMEM] * 2,
        out_shape=[jax.ShapeDtypeStruct((512, NARROW), BF)] * 2,
        scratch_shapes=[pltpu.VMEM((4, 8, 32, NARROW), BF), pltpu.SemaphoreType.DMA],
        compiler_params=pltpu.CompilerParams(vmem_limit_bytes=16 * 2**20),
        cost_estimate=cost(2 * 512 * 512 * 1024, 3 * 2**20),
        name="project",
    )(own, other, *os)


def place_kernel(counts_ref, own, other, out_ref, zero_ref, sem):
    even = even_count(counts_ref)
    parity = lax.axis_index("z") % 2
    zero_ref[...] = jnp.zeros_like(zero_ref)
    waits = []
    for slot in range(4):
        tile = slot + parity * even
        live = jnp.where(parity == 1, tile < 4, slot < even)
        ours = tile // 2 == parity
        target = out_ref.at[slot]

        @pl.when(live & ours)
        def _():
            pltpu.make_async_copy(own.at[tile % 2], target, sem).start()

        @pl.when(live & jnp.logical_not(ours))
        def _():
            pltpu.make_async_copy(other.at[tile % 2], target, sem).start()

        @pl.when(jnp.logical_not(live))
        def _():
            pltpu.make_async_copy(zero_ref, target, sem).start()

        waits.append(pltpu.make_async_copy(zero_ref, target, sem))
    for wait in waits:
        wait.wait()


def place_tiles(counts, own, other):
    return pl.pallas_call(
        place_kernel,
        in_specs=[SMEM, VMEM, VMEM],
        out_specs=HBM,
        out_shape=jax.ShapeDtypeStruct((4, TOK, NARROW), BF),
        scratch_shapes=[pltpu.VMEM((TOK, NARROW), BF), pltpu.SemaphoreType.DMA],
        cost_estimate=cost(0, 2**21),
        name="place",
    )(counts, own, other)


def mix(earlier, later, share):
    return ((1.0 - share) * earlier.astype(F32) + share * later.astype(F32)).astype(BF)


def join_rows(strip, region, shares):
    count = strip.shape[1]
    share = shares.reshape(W, 1, 1)
    top, bottom = strip[:W], strip[S - W :]
    later = shift(top.reshape(W * count, NARROW), -4, lambda i: True)
    earlier = shift(bottom.reshape(W * count, NARROW), 4, lambda i: True)
    later, earlier = lax.optimization_barrier((later, earlier))
    top = jnp.where(region >= 4, mix(earlier.reshape(W, count, NARROW), top, share), top)
    bottom = jnp.where(region < 60, mix(bottom, later.reshape(W, count, NARROW), share), bottom)
    return jnp.concatenate([top, strip[W : S - W], bottom], axis=0)


def blend(tiles, region, shares):
    first, second = tiles[0], tiles[1]
    share = shares.reshape(1, W, 1)
    west, east = first[:, :W], second[:, S - W :]
    later = shift(west, -1, lambda i: i % 4 != 0)
    earlier = shift(east, 1, lambda i: i % 4 != 3)
    later, earlier = lax.optimization_barrier((later, earlier))
    place = region % 4
    left = jnp.where(place != 0, mix(earlier, west, share), west)
    right = jnp.where(place != 3, mix(east, later, share), east)
    inner = mix(first[:, S - W :], second[:, :W], share)
    strip = jnp.concatenate(
        [left, first[:, W : S - W], inner, second[:, W : S - W], right], axis=1
    )
    strip = join_rows(strip, region, shares)
    return jnp.stack([strip[:, :S], strip[:, S - W :]])


def on_device(tile_data, tile_counts, modulation, qkv_weight, out_weight, blend_weights):
    h, x, z, _, _ = where_am_i()
    region = h * 32 + x * 8 + z

    own_blocks, sent_blocks = packed(qkv_weight.transpose(1, 0, 2), out_weight)
    came_blocks = xor_swap(sent_blocks, "h", 1)

    tile_data, sent_blocks = lax.optimization_barrier((tile_data, sent_blocks))
    away, kept = split_tiles(tile_counts, tile_data)
    came = xor_swap(away, "z", 1)
    came_mod = xor_swap(modulation, "z", 1)

    came_blocks, kept = lax.optimization_barrier((came_blocks, kept))
    qkv = jnp.concatenate([own_blocks[:3], came_blocks[:3]])
    pieces = [qkv] + [xor_swap(qkv, "x", bit) for bit in (1, 2, 3)]
    block = jnp.concatenate(pieces + [own_blocks[3:], came_blocks[3:]])
    gathered = lax.all_gather(block, "z", axis=0)

    tiles, mods, gate = choose(tile_counts, kept, came, modulation, came_mod)
    ring = ("h", "yl")
    mine = tiles.reshape(512, NARROW)
    _, near, across, side = ring_of_four(mine, ring, 0)
    mods_across = xor_swap(mods, "h", 1)
    own_pieces = (mine, xor_swap(mine, "c", 1), near, xor_swap(near, "c", 1))
    other_pieces = (across, xor_swap(across, "c", 1), side, xor_swap(side, "c", 1))

    o_block = gathered[:, 24:]
    o_near, o_side = xor_swap(o_block, "x", 1), xor_swap(o_block, "x", 3)
    att_sent = attended_of(other_pieces, mods_across, gathered)
    att_near, att_side = xor_swap(att_sent, ring, 1), xor_swap(att_sent, ring, 3)
    att_own = attended_of(own_pieces, mods, gathered)
    o_near, o_side, att_near, att_side, att_own = lax.optimization_barrier(
        (o_near, o_side, att_near, att_side, att_own)
    )
    att_other = opposite(att_near, att_side, ring, 0)
    o_all = (o_block, o_near, opposite(o_near, o_side, "x", 0), o_side)

    far_keep, far_send = partial_of(1, att_own, att_other, o_all)
    far = (far_keep.astype(F32) + xor_swap(far_send, "c", 1).astype(F32)).astype(BF)
    far = xor_swap(far, "yl", 1)
    keep, send = partial_of(0, att_own, att_other, o_all)
    summed = keep.astype(F32) + xor_swap(send, "c", 1).astype(F32) + far.astype(F32)
    updated = tiles.astype(F32) + gate * summed.reshape(2, TOK, NARROW)
    updated = updated.astype(BF).reshape(2, S, S, NARROW)
    finished = blend(updated, region, blend_weights).reshape(2, TOK, NARROW)
    return place_tiles(tile_counts, finished, xor_swap(finished, "z", 1))


def solution(mesh):
    fine = Mesh(mesh.devices.reshape(2, 4, 8, 2, 2), REGION + MP)
    return jax.shard_map(
        on_device,
        mesh=fine,
        in_specs=(
            P(REGION, None, MP),
            P(),
            P(REGION, None, None),
            P(REGION, None, MP),
            P(REGION, MP),
            P(),
        ),
        out_specs=P(REGION, None, MP),
        check_vma=False,
    )
```

time: 243 us -> 187 us (0.77)
  the two profiles are of different devices: /device:TPU:80 before, /device:TPU:24 now
where the time goes in v3:
time: 187 us; the launch traced here: 186 us
  waiting for transfers between devices  93.4 us (50%)
  starting transfers between devices  42.1 us (23%)
  Pallas kernels  26.8 us (14%)
  between operations  13.9 us (7%)
  local copies, waits for them, and re-layouts  8.09 us (4%)
    ppermute x27, waiting for transfers between devices, xor_swap(): return lax.ppermute(block, axis, [(i, i ^ bit) for i in range(size)])  65.8 us
    ppermute x27, starting transfers between devices, xor_swap(): return lax.ppermute(block, axis, [(i, i ^ bit) for i in range(size)])  26.5 us
    ppermute x4, waiting for transfers between devices, shift(): return lax.ppermute(block, REGION, route)  18.7 us
    pallas_call x2, Pallas kernels, attended_of(): pl.pallas_call(attend_kernel, in_specs=[HBM] * 4 + [VMEM, HBM], out_specs...  16.4 us
    ppermute x4, starting transfers between devices, shift(): return lax.ppermute(block, REGION, route)  15.6 us
    all_gather x1, waiting for transfers between devices, on_device(): gathered = lax.all_gather(block, 'z', axis=0)  8.89 us
    unnamed x36, local copies, waits for them, and re-layouts  4.76 us
  transfers between devices with their start and end apart: 32, of which 20 were waited for; matrix products, arithmetic and copies ran while one was open for 1% of the time, Pallas kernels for 12%

profile of v3, /device:TPU:24, one launch (start us, length us, event | category | flops | bytes accessed | tf_op | source)
XLA Modules:
  0.0 185.5 jit_solution(6603418575187095154)
XLA Ops:
  6.5 1.6 pack.1
  10.2 2.9 %split.1 = (bf16[2,256,512]{2,1,0:T(8,128)(2,1)}, bf16[2,256,512]{2,1,0:T(8,128)(2,1)}) custom-call(s32[64]{0:T(128)} %counts_ref.5, bf16[4,256,512]{2,1,0:T(8,128)(2,1)} %data_ref), custom_call_target="tpu_custom_call" | custom-call | bytes 2097152 | tf_op jit(solution)/shard_map/split/pallas_call | solution.py:112
  14.3 1.6 collective-permute-start.3
  15.9 2.7 %collective-permute-start.4 = (bf16[6,32,256]{2,1,0:T(8,128)(2,1)S(1)}, bf16[6,32,256]{2,1,0:T(8,128)(2,1)S(1)}, u32[]{:S(2)}, u32[]{:S(2)}) collective-permute-start(bf16[6,32,256]{2,1,0:T(8,128)(2,1)S(1)} %pad_maximum_fusion.2), channel_id=1, source_target_pairs={{0,64},{32,96},{64,0},{96,32},{1,65},{33,97},{65,1},{97,33},{2,66}... | collective-permute-start | bytes 294920 | tf_op jit(solution)/shard_map/ppermute | solution.py:26
  19.9 2.4 %collective-permute-done.4 = bf16[6,32,256]{2,1,0:T(8,128)(2,1)S(1)} collective-permute-done((bf16[6,32,256]{2,1,0:T(8,128)(2,1)S(1)}, bf16[6,32,256]{2,1,0:T(8,128)(2,1)S(1)}, u32[]{:S(2)}, u32[]{:S(2)}) %collective-permute-start.4) | collective-permute-done | bytes 98336 | tf_op jit(solution)/shard_map/ppermute | solution.py:26
  22.4 2.1 %collective-permute-done.5 = bf16[6,32,256]{2,1,0:T(8,128)(2,1)S(1)} collective-permute-done((bf16[6,32,256]{2,1,0:T(8,128)(2,1)S(1)}, bf16[6,32,256]{2,1,0:T(8,128)(2,1)S(1)}, u32[]{:S(2)}, u32[]{:S(2)}) %collective-permute-start.5) | collective-permute-done | bytes 98336 | tf_op jit(solution)/shard_map/ppermute | solution.py:26
  26.0 2.0 %collective-permute-start.1 = (bf16[2,256,512]{2,1,0:T(8,128)(2,1)}, bf16[2,256,512]{2,1,0:T(8,128)(2,1)S(1)}, u32[]{:S(2)}, u32[]{:S(2)}) collective-permute-start(bf16[2,256,512]{2,1,0:T(8,128)(2,1)} %get-tuple-element.32), channel_id=1, source_target_pairs={{0,4},{4,0},{8,12},{12,8},{16,20},{20,16},{24,28},{28,24},{1,5},{5... | collective-permute-start | bytes 1572872 | tf_op jit(solution)/shard_map/ppermute | solution.py:26
  28.1 10.6 %collective-permute-done.2.other_mod = bf16[1,3,2048]{2,1,0:T(4,128)(2,1)S(1)} collective-permute-done((bf16[1,3,2048]{2,1,0:T(4,128)(2,1)}, bf16[1,3,2048]{2,1,0:T(4,128)(2,1)S(1)}, u32[]{:S(2)}, u32[]{:S(2)}) %collective-permute-start.2) | collective-permute-done | bytes 12320 | tf_op jit(solution)/shard_map/ppermute | solution.py:26
  40.1 2.1 %choose.1 = (bf16[2,256,512]{2,1,0:T(8,128)(2,1)}, bf16[2,3,2048]{2,1,0:T(4,128)(2,1)}, f32[2,1,512]{2,1,0:T(1,128)}) custom-call(s32[64]{0:T(128)} %counts_ref.5, bf16[2,256,512]{2,1,0:T(8,128)(2,1)} %get-tuple-element.31.kept, bf16[2,256,512]{2,1,0:T(8,128)(2,1)} %copy-done.4, bf16[1,3,2048]{2,1,0:T(4,128)(2,1)} %mod.1, bf16[1,3,2048]{2,1,0:T(4,128)(2,1)} %copy-done.9), custom_call_target="tpu_custom_call" | custom-call | bytes 2097152 | tf_op jit(solution)/shard_map/choose/pallas_call | solution.py:145
  42.2 5.3 %collective-permute-start.8 = (bf16[512,512]{1,0:T(8,128)(2,1)}, bf16[512,512]{1,0:T(8,128)(2,1)S(1)}, u32[]{:S(2)}, u32[]{:S(2)}) collective-permute-start(bf16[512,512]{1,0:T(8,128)(2,1)} %bitcast.22), channel_id=1, source_target_pairs={{0,130},{2,128},{128,2},{130,0},{1,131},{3,129},{129,3},{131,1},{4... | collective-permute-start | bytes 1572872 | tf_op jit(solution)/shard_map/ppermute | solution.py:26
  47.5 8.2 %collective-permute-done.8.c_hbm = bf16[512,512]{1,0:T(8,128)(2,1)S(1)} collective-permute-done((bf16[512,512]{1,0:T(8,128)(2,1)}, bf16[512,512]{1,0:T(8,128)(2,1)S(1)}, u32[]{:S(2)}, u32[]{:S(2)}) %collective-permute-start.8) | collective-permute-done | bytes 524320 | tf_op jit(solution)/shard_map/ppermute | solution.py:26
  55.9 3.8 %collective-permute-done.10.c_hbm = bf16[512,512]{1,0:T(8,128)(2,1)S(1)} collective-permute-done((bf16[512,512]{1,0:T(8,128)(2,1)}, bf16[512,512]{1,0:T(8,128)(2,1)S(1)}, u32[]{:S(2)}, u32[]{:S(2)}) %collective-permute-start.10) | collective-permute-done | bytes 524320 | tf_op jit(solution)/shard_map/ppermute | solution.py:26
  60.0 2.6 %collective-permute-done.9 = bf16[256,512]{1,0:T(8,128)(2,1)S(1)} collective-permute-done((bf16[256,512]{1,0:T(8,128)(2,1)S(1)}, bf16[256,512]{1,0:T(8,128)(2,1)S(1)}, u32[]{:S(2)}, u32[]{:S(2)}) %collective-permute-start.9) | collective-permute-done | bytes 262176 | tf_op jit(solution)/shard_map/ppermute | solution.py:26
  62.6 4.9 %collective-permute-done.11 = bf16[256,512]{1,0:T(8,128)(2,1)S(1)} collective-permute-done((bf16[256,512]{1,0:T(8,128)(2,1)S(1)}, bf16[256,512]{1,0:T(8,128)(2,1)S(1)}, u32[]{:S(2)}, u32[]{:S(2)}) %collective-permute-start.11) | collective-permute-done | bytes 262176 | tf_op jit(solution)/shard_map/ppermute | solution.py:26
  68.2 8.9 %all-gather.3.cloned.1.call-done = bf16[224,32,256]{2,1,0:T(8,128)(2,1)} async-done(((bf16[28,32,256]{2,1,0:T(8,128)(2,1)}), bf16[224,32,256]{2,1,0:T(8,128)(2,1)}) %all-gather.3.cloned.1.call-update) | async-done | bytes 3670032 | tf_op jit(solution)/shard_map/all_gather | solution.py:377
  79.1 2.1 %collective-permute-start.7 = (bf16[8,4,32,256]{3,2,1,0:T(8,128)(2,1)S(1)}, bf16[8,4,32,256]{3,2,1,0:T(8,128)(2,1)S(1)}, u32[]{:S(2)}, u32[]{:S(2)}) collective-permute-start(bf16[8,4,32,256]{3,2,1,0:T(8,128)(2,1)S(1)} %slice.98.o0), channel_id=1, source_target_pairs={{0,96},{32,64},{64,32},{96,0},{1,97},{33,65},{65,33},{97,1},{2,98}... | collective-permute-start | bytes 1572872 | tf_op jit(solution)/shard_map/ppermute | solution.py:26
  81.2 8.2 %attend.2 = bf16[512,256]{1,0:T(8,128)(2,1)} custom-call(bf16[512,512]{1,0:T(8,128)(2,1)} %copy-done.8, bf16[512,512]{1,0:T(8,128)(2,1)} %collective-permute-done.12.b_hbm, bf16[512,512]{1,0:T(8,128)(2,1)} %copy-done.7, bf16[512,512]{1,0:T(8,128)(2,1)} %collective-permute-done.13.d_hbm, bf16[2,3,2048]{2,1,0:T(4,128)(2,1)} %copy-done.13, ...), custom_call_target="tpu_custom_call" | custom-call | flops 1744830464 | bytes 6291456 | tf_op jit(solution)/shard_map/attend/pallas_call | solution.py:226
  91.5 8.2 %attend.3.own_ref = bf16[512,256]{1,0:T(8,128)(2,1)} custom-call(bf16[512,512]{1,0:T(8,128)(2,1)} %bitcast.25, bf16[512,512]{1,0:T(8,128)(2,1)} %copy-done.12, bf16[512,512]{1,0:T(8,128)(2,1)} %copy-done.6, bf16[512,512]{1,0:T(8,128)(2,1)} %collective-permute-done.18.d_hbm, bf16[2,3,2048]{2,1,0:T(4,128)(2,1)} %get-tuple-element.37.mod_ref, ...), custom_call_target="tpu_custom_call" | custom-call | flops 1744830464 | bytes 6291456 | tf_op jit(solution)/shard_map/attend/pallas_call | solution.py:226
  101.9 1.5 collective-permute-start.20
  103.4 1.8 collective-permute-start.22
  105.2 3.0 %collective-permute-done.20 = bf16[256,256]{1,0:T(8,128)(2,1)S(1)} collective-permute-done((bf16[256,256]{1,0:T(8,128)(2,1)S(1)}, bf16[256,256]{1,0:T(8,128)(2,1)S(1)}, u32[]{:S(2)}, u32[]{:S(2)}) %collective-permute-start.20) | collective-permute-done | bytes 131104 | tf_op jit(solution)/shard_map/ppermute | solution.py:26
  108.3 3.0 %collective-permute-done.22 = bf16[4,4,32,256]{3,2,1,0:T(8,128)(2,1)S(1)} collective-permute-done((bf16[4,4,32,256]{3,2,1,0:T(8,128)(2,1)S(1)}, bf16[4,4,32,256]{3,2,1,0:T(8,128)(2,1)S(1)}, u32[]{:S(2)}, u32[]{:S(2)}) %collective-permute-start.22) | collective-permute-done | bytes 262176 | tf_op jit(solution)/shard_map/ppermute | solution.py:26
  116.2 13.1 %collective-permute-done.25 = bf16[512,512]{1,0:T(8,128)(2,1)S(1)} collective-permute-done((bf16[512,512]{1,0:T(8,128)(2,1)S(1)}, bf16[512,512]{1,0:T(8,128)(2,1)S(1)}, u32[]{:S(2)}, u32[]{:S(2)}) %collective-permute-start.25) | collective-permute-done | bytes 524320 | tf_op jit(solution)/shard_map/ppermute | solution.py:26
  129.8 1.3 collective-permute-start.26
  131.1 4.6 %collective-permute-start.27 = (bf16[16,6,512]{2,1,0:T(8,128)(2,1)S(1)}, bf16[16,6,512]{2,1,0:T(8,128)(2,1)S(1)}, u32[]{:S(2)}, u32[]{:S(2)}) collective-permute-start(bf16[16,6,512]{2,1,0:T(8,128)(2,1)S(1)} %slice.104), channel_id=1, source_target_pairs={{0,4},{4,8},{8,12},{16,20},{20,24},{24,28},{32,36},{36,40},{40,44}... | collective-permute-start | bytes 294920 | tf_op jit(solution)/shard_map/ppermute | solution.py:36
  136.6 1.5 collective-permute-done.27
  139.3 7.5 %collective-permute-start.28 = (bf16[156,512]{1,0:T(8,128)(2,1)S(1)}, bf16[156,512]{1,0:T(8,128)(2,1)S(1)}, u32[]{:S(2)}, u32[]{:S(2)}) collective-permute-start(bf16[156,512]{1,0:T(8,128)(2,1)S(1)} %reshape.38), channel_id=1, source_target_pairs={{16,0},{20,4},{24,8},{28,12},{32,16},{36,20},{40,24},{44,28},{48,3... | collective-permute-start | bytes 479240 | tf_op jit(solution)/shard_map/ppermute | solution.py:36
  146.8 2.3 %collective-permute-start.29 = (bf16[156,512]{1,0:T(8,128)(2,1)S(1)}, bf16[156,512]{1,0:T(8,128)(2,1)S(1)}, u32[]{:S(2)}, u32[]{:S(2)}) collective-permute-start(bf16[156,512]{1,0:T(8,128)(2,1)S(1)} %reshape.39), channel_id=1, source_target_pairs={{0,16},{4,20},{8,24},{12,28},{16,32},{20,36},{24,40},{28,44},{32,4... | collective-permute-start | bytes 479240 | tf_op jit(solution)/shard_map/ppermute | solution.py:36
  149.1 5.1 %collective-permute-done.28 = bf16[156,512]{1,0:T(8,128)(2,1)S(1)} collective-permute-done((bf16[156,512]{1,0:T(8,128)(2,1)S(1)}, bf16[156,512]{1,0:T(8,128)(2,1)S(1)}, u32[]{:S(2)}, u32[]{:S(2)}) %collective-permute-start.28) | collective-permute-done | bytes 159776 | tf_op jit(solution)/shard_map/ppermute | solution.py:36
  154.3 11.3 %collective-permute-done.29 = bf16[156,512]{1,0:T(8,128)(2,1)S(1)} collective-permute-done((bf16[156,512]{1,0:T(8,128)(2,1)S(1)}, bf16[156,512]{1,0:T(8,128)(2,1)S(1)}, u32[]{:S(2)}, u32[]{:S(2)}) %collective-permute-start.29) | collective-permute-done | bytes 159776 | tf_op jit(solution)/shard_map/ppermute | solution.py:36
  166.2 9.4 %collective-permute-done.30.other = bf16[2,256,512]{2,1,0:T(8,128)(2,1)S(1)} collective-permute-done((bf16[2,256,512]{2,1,0:T(8,128)(2,1)S(1)}, bf16[2,256,512]{2,1,0:T(8,128)(2,1)S(1)}, u32[]{:S(2)}, u32[]{:S(2)}) %collective-permute-start.30) | collective-permute-done | bytes 524320 | tf_op jit(solution)/shard_map/ppermute | solution.py:26
  176.4 2.2 %place.1 = bf16[4,256,512]{2,1,0:T(8,128)(2,1)} custom-call(s32[64]{0:T(128)} %counts_ref.5, bf16[2,256,512]{2,1,0:T(8,128)(2,1)} %copy-done.1, bf16[2,256,512]{2,1,0:T(8,128)(2,1)} %copy-done.3), custom_call_target="tpu_custom_call" | custom-call | bytes 2097152 | tf_op jit(solution)/shard_map/place/pallas_call | solution.py:316
  (113 shorter events, 23.9 us)
Async XLA Ops:
  6.5 70.5 %all-gather.3.cloned.1.call-start = ((), (), s32[]{:S(2)}) async-start(), calls=%async_computation | async-start | bytes 4128768 | tf_op jit(solution)/shard_map/all_gather | solution.py:377
  8.1 6.2 %collective-permute-start = (bf16[5,32,256]{2,1,0:T(8,128)(2,1)}, bf16[5,32,256]{2,1,0:T(8,128)(2,1)S(1)}, u32[]{:S(2)}, u32[]{:S(2)}) collective-permute-start(bf16[5,32,256]{2,1,0:T(8,128)(2,1)} %get-tuple-element.28), channel_id=1, source_target_pairs={{0,128},{128,0},{1,129},{129,1},{2,130},{130,2},{3,131},{131,3},{4... | collective-permute-start | bytes 245768 | tf_op jit(solution)/shard_map/ppermute | solution.py:26
  14.3 5.6 %collective-permute-start.3 = (bf16[6,32,256]{2,1,0:T(8,128)(2,1)S(1)}, bf16[6,32,256]{2,1,0:T(8,128)(2,1)S(1)}, u32[]{:S(2)}, u32[]{:S(2)}) collective-permute-start(bf16[6,32,256]{2,1,0:T(8,128)(2,1)S(1)} %pad_maximum_fusion.2), channel_id=1, source_target_pairs={{0,32},{32,0},{64,96},{96,64},{1,33},{33,1},{65,97},{97,65},{2,34}... | collective-permute-start | bytes 294920 | tf_op jit(solution)/shard_map/ppermute | solution.py:26
  15.9 6.5 %collective-permute-start.4 = (bf16[6,32,256]{2,1,0:T(8,128)(2,1)S(1)}, bf16[6,32,256]{2,1,0:T(8,128)(2,1)S(1)}, u32[]{:S(2)}, u32[]{:S(2)}) collective-permute-start(bf16[6,32,256]{2,1,0:T(8,128)(2,1)S(1)} %pad_maximum_fusion.2), channel_id=1, source_target_pairs={{0,64},{32,96},{64,0},{96,32},{1,65},{33,97},{65,1},{97,33},{2,66}... | collective-permute-start | bytes 294920 | tf_op jit(solution)/shard_map/ppermute | solution.py:26
  18.6 5.8 %collective-permute-start.5 = (bf16[6,32,256]{2,1,0:T(8,128)(2,1)S(1)}, bf16[6,32,256]{2,1,0:T(8,128)(2,1)S(1)}, u32[]{:S(2)}, u32[]{:S(2)}) collective-permute-start(bf16[6,32,256]{2,1,0:T(8,128)(2,1)S(1)} %pad_maximum_fusion.2), channel_id=1, source_target_pairs={{0,96},{32,64},{64,32},{96,0},{1,97},{33,65},{65,33},{97,1},{2,98}... | collective-permute-start | bytes 294920 | tf_op jit(solution)/shard_map/ppermute | solution.py:26
  26.0 12.7 %collective-permute-start.1 = (bf16[2,256,512]{2,1,0:T(8,128)(2,1)}, bf16[2,256,512]{2,1,0:T(8,128)(2,1)S(1)}, u32[]{:S(2)}, u32[]{:S(2)}) collective-permute-start(bf16[2,256,512]{2,1,0:T(8,128)(2,1)} %get-tuple-element.32), channel_id=1, source_target_pairs={{0,4},{4,0},{8,12},{12,8},{16,20},{20,16},{24,28},{28,24},{1,5},{5... | collective-permute-start | bytes 1572872 | tf_op jit(solution)/shard_map/ppermute | solution.py:26
  28.0 10.7 %collective-permute-start.2 = (bf16[1,3,2048]{2,1,0:T(4,128)(2,1)}, bf16[1,3,2048]{2,1,0:T(4,128)(2,1)S(1)}, u32[]{:S(2)}, u32[]{:S(2)}) collective-permute-start(bf16[1,3,2048]{2,1,0:T(4,128)(2,1)} %mod.1), channel_id=1, source_target_pairs={{0,4},{4,0},{8,12},{12,8},{16,20},{20,16},{24,28},{28,24},{1,5},{5... | collective-permute-start | bytes 36872 | tf_op jit(solution)/shard_map/ppermute | solution.py:26
  42.2 13.6 %collective-permute-start.8 = (bf16[512,512]{1,0:T(8,128)(2,1)}, bf16[512,512]{1,0:T(8,128)(2,1)S(1)}, u32[]{:S(2)}, u32[]{:S(2)}) collective-permute-start(bf16[512,512]{1,0:T(8,128)(2,1)} %bitcast.22), channel_id=1, source_target_pairs={{0,130},{2,128},{128,2},{130,0},{1,131},{3,129},{129,3},{131,1},{4... | collective-permute-start | bytes 1572872 | tf_op jit(solution)/shard_map/ppermute | solution.py:26
  47.5 12.2 %collective-permute-start.10 = (bf16[512,512]{1,0:T(8,128)(2,1)}, bf16[512,512]{1,0:T(8,128)(2,1)S(1)}, u32[]{:S(2)}, u32[]{:S(2)}) collective-permute-start(bf16[512,512]{1,0:T(8,128)(2,1)} %bitcast.23), channel_id=1, source_target_pairs={{0,2},{2,0},{128,130},{130,128},{1,3},{3,1},{129,131},{131,129},{4... | collective-permute-start | bytes 1572872 | tf_op jit(solution)/shard_map/ppermute | solution.py:26
  55.8 6.8 %collective-permute-start.9 = (bf16[256,512]{1,0:T(8,128)(2,1)S(1)}, bf16[256,512]{1,0:T(8,128)(2,1)S(1)}, u32[]{:S(2)}, u32[]{:S(2)}) collective-permute-start(bf16[256,512]{1,0:T(8,128)(2,1)S(1)} %slice.99), channel_id=1, source_target_pairs={{0,2},{2,0},{128,130},{130,128},{1,3},{3,1},{129,131},{131,129},{4... | collective-permute-start | bytes 786440 | tf_op jit(solution)/shard_map/ppermute | solution.py:26
  59.8 7.7 %collective-permute-start.11 = (bf16[256,512]{1,0:T(8,128)(2,1)S(1)}, bf16[256,512]{1,0:T(8,128)(2,1)S(1)}, u32[]{:S(2)}, u32[]{:S(2)}) collective-permute-start(bf16[256,512]{1,0:T(8,128)(2,1)S(1)} %slice.100), channel_id=1, source_target_pairs={{0,130},{2,128},{128,2},{130,0},{1,131},{3,129},{129,3},{131,1},{4... | collective-permute-start | bytes 786440 | tf_op jit(solution)/shard_map/ppermute | solution.py:26
  59.9 19.3 %collective-permute-start.13 = (bf16[512,512]{1,0:T(8,128)(2,1)S(1)}, bf16[512,512]{1,0:T(8,128)(2,1)}, u32[]{:S(2)}, u32[]{:S(2)}) collective-permute-start(bf16[512,512]{1,0:T(8,128)(2,1)S(1)} %collective-permute-done.8.c_hbm), channel_id=1, source_target_pairs={{0,1},{1,0},{2,3},{3,2},{4,5},{5,4},{6,7},{7,6},{8,9},{9,8},{10,11... | collective-permute-start | bytes 1572872 | tf_op jit(solution)/shard_map/ppermute | solution.py:26
  67.5 13.7 %collective-permute-start.12 = (bf16[512,512]{1,0:T(8,128)(2,1)S(1)}, bf16[512,512]{1,0:T(8,128)(2,1)}, u32[]{:S(2)}, u32[]{:S(2)}) collective-permute-start(bf16[512,512]{1,0:T(8,128)(2,1)S(1)} %constant_dynamic-update-slice_fusion.5.a_hbm), channel_id=1, source_target_pairs={{0,1},{1,0},{2,3},{3,2},{4,5},{5,4},{6,7},{7,6},{8,9},{9,8},{10,11... | collective-permute-start | bytes 1572872 | tf_op jit(solution)/shard_map/ppermute | solution.py:26
  67.6 22.8 %collective-permute-start.17 = (bf16[512,512]{1,0:T(8,128)(2,1)}, bf16[512,512]{1,0:T(8,128)(2,1)S(1)}, u32[]{:S(2)}, u32[]{:S(2)}) collective-permute-start(bf16[512,512]{1,0:T(8,128)(2,1)} %bitcast.24), channel_id=1, source_target_pairs={{0,1},{1,0},{2,3},{3,2},{4,5},{5,4},{6,7},{7,6},{8,9},{9,8},{10,11... | collective-permute-start | bytes 1572872 | tf_op jit(solution)/shard_map/ppermute | solution.py:26
  68.1 23.4 %collective-permute-start.18 = (bf16[512,512]{1,0:T(8,128)(2,1)S(1)}, bf16[512,512]{1,0:T(8,128)(2,1)}, u32[]{:S(2)}, u32[]{:S(2)}) collective-permute-start(bf16[512,512]{1,0:T(8,128)(2,1)S(1)} %collective-permute-done.10.c_hbm), channel_id=1, source_target_pairs={{0,1},{1,0},{2,3},{3,2},{4,5},{5,4},{6,7},{7,6},{8,9},{9,8},{10,11... | collective-permute-start | bytes 1572872 | tf_op jit(solution)/shard_map/ppermute | solution.py:26
  68.2 10.0 %collective-permute-start.14 = (bf16[2,3,2048]{2,1,0:T(4,128)(2,1)}, bf16[2,3,2048]{2,1,0:T(4,128)(2,1)S(1)}, u32[]{:S(2)}, u32[]{:S(2)}) collective-permute-start(bf16[2,3,2048]{2,1,0:T(4,128)(2,1)} %get-tuple-element.37.mod_ref), channel_id=1, source_target_pairs={{0,128},{128,0},{1,129},{129,1},{2,130},{130,2},{3,131},{131,3},{4... | collective-permute-start | bytes 73736 | tf_op jit(solution)/shard_map/ppermute | solution.py:26
  78.2 21.6 %collective-permute-start.6 = (bf16[8,4,32,256]{3,2,1,0:T(8,128)(2,1)S(1)}, bf16[8,4,32,256]{3,2,1,0:T(8,128)(2,1)S(1)}, u32[]{:S(2)}, u32[]{:S(2)}) collective-permute-start(bf16[8,4,32,256]{3,2,1,0:T(8,128)(2,1)S(1)} %slice.98.o0), channel_id=1, source_target_pairs={{0,32},{32,0},{64,96},{96,64},{1,33},{33,1},{65,97},{97,65},{2,34}... | collective-permute-start | bytes 1572872 | tf_op jit(solution)/shard_map/ppermute | solution.py:26
  79.1 20.6 %collective-permute-start.7 = (bf16[8,4,32,256]{3,2,1,0:T(8,128)(2,1)S(1)}, bf16[8,4,32,256]{3,2,1,0:T(8,128)(2,1)S(1)}, u32[]{:S(2)}, u32[]{:S(2)}) collective-permute-start(bf16[8,4,32,256]{3,2,1,0:T(8,128)(2,1)S(1)} %slice.98.o0), channel_id=1, source_target_pairs={{0,96},{32,64},{64,32},{96,0},{1,97},{33,65},{65,33},{97,1},{2,98}... | collective-permute-start | bytes 1572872 | tf_op jit(solution)/shard_map/ppermute | solution.py:26
  89.4 10.3 %collective-permute-start.15 = (bf16[512,256]{1,0:T(8,128)(2,1)}, bf16[512,256]{1,0:T(8,128)(2,1)S(1)}, u32[]{:S(2)}, u32[]{:S(2)}) collective-permute-start(bf16[512,256]{1,0:T(8,128)(2,1)} %attend.2), channel_id=1, source_target_pairs={{0,2},{2,0},{128,130},{130,128},{1,3},{3,1},{129,131},{131,129},{4... | collective-permute-start | bytes 786440 | tf_op jit(solution)/shard_map/ppermute | solution.py:26
  90.4 9.4 %collective-permute-start.16 = (bf16[512,256]{1,0:T(8,128)(2,1)}, bf16[512,256]{1,0:T(8,128)(2,1)S(1)}, u32[]{:S(2)}, u32[]{:S(2)}) collective-permute-start(bf16[512,256]{1,0:T(8,128)(2,1)} %attend.2), channel_id=1, source_target_pairs={{0,130},{2,128},{128,2},{130,0},{1,131},{3,129},{129,3},{131,1},{4... | collective-permute-start | bytes 786440 | tf_op jit(solution)/shard_map/ppermute | solution.py:26
  99.8 5.4 %collective-permute-start.19 = (bf16[256,256]{1,0:T(8,128)(2,1)S(1)}, bf16[256,256]{1,0:T(8,128)(2,1)S(1)}, u32[]{:S(2)}, u32[]{:S(2)}) collective-permute-start(bf16[256,256]{1,0:T(8,128)(2,1)S(1)} %slice.81), channel_id=1, source_target_pairs={{0,2},{2,0},{128,130},{130,128},{1,3},{3,1},{129,131},{131,129},{4... | collective-permute-start | bytes 393224 | tf_op jit(solution)/shard_map/ppermute | solution.py:26
  100.7 7.5 %collective-permute-start.21 = (bf16[4,4,32,256]{3,2,1,0:T(8,128)(2,1)S(1)}, bf16[4,4,32,256]{3,2,1,0:T(8,128)(2,1)S(1)}, u32[]{:S(2)}, u32[]{:S(2)}) collective-permute-start(bf16[4,4,32,256]{3,2,1,0:T(8,128)(2,1)S(1)} %slice.83), channel_id=1, source_target_pairs={{0,32},{32,0},{64,96},{96,64},{1,33},{33,1},{65,97},{97,65},{2,34}... | collective-permute-start | bytes 786440 | tf_op jit(solution)/shard_map/ppermute | solution.py:26
  101.9 6.3 %collective-permute-start.20 = (bf16[256,256]{1,0:T(8,128)(2,1)S(1)}, bf16[256,256]{1,0:T(8,128)(2,1)S(1)}, u32[]{:S(2)}, u32[]{:S(2)}) collective-permute-start(bf16[256,256]{1,0:T(8,128)(2,1)S(1)} %slice.82), channel_id=1, source_target_pairs={{0,130},{2,128},{128,2},{130,0},{1,131},{3,129},{129,3},{131,1},{4... | collective-permute-start | bytes 393224 | tf_op jit(solution)/shard_map/ppermute | solution.py:26
  103.4 7.9 %collective-permute-start.22 = (bf16[4,4,32,256]{3,2,1,0:T(8,128)(2,1)S(1)}, bf16[4,4,32,256]{3,2,1,0:T(8,128)(2,1)S(1)}, u32[]{:S(2)}, u32[]{:S(2)}) collective-permute-start(bf16[4,4,32,256]{3,2,1,0:T(8,128)(2,1)S(1)} %slice.84), channel_id=1, source_target_pairs={{0,96},{32,64},{64,32},{96,0},{1,97},{33,65},{65,33},{97,1},{2,98}... | collective-permute-start | bytes 786440 | tf_op jit(solution)/shard_map/ppermute | solution.py:26
  113.1 2.0 %collective-permute-start.24 = (bf16[512,512]{1,0:T(8,128)(2,1)S(1)}, bf16[512,512]{1,0:T(8,128)(2,1)S(1)}, u32[]{:S(2)}, u32[]{:S(2)}) collective-permute-start(bf16[512,512]{1,0:T(8,128)(2,1)S(1)} %get-tuple-element.46), channel_id=1, source_target_pairs={{0,1},{1,0},{2,3},{3,2},{4,5},{5,4},{6,7},{7,6},{8,9},{9,8},{10,11... | collective-permute-start | bytes 1572872 | tf_op jit(solution)/shard_map/ppermute | solution.py:26
  114.1 2.1 %collective-permute-start.23 = (bf16[512,512]{1,0:T(8,128)(2,1)S(1)}, bf16[512,512]{1,0:T(8,128)(2,1)S(1)}, u32[]{:S(2)}, u32[]{:S(2)}) collective-permute-start(bf16[512,512]{1,0:T(8,128)(2,1)S(1)} %get-tuple-element.44), channel_id=1, source_target_pairs={{0,1},{1,0},{2,3},{3,2},{4,5},{5,4},{6,7},{7,6},{8,9},{9,8},{10,11... | collective-permute-start | bytes 1572872 | tf_op jit(solution)/shard_map/ppermute | solution.py:26
  115.3 14.1 %collective-permute-start.25 = (bf16[512,512]{1,0:T(8,128)(2,1)S(1)}, bf16[512,512]{1,0:T(8,128)(2,1)S(1)}, u32[]{:S(2)}, u32[]{:S(2)}) collective-permute-start(bf16[512,512]{1,0:T(8,128)(2,1)S(1)} %add_convert_fusion.1), channel_id=1, source_target_pairs={{0,2},{2,0},{1,3},{3,1},{4,6},{6,4},{5,7},{7,5},{8,10},{10,8},{9,1... | collective-permute-start | bytes 1572872 | tf_op jit(solution)/shard_map/ppermute | solution.py:26
  129.8 6.9 %collective-permute-start.26 = (bf16[16,6,512]{2,1,0:T(8,128)(2,1)S(1)}, bf16[16,6,512]{2,1,0:T(8,128)(2,1)S(1)}, u32[]{:S(2)}, u32[]{:S(2)}) collective-permute-start(bf16[16,6,512]{2,1,0:T(8,128)(2,1)S(1)} %slice.102), channel_id=1, source_target_pairs={{4,0},{8,4},{12,8},{20,16},{24,20},{28,24},{36,32},{40,36},{44,40}... | collective-permute-start | bytes 294920 | tf_op jit(solution)/shard_map/ppermute | solution.py:36
  131.1 7.1 %collective-permute-start.27 = (bf16[16,6,512]{2,1,0:T(8,128)(2,1)S(1)}, bf16[16,6,512]{2,1,0:T(8,128)(2,1)S(1)}, u32[]{:S(2)}, u32[]{:S(2)}) collective-permute-start(bf16[16,6,512]{2,1,0:T(8,128)(2,1)S(1)} %slice.104), channel_id=1, source_target_pairs={{0,4},{4,8},{8,12},{16,20},{20,24},{24,28},{32,36},{36,40},{40,44}... | collective-permute-start | bytes 294920 | tf_op jit(solution)/shard_map/ppermute | solution.py:36
  139.3 15.0 %collective-permute-start.28 = (bf16[156,512]{1,0:T(8,128)(2,1)S(1)}, bf16[156,512]{1,0:T(8,128)(2,1)S(1)}, u32[]{:S(2)}, u32[]{:S(2)}) collective-permute-start(bf16[156,512]{1,0:T(8,128)(2,1)S(1)} %reshape.38), channel_id=1, source_target_pairs={{16,0},{20,4},{24,8},{28,12},{32,16},{36,20},{40,24},{44,28},{48,3... | collective-permute-start | bytes 479240 | tf_op jit(solution)/shard_map/ppermute | solution.py:36
  146.8 18.7 %collective-permute-start.29 = (bf16[156,512]{1,0:T(8,128)(2,1)S(1)}, bf16[156,512]{1,0:T(8,128)(2,1)S(1)}, u32[]{:S(2)}, u32[]{:S(2)}) collective-permute-start(bf16[156,512]{1,0:T(8,128)(2,1)S(1)} %reshape.39), channel_id=1, source_target_pairs={{0,16},{4,20},{8,24},{12,28},{16,32},{20,36},{24,40},{28,44},{32,4... | collective-permute-start | bytes 479240 | tf_op jit(solution)/shard_map/ppermute | solution.py:36
  166.1 9.5 %collective-permute-start.30 = (bf16[2,256,512]{2,1,0:T(8,128)(2,1)S(1)}, bf16[2,256,512]{2,1,0:T(8,128)(2,1)S(1)}, u32[]{:S(2)}, u32[]{:S(2)}) collective-permute-start(bf16[2,256,512]{2,1,0:T(8,128)(2,1)S(1)} %pad_maximum_fusion.1.own), channel_id=1, source_target_pairs={{0,4},{4,0},{8,12},{12,8},{16,20},{20,16},{24,28},{28,24},{1,5},{5... | collective-permute-start | bytes 1572872 | tf_op jit(solution)/shard_map/ppermute | solution.py:26
  (14 other events, 118.6 us)
Sparse Core Ops, SparseCore 0:
  26.1 50.8 all-gather.2

commit v4 on v3

v4 whole, which is shorter than its diff:
```python
import functools
import math

import jax
import jax.numpy as jnp
from jax import lax
from jax.experimental import pallas as pl
from jax.experimental.pallas import tpu as pltpu
from jax.sharding import Mesh, PartitionSpec as P

D = 2048
HDIM = 128
S = 16
W = 6
TOK = 256
NARROW = 512
HALF = 256
REGION = ("h", "x", "z")
MP = ("yl", "c")
BF = jnp.bfloat16
F32 = jnp.float32


def xor_swap(block, axis, bit):
    size = math.prod(lax.axis_size(a) for a in ((axis,) if isinstance(axis, str) else axis))
    return lax.ppermute(block, axis, [(i, i ^ bit) for i in range(size)])


def rotate(block, axis, step):
    size = lax.axis_size(axis)
    return lax.ppermute(block, axis, [(i, (i + step) % size) for i in range(size)])


def trade(block, distance, lower):
    route = []
    for i in range(64):
        j = i + distance if lower(i) else i - distance
        if 0 <= j < 64:
            route.append((i, j))
    return lax.ppermute(block, REGION, route)


def opposite(near, side, axis, split_axis):
    size = near.shape[split_axis]
    first = xor_swap(lax.slice_in_dim(side, 0, size // 2, axis=split_axis), axis, 1)
    second = xor_swap(lax.slice_in_dim(near, size // 2, size, axis=split_axis), axis, 3)
    return jnp.concatenate([first, second], axis=split_axis)


def ring_of_four(block, axis, split_axis):
    near = xor_swap(block, axis, 1)
    side = xor_swap(block, axis, 3)
    return block, near, opposite(near, side, axis, split_axis), side


def where_am_i():
    h, x, z = (lax.axis_index(a) for a in REGION)
    yl, c = (lax.axis_index(a) for a in MP)
    return h, x, z, yl, c


def even_count(counts_ref):
    h, x, z, _, _ = where_am_i()
    return counts_ref[h * 32 + x * 8 + (z // 2) * 2]


SMEM = pl.BlockSpec(memory_space=pltpu.SMEM)
VMEM = pl.BlockSpec(memory_space=pltpu.VMEM)
HBM = pl.BlockSpec(memory_space=pltpu.HBM)


def cost(flops, size, special=0):
    return pl.CostEstimate(flops=flops, bytes_accessed=size, transcendentals=special)


def pack_kernel(qkv_ref, out_ref, own, sent):
    h = lax.axis_index("h")
    mine = pl.ds(pl.multiple_of(h * HALF, HALF), HALF)
    theirs = pl.ds(pl.multiple_of((1 - h) * HALF, HALF), HALF)
    for n in range(3):
        own[n] = qkv_ref[n, :, mine]
        sent[n] = qkv_ref[n, :, theirs]
    for n in range(2):
        own[3 + n] = out_ref[:, n * HALF : (n + 1) * HALF]
        sent[3 + n] = out_ref[:, n * HALF : (n + 1) * HALF]


def packed(qkv, out):
    return pl.pallas_call(
        pack_kernel,
        in_specs=[VMEM] * 2,
        out_specs=[VMEM] * 2,
        out_shape=[jax.ShapeDtypeStruct((5, 32, HALF), BF)] * 2,
        cost_estimate=cost(0, 2**18),
        compiler_params=pltpu.CompilerParams(vmem_limit_bytes=8 * 2**20),
        name="pack",
    )(qkv, out)


def split_kernel(counts_ref, data_ref, sent_ref, kept_ref, sem):
    even = even_count(counts_ref)
    odd = lax.axis_index("z") % 2 == 1
    copies = []
    for s in range(2):
        away = jnp.where(odd, jnp.clip(s - even, 0, 3), 2 + s)
        stays = jnp.where(odd, jnp.clip(2 + s - even, 0, 3), s)
        copies.append(pltpu.make_async_copy(data_ref.at[away], sent_ref.at[s], sem))
        copies.append(pltpu.make_async_copy(data_ref.at[stays], kept_ref.at[s], sem))
    for copy in copies:
        copy.start()
    for copy in copies:
        copy.wait()


def split_tiles(counts, data):
    return pl.pallas_call(
        split_kernel,
        in_specs=[SMEM, HBM],
        out_specs=[VMEM, VMEM],
        out_shape=[jax.ShapeDtypeStruct((2, TOK, NARROW), BF)] * 2,
        scratch_shapes=[pltpu.SemaphoreType.DMA],
        cost_estimate=cost(0, 2**21),
        compiler_params=pltpu.CompilerParams(vmem_limit_bytes=12 * 2**20),
        name="split",
    )(counts, data)


def choose_kernel(counts_ref, kept, came, mod, other_mod, tiles, mods, gate):
    even = even_count(counts_ref)
    odd = lax.axis_index("z") % 2 == 1
    place = lax.axis_index("yl") * 2 + lax.axis_index("c")
    cols = pl.ds(pl.multiple_of(place * NARROW, NARROW), NARROW)
    for s in range(2):
        use_other = jnp.where(odd, 2 + s < even, s >= even)

        @pl.when(use_other)
        def _():
            tiles[s] = came[s]
            mods[s] = other_mod[0]
            gate[s] = other_mod[0, 2:3, cols].astype(F32)

        @pl.when(jnp.logical_not(use_other))
        def _():
            tiles[s] = kept[s]
            mods[s] = mod[0]
            gate[s] = mod[0, 2:3, cols].astype(F32)


def choose(counts, kept, came, mod, other_mod):
    return pl.pallas_call(
        choose_kernel,
        in_specs=[SMEM] + [VMEM] * 4,
        out_specs=[VMEM] * 3,
        out_shape=[
            jax.ShapeDtypeStruct((2, TOK, NARROW), BF),
            jax.ShapeDtypeStruct((2, 3, D), BF),
            jax.ShapeDtypeStruct((2, 1, NARROW), F32),
        ],
        cost_estimate=cost(0, 2**21),
        compiler_params=pltpu.CompilerParams(vmem_limit_bytes=12 * 2**20),
        name="choose",
    )(counts, kept, came, mod, other_mod)


def hidden_kernel(a_ref, b_ref, c_ref, d_ref, mod_ref, out_ref):
    place = lax.axis_index("yl") * 2 + lax.axis_index("c")
    parts = [r[...].astype(F32) for r in (a_ref, b_ref, c_ref, d_ref)]
    mean = sum(jnp.sum(p, axis=-1, keepdims=True) for p in parts) * (1.0 / D)
    parts = [p - mean for p in parts]
    spread = sum(jnp.sum(p * p, axis=-1, keepdims=True) for p in parts) * (1.0 / D)
    scale = lax.rsqrt(spread + 1e-06)
    for j, p in enumerate(parts):
        source = pl.ds(pl.multiple_of((place ^ j) * NARROW, NARROW), NARROW)
        gain = 1.0 + mod_ref[0, 1:2, source].astype(F32)
        value = p * scale * gain + mod_ref[0, 0:1, source].astype(F32)
        out_ref[:, j * NARROW : (j + 1) * NARROW] = value.astype(BF)


def hidden_of(pieces, mods):
    rows = 256
    piece = pl.BlockSpec((rows, NARROW), lambda i: (i, 0))
    return pl.pallas_call(
        hidden_kernel,
        grid=(512 // rows,),
        in_specs=[piece] * 4 + [pl.BlockSpec((1, 3, D), lambda i: (i * rows // TOK, 0, 0))],
        out_specs=pl.BlockSpec((rows, D), lambda i: (i, 0)),
        out_shape=jax.ShapeDtypeStruct((512, D), BF),
        cost_estimate=cost(8 * 512 * D, 4 * 512 * D, 512),
        compiler_params=pltpu.CompilerParams(vmem_limit_bytes=24 * 2**20),
        name="hidden",
    )(*pieces, mods)


def attend_kernel(hid_hbm, g_ref, out_ref, hid_ref, w_ref, total_ref, sem):
    h, x, _, yl, c = where_am_i()
    copies = []
    for j in range(4):
        cols = pl.ds(j * NARROW, NARROW)
        group = [pltpu.make_async_copy(hid_hbm.at[:, cols], hid_ref.at[:, cols], sem.at[j])]
        hr = (yl ^ (j // 2)) ^ h
        for half in range(2):
            xr = ((c ^ (j % 2)) * 2 + half) ^ x
            for n in range(3):
                group.append(
                    pltpu.make_async_copy(
                        g_ref.at[:, (xr * 2 + hr) * 3 + n],
                        w_ref.at[j, half, :, :, pl.ds(n * HALF, HALF)],
                        sem.at[j],
                    )
                )
        for copy in group:
            copy.start()
        copies.append(group)
    for j, group in enumerate(copies):
        for copy in group:
            copy.wait()
        part = jnp.dot(
            hid_ref[:, j * NARROW : (j + 1) * NARROW],
            w_ref[j].reshape(NARROW, 3 * HALF),
            preferred_element_type=F32,
        )
        if j == 0:
            total_ref[...] = part
        elif j < 3:
            total_ref[...] += part
    proj = (total_ref[...] + part).astype(BF)

    def block(t, kind, n):
        start = kind * HALF + n * HDIM
        return proj[t * TOK : (t + 1) * TOK, start : start + HDIM]

    units = [(t, n) for t in range(2) for n in range(2)]
    scores = [
        lax.dot_general(
            block(t, 0, n), block(t, 1, n), (((1,), (1,)), ((), ())), preferred_element_type=F32
        )
        * (1.0 / math.sqrt(HDIM))
        for t, n in units
    ]
    exps = [jnp.exp(s - jnp.max(s, axis=-1, keepdims=True)) for s in scores]
    for e, (t, n) in zip(exps, units):
        got = jnp.dot(e.astype(BF), block(t, 2, n), preferred_element_type=F32)
        got = got / jnp.sum(e, axis=-1, keepdims=True)
        out_ref[t * TOK : (t + 1) * TOK, n * HDIM : (n + 1) * HDIM] = got.astype(BF)


def attended_of(hidden, gathered):
    return pl.pallas_call(
        attend_kernel,
        in_specs=[HBM] * 2,
        out_specs=VMEM,
        out_shape=jax.ShapeDtypeStruct((512, HALF), BF),
        scratch_shapes=[
            pltpu.VMEM((512, D), BF),
            pltpu.VMEM((4, 2, 8, 32, 3 * HALF), BF),
            pltpu.VMEM((512, 3 * HALF), F32),
            pltpu.SemaphoreType.DMA((4,)),
        ],
        compiler_params=pltpu.CompilerParams(vmem_limit_bytes=60 * 2**20),
        cost_estimate=cost(
            2 * (2 * 512 * D * 768 + 4 * 4 * TOK * TOK * HDIM), 6 * 2**20, 4 * TOK * TOK
        ),
        name="attend",
    )(hidden, gathered)


def project_kernel(a_ref, b_ref, c_ref, d_ref, o0, o1, o2, o3, keep_ref, send_ref, w_ref, sem):
    h, x, _, _, c = where_am_i()
    copies = []
    for xr, piece in enumerate((o0, o1, o2, o3)):
        px = x ^ xr
        slot = ((px // 2) ^ c) * 2 + px % 2
        for j in range(4):
            block = (j % 2) * 2 + (h ^ (j // 2))
            copies.append(
                pltpu.make_async_copy(
                    piece.at[:, block], w_ref.at[slot, :, :, pl.ds(j * HALF, HALF)], sem
                )
            )
    for copy in copies:
        copy.start()
    for copy in copies:
        copy.wait()
    attended = jnp.concatenate([r[...] for r in (a_ref, b_ref, c_ref, d_ref)], axis=1)
    for b, out_ref in ((1, send_ref), (0, keep_ref)):
        weight = w_ref[2 * b : 2 * b + 2].reshape(NARROW, 4 * HALF)
        total = lax.dot_general(
            attended, weight, (((1,), (1,)), ((), ())), preferred_element_type=F32
        )
        out_ref[...] = total.astype(out_ref.dtype)


def partial_of(attended, os):
    return pl.pallas_call(
        project_kernel,
        in_specs=[VMEM] * 4 + [HBM] * 4,
        out_specs=[VMEM] * 2,
        out_shape=[
            jax.ShapeDtypeStruct((512, NARROW), F32),
            jax.ShapeDtypeStruct((512, NARROW), BF),
        ],
        scratch_shapes=[pltpu.VMEM((4, 8, 32, 4 * HALF), BF), pltpu.SemaphoreType.DMA],
        compiler_params=pltpu.CompilerParams(vmem_limit_bytes=16 * 2**20),
        cost_estimate=cost(2 * 512 * 1024 * 1024, 4 * 2**20),
        name="project",
    )(*attended, *os)


def place_kernel(counts_ref, own, other, out_ref, zero_ref, sem):
    even = even_count(counts_ref)
    parity = lax.axis_index("z") % 2
    zero_ref[...] = jnp.zeros_like(zero_ref)
    waits = []
    for slot in range(4):
        tile = slot + parity * even
        live = jnp.where(parity == 1, tile < 4, slot < even)
        ours = tile // 2 == parity
        target = out_ref.at[slot]

        @pl.when(live & ours)
        def _():
            pltpu.make_async_copy(own.at[tile % 2], target, sem).start()

        @pl.when(live & jnp.logical_not(ours))
        def _():
            pltpu.make_async_copy(other.at[tile % 2], target, sem).start()

        @pl.when(jnp.logical_not(live))
        def _():
            pltpu.make_async_copy(zero_ref, target, sem).start()

        waits.append(pltpu.make_async_copy(zero_ref, target, sem))
    for wait in waits:
        wait.wait()


def place_tiles(counts, own, other):
    return pl.pallas_call(
        place_kernel,
        in_specs=[SMEM, VMEM, VMEM],
        out_specs=HBM,
        out_shape=jax.ShapeDtypeStruct((4, TOK, NARROW), BF),
        scratch_shapes=[pltpu.VMEM((TOK, NARROW), BF), pltpu.SemaphoreType.DMA],
        cost_estimate=cost(0, 2**21),
        compiler_params=pltpu.CompilerParams(vmem_limit_bytes=12 * 2**20),
        name="place",
    )(counts, own, other)


def mix(earlier, later, share):
    return ((1.0 - share) * earlier.astype(F32) + share * later.astype(F32)).astype(BF)


def join_rows(strip, region, shares):
    count = strip.shape[1]
    share = shares.reshape(W, 1, 1)
    top, bottom = strip[:W], strip[S - W :]
    north, south = top.reshape(W * count, NARROW), bottom.reshape(W * count, NARROW)
    first = region % 8 < 4
    same = trade(jnp.where(first, south, north), 4, lambda i: i % 8 < 4)
    cross = trade(jnp.where(first, north, south), 4, lambda i: i % 8 >= 4)
    same, cross = lax.optimization_barrier((same, cross))
    later, earlier = jnp.where(first, same, cross), jnp.where(first, cross, same)
    top = jnp.where(region >= 4, mix(earlier.reshape(W, count, NARROW), top, share), top)
    bottom = jnp.where(region < 60, mix(bottom, later.reshape(W, count, NARROW), share), bottom)
    return jnp.concatenate([top, strip[W : S - W], bottom], axis=0)


def blend(tiles, region, shares):
    first, second = tiles[0], tiles[1]
    share = shares.reshape(1, W, 1)
    west, east = first[:, :W], second[:, S - W :]
    odd = region % 2 == 1
    near = trade(jnp.where(odd, west, east), 1, lambda i: i % 2 == 0)
    across = trade(jnp.where(odd, east, west), 1, lambda i: i % 2 == 1)
    near, across = lax.optimization_barrier((near, across))
    later, earlier = jnp.where(odd, across, near), jnp.where(odd, near, across)
    place = region % 4
    left = jnp.where(place != 0, mix(earlier, west, share), west)
    right = jnp.where(place != 3, mix(east, later, share), east)
    inner = mix(first[:, S - W :], second[:, :W], share)
    strip = jnp.concatenate(
        [left, first[:, W : S - W], inner, second[:, W : S - W], right], axis=1
    )
    strip = join_rows(strip, region, shares)
    return jnp.stack([strip[:, :S], strip[:, S - W :]])


def on_device(tile_data, tile_counts, modulation, qkv_weight, out_weight, blend_weights):
    h, x, z, yl, _ = where_am_i()
    region = h * 32 + x * 8 + z
    ring = ("h", "yl")

    own_blocks, sent_blocks = packed(qkv_weight.transpose(1, 0, 2), out_weight)
    came_blocks = xor_swap(sent_blocks, "h", 1)

    tile_data, sent_blocks = lax.optimization_barrier((tile_data, sent_blocks))
    away, kept = split_tiles(tile_counts, tile_data)
    came = xor_swap(away, "z", 1)
    came_mod = xor_swap(modulation, "z", 1)

    came_blocks, kept = lax.optimization_barrier((came_blocks, kept))
    straight = yl == h
    out_kept = jnp.where(straight, own_blocks[3:], came_blocks[3:])
    out_sent = jnp.where(straight, came_blocks[3:], own_blocks[3:])
    qkv = jnp.concatenate([own_blocks[:3], came_blocks[:3]])
    qkv, out_sent = lax.optimization_barrier((qkv, out_sent))
    pieces = [xor_swap(qkv, "x", bit) for bit in (1, 2, 3)]
    out_came = xor_swap(out_sent, "yl", 1)
    *pieces, out_came = lax.optimization_barrier((*pieces, out_came))
    block = jnp.concatenate([qkv, *pieces, out_kept, out_came])
    gathered = lax.all_gather(block, "z", axis=0)

    tiles, mods, gate = choose(tile_counts, kept, came, modulation, came_mod)
    mine = tiles.reshape(512, NARROW)
    _, near, across, side = ring_of_four(mine, ring, 0)
    mods_across = xor_swap(mods, "h", 1)
    hid_own = hidden_of((mine, xor_swap(mine, "c", 1), near, xor_swap(near, "c", 1)), mods)
    across, hid_own = lax.optimization_barrier((across, hid_own))
    hid_other = hidden_of(
        (across, xor_swap(across, "c", 1), side, xor_swap(side, "c", 1)), mods_across
    )
    hid_own, hid_other = lax.optimization_barrier((hid_own, hid_other))

    att_sent = attended_of(hid_other, gathered)
    o_block = gathered[:, 24:]
    hid_own, att_sent = lax.optimization_barrier((hid_own, att_sent))
    o_near, o_side = xor_swap(o_block, "x", 1), xor_swap(o_block, "x", 3)
    att_side, att_relay = xor_swap(att_sent, ring, 3), xor_swap(att_sent, ring, 1)
    att_own = attended_of(hid_own, gathered)
    o_near, o_side, att_side, att_relay, att_own = lax.optimization_barrier(
        (o_near, o_side, att_side, att_relay, att_own)
    )
    att_near, att_across = xor_swap(att_own, ring, 1), xor_swap(att_relay, ring, 3)
    o_all = (o_block, o_near, opposite(o_near, o_side, "x", 0), o_side)

    keep, send = partial_of((att_own, att_near, att_across, att_side), o_all)
    summed = keep + xor_swap(send, "c", 1).astype(F32)
    updated = tiles.astype(F32) + gate * summed.reshape(2, TOK, NARROW)
    updated = updated.astype(BF).reshape(2, S, S, NARROW)
    finished = blend(updated, region, blend_weights).reshape(2, TOK, NARROW)
    return place_tiles(tile_counts, finished, xor_swap(finished, "z", 1))


def solution(mesh):
    fine = Mesh(mesh.devices.reshape(2, 4, 8, 2, 2), REGION + MP)
    return jax.shard_map(
        on_device,
        mesh=fine,
        in_specs=(
            P(REGION, None, MP),
            P(),
            P(REGION, None, None),
            P(REGION, None, MP),
            P(REGION, MP),
            P(),
        ),
        out_specs=P(REGION, None, MP),
        check_vma=False,
    )
```

time: 187 us -> 165 us (0.88)
  waiting for transfers between devices: 93.4 us -> 83.4 us
  Pallas kernels: 26.8 us -> 17.2 us
  starting transfers between devices: 42.1 us -> 39.4 us
    pallas_call x5 -> x6, Pallas kernels: 19.7 us -> 14.4 us  [the longest x2 9.59 us: attended_of(): pl.pallas_call(attend_kernel, in_specs=[HBM] * 2, out_specs=VMEM, out_sha...]
    all_gather x1, waiting for transfers between devices: 8.89 us -> 4.69 us  [on_device(): gathered = lax.all_gather(block, 'z', axis=0)]
    ppermute x27 -> x26, waiting for transfers between devices: 65.8 us -> 62 us  [xor_swap(): return lax.ppermute(block, axis, [(i, i ^ bit) for i in range(size)])]
    unnamed x36 -> x27, local copies, waits for them, and re-layouts: 4.76 us -> 7.05 us
    pallas_call x1, Pallas kernels: 2.85 us -> 0.66 us  [split_tiles(): pl.pallas_call(split_kernel, in_specs=[SMEM, HBM], out_specs=[VMEM, VMEM]...]
    ppermute x27 -> x26, starting transfers between devices: 26.5 us -> 24.3 us  [xor_swap(): return lax.ppermute(block, axis, [(i, i ^ bit) for i in range(size)])]
    ppermute x4, waiting for transfers between devices: 18.7 us -> 16.8 us  [trade(): return lax.ppermute(block, REGION, route)]
  transfers between devices with their start and end apart: 32 -> 31, of which waited for: 20 -> 19; matrix products, arithmetic and copies ran while one was open for 1% -> 0% of each run, Pallas kernels for 12% -> 9%
where the time goes in v4:
time: 165 us
  waiting for transfers between devices  83.4 us (51%)
  starting transfers between devices  39.4 us (24%)
  Pallas kernels  17.2 us (10%)
  between operations  13.9 us (8%)
  local copies, waits for them, and re-layouts  9.45 us (6%)
    ppermute x26, waiting for transfers between devices, xor_swap(): return lax.ppermute(block, axis, [(i, i ^ bit) for i in range(size)])  62 us
    ppermute x26, starting transfers between devices, xor_swap(): return lax.ppermute(block, axis, [(i, i ^ bit) for i in range(size)])  24.3 us
    ppermute x4, waiting for transfers between devices, trade(): return lax.ppermute(block, REGION, route)  16.8 us
    ppermute x4, starting transfers between devices, trade(): return lax.ppermute(block, REGION, route)  15.1 us
    pallas_call x2, Pallas kernels, attended_of(): pl.pallas_call(attend_kernel, in_specs=[HBM] * 2, out_specs=VMEM, out_sha...  9.59 us
    unnamed x27, local copies, waits for them, and re-layouts  7.05 us
    all_gather x1, waiting for transfers between devices, on_device(): gathered = lax.all_gather(block, 'z', axis=0)  4.69 us
  transfers between devices with their start and end apart: 31, of which 19 were waited for; matrix products, arithmetic and copies ran while one was open for 0% of the time, Pallas kernels for 9%

profile of v4, /device:TPU:24, one launch (start us, length us, event | category | flops | bytes accessed | tf_op | source)
XLA Modules:
  0.0 164.7 jit_solution(2786853889459274614)
XLA Ops:
  12.1 2.2 %collective-permute-done = bf16[5,32,256]{2,1,0:T(8,128)(2,1)S(1)} collective-permute-done((bf16[5,32,256]{2,1,0:T(8,128)(2,1)S(1)}, bf16[5,32,256]{2,1,0:T(8,128)(2,1)S(1)}, u32[]{:S(2)}, u32[]{:S(2)}) %collective-permute-start) | collective-permute-done | bytes 81952 | tf_op jit(solution)/shard_map/ppermute | solution.py:26
  14.3 1.6 collective-permute-start.3
  15.9 2.7 %collective-permute-start.4 = (bf16[6,32,256]{2,1,0:T(8,128)(2,1)S(1)}, bf16[6,32,256]{2,1,0:T(8,128)(2,1)S(1)}, u32[]{:S(2)}, u32[]{:S(2)}) collective-permute-start(bf16[6,32,256]{2,1,0:T(8,128)(2,1)S(1)} %pad_maximum_fusion.4), channel_id=1, source_target_pairs={{0,64},{32,96},{64,0},{96,32},{1,65},{33,97},{65,1},{97,33},{2,66}... | collective-permute-start | bytes 294920 | tf_op jit(solution)/shard_map/ppermute | solution.py:26
  19.8 3.2 %collective-permute-done.6 = bf16[2,32,256]{2,1,0:T(8,128)(2,1)S(1)} collective-permute-done((bf16[2,32,256]{2,1,0:T(8,128)(2,1)S(1)}, bf16[2,32,256]{2,1,0:T(8,128)(2,1)S(1)}, u32[]{:S(2)}, u32[]{:S(2)}) %collective-permute-start.6) | collective-permute-done | bytes 32800 | tf_op jit(solution)/shard_map/ppermute | solution.py:26
  25.3 2.0 %collective-permute-start.1 = (bf16[2,256,512]{2,1,0:T(8,128)(2,1)S(1)}, bf16[2,256,512]{2,1,0:T(8,128)(2,1)S(1)}, u32[]{:S(2)}, u32[]{:S(2)}) collective-permute-start(bf16[2,256,512]{2,1,0:T(8,128)(2,1)S(1)} %get-tuple-element.42), channel_id=1, source_target_pairs={{0,4},{4,0},{8,12},{12,8},{16,20},{20,16},{24,28},{28,24},{1,5},{5... | collective-permute-start | bytes 1572872 | tf_op jit(solution)/shard_map/ppermute | solution.py:26
  27.4 10.4 %collective-permute-done.2.other_mod = bf16[1,3,2048]{2,1,0:T(4,128)(2,1)S(1)} collective-permute-done((bf16[1,3,2048]{2,1,0:T(4,128)(2,1)S(1)}, bf16[1,3,2048]{2,1,0:T(4,128)(2,1)S(1)}, u32[]{:S(2)}, u32[]{:S(2)}) %collective-permute-start.2) | collective-permute-done | bytes 12320 | tf_op jit(solution)/shard_map/ppermute | solution.py:26
  40.3 9.3 %collective-permute-done.11.c_ref = bf16[512,512]{1,0:T(8,128)(2,1)S(1)} collective-permute-done((bf16[512,512]{1,0:T(8,128)(2,1)S(1)}, bf16[512,512]{1,0:T(8,128)(2,1)S(1)}, u32[]{:S(2)}, u32[]{:S(2)}) %collective-permute-start.11) | collective-permute-done | bytes 524320 | tf_op jit(solution)/shard_map/ppermute | solution.py:26
  49.6 1.7 %collective-permute-done.9.c_ref = bf16[512,512]{1,0:T(8,128)(2,1)S(1)} collective-permute-done((bf16[512,512]{1,0:T(8,128)(2,1)S(1)}, bf16[512,512]{1,0:T(8,128)(2,1)S(1)}, u32[]{:S(2)}, u32[]{:S(2)}) %collective-permute-start.9) | collective-permute-done | bytes 524320 | tf_op jit(solution)/shard_map/ppermute | solution.py:26
  52.9 5.6 %collective-permute-done.10 = bf16[256,512]{1,0:T(8,128)(2,1)S(1)} collective-permute-done((bf16[256,512]{1,0:T(8,128)(2,1)S(1)}, bf16[256,512]{1,0:T(8,128)(2,1)S(1)}, u32[]{:S(2)}, u32[]{:S(2)}) %collective-permute-start.10) | collective-permute-done | bytes 262176 | tf_op jit(solution)/shard_map/ppermute | solution.py:26
  58.4 1.8 %collective-permute-done.12 = bf16[256,512]{1,0:T(8,128)(2,1)S(1)} collective-permute-done((bf16[256,512]{1,0:T(8,128)(2,1)S(1)}, bf16[256,512]{1,0:T(8,128)(2,1)S(1)}, u32[]{:S(2)}, u32[]{:S(2)}) %collective-permute-start.12) | collective-permute-done | bytes 262176 | tf_op jit(solution)/shard_map/ppermute | solution.py:26
  60.3 1.6 hidden.2.hid_hbm
  64.1 4.6 %collective-permute-done.17.mod_ref = bf16[2,3,2048]{2,1,0:T(4,128)(2,1)S(1)} collective-permute-done((bf16[2,3,2048]{2,1,0:T(4,128)(2,1)S(1)}, bf16[2,3,2048]{2,1,0:T(4,128)(2,1)S(1)}, u32[]{:S(2)}, u32[]{:S(2)}) %collective-permute-start.17) | collective-permute-done | bytes 24608 | tf_op jit(solution)/shard_map/ppermute | solution.py:26
  68.7 1.6 hidden.3.hid_hbm
  71.7 4.7 %all-gather.3.cloned.1.call-done = bf16[224,32,256]{2,1,0:T(8,128)(2,1)} async-done(((bf16[28,32,256]{2,1,0:T(8,128)(2,1)}), bf16[224,32,256]{2,1,0:T(8,128)(2,1)}) %all-gather.3.cloned.1.call-update) | async-done | bytes 3670032 | tf_op jit(solution)/shard_map/all_gather | solution.py:412
  77.5 1.6 collective-permute-start.7
  79.0 2.1 %collective-permute-start.8 = (bf16[8,4,32,256]{3,2,1,0:T(8,128)(2,1)S(1)}, bf16[8,4,32,256]{3,2,1,0:T(8,128)(2,1)S(1)}, u32[]{:S(2)}, u32[]{:S(2)}) collective-permute-start(bf16[8,4,32,256]{3,2,1,0:T(8,128)(2,1)S(1)} %slice.92.o0), channel_id=1, source_target_pairs={{0,96},{32,64},{64,32},{96,0},{1,97},{33,65},{65,33},{97,1},{2,98}... | collective-permute-start | bytes 1572872 | tf_op jit(solution)/shard_map/ppermute | solution.py:26
  81.1 4.8 %attend.2 = bf16[512,256]{1,0:T(8,128)(2,1)} custom-call(bf16[512,2048]{1,0:T(8,128)(2,1)} %copy-done.1, bf16[8,28,32,256]{3,2,1,0:T(8,128)(2,1)} %bitcast.28), custom_call_target="tpu_custom_call" | custom-call | flops 3489660928 | bytes 6291456 | tf_op jit(solution)/shard_map/attend/pallas_call | solution.py:248
  87.4 4.8 %attend.3.a_ref = bf16[512,256]{1,0:T(8,128)(2,1)} custom-call(bf16[512,2048]{1,0:T(8,128)(2,1)} %copy-done, bf16[8,28,32,256]{3,2,1,0:T(8,128)(2,1)} %bitcast.29), custom_call_target="tpu_custom_call" | custom-call | flops 3489660928 | bytes 6291456 | tf_op jit(solution)/shard_map/attend/pallas_call | solution.py:248
  92.2 2.7 %collective-permute-done.18.d_ref = bf16[512,256]{1,0:T(8,128)(2,1)S(1)} collective-permute-done((bf16[512,256]{1,0:T(8,128)(2,1)}, bf16[512,256]{1,0:T(8,128)(2,1)S(1)}, u32[]{:S(2)}, u32[]{:S(2)}) %collective-permute-start.18) | collective-permute-done | bytes 262176 | tf_op jit(solution)/shard_map/ppermute | solution.py:26
  96.7 1.9 %collective-permute-start.21 = (bf16[512,256]{1,0:T(8,128)(2,1)S(1)}, bf16[512,256]{1,0:T(8,128)(2,1)S(1)}, u32[]{:S(2)}, u32[]{:S(2)}) collective-permute-start(bf16[512,256]{1,0:T(8,128)(2,1)S(1)} %collective-permute-done.19), channel_id=1, source_target_pairs={{0,130},{2,128},{128,2},{130,0},{1,131},{3,129},{129,3},{131,1},{4... | collective-permute-start | bytes 786440 | tf_op jit(solution)/shard_map/ppermute | solution.py:26
  98.6 2.9 %collective-permute-done.22 = bf16[4,4,32,256]{3,2,1,0:T(8,128)(2,1)S(1)} collective-permute-done((bf16[4,4,32,256]{3,2,1,0:T(8,128)(2,1)S(1)}, bf16[4,4,32,256]{3,2,1,0:T(8,128)(2,1)S(1)}, u32[]{:S(2)}, u32[]{:S(2)}) %collective-permute-start.22) | collective-permute-done | bytes 262176 | tf_op jit(solution)/shard_map/ppermute | solution.py:26
  101.6 1.7 %collective-permute-done.23 = bf16[4,4,32,256]{3,2,1,0:T(8,128)(2,1)S(1)} collective-permute-done((bf16[4,4,32,256]{3,2,1,0:T(8,128)(2,1)S(1)}, bf16[4,4,32,256]{3,2,1,0:T(8,128)(2,1)S(1)}, u32[]{:S(2)}, u32[]{:S(2)}) %collective-permute-start.23) | collective-permute-done | bytes 262176 | tf_op jit(solution)/shard_map/ppermute | solution.py:26
  104.3 1.6 project.1
  106.1 1.8 %collective-permute-done.24 = bf16[512,512]{1,0:T(8,128)(2,1)S(1)} collective-permute-done((bf16[512,512]{1,0:T(8,128)(2,1)S(1)}, bf16[512,512]{1,0:T(8,128)(2,1)S(1)}, u32[]{:S(2)}, u32[]{:S(2)}) %collective-permute-start.24) | collective-permute-done | bytes 524320 | tf_op jit(solution)/shard_map/ppermute | solution.py:26
  108.5 7.7 %collective-permute-start.26 = (bf16[16,6,512]{2,1,0:T(8,128)(2,1)S(1)}, bf16[16,6,512]{2,1,0:T(8,128)(2,1)S(1)}, u32[]{:S(2)}, u32[]{:S(2)}) collective-permute-start(bf16[16,6,512]{2,1,0:T(8,128)(2,1)S(1)} %get-tuple-element.77), channel_id=1, source_target_pairs={{4,8},{8,4},{12,16},{16,12},{20,24},{24,20},{28,32},{32,28},{36,40... | collective-permute-start | bytes 294920 | tf_op jit(solution)/shard_map/ppermute | solution.py:40
  116.4 5.2 %collective-permute-done.26 = bf16[16,6,512]{2,1,0:T(8,128)(2,1)S(1)} collective-permute-done((bf16[16,6,512]{2,1,0:T(8,128)(2,1)S(1)}, bf16[16,6,512]{2,1,0:T(8,128)(2,1)S(1)}, u32[]{:S(2)}, u32[]{:S(2)}) %collective-permute-start.26) | collective-permute-done | bytes 98336 | tf_op jit(solution)/shard_map/ppermute | solution.py:40
  122.9 7.3 %collective-permute-start.28 = (bf16[156,512]{1,0:T(8,128)(2,1)S(1)}, bf16[156,512]{1,0:T(8,128)(2,1)S(1)}, u32[]{:S(2)}, u32[]{:S(2)}) collective-permute-start(bf16[156,512]{1,0:T(8,128)(2,1)S(1)} %select_n.122), channel_id=1, source_target_pairs={{16,32},{20,36},{24,40},{28,44},{32,16},{36,20},{40,24},{44,28},{4... | collective-permute-start | bytes 479240 | tf_op jit(solution)/shard_map/ppermute | solution.py:40
  130.2 3.8 %collective-permute-done.27 = bf16[156,512]{1,0:T(8,128)(2,1)S(1)} collective-permute-done((bf16[156,512]{1,0:T(8,128)(2,1)S(1)}, bf16[156,512]{1,0:T(8,128)(2,1)S(1)}, u32[]{:S(2)}, u32[]{:S(2)}) %collective-permute-start.27) | collective-permute-done | bytes 159776 | tf_op jit(solution)/shard_map/ppermute | solution.py:40
  134.0 7.7 %collective-permute-done.28 = bf16[156,512]{1,0:T(8,128)(2,1)S(1)} collective-permute-done((bf16[156,512]{1,0:T(8,128)(2,1)S(1)}, bf16[156,512]{1,0:T(8,128)(2,1)S(1)}, u32[]{:S(2)}, u32[]{:S(2)}) %collective-permute-start.28) | collective-permute-done | bytes 159776 | tf_op jit(solution)/shard_map/ppermute | solution.py:40
  142.4 2.2 %collective-permute-start.29 = (bf16[2,256,512]{2,1,0:T(8,128)(2,1)S(1)}, bf16[2,256,512]{2,1,0:T(8,128)(2,1)S(1)}, u32[]{:S(2)}, u32[]{:S(2)}) collective-permute-start(bf16[2,256,512]{2,1,0:T(8,128)(2,1)S(1)} %pad_maximum_fusion.3.own), channel_id=1, source_target_pairs={{0,4},{4,0},{8,12},{12,8},{16,20},{20,16},{24,28},{28,24},{1,5},{5... | collective-permute-start | bytes 1572872 | tf_op jit(solution)/shard_map/ppermute | solution.py:26
  144.6 11.7 %collective-permute-done.29.other = bf16[2,256,512]{2,1,0:T(8,128)(2,1)S(1)} collective-permute-done((bf16[2,256,512]{2,1,0:T(8,128)(2,1)S(1)}, bf16[2,256,512]{2,1,0:T(8,128)(2,1)S(1)}, u32[]{:S(2)}, u32[]{:S(2)}) %collective-permute-start.29) | collective-permute-done | bytes 524320 | tf_op jit(solution)/shard_map/ppermute | solution.py:26
  156.3 1.5 place.1
  (101 shorter events, 24.9 us)
Async XLA Ops:
  6.5 31.2 %copy-start.7 = (s32[64]{0:T(128)S(1)}, s32[64]{0:T(128)}, u32[]{:S(2)}) copy-start(s32[64]{0:T(128)} %counts_ref.5) | copy-start | bytes 772
  6.5 69.8 %all-gather.3.cloned.1.call-start = ((), (), s32[]{:S(2)}) async-start(), calls=%async_computation | async-start | bytes 4128768 | tf_op jit(solution)/shard_map/all_gather | solution.py:412
  8.2 6.0 %collective-permute-start = (bf16[5,32,256]{2,1,0:T(8,128)(2,1)S(1)}, bf16[5,32,256]{2,1,0:T(8,128)(2,1)S(1)}, u32[]{:S(2)}, u32[]{:S(2)}) collective-permute-start(bf16[5,32,256]{2,1,0:T(8,128)(2,1)S(1)} %get-tuple-element.38), channel_id=1, source_target_pairs={{0,128},{128,0},{1,129},{129,1},{2,130},{130,2},{3,131},{131,3},{4... | collective-permute-start | bytes 245768 | tf_op jit(solution)/shard_map/ppermute | solution.py:26
  14.3 8.7 %collective-permute-start.3 = (bf16[6,32,256]{2,1,0:T(8,128)(2,1)S(1)}, bf16[6,32,256]{2,1,0:T(8,128)(2,1)S(1)}, u32[]{:S(2)}, u32[]{:S(2)}) collective-permute-start(bf16[6,32,256]{2,1,0:T(8,128)(2,1)S(1)} %pad_maximum_fusion.4), channel_id=1, source_target_pairs={{0,32},{32,0},{64,96},{96,64},{1,33},{33,1},{65,97},{97,65},{2,34}... | collective-permute-start | bytes 294920 | tf_op jit(solution)/shard_map/ppermute | solution.py:26
  15.9 7.1 %collective-permute-start.4 = (bf16[6,32,256]{2,1,0:T(8,128)(2,1)S(1)}, bf16[6,32,256]{2,1,0:T(8,128)(2,1)S(1)}, u32[]{:S(2)}, u32[]{:S(2)}) collective-permute-start(bf16[6,32,256]{2,1,0:T(8,128)(2,1)S(1)} %pad_maximum_fusion.4), channel_id=1, source_target_pairs={{0,64},{32,96},{64,0},{96,32},{1,65},{33,97},{65,1},{97,33},{2,66}... | collective-permute-start | bytes 294920 | tf_op jit(solution)/shard_map/ppermute | solution.py:26
  18.6 5.8 %collective-permute-start.5 = (bf16[6,32,256]{2,1,0:T(8,128)(2,1)S(1)}, bf16[6,32,256]{2,1,0:T(8,128)(2,1)S(1)}, u32[]{:S(2)}, u32[]{:S(2)}) collective-permute-start(bf16[6,32,256]{2,1,0:T(8,128)(2,1)S(1)} %pad_maximum_fusion.4), channel_id=1, source_target_pairs={{0,96},{32,64},{64,32},{96,0},{1,97},{33,65},{65,33},{97,1},{2,98}... | collective-permute-start | bytes 294920 | tf_op jit(solution)/shard_map/ppermute | solution.py:26
  19.1 3.9 %collective-permute-start.6 = (bf16[2,32,256]{2,1,0:T(8,128)(2,1)S(1)}, bf16[2,32,256]{2,1,0:T(8,128)(2,1)S(1)}, u32[]{:S(2)}, u32[]{:S(2)}) collective-permute-start(bf16[2,32,256]{2,1,0:T(8,128)(2,1)S(1)} %broadcast_select_fusion.4), channel_id=1, source_target_pairs={{0,2},{2,0},{1,3},{3,1},{4,6},{6,4},{5,7},{7,5},{8,10},{10,8},{9,1... | collective-permute-start | bytes 98312 | tf_op jit(solution)/shard_map/ppermute | solution.py:26
  25.3 12.5 %collective-permute-start.1 = (bf16[2,256,512]{2,1,0:T(8,128)(2,1)S(1)}, bf16[2,256,512]{2,1,0:T(8,128)(2,1)S(1)}, u32[]{:S(2)}, u32[]{:S(2)}) collective-permute-start(bf16[2,256,512]{2,1,0:T(8,128)(2,1)S(1)} %get-tuple-element.42), channel_id=1, source_target_pairs={{0,4},{4,0},{8,12},{12,8},{16,20},{20,16},{24,28},{28,24},{1,5},{5... | collective-permute-start | bytes 1572872 | tf_op jit(solution)/shard_map/ppermute | solution.py:26
  27.3 10.5 %collective-permute-start.2 = (bf16[1,3,2048]{2,1,0:T(4,128)(2,1)S(1)}, bf16[1,3,2048]{2,1,0:T(4,128)(2,1)S(1)}, u32[]{:S(2)}, u32[]{:S(2)}) collective-permute-start(bf16[1,3,2048]{2,1,0:T(4,128)(2,1)S(1)} %copy-done.5), channel_id=1, source_target_pairs={{0,4},{4,0},{8,12},{12,8},{16,20},{20,16},{24,28},{28,24},{1,5},{5... | collective-permute-start | bytes 36872 | tf_op jit(solution)/shard_map/ppermute | solution.py:26
  38.4 11.2 %collective-permute-start.11 = (bf16[512,512]{1,0:T(8,128)(2,1)S(1)}, bf16[512,512]{1,0:T(8,128)(2,1)S(1)}, u32[]{:S(2)}, u32[]{:S(2)}) collective-permute-start(bf16[512,512]{1,0:T(8,128)(2,1)S(1)} %bitcast.11), channel_id=1, source_target_pairs={{0,2},{2,0},{128,130},{130,128},{1,3},{3,1},{129,131},{131,129},{4... | collective-permute-start | bytes 1572872 | tf_op jit(solution)/shard_map/ppermute | solution.py:26
  39.2 12.0 %collective-permute-start.9 = (bf16[512,512]{1,0:T(8,128)(2,1)S(1)}, bf16[512,512]{1,0:T(8,128)(2,1)S(1)}, u32[]{:S(2)}, u32[]{:S(2)}) collective-permute-start(bf16[512,512]{1,0:T(8,128)(2,1)S(1)} %bitcast.12), channel_id=1, source_target_pairs={{0,130},{2,128},{128,2},{130,0},{1,131},{3,129},{129,3},{131,1},{4... | collective-permute-start | bytes 1572872 | tf_op jit(solution)/shard_map/ppermute | solution.py:26
  40.3 20.0 %collective-permute-start.13 = (bf16[512,512]{1,0:T(8,128)(2,1)S(1)}, bf16[512,512]{1,0:T(8,128)(2,1)S(1)}, u32[]{:S(2)}, u32[]{:S(2)}) collective-permute-start(bf16[512,512]{1,0:T(8,128)(2,1)S(1)} %bitcast.13), channel_id=1, source_target_pairs={{0,1},{1,0},{2,3},{3,2},{4,5},{5,4},{6,7},{7,6},{8,9},{9,8},{10,11... | collective-permute-start | bytes 1572872 | tf_op jit(solution)/shard_map/ppermute | solution.py:26
  49.6 10.7 %collective-permute-start.14 = (bf16[512,512]{1,0:T(8,128)(2,1)S(1)}, bf16[512,512]{1,0:T(8,128)(2,1)S(1)}, u32[]{:S(2)}, u32[]{:S(2)}) collective-permute-start(bf16[512,512]{1,0:T(8,128)(2,1)S(1)} %collective-permute-done.11.c_ref), channel_id=1, source_target_pairs={{0,1},{1,0},{2,3},{3,2},{4,5},{5,4},{6,7},{7,6},{8,9},{9,8},{10,11... | collective-permute-start | bytes 1572872 | tf_op jit(solution)/shard_map/ppermute | solution.py:26
  51.3 7.1 %collective-permute-start.10 = (bf16[256,512]{1,0:T(8,128)(2,1)S(1)}, bf16[256,512]{1,0:T(8,128)(2,1)S(1)}, u32[]{:S(2)}, u32[]{:S(2)}) collective-permute-start(bf16[256,512]{1,0:T(8,128)(2,1)S(1)} %slice.93), channel_id=1, source_target_pairs={{0,2},{2,0},{128,130},{130,128},{1,3},{3,1},{129,131},{131,129},{4... | collective-permute-start | bytes 786440 | tf_op jit(solution)/shard_map/ppermute | solution.py:26
  51.5 8.7 %collective-permute-start.12 = (bf16[256,512]{1,0:T(8,128)(2,1)S(1)}, bf16[256,512]{1,0:T(8,128)(2,1)S(1)}, u32[]{:S(2)}, u32[]{:S(2)}) collective-permute-start(bf16[256,512]{1,0:T(8,128)(2,1)S(1)} %slice.94), channel_id=1, source_target_pairs={{0,130},{2,128},{128,2},{130,0},{1,131},{3,129},{129,3},{131,1},{4... | collective-permute-start | bytes 786440 | tf_op jit(solution)/shard_map/ppermute | solution.py:26
  52.9 15.8 %collective-permute-start.16 = (bf16[512,512]{1,0:T(8,128)(2,1)S(1)}, bf16[512,512]{1,0:T(8,128)(2,1)S(1)}, u32[]{:S(2)}, u32[]{:S(2)}) collective-permute-start(bf16[512,512]{1,0:T(8,128)(2,1)S(1)} %collective-permute-done.9.c_ref), channel_id=1, source_target_pairs={{0,1},{1,0},{2,3},{3,2},{4,5},{5,4},{6,7},{7,6},{8,9},{9,8},{10,11... | collective-permute-start | bytes 1572872 | tf_op jit(solution)/shard_map/ppermute | solution.py:26
  63.3 5.4 %collective-permute-start.15 = (bf16[512,512]{1,0:T(8,128)(2,1)S(1)}, bf16[512,512]{1,0:T(8,128)(2,1)S(1)}, u32[]{:S(2)}, u32[]{:S(2)}) collective-permute-start(bf16[512,512]{1,0:T(8,128)(2,1)S(1)} %pad_maximum_fusion.a_ref), channel_id=1, source_target_pairs={{0,1},{1,0},{2,3},{3,2},{4,5},{5,4},{6,7},{7,6},{8,9},{9,8},{10,11... | collective-permute-start | bytes 1572872 | tf_op jit(solution)/shard_map/ppermute | solution.py:26
  63.3 5.4 %collective-permute-start.17 = (bf16[2,3,2048]{2,1,0:T(4,128)(2,1)S(1)}, bf16[2,3,2048]{2,1,0:T(4,128)(2,1)S(1)}, u32[]{:S(2)}, u32[]{:S(2)}) collective-permute-start(bf16[2,3,2048]{2,1,0:T(4,128)(2,1)S(1)} %get-tuple-element.53.mod_ref), channel_id=1, source_target_pairs={{0,128},{128,0},{1,129},{129,1},{2,130},{130,2},{3,131},{131,3},{4... | collective-permute-start | bytes 73736 | tf_op jit(solution)/shard_map/ppermute | solution.py:26
  77.5 17.4 %collective-permute-start.7 = (bf16[8,4,32,256]{3,2,1,0:T(8,128)(2,1)S(1)}, bf16[8,4,32,256]{3,2,1,0:T(8,128)(2,1)S(1)}, u32[]{:S(2)}, u32[]{:S(2)}) collective-permute-start(bf16[8,4,32,256]{3,2,1,0:T(8,128)(2,1)S(1)} %slice.92.o0), channel_id=1, source_target_pairs={{0,32},{32,0},{64,96},{96,64},{1,33},{33,1},{65,97},{97,65},{2,34}... | collective-permute-start | bytes 1572872 | tf_op jit(solution)/shard_map/ppermute | solution.py:26
  79.0 15.9 %collective-permute-start.8 = (bf16[8,4,32,256]{3,2,1,0:T(8,128)(2,1)S(1)}, bf16[8,4,32,256]{3,2,1,0:T(8,128)(2,1)S(1)}, u32[]{:S(2)}, u32[]{:S(2)}) collective-permute-start(bf16[8,4,32,256]{3,2,1,0:T(8,128)(2,1)S(1)} %slice.92.o0), channel_id=1, source_target_pairs={{0,96},{32,64},{64,32},{96,0},{1,97},{33,65},{65,33},{97,1},{2,98}... | collective-permute-start | bytes 1572872 | tf_op jit(solution)/shard_map/ppermute | solution.py:26
  85.9 9.0 %collective-permute-start.18 = (bf16[512,256]{1,0:T(8,128)(2,1)}, bf16[512,256]{1,0:T(8,128)(2,1)S(1)}, u32[]{:S(2)}, u32[]{:S(2)}) collective-permute-start(bf16[512,256]{1,0:T(8,128)(2,1)} %attend.2), channel_id=1, source_target_pairs={{0,130},{2,128},{128,2},{130,0},{1,131},{3,129},{129,3},{131,1},{4... | collective-permute-start | bytes 786440 | tf_op jit(solution)/shard_map/ppermute | solution.py:26
  86.5 8.4 %collective-permute-start.19 = (bf16[512,256]{1,0:T(8,128)(2,1)}, bf16[512,256]{1,0:T(8,128)(2,1)S(1)}, u32[]{:S(2)}, u32[]{:S(2)}) collective-permute-start(bf16[512,256]{1,0:T(8,128)(2,1)} %attend.2), channel_id=1, source_target_pairs={{0,2},{2,0},{128,130},{130,128},{1,3},{3,1},{129,131},{131,129},{4... | collective-permute-start | bytes 786440 | tf_op jit(solution)/shard_map/ppermute | solution.py:26
  94.9 6.7 %collective-permute-start.22 = (bf16[4,4,32,256]{3,2,1,0:T(8,128)(2,1)S(1)}, bf16[4,4,32,256]{3,2,1,0:T(8,128)(2,1)S(1)}, u32[]{:S(2)}, u32[]{:S(2)}) collective-permute-start(bf16[4,4,32,256]{3,2,1,0:T(8,128)(2,1)S(1)} %slice.77), channel_id=1, source_target_pairs={{0,32},{32,0},{64,96},{96,64},{1,33},{33,1},{65,97},{97,65},{2,34}... | collective-permute-start | bytes 786440 | tf_op jit(solution)/shard_map/ppermute | solution.py:26
  95.6 7.7 %collective-permute-start.23 = (bf16[4,4,32,256]{3,2,1,0:T(8,128)(2,1)S(1)}, bf16[4,4,32,256]{3,2,1,0:T(8,128)(2,1)S(1)}, u32[]{:S(2)}, u32[]{:S(2)}) collective-permute-start(bf16[4,4,32,256]{3,2,1,0:T(8,128)(2,1)S(1)} %slice.78), channel_id=1, source_target_pairs={{0,96},{32,64},{64,32},{96,0},{1,97},{33,65},{65,33},{97,1},{2,98}... | collective-permute-start | bytes 786440 | tf_op jit(solution)/shard_map/ppermute | solution.py:26
  96.6 6.8 %collective-permute-start.20 = (bf16[512,256]{1,0:T(8,128)(2,1)}, bf16[512,256]{1,0:T(8,128)(2,1)S(1)}, u32[]{:S(2)}, u32[]{:S(2)}) collective-permute-start(bf16[512,256]{1,0:T(8,128)(2,1)} %attend.3.a_ref), channel_id=1, source_target_pairs={{0,2},{2,0},{128,130},{130,128},{1,3},{3,1},{129,131},{131,129},{4... | collective-permute-start | bytes 786440 | tf_op jit(solution)/shard_map/ppermute | solution.py:26
  96.7 7.6 %collective-permute-start.21 = (bf16[512,256]{1,0:T(8,128)(2,1)S(1)}, bf16[512,256]{1,0:T(8,128)(2,1)S(1)}, u32[]{:S(2)}, u32[]{:S(2)}) collective-permute-start(bf16[512,256]{1,0:T(8,128)(2,1)S(1)} %collective-permute-done.19), channel_id=1, source_target_pairs={{0,130},{2,128},{128,2},{130,0},{1,131},{3,129},{129,3},{131,1},{4... | collective-permute-start | bytes 786440 | tf_op jit(solution)/shard_map/ppermute | solution.py:26
  105.9 2.0 %collective-permute-start.24 = (bf16[512,512]{1,0:T(8,128)(2,1)S(1)}, bf16[512,512]{1,0:T(8,128)(2,1)S(1)}, u32[]{:S(2)}, u32[]{:S(2)}) collective-permute-start(bf16[512,512]{1,0:T(8,128)(2,1)S(1)} %get-tuple-element.66), channel_id=1, source_target_pairs={{0,1},{1,0},{2,3},{3,2},{4,5},{5,4},{6,7},{7,6},{8,9},{9,8},{10,11... | collective-permute-start | bytes 1572872 | tf_op jit(solution)/shard_map/ppermute | solution.py:26
  108.4 8.0 %collective-permute-start.25 = (bf16[16,6,512]{2,1,0:T(8,128)(2,1)S(1)}, bf16[16,6,512]{2,1,0:T(8,128)(2,1)S(1)}, u32[]{:S(2)}, u32[]{:S(2)}) collective-permute-start(bf16[16,6,512]{2,1,0:T(8,128)(2,1)S(1)} %get-tuple-element.78), channel_id=1, source_target_pairs={{0,4},{4,0},{8,12},{12,8},{16,20},{20,16},{24,28},{28,24},{32,36},... | collective-permute-start | bytes 294920 | tf_op jit(solution)/shard_map/ppermute | solution.py:40
  108.5 13.2 %collective-permute-start.26 = (bf16[16,6,512]{2,1,0:T(8,128)(2,1)S(1)}, bf16[16,6,512]{2,1,0:T(8,128)(2,1)S(1)}, u32[]{:S(2)}, u32[]{:S(2)}) collective-permute-start(bf16[16,6,512]{2,1,0:T(8,128)(2,1)S(1)} %get-tuple-element.77), channel_id=1, source_target_pairs={{4,8},{8,4},{12,16},{16,12},{20,24},{24,20},{28,32},{32,28},{36,40... | collective-permute-start | bytes 294920 | tf_op jit(solution)/shard_map/ppermute | solution.py:40
  122.8 11.3 %collective-permute-start.27 = (bf16[156,512]{1,0:T(8,128)(2,1)S(1)}, bf16[156,512]{1,0:T(8,128)(2,1)S(1)}, u32[]{:S(2)}, u32[]{:S(2)}) collective-permute-start(bf16[156,512]{1,0:T(8,128)(2,1)S(1)} %select_n.120), channel_id=1, source_target_pairs={{0,16},{4,20},{8,24},{12,28},{16,0},{20,4},{24,8},{28,12},{32,48},... | collective-permute-start | bytes 479240 | tf_op jit(solution)/shard_map/ppermute | solution.py:40
  122.9 18.8 %collective-permute-start.28 = (bf16[156,512]{1,0:T(8,128)(2,1)S(1)}, bf16[156,512]{1,0:T(8,128)(2,1)S(1)}, u32[]{:S(2)}, u32[]{:S(2)}) collective-permute-start(bf16[156,512]{1,0:T(8,128)(2,1)S(1)} %select_n.122), channel_id=1, source_target_pairs={{16,32},{20,36},{24,40},{28,44},{32,16},{36,20},{40,24},{44,28},{4... | collective-permute-start | bytes 479240 | tf_op jit(solution)/shard_map/ppermute | solution.py:40
  142.4 13.9 %collective-permute-start.29 = (bf16[2,256,512]{2,1,0:T(8,128)(2,1)S(1)}, bf16[2,256,512]{2,1,0:T(8,128)(2,1)S(1)}, u32[]{:S(2)}, u32[]{:S(2)}) collective-permute-start(bf16[2,256,512]{2,1,0:T(8,128)(2,1)S(1)} %pad_maximum_fusion.3.own), channel_id=1, source_target_pairs={{0,4},{4,0},{8,12},{12,8},{16,20},{20,16},{24,28},{28,24},{1,5},{5... | collective-permute-start | bytes 1572872 | tf_op jit(solution)/shard_map/ppermute | solution.py:26
  (10 other events, 41.0 us)
Sparse Core Ops, SparseCore 0:
  25.4 50.9 all-gather.2

commit v5 on v4

--- a/solution.py
+++ b/solution.py
@@ -306,7 +306,7 @@
     )(*attended, *os)
 
 
-def place_kernel(counts_ref, own, other, out_ref, zero_ref, sem):
+def place_kernel(counts_ref, tiles_ref, out_ref, zero_ref, sem):
     even = even_count(counts_ref)
     parity = lax.axis_index("z") % 2
     zero_ref[...] = jnp.zeros_like(zero_ref)
@@ -314,16 +314,11 @@
     for slot in range(4):
         tile = slot + parity * even
         live = jnp.where(parity == 1, tile < 4, slot < even)
-        ours = tile // 2 == parity
         target = out_ref.at[slot]
 
-        @pl.when(live & ours)
+        @pl.when(live)
         def _():
-            pltpu.make_async_copy(own.at[tile % 2], target, sem).start()
-
-        @pl.when(live & jnp.logical_not(ours))
-        def _():
-            pltpu.make_async_copy(other.at[tile % 2], target, sem).start()
+            pltpu.make_async_copy(tiles_ref.at[jnp.minimum(tile, 3)], target, sem).start()
 
         @pl.when(jnp.logical_not(live))
         def _():
@@ -334,17 +329,17 @@
         wait.wait()
 
 
-def place_tiles(counts, own, other):
+def place_tiles(counts, tiles):
     return pl.pallas_call(
         place_kernel,
-        in_specs=[SMEM, VMEM, VMEM],
+        in_specs=[SMEM, VMEM],
         out_specs=HBM,
         out_shape=jax.ShapeDtypeStruct((4, TOK, NARROW), BF),
         scratch_shapes=[pltpu.VMEM((TOK, NARROW), BF), pltpu.SemaphoreType.DMA],
         cost_estimate=cost(0, 2**21),
         compiler_params=pltpu.CompilerParams(vmem_limit_bytes=12 * 2**20),
         name="place",
-    )(counts, own, other)
+    )(counts, tiles)
 
 
 def mix(earlier, later, share):
@@ -366,24 +361,31 @@
     return jnp.concatenate([top, strip[W : S - W], bottom], axis=0)
 
 
-def blend(tiles, region, shares):
+def join_tiles(tiles, region, shares):
     first, second = tiles[0], tiles[1]
+    inner = mix(first[:, S - W :], second[:, :W], shares.reshape(1, W, 1))
+    strip = jnp.concatenate([first[:, : S - W], inner, second[:, W:]], axis=1)
+    return join_rows(strip, region, shares)
+
+
+def join_pair(own, other, edge, region, shares):
     share = shares.reshape(1, W, 1)
-    west, east = first[:, :W], second[:, S - W :]
     odd = region % 2 == 1
-    near = trade(jnp.where(odd, west, east), 1, lambda i: i % 2 == 0)
-    across = trade(jnp.where(odd, east, west), 1, lambda i: i % 2 == 1)
-    near, across = lax.optimization_barrier((near, across))
-    later, earlier = jnp.where(odd, across, near), jnp.where(odd, near, across)
-    place = region % 4
-    left = jnp.where(place != 0, mix(earlier, west, share), west)
-    right = jnp.where(place != 3, mix(east, later, share), east)
-    inner = mix(first[:, S - W :], second[:, :W], share)
-    strip = jnp.concatenate(
-        [left, first[:, W : S - W], inner, second[:, W : S - W], right], axis=1
-    )
-    strip = join_rows(strip, region, shares)
-    return jnp.stack([strip[:, :S], strip[:, S - W :]])
+    low, high = jnp.where(odd, other, own), jnp.where(odd, own, other)
+    west, east = low[:, :W], high[:, -W:]
+    front = region % 4 < 2
+    west = jnp.where(front, west, mix(edge, west, share))
+    east = jnp.where(front, mix(east, edge, share), east)
+    middle = mix(low[:, -W:], high[:, :W], share)
+    n = 2 * S - W
+    return jnp.stack(
+        [
+            jnp.concatenate([west, low[:, W:S]], axis=1),
+            jnp.concatenate([low[:, S - W : n - W], middle], axis=1),
+            jnp.concatenate([middle, high[:, W:S]], axis=1),
+            jnp.concatenate([high[:, S - W : n - W], east], axis=1),
+        ]
+    )
 
 
 def on_device(tile_data, tile_counts, modulation, qkv_weight, out_weight, blend_weights):
@@ -438,8 +440,20 @@
     summed = keep + xor_swap(send, "c", 1).astype(F32)
     updated = tiles.astype(F32) + gate * summed.reshape(2, TOK, NARROW)
     updated = updated.astype(BF).reshape(2, S, S, NARROW)
-    finished = blend(updated, region, blend_weights).reshape(2, TOK, NARROW)
-    return place_tiles(tile_counts, finished, xor_swap(finished, "z", 1))
+    strip = join_tiles(updated, region, blend_weights)
+
+    edge = jnp.where(region % 4 == 1, strip[:, -W:], strip[:, :W]).reshape(S * W, NARROW)
+    beside = lax.ppermute(
+        edge, REGION, [(i, i ^ 3) for i in range(64) if i % 4 in (1, 2)]
+    )
+    beyond = lax.ppermute(
+        edge, REGION, [(i, i ^ 2) for i in range(64) if i % 4 in (1, 2)]
+    )
+    other = xor_swap(strip.reshape(-1, NARROW), "z", 1)
+    other, beside, beyond = lax.optimization_barrier((other, beside, beyond))
+    edge = jnp.where((region % 4 == 1) | (region % 4 == 2), beside, beyond).reshape(S, W, NARROW)
+    joined = join_pair(strip, other.reshape(strip.shape), edge, region, blend_weights)
+    return place_tiles(tile_counts, joined.reshape(4, TOK, NARROW))
 
 
 def solution(mesh):

time: 165 us -> 158 us (0.958)
  waiting for transfers between devices: 83.4 us -> 76.3 us
    ppermute x26, waiting for transfers between devices: 62 us -> 53.8 us  [xor_swap(): return lax.ppermute(block, axis, [(i, i ^ bit) for i in range(size)])]
    ppermute x0 -> x2, waiting for transfers between devices: none -> 6.14 us  [the longest x1 6.13 us: on_device(): lax.ppermute(edge, REGION, [(i, i ^ 2) for i in range(64) if i % 4 in (1,...]
    ppermute x4 -> x2, waiting for transfers between devices: 16.8 us -> 11.7 us  [trade(): return lax.ppermute(block, REGION, route)]
    ppermute x4 -> x2, starting transfers between devices: 15.1 us -> 11 us  [trade(): return lax.ppermute(block, REGION, route)]
    ppermute x0 -> x2, starting transfers between devices: none -> 1.96 us  [the longest x1 1.29 us: on_device(): lax.ppermute(edge, REGION, [(i, i ^ 2) for i in range(64) if i % 4 in (1,...]
    ppermute x26, starting transfers between devices: 24.3 us -> 26.1 us  [xor_swap(): return lax.ppermute(block, axis, [(i, i ^ bit) for i in range(size)])]
where the time goes in v5:
time: 158 us
  waiting for transfers between devices  76.3 us (48%)
  starting transfers between devices  39 us (25%)
  Pallas kernels  17.2 us (11%)
  between operations  13.9 us (9%)
  local copies, waits for them, and re-layouts  9.16 us (6%)
  other arithmetic  2.01 us (1%)
    ppermute x26, waiting for transfers between devices, xor_swap(): return lax.ppermute(block, axis, [(i, i ^ bit) for i in range(size)])  53.8 us
    ppermute x26, starting transfers between devices, xor_swap(): return lax.ppermute(block, axis, [(i, i ^ bit) for i in range(size)])  26.1 us
    ppermute x2, waiting for transfers between devices, trade(): return lax.ppermute(block, REGION, route)  11.7 us
    ppermute x2, starting transfers between devices, trade(): return lax.ppermute(block, REGION, route)  11 us
    pallas_call x2, Pallas kernels, attended_of(): pl.pallas_call(attend_kernel, in_specs=[HBM] * 2, out_specs=VMEM, out_sha...  9.58 us
    unnamed x27, local copies, waits for them, and re-layouts  7.06 us
    ppermute x1, waiting for transfers between devices, on_device(): lax.ppermute(edge, REGION, [(i, i ^ 2) for i in range(64) if i % 4 in (1,...  6.13 us
    all_gather x1, waiting for transfers between devices, on_device(): gathered = lax.all_gather(block, 'z', axis=0)  4.68 us
  transfers between devices with their start and end apart: 31, of which 19 were waited for; matrix products, arithmetic and copies ran while one was open for 0% of the time, Pallas kernels for 9%

profile of v5, /device:TPU:24, one launch (start us, length us, event | category | flops | bytes accessed | tf_op | source)
XLA Modules:
  0.0 157.7 jit_solution(8349883915208461188)
XLA Ops:
  12.1 2.2 %collective-permute-done = bf16[5,32,256]{2,1,0:T(8,128)(2,1)S(1)} collective-permute-done((bf16[5,32,256]{2,1,0:T(8,128)(2,1)S(1)}, bf16[5,32,256]{2,1,0:T(8,128)(2,1)S(1)}, u32[]{:S(2)}, u32[]{:S(2)}) %collective-permute-start) | collective-permute-done | bytes 81952 | tf_op jit(solution)/shard_map/ppermute | solution.py:26
  14.3 1.6 %collective-permute-start.3 = (bf16[6,32,256]{2,1,0:T(8,128)(2,1)S(1)}, bf16[6,32,256]{2,1,0:T(8,128)(2,1)S(1)}, u32[]{:S(2)}, u32[]{:S(2)}) collective-permute-start(bf16[6,32,256]{2,1,0:T(8,128)(2,1)S(1)} %pad_maximum_fusion.9), channel_id=1, source_target_pairs={{0,32},{32,0},{64,96},{96,64},{1,33},{33,1},{65,97},{97,65},{2,34}... | collective-permute-start | bytes 294920 | tf_op jit(solution)/shard_map/ppermute | solution.py:26
  15.9 2.7 %collective-permute-start.4 = (bf16[6,32,256]{2,1,0:T(8,128)(2,1)S(1)}, bf16[6,32,256]{2,1,0:T(8,128)(2,1)S(1)}, u32[]{:S(2)}, u32[]{:S(2)}) collective-permute-start(bf16[6,32,256]{2,1,0:T(8,128)(2,1)S(1)} %pad_maximum_fusion.9), channel_id=1, source_target_pairs={{0,64},{32,96},{64,0},{96,32},{1,65},{33,97},{65,1},{97,33},{2,66}... | collective-permute-start | bytes 294920 | tf_op jit(solution)/shard_map/ppermute | solution.py:26
  19.8 3.2 %collective-permute-done.6 = bf16[2,32,256]{2,1,0:T(8,128)(2,1)S(1)} collective-permute-done((bf16[2,32,256]{2,1,0:T(8,128)(2,1)S(1)}, bf16[2,32,256]{2,1,0:T(8,128)(2,1)S(1)}, u32[]{:S(2)}, u32[]{:S(2)}) %collective-permute-start.6) | collective-permute-done | bytes 32800 | tf_op jit(solution)/shard_map/ppermute | solution.py:26
  25.3 2.0 %collective-permute-start.1 = (bf16[2,256,512]{2,1,0:T(8,128)(2,1)S(1)}, bf16[2,256,512]{2,1,0:T(8,128)(2,1)S(1)}, u32[]{:S(2)}, u32[]{:S(2)}) collective-permute-start(bf16[2,256,512]{2,1,0:T(8,128)(2,1)S(1)} %get-tuple-element.43), channel_id=1, source_target_pairs={{0,4},{4,0},{8,12},{12,8},{16,20},{20,16},{24,28},{28,24},{1,5},{5... | collective-permute-start | bytes 1572872 | tf_op jit(solution)/shard_map/ppermute | solution.py:26
  27.4 10.4 %collective-permute-done.2.other_mod = bf16[1,3,2048]{2,1,0:T(4,128)(2,1)S(1)} collective-permute-done((bf16[1,3,2048]{2,1,0:T(4,128)(2,1)S(1)}, bf16[1,3,2048]{2,1,0:T(4,128)(2,1)S(1)}, u32[]{:S(2)}, u32[]{:S(2)}) %collective-permute-start.2) | collective-permute-done | bytes 12320 | tf_op jit(solution)/shard_map/ppermute | solution.py:26
  40.3 9.3 %collective-permute-done.11.c_ref = bf16[512,512]{1,0:T(8,128)(2,1)S(1)} collective-permute-done((bf16[512,512]{1,0:T(8,128)(2,1)S(1)}, bf16[512,512]{1,0:T(8,128)(2,1)S(1)}, u32[]{:S(2)}, u32[]{:S(2)}) %collective-permute-start.11) | collective-permute-done | bytes 524320 | tf_op jit(solution)/shard_map/ppermute | solution.py:26
  49.6 1.7 %collective-permute-done.9.c_ref = bf16[512,512]{1,0:T(8,128)(2,1)S(1)} collective-permute-done((bf16[512,512]{1,0:T(8,128)(2,1)S(1)}, bf16[512,512]{1,0:T(8,128)(2,1)S(1)}, u32[]{:S(2)}, u32[]{:S(2)}) %collective-permute-start.9) | collective-permute-done | bytes 524320 | tf_op jit(solution)/shard_map/ppermute | solution.py:26
  52.9 5.6 %collective-permute-done.10 = bf16[256,512]{1,0:T(8,128)(2,1)S(1)} collective-permute-done((bf16[256,512]{1,0:T(8,128)(2,1)S(1)}, bf16[256,512]{1,0:T(8,128)(2,1)S(1)}, u32[]{:S(2)}, u32[]{:S(2)}) %collective-permute-start.10) | collective-permute-done | bytes 262176 | tf_op jit(solution)/shard_map/ppermute | solution.py:26
  58.4 1.8 %collective-permute-done.12 = bf16[256,512]{1,0:T(8,128)(2,1)S(1)} collective-permute-done((bf16[256,512]{1,0:T(8,128)(2,1)S(1)}, bf16[256,512]{1,0:T(8,128)(2,1)S(1)}, u32[]{:S(2)}, u32[]{:S(2)}) %collective-permute-start.12) | collective-permute-done | bytes 262176 | tf_op jit(solution)/shard_map/ppermute | solution.py:26
  60.3 1.6 %hidden.2.hid_hbm = bf16[512,2048]{1,0:T(8,128)(2,1)S(1)} custom-call(bf16[512,512]{1,0:T(8,128)(2,1)S(1)} %bitcast.17, bf16[512,512]{1,0:T(8,128)(2,1)S(1)} %collective-permute-done.13.b_ref, bf16[512,512]{1,0:T(8,128)(2,1)S(1)} %collective-permute-done.11.c_ref, bf16[512,512]{1,0:T(8,128)(2,1)S(1)} %collective-permute-done.14.d_ref, ...), custom_call_target="tpu_custom_call" | custom-call | flops 8388608 | bytes 4194304 | tf_op jit(solution)/shard_map/hidden/pallas_call | solution.py:182
  64.1 4.6 %collective-permute-done.17.mod_ref = bf16[2,3,2048]{2,1,0:T(4,128)(2,1)S(1)} collective-permute-done((bf16[2,3,2048]{2,1,0:T(4,128)(2,1)S(1)}, bf16[2,3,2048]{2,1,0:T(4,128)(2,1)S(1)}, u32[]{:S(2)}, u32[]{:S(2)}) %collective-permute-start.17) | collective-permute-done | bytes 24608 | tf_op jit(solution)/shard_map/ppermute | solution.py:26
  68.7 1.6 %hidden.3.hid_hbm = bf16[512,2048]{1,0:T(8,128)(2,1)S(1)} custom-call(bf16[512,512]{1,0:T(8,128)(2,1)S(1)} %pad_maximum_fusion.3.a_ref, bf16[512,512]{1,0:T(8,128)(2,1)S(1)} %collective-permute-done.15.b_ref, bf16[512,512]{1,0:T(8,128)(2,1)S(1)} %collective-permute-done.9.c_ref, bf16[512,512]{1,0:T(8,128)(2,1)S(1)} %collective-permute-done.16.d_ref, ...), custom_call_target="tpu_custom_call" | custom-call | flops 8388608 | bytes 4194304 | tf_op jit(solution)/shard_map/hidden/pallas_call | solution.py:182
  71.7 4.7 %all-gather.3.cloned.1.call-done = bf16[224,32,256]{2,1,0:T(8,128)(2,1)} async-done(((bf16[28,32,256]{2,1,0:T(8,128)(2,1)}), bf16[224,32,256]{2,1,0:T(8,128)(2,1)}) %all-gather.3.cloned.1.call-update) | async-done | bytes 3670032 | tf_op jit(solution)/shard_map/all_gather | solution.py:414
  77.5 1.6 collective-permute-start.7
  79.0 2.1 %collective-permute-start.8 = (bf16[8,4,32,256]{3,2,1,0:T(8,128)(2,1)S(1)}, bf16[8,4,32,256]{3,2,1,0:T(8,128)(2,1)S(1)}, u32[]{:S(2)}, u32[]{:S(2)}) collective-permute-start(bf16[8,4,32,256]{3,2,1,0:T(8,128)(2,1)S(1)} %slice.116.o0), channel_id=1, source_target_pairs={{0,96},{32,64},{64,32},{96,0},{1,97},{33,65},{65,33},{97,1},{2,98}... | collective-permute-start | bytes 1572872 | tf_op jit(solution)/shard_map/ppermute | solution.py:26
  81.1 4.8 %attend.2 = bf16[512,256]{1,0:T(8,128)(2,1)} custom-call(bf16[512,2048]{1,0:T(8,128)(2,1)} %copy-done.1, bf16[8,28,32,256]{3,2,1,0:T(8,128)(2,1)} %bitcast.30), custom_call_target="tpu_custom_call" | custom-call | flops 3489660928 | bytes 6291456 | tf_op jit(solution)/shard_map/attend/pallas_call | solution.py:248
  87.3 4.8 %attend.3.a_ref = bf16[512,256]{1,0:T(8,128)(2,1)} custom-call(bf16[512,2048]{1,0:T(8,128)(2,1)} %copy-done, bf16[8,28,32,256]{3,2,1,0:T(8,128)(2,1)} %bitcast.31), custom_call_target="tpu_custom_call" | custom-call | flops 3489660928 | bytes 6291456 | tf_op jit(solution)/shard_map/attend/pallas_call | solution.py:248
  92.2 2.7 %collective-permute-done.18.d_ref = bf16[512,256]{1,0:T(8,128)(2,1)S(1)} collective-permute-done((bf16[512,256]{1,0:T(8,128)(2,1)}, bf16[512,256]{1,0:T(8,128)(2,1)S(1)}, u32[]{:S(2)}, u32[]{:S(2)}) %collective-permute-start.18) | collective-permute-done | bytes 262176 | tf_op jit(solution)/shard_map/ppermute | solution.py:26
  96.7 1.9 %collective-permute-start.21 = (bf16[512,256]{1,0:T(8,128)(2,1)S(1)}, bf16[512,256]{1,0:T(8,128)(2,1)S(1)}, u32[]{:S(2)}, u32[]{:S(2)}) collective-permute-start(bf16[512,256]{1,0:T(8,128)(2,1)S(1)} %collective-permute-done.19), channel_id=1, source_target_pairs={{0,130},{2,128},{128,2},{130,0},{1,131},{3,129},{129,3},{131,1},{4... | collective-permute-start | bytes 786440 | tf_op jit(solution)/shard_map/ppermute | solution.py:26
  98.6 2.9 %collective-permute-done.22 = bf16[4,4,32,256]{3,2,1,0:T(8,128)(2,1)S(1)} collective-permute-done((bf16[4,4,32,256]{3,2,1,0:T(8,128)(2,1)S(1)}, bf16[4,4,32,256]{3,2,1,0:T(8,128)(2,1)S(1)}, u32[]{:S(2)}, u32[]{:S(2)}) %collective-permute-start.22) | collective-permute-done | bytes 262176 | tf_op jit(solution)/shard_map/ppermute | solution.py:26
  101.6 1.7 %collective-permute-done.23 = bf16[4,4,32,256]{3,2,1,0:T(8,128)(2,1)S(1)} collective-permute-done((bf16[4,4,32,256]{3,2,1,0:T(8,128)(2,1)S(1)}, bf16[4,4,32,256]{3,2,1,0:T(8,128)(2,1)S(1)}, u32[]{:S(2)}, u32[]{:S(2)}) %collective-permute-start.23) | collective-permute-done | bytes 262176 | tf_op jit(solution)/shard_map/ppermute | solution.py:26
  104.3 1.6 %project.1 = (f32[512,512]{1,0:T(8,128)S(1)}, bf16[512,512]{1,0:T(8,128)(2,1)S(1)}) custom-call(bf16[512,256]{1,0:T(8,128)(2,1)S(1)} %copy-done.8, bf16[512,256]{1,0:T(8,128)(2,1)S(1)} %collective-permute-done.20.b_ref, bf16[512,256]{1,0:T(8,128)(2,1)S(1)} %collective-permute-done.21.c_ref, bf16[512,256]{1,0:T(8,128)(2,1)S(1)} %collective-permute-done.18.d_ref, ...), custom_call_target="tpu_custom_call" | custom-call | flops 1073741824 | bytes 4194304 | tf_op jit(solution)/shard_map/project/pallas_call | solution.py:294
  106.1 1.8 %collective-permute-done.24 = bf16[512,512]{1,0:T(8,128)(2,1)S(1)} collective-permute-done((bf16[512,512]{1,0:T(8,128)(2,1)S(1)}, bf16[512,512]{1,0:T(8,128)(2,1)S(1)}, u32[]{:S(2)}, u32[]{:S(2)}) %collective-permute-start.24) | collective-permute-done | bytes 524320 | tf_op jit(solution)/shard_map/ppermute | solution.py:26
  108.7 3.2 %collective-permute-start.25 = (bf16[156,512]{1,0:T(8,128)(2,1)S(1)}, bf16[156,512]{1,0:T(8,128)(2,1)S(1)}, u32[]{:S(2)}, u32[]{:S(2)}) collective-permute-start(bf16[156,512]{1,0:T(8,128)(2,1)S(1)} %select_n.125), channel_id=1, source_target_pairs={{0,16},{4,20},{8,24},{12,28},{16,0},{20,4},{24,8},{28,12},{32,48},... | collective-permute-start | bytes 479240 | tf_op jit(solution)/shard_map/ppermute | solution.py:40
  112.0 7.8 %collective-permute-start.26 = (bf16[156,512]{1,0:T(8,128)(2,1)S(1)}, bf16[156,512]{1,0:T(8,128)(2,1)S(1)}, u32[]{:S(2)}, u32[]{:S(2)}) collective-permute-start(bf16[156,512]{1,0:T(8,128)(2,1)S(1)} %select_n.127), channel_id=1, source_target_pairs={{16,32},{20,36},{24,40},{28,44},{32,16},{36,20},{40,24},{44,28},{4... | collective-permute-start | bytes 479240 | tf_op jit(solution)/shard_map/ppermute | solution.py:40
  119.8 2.3 %collective-permute-done.25 = bf16[156,512]{1,0:T(8,128)(2,1)S(1)} collective-permute-done((bf16[156,512]{1,0:T(8,128)(2,1)S(1)}, bf16[156,512]{1,0:T(8,128)(2,1)S(1)}, u32[]{:S(2)}, u32[]{:S(2)}) %collective-permute-start.25) | collective-permute-done | bytes 159776 | tf_op jit(solution)/shard_map/ppermute | solution.py:40
  122.1 9.4 %collective-permute-done.26 = bf16[156,512]{1,0:T(8,128)(2,1)S(1)} collective-permute-done((bf16[156,512]{1,0:T(8,128)(2,1)S(1)}, bf16[156,512]{1,0:T(8,128)(2,1)S(1)}, u32[]{:S(2)}, u32[]{:S(2)}) %collective-permute-start.26) | collective-permute-done | bytes 159776 | tf_op jit(solution)/shard_map/ppermute | solution.py:40
  132.0 4.0 %collective-permute-start.27 = (bf16[416,512]{1,0:T(8,128)(2,1)S(1)}, bf16[416,512]{1,0:T(8,128)(2,1)S(1)}, u32[]{:S(2)}, u32[]{:S(2)}) collective-permute-start(bf16[416,512]{1,0:T(8,128)(2,1)S(1)} %reshape.55), channel_id=1, source_target_pairs={{0,4},{4,0},{8,12},{12,8},{16,20},{20,16},{24,28},{28,24},{1,5},{5... | collective-permute-start | bytes 1277960 | tf_op jit(solution)/shard_map/ppermute | solution.py:26
  138.2 6.1 %collective-permute-done.29 = bf16[96,512]{1,0:T(8,128)(2,1)S(1)} collective-permute-done((bf16[96,512]{1,0:T(8,128)(2,1)S(1)}, bf16[96,512]{1,0:T(8,128)(2,1)S(1)}, u32[]{:S(2)}, u32[]{:S(2)}) %collective-permute-start.29) | collective-permute-done | bytes 98336 | tf_op jit(solution)/shard_map/ppermute | solution.py:449
  144.3 3.6 %collective-permute-done.27 = bf16[416,512]{1,0:T(8,128)(2,1)S(1)} collective-permute-done((bf16[416,512]{1,0:T(8,128)(2,1)S(1)}, bf16[416,512]{1,0:T(8,128)(2,1)S(1)}, u32[]{:S(2)}, u32[]{:S(2)}) %collective-permute-start.27) | collective-permute-done | bytes 426016 | tf_op jit(solution)/shard_map/ppermute | solution.py:26
  149.3 1.5 place.1
  (109 shorter events, 27.1 us)
Async XLA Ops:
  6.5 31.2 %copy-start.7 = (s32[64]{0:T(128)S(1)}, s32[64]{0:T(128)}, u32[]{:S(2)}) copy-start(s32[64]{0:T(128)} %counts_ref.5) | copy-start | bytes 772
  6.5 69.8 %all-gather.3.cloned.1.call-start = ((), (), s32[]{:S(2)}) async-start(), calls=%async_computation | async-start | bytes 4128768 | tf_op jit(solution)/shard_map/all_gather | solution.py:414
  8.2 6.0 %collective-permute-start = (bf16[5,32,256]{2,1,0:T(8,128)(2,1)S(1)}, bf16[5,32,256]{2,1,0:T(8,128)(2,1)S(1)}, u32[]{:S(2)}, u32[]{:S(2)}) collective-permute-start(bf16[5,32,256]{2,1,0:T(8,128)(2,1)S(1)} %get-tuple-element.39), channel_id=1, source_target_pairs={{0,128},{128,0},{1,129},{129,1},{2,130},{130,2},{3,131},{131,3},{4... | collective-permute-start | bytes 245768 | tf_op jit(solution)/shard_map/ppermute | solution.py:26
  14.3 8.7 %collective-permute-start.3 = (bf16[6,32,256]{2,1,0:T(8,128)(2,1)S(1)}, bf16[6,32,256]{2,1,0:T(8,128)(2,1)S(1)}, u32[]{:S(2)}, u32[]{:S(2)}) collective-permute-start(bf16[6,32,256]{2,1,0:T(8,128)(2,1)S(1)} %pad_maximum_fusion.9), channel_id=1, source_target_pairs={{0,32},{32,0},{64,96},{96,64},{1,33},{33,1},{65,97},{97,65},{2,34}... | collective-permute-start | bytes 294920 | tf_op jit(solution)/shard_map/ppermute | solution.py:26
  15.9 7.1 %collective-permute-start.4 = (bf16[6,32,256]{2,1,0:T(8,128)(2,1)S(1)}, bf16[6,32,256]{2,1,0:T(8,128)(2,1)S(1)}, u32[]{:S(2)}, u32[]{:S(2)}) collective-permute-start(bf16[6,32,256]{2,1,0:T(8,128)(2,1)S(1)} %pad_maximum_fusion.9), channel_id=1, source_target_pairs={{0,64},{32,96},{64,0},{96,32},{1,65},{33,97},{65,1},{97,33},{2,66}... | collective-permute-start | bytes 294920 | tf_op jit(solution)/shard_map/ppermute | solution.py:26
  18.6 5.8 %collective-permute-start.5 = (bf16[6,32,256]{2,1,0:T(8,128)(2,1)S(1)}, bf16[6,32,256]{2,1,0:T(8,128)(2,1)S(1)}, u32[]{:S(2)}, u32[]{:S(2)}) collective-permute-start(bf16[6,32,256]{2,1,0:T(8,128)(2,1)S(1)} %pad_maximum_fusion.9), channel_id=1, source_target_pairs={{0,96},{32,64},{64,32},{96,0},{1,97},{33,65},{65,33},{97,1},{2,98}... | collective-permute-start | bytes 294920 | tf_op jit(solution)/shard_map/ppermute | solution.py:26
  19.1 3.9 %collective-permute-start.6 = (bf16[2,32,256]{2,1,0:T(8,128)(2,1)S(1)}, bf16[2,32,256]{2,1,0:T(8,128)(2,1)S(1)}, u32[]{:S(2)}, u32[]{:S(2)}) collective-permute-start(bf16[2,32,256]{2,1,0:T(8,128)(2,1)S(1)} %broadcast_select_fusion.4), channel_id=1, source_target_pairs={{0,2},{2,0},{1,3},{3,1},{4,6},{6,4},{5,7},{7,5},{8,10},{10,8},{9,1... | collective-permute-start | bytes 98312 | tf_op jit(solution)/shard_map/ppermute | solution.py:26
  25.3 12.5 %collective-permute-start.1 = (bf16[2,256,512]{2,1,0:T(8,128)(2,1)S(1)}, bf16[2,256,512]{2,1,0:T(8,128)(2,1)S(1)}, u32[]{:S(2)}, u32[]{:S(2)}) collective-permute-start(bf16[2,256,512]{2,1,0:T(8,128)(2,1)S(1)} %get-tuple-element.43), channel_id=1, source_target_pairs={{0,4},{4,0},{8,12},{12,8},{16,20},{20,16},{24,28},{28,24},{1,5},{5... | collective-permute-start | bytes 1572872 | tf_op jit(solution)/shard_map/ppermute | solution.py:26
  27.3 10.5 %collective-permute-start.2 = (bf16[1,3,2048]{2,1,0:T(4,128)(2,1)S(1)}, bf16[1,3,2048]{2,1,0:T(4,128)(2,1)S(1)}, u32[]{:S(2)}, u32[]{:S(2)}) collective-permute-start(bf16[1,3,2048]{2,1,0:T(4,128)(2,1)S(1)} %copy-done.5), channel_id=1, source_target_pairs={{0,4},{4,0},{8,12},{12,8},{16,20},{20,16},{24,28},{28,24},{1,5},{5... | collective-permute-start | bytes 36872 | tf_op jit(solution)/shard_map/ppermute | solution.py:26
  38.4 11.2 %collective-permute-start.11 = (bf16[512,512]{1,0:T(8,128)(2,1)S(1)}, bf16[512,512]{1,0:T(8,128)(2,1)S(1)}, u32[]{:S(2)}, u32[]{:S(2)}) collective-permute-start(bf16[512,512]{1,0:T(8,128)(2,1)S(1)} %bitcast.14), channel_id=1, source_target_pairs={{0,2},{2,0},{128,130},{130,128},{1,3},{3,1},{129,131},{131,129},{4... | collective-permute-start | bytes 1572872 | tf_op jit(solution)/shard_map/ppermute | solution.py:26
  39.2 12.0 %collective-permute-start.9 = (bf16[512,512]{1,0:T(8,128)(2,1)S(1)}, bf16[512,512]{1,0:T(8,128)(2,1)S(1)}, u32[]{:S(2)}, u32[]{:S(2)}) collective-permute-start(bf16[512,512]{1,0:T(8,128)(2,1)S(1)} %bitcast.15), channel_id=1, source_target_pairs={{0,130},{2,128},{128,2},{130,0},{1,131},{3,129},{129,3},{131,1},{4... | collective-permute-start | bytes 1572872 | tf_op jit(solution)/shard_map/ppermute | solution.py:26
  40.3 20.0 %collective-permute-start.13 = (bf16[512,512]{1,0:T(8,128)(2,1)S(1)}, bf16[512,512]{1,0:T(8,128)(2,1)S(1)}, u32[]{:S(2)}, u32[]{:S(2)}) collective-permute-start(bf16[512,512]{1,0:T(8,128)(2,1)S(1)} %bitcast.16), channel_id=1, source_target_pairs={{0,1},{1,0},{2,3},{3,2},{4,5},{5,4},{6,7},{7,6},{8,9},{9,8},{10,11... | collective-permute-start | bytes 1572872 | tf_op jit(solution)/shard_map/ppermute | solution.py:26
  49.6 10.7 %collective-permute-start.14 = (bf16[512,512]{1,0:T(8,128)(2,1)S(1)}, bf16[512,512]{1,0:T(8,128)(2,1)S(1)}, u32[]{:S(2)}, u32[]{:S(2)}) collective-permute-start(bf16[512,512]{1,0:T(8,128)(2,1)S(1)} %collective-permute-done.11.c_ref), channel_id=1, source_target_pairs={{0,1},{1,0},{2,3},{3,2},{4,5},{5,4},{6,7},{7,6},{8,9},{9,8},{10,11... | collective-permute-start | bytes 1572872 | tf_op jit(solution)/shard_map/ppermute | solution.py:26
  51.3 7.1 %collective-permute-start.10 = (bf16[256,512]{1,0:T(8,128)(2,1)S(1)}, bf16[256,512]{1,0:T(8,128)(2,1)S(1)}, u32[]{:S(2)}, u32[]{:S(2)}) collective-permute-start(bf16[256,512]{1,0:T(8,128)(2,1)S(1)} %slice.117), channel_id=1, source_target_pairs={{0,2},{2,0},{128,130},{130,128},{1,3},{3,1},{129,131},{131,129},{4... | collective-permute-start | bytes 786440 | tf_op jit(solution)/shard_map/ppermute | solution.py:26
  51.5 8.7 %collective-permute-start.12 = (bf16[256,512]{1,0:T(8,128)(2,1)S(1)}, bf16[256,512]{1,0:T(8,128)(2,1)S(1)}, u32[]{:S(2)}, u32[]{:S(2)}) collective-permute-start(bf16[256,512]{1,0:T(8,128)(2,1)S(1)} %slice.118), channel_id=1, source_target_pairs={{0,130},{2,128},{128,2},{130,0},{1,131},{3,129},{129,3},{131,1},{4... | collective-permute-start | bytes 786440 | tf_op jit(solution)/shard_map/ppermute | solution.py:26
  52.9 15.8 %collective-permute-start.16 = (bf16[512,512]{1,0:T(8,128)(2,1)S(1)}, bf16[512,512]{1,0:T(8,128)(2,1)S(1)}, u32[]{:S(2)}, u32[]{:S(2)}) collective-permute-start(bf16[512,512]{1,0:T(8,128)(2,1)S(1)} %collective-permute-done.9.c_ref), channel_id=1, source_target_pairs={{0,1},{1,0},{2,3},{3,2},{4,5},{5,4},{6,7},{7,6},{8,9},{9,8},{10,11... | collective-permute-start | bytes 1572872 | tf_op jit(solution)/shard_map/ppermute | solution.py:26
  63.3 5.4 %collective-permute-start.15 = (bf16[512,512]{1,0:T(8,128)(2,1)S(1)}, bf16[512,512]{1,0:T(8,128)(2,1)S(1)}, u32[]{:S(2)}, u32[]{:S(2)}) collective-permute-start(bf16[512,512]{1,0:T(8,128)(2,1)S(1)} %pad_maximum_fusion.3.a_ref), channel_id=1, source_target_pairs={{0,1},{1,0},{2,3},{3,2},{4,5},{5,4},{6,7},{7,6},{8,9},{9,8},{10,11... | collective-permute-start | bytes 1572872 | tf_op jit(solution)/shard_map/ppermute | solution.py:26
  63.3 5.4 %collective-permute-start.17 = (bf16[2,3,2048]{2,1,0:T(4,128)(2,1)S(1)}, bf16[2,3,2048]{2,1,0:T(4,128)(2,1)S(1)}, u32[]{:S(2)}, u32[]{:S(2)}) collective-permute-start(bf16[2,3,2048]{2,1,0:T(4,128)(2,1)S(1)} %get-tuple-element.54.mod_ref), channel_id=1, source_target_pairs={{0,128},{128,0},{1,129},{129,1},{2,130},{130,2},{3,131},{131,3},{4... | collective-permute-start | bytes 73736 | tf_op jit(solution)/shard_map/ppermute | solution.py:26
  77.5 17.4 %collective-permute-start.7 = (bf16[8,4,32,256]{3,2,1,0:T(8,128)(2,1)S(1)}, bf16[8,4,32,256]{3,2,1,0:T(8,128)(2,1)S(1)}, u32[]{:S(2)}, u32[]{:S(2)}) collective-permute-start(bf16[8,4,32,256]{3,2,1,0:T(8,128)(2,1)S(1)} %slice.116.o0), channel_id=1, source_target_pairs={{0,32},{32,0},{64,96},{96,64},{1,33},{33,1},{65,97},{97,65},{2,34}... | collective-permute-start | bytes 1572872 | tf_op jit(solution)/shard_map/ppermute | solution.py:26
  79.0 15.9 %collective-permute-start.8 = (bf16[8,4,32,256]{3,2,1,0:T(8,128)(2,1)S(1)}, bf16[8,4,32,256]{3,2,1,0:T(8,128)(2,1)S(1)}, u32[]{:S(2)}, u32[]{:S(2)}) collective-permute-start(bf16[8,4,32,256]{3,2,1,0:T(8,128)(2,1)S(1)} %slice.116.o0), channel_id=1, source_target_pairs={{0,96},{32,64},{64,32},{96,0},{1,97},{33,65},{65,33},{97,1},{2,98}... | collective-permute-start | bytes 1572872 | tf_op jit(solution)/shard_map/ppermute | solution.py:26
  85.9 9.0 %collective-permute-start.18 = (bf16[512,256]{1,0:T(8,128)(2,1)}, bf16[512,256]{1,0:T(8,128)(2,1)S(1)}, u32[]{:S(2)}, u32[]{:S(2)}) collective-permute-start(bf16[512,256]{1,0:T(8,128)(2,1)} %attend.2), channel_id=1, source_target_pairs={{0,130},{2,128},{128,2},{130,0},{1,131},{3,129},{129,3},{131,1},{4... | collective-permute-start | bytes 786440 | tf_op jit(solution)/shard_map/ppermute | solution.py:26
  86.5 8.4 %collective-permute-start.19 = (bf16[512,256]{1,0:T(8,128)(2,1)}, bf16[512,256]{1,0:T(8,128)(2,1)S(1)}, u32[]{:S(2)}, u32[]{:S(2)}) collective-permute-start(bf16[512,256]{1,0:T(8,128)(2,1)} %attend.2), channel_id=1, source_target_pairs={{0,2},{2,0},{128,130},{130,128},{1,3},{3,1},{129,131},{131,129},{4... | collective-permute-start | bytes 786440 | tf_op jit(solution)/shard_map/ppermute | solution.py:26
  94.9 6.7 %collective-permute-start.22 = (bf16[4,4,32,256]{3,2,1,0:T(8,128)(2,1)S(1)}, bf16[4,4,32,256]{3,2,1,0:T(8,128)(2,1)S(1)}, u32[]{:S(2)}, u32[]{:S(2)}) collective-permute-start(bf16[4,4,32,256]{3,2,1,0:T(8,128)(2,1)S(1)} %slice.95), channel_id=1, source_target_pairs={{0,32},{32,0},{64,96},{96,64},{1,33},{33,1},{65,97},{97,65},{2,34}... | collective-permute-start | bytes 786440 | tf_op jit(solution)/shard_map/ppermute | solution.py:26
  95.6 7.7 %collective-permute-start.23 = (bf16[4,4,32,256]{3,2,1,0:T(8,128)(2,1)S(1)}, bf16[4,4,32,256]{3,2,1,0:T(8,128)(2,1)S(1)}, u32[]{:S(2)}, u32[]{:S(2)}) collective-permute-start(bf16[4,4,32,256]{3,2,1,0:T(8,128)(2,1)S(1)} %slice.96), channel_id=1, source_target_pairs={{0,96},{32,64},{64,32},{96,0},{1,97},{33,65},{65,33},{97,1},{2,98}... | collective-permute-start | bytes 786440 | tf_op jit(solution)/shard_map/ppermute | solution.py:26
  96.6 6.8 %collective-permute-start.20 = (bf16[512,256]{1,0:T(8,128)(2,1)}, bf16[512,256]{1,0:T(8,128)(2,1)S(1)}, u32[]{:S(2)}, u32[]{:S(2)}) collective-permute-start(bf16[512,256]{1,0:T(8,128)(2,1)} %attend.3.a_ref), channel_id=1, source_target_pairs={{0,2},{2,0},{128,130},{130,128},{1,3},{3,1},{129,131},{131,129},{4... | collective-permute-start | bytes 786440 | tf_op jit(solution)/shard_map/ppermute | solution.py:26
  96.7 7.6 %collective-permute-start.21 = (bf16[512,256]{1,0:T(8,128)(2,1)S(1)}, bf16[512,256]{1,0:T(8,128)(2,1)S(1)}, u32[]{:S(2)}, u32[]{:S(2)}) collective-permute-start(bf16[512,256]{1,0:T(8,128)(2,1)S(1)} %collective-permute-done.19), channel_id=1, source_target_pairs={{0,130},{2,128},{128,2},{130,0},{1,131},{3,129},{129,3},{131,1},{4... | collective-permute-start | bytes 786440 | tf_op jit(solution)/shard_map/ppermute | solution.py:26
  105.9 2.0 %collective-permute-start.24 = (bf16[512,512]{1,0:T(8,128)(2,1)S(1)}, bf16[512,512]{1,0:T(8,128)(2,1)S(1)}, u32[]{:S(2)}, u32[]{:S(2)}) collective-permute-start(bf16[512,512]{1,0:T(8,128)(2,1)S(1)} %get-tuple-element.67), channel_id=1, source_target_pairs={{0,1},{1,0},{2,3},{3,2},{4,5},{5,4},{6,7},{7,6},{8,9},{9,8},{10,11... | collective-permute-start | bytes 1572872 | tf_op jit(solution)/shard_map/ppermute | solution.py:26
  108.7 13.3 %collective-permute-start.25 = (bf16[156,512]{1,0:T(8,128)(2,1)S(1)}, bf16[156,512]{1,0:T(8,128)(2,1)S(1)}, u32[]{:S(2)}, u32[]{:S(2)}) collective-permute-start(bf16[156,512]{1,0:T(8,128)(2,1)S(1)} %select_n.125), channel_id=1, source_target_pairs={{0,16},{4,20},{8,24},{12,28},{16,0},{20,4},{24,8},{28,12},{32,48},... | collective-permute-start | bytes 479240 | tf_op jit(solution)/shard_map/ppermute | solution.py:40
  112.0 19.5 %collective-permute-start.26 = (bf16[156,512]{1,0:T(8,128)(2,1)S(1)}, bf16[156,512]{1,0:T(8,128)(2,1)S(1)}, u32[]{:S(2)}, u32[]{:S(2)}) collective-permute-start(bf16[156,512]{1,0:T(8,128)(2,1)S(1)} %select_n.127), channel_id=1, source_target_pairs={{16,32},{20,36},{24,40},{28,44},{32,16},{36,20},{40,24},{44,28},{4... | collective-permute-start | bytes 479240 | tf_op jit(solution)/shard_map/ppermute | solution.py:40
  132.0 15.8 %collective-permute-start.27 = (bf16[416,512]{1,0:T(8,128)(2,1)S(1)}, bf16[416,512]{1,0:T(8,128)(2,1)S(1)}, u32[]{:S(2)}, u32[]{:S(2)}) collective-permute-start(bf16[416,512]{1,0:T(8,128)(2,1)S(1)} %reshape.55), channel_id=1, source_target_pairs={{0,4},{4,0},{8,12},{12,8},{16,20},{20,16},{24,28},{28,24},{1,5},{5... | collective-permute-start | bytes 1277960 | tf_op jit(solution)/shard_map/ppermute | solution.py:26
  136.2 2.0 %collective-permute-start.28 = (bf16[96,512]{1,0:T(8,128)(2,1)S(1)}, bf16[96,512]{1,0:T(8,128)(2,1)S(1)}, u32[]{:S(2)}, u32[]{:S(2)}) collective-permute-start(bf16[96,512]{1,0:T(8,128)(2,1)S(1)} %reshape.56), channel_id=1, source_target_pairs={{4,8},{8,4},{20,24},{24,20},{36,40},{40,36},{52,56},{56,52},{68,72... | collective-permute-start | bytes 294920 | tf_op jit(solution)/shard_map/ppermute | solution.py:446
  136.9 7.5 %collective-permute-start.29 = (bf16[96,512]{1,0:T(8,128)(2,1)S(1)}, bf16[96,512]{1,0:T(8,128)(2,1)S(1)}, u32[]{:S(2)}, u32[]{:S(2)}) collective-permute-start(bf16[96,512]{1,0:T(8,128)(2,1)S(1)} %reshape.56), channel_id=1, source_target_pairs={{4,12},{8,0},{20,28},{24,16},{36,44},{40,32},{52,60},{56,48},{68,7... | collective-permute-start | bytes 294920 | tf_op jit(solution)/shard_map/ppermute | solution.py:449
  (10 other events, 41.1 us)
Sparse Core Ops, SparseCore 0:
  25.4 50.9 all-gather.2

commit v6 on v5

--- a/solution.py
+++ b/solution.py
@@ -352,9 +352,9 @@
     top, bottom = strip[:W], strip[S - W :]
     north, south = top.reshape(W * count, NARROW), bottom.reshape(W * count, NARROW)
     first = region % 8 < 4
+    cross = trade(jnp.where(first, north, south), 4, lambda i: i % 8 >= 4)
     same = trade(jnp.where(first, south, north), 4, lambda i: i % 8 < 4)
-    cross = trade(jnp.where(first, north, south), 4, lambda i: i % 8 >= 4)
-    same, cross = lax.optimization_barrier((same, cross))
+    cross, same = lax.optimization_barrier((cross, same))
     later, earlier = jnp.where(first, same, cross), jnp.where(first, cross, same)
     top = jnp.where(region >= 4, mix(earlier.reshape(W, count, NARROW), top, share), top)
     bottom = jnp.where(region < 60, mix(bottom, later.reshape(W, count, NARROW), share), bottom)
@@ -407,10 +407,10 @@
     out_sent = jnp.where(straight, came_blocks[3:], own_blocks[3:])
     qkv = jnp.concatenate([own_blocks[:3], came_blocks[:3]])
     qkv, out_sent = lax.optimization_barrier((qkv, out_sent))
-    pieces = [xor_swap(qkv, "x", bit) for bit in (1, 2, 3)]
+    x_far, x_near, x_side = (xor_swap(qkv, "x", bit) for bit in (2, 1, 3))
     out_came = xor_swap(out_sent, "yl", 1)
-    *pieces, out_came = lax.optimization_barrier((*pieces, out_came))
-    block = jnp.concatenate([qkv, *pieces, out_kept, out_came])
+    x_far, x_near, x_side, out_came = lax.optimization_barrier((x_far, x_near, x_side, out_came))
+    block = jnp.concatenate([qkv, x_near, x_far, x_side, out_kept, out_came])
     gathered = lax.all_gather(block, "z", axis=0)
 
     tiles, mods, gate = choose(tile_counts, kept, came, modulation, came_mod)
@@ -442,6 +442,7 @@
     updated = updated.astype(BF).reshape(2, S, S, NARROW)
     strip = join_tiles(updated, region, blend_weights)
 
+    other = xor_swap(strip.reshape(-1, NARROW), "z", 1)
     edge = jnp.where(region % 4 == 1, strip[:, -W:], strip[:, :W]).reshape(S * W, NARROW)
     beside = lax.ppermute(
         edge, REGION, [(i, i ^ 3) for i in range(64) if i % 4 in (1, 2)]
@@ -449,8 +450,7 @@
     beyond = lax.ppermute(
         edge, REGION, [(i, i ^ 2) for i in range(64) if i % 4 in (1, 2)]
     )
-    other = xor_swap(strip.reshape(-1, NARROW), "z", 1)
-    other, beside, beyond = lax.optimization_barrier((other, beside, beyond))
+    beside, beyond, other = lax.optimization_barrier((beside, beyond, other))
     edge = jnp.where((region % 4 == 1) | (region % 4 == 2), beside, beyond).reshape(S, W, NARROW)
     joined = join_pair(strip, other.reshape(strip.shape), edge, region, blend_weights)
     return place_tiles(tile_counts, joined.reshape(4, TOK, NARROW))

time: 158 us -> 157 us (level); the launches traced: 158 us -> 154 us
  starting transfers between devices: 39 us -> 35.9 us
    ppermute x26, waiting for transfers between devices: 53.8 us -> 50.8 us  [xor_swap(): return lax.ppermute(block, axis, [(i, i ^ bit) for i in range(size)])]
    ppermute x2, starting transfers between devices: 11 us -> 8.76 us  [trade(): return lax.ppermute(block, REGION, route)]
    ppermute x1, waiting for transfers between devices: 6.13 us -> 7.8 us  [on_device(): lax.ppermute(edge, REGION, [(i, i ^ 2) for i in range(64) if i % 4 in (1,...]
  transfers between devices with their start and end apart: 31 -> 31, of which waited for: 19 -> 18; matrix products, arithmetic and copies ran while one was open for 0% -> 0% of each run, Pallas kernels for 9% -> 9%
where the time goes in v6:
time: 157 us; the launch traced here: 154 us
  waiting for transfers between devices  75.8 us (48%)
  starting transfers between devices  35.9 us (23%)
  Pallas kernels  17.2 us (11%)
  between operations  13.9 us (9%)
  local copies, waits for them, and re-layouts  9.16 us (6%)
  other arithmetic  2.01 us (1%)
    ppermute x26, waiting for transfers between devices, xor_swap(): return lax.ppermute(block, axis, [(i, i ^ bit) for i in range(size)])  50.8 us
    ppermute x26, starting transfers between devices, xor_swap(): return lax.ppermute(block, axis, [(i, i ^ bit) for i in range(size)])  25.2 us
    ppermute x2, waiting for transfers between devices, trade(): return lax.ppermute(block, REGION, route)  11.7 us
    pallas_call x2, Pallas kernels, attended_of(): pl.pallas_call(attend_kernel, in_specs=[HBM] * 2, out_specs=VMEM, out_sha...  9.58 us
    ppermute x2, starting transfers between devices, trade(): return lax.ppermute(block, REGION, route)  8.76 us
    ppermute x1, waiting for transfers between devices, on_device(): lax.ppermute(edge, REGION, [(i, i ^ 2) for i in range(64) if i % 4 in (1,...  7.8 us
    unnamed x27, local copies, waits for them, and re-layouts  7.06 us
    all_gather x1, waiting for transfers between devices, on_device(): gathered = lax.all_gather(block, 'z', axis=0)  5.5 us
  transfers between devices with their start and end apart: 31, of which 18 were waited for; matrix products, arithmetic and copies ran while one was open for 0% of the time, Pallas kernels for 9%

profile of v6, /device:TPU:24, one launch (start us, length us, event | category | flops | bytes accessed | tf_op | source)
XLA Modules:
  0.0 154.1 jit_solution(15933147340799761751)
XLA Ops:
  12.1 2.2 %collective-permute-done = bf16[5,32,256]{2,1,0:T(8,128)(2,1)S(1)} collective-permute-done((bf16[5,32,256]{2,1,0:T(8,128)(2,1)S(1)}, bf16[5,32,256]{2,1,0:T(8,128)(2,1)S(1)}, u32[]{:S(2)}, u32[]{:S(2)}) %collective-permute-start) | collective-permute-done | bytes 81952 | tf_op jit(solution)/shard_map/ppermute | solution.py:26
  14.3 3.1 %collective-permute-start.3 = (bf16[6,32,256]{2,1,0:T(8,128)(2,1)S(1)}, bf16[6,32,256]{2,1,0:T(8,128)(2,1)S(1)}, u32[]{:S(2)}, u32[]{:S(2)}) collective-permute-start(bf16[6,32,256]{2,1,0:T(8,128)(2,1)S(1)} %pad_maximum_fusion.9), channel_id=1, source_target_pairs={{0,64},{32,96},{64,0},{96,32},{1,65},{33,97},{65,1},{97,33},{2,66}... | collective-permute-start | bytes 294920 | tf_op jit(solution)/shard_map/ppermute | solution.py:26
  19.3 3.2 %collective-permute-done.6 = bf16[2,32,256]{2,1,0:T(8,128)(2,1)S(1)} collective-permute-done((bf16[2,32,256]{2,1,0:T(8,128)(2,1)S(1)}, bf16[2,32,256]{2,1,0:T(8,128)(2,1)S(1)}, u32[]{:S(2)}, u32[]{:S(2)}) %collective-permute-start.6) | collective-permute-done | bytes 32800 | tf_op jit(solution)/shard_map/ppermute | solution.py:26
  22.5 1.4 collective-permute-done.5
  24.7 2.0 %collective-permute-start.1 = (bf16[2,256,512]{2,1,0:T(8,128)(2,1)S(1)}, bf16[2,256,512]{2,1,0:T(8,128)(2,1)S(1)}, u32[]{:S(2)}, u32[]{:S(2)}) collective-permute-start(bf16[2,256,512]{2,1,0:T(8,128)(2,1)S(1)} %get-tuple-element.43), channel_id=1, source_target_pairs={{0,4},{4,0},{8,12},{12,8},{16,20},{20,16},{24,28},{28,24},{1,5},{5... | collective-permute-start | bytes 1572872 | tf_op jit(solution)/shard_map/ppermute | solution.py:26
  26.8 10.1 %collective-permute-done.2.other_mod = bf16[1,3,2048]{2,1,0:T(4,128)(2,1)S(1)} collective-permute-done((bf16[1,3,2048]{2,1,0:T(4,128)(2,1)S(1)}, bf16[1,3,2048]{2,1,0:T(4,128)(2,1)S(1)}, u32[]{:S(2)}, u32[]{:S(2)}) %collective-permute-start.2) | collective-permute-done | bytes 12320 | tf_op jit(solution)/shard_map/ppermute | solution.py:26
  39.4 9.0 %collective-permute-done.11.c_ref = bf16[512,512]{1,0:T(8,128)(2,1)S(1)} collective-permute-done((bf16[512,512]{1,0:T(8,128)(2,1)S(1)}, bf16[512,512]{1,0:T(8,128)(2,1)S(1)}, u32[]{:S(2)}, u32[]{:S(2)}) %collective-permute-start.11) | collective-permute-done | bytes 524320 | tf_op jit(solution)/shard_map/ppermute | solution.py:26
  48.5 1.7 %collective-permute-done.9.c_ref = bf16[512,512]{1,0:T(8,128)(2,1)S(1)} collective-permute-done((bf16[512,512]{1,0:T(8,128)(2,1)S(1)}, bf16[512,512]{1,0:T(8,128)(2,1)S(1)}, u32[]{:S(2)}, u32[]{:S(2)}) %collective-permute-start.9) | collective-permute-done | bytes 524320 | tf_op jit(solution)/shard_map/ppermute | solution.py:26
  50.3 1.6 %collective-permute-start.12 = (bf16[256,512]{1,0:T(8,128)(2,1)S(1)}, bf16[256,512]{1,0:T(8,128)(2,1)S(1)}, u32[]{:S(2)}, u32[]{:S(2)}) collective-permute-start(bf16[256,512]{1,0:T(8,128)(2,1)S(1)} %slice.118), channel_id=1, source_target_pairs={{0,130},{2,128},{128,2},{130,0},{1,131},{3,129},{129,3},{131,1},{4... | collective-permute-start | bytes 786440 | tf_op jit(solution)/shard_map/ppermute | solution.py:26
  51.9 5.4 %collective-permute-done.10 = bf16[256,512]{1,0:T(8,128)(2,1)S(1)} collective-permute-done((bf16[256,512]{1,0:T(8,128)(2,1)S(1)}, bf16[256,512]{1,0:T(8,128)(2,1)S(1)}, u32[]{:S(2)}, u32[]{:S(2)}) %collective-permute-start.10) | collective-permute-done | bytes 262176 | tf_op jit(solution)/shard_map/ppermute | solution.py:26
  57.3 1.8 %collective-permute-done.12 = bf16[256,512]{1,0:T(8,128)(2,1)S(1)} collective-permute-done((bf16[256,512]{1,0:T(8,128)(2,1)S(1)}, bf16[256,512]{1,0:T(8,128)(2,1)S(1)}, u32[]{:S(2)}, u32[]{:S(2)}) %collective-permute-start.12) | collective-permute-done | bytes 262176 | tf_op jit(solution)/shard_map/ppermute | solution.py:26
  59.1 1.6 %hidden.2.hid_hbm = bf16[512,2048]{1,0:T(8,128)(2,1)S(1)} custom-call(bf16[512,512]{1,0:T(8,128)(2,1)S(1)} %bitcast.17, bf16[512,512]{1,0:T(8,128)(2,1)S(1)} %collective-permute-done.13.b_ref, bf16[512,512]{1,0:T(8,128)(2,1)S(1)} %collective-permute-done.11.c_ref, bf16[512,512]{1,0:T(8,128)(2,1)S(1)} %collective-permute-done.14.d_ref, ...), custom_call_target="tpu_custom_call" | custom-call | flops 8388608 | bytes 4194304 | tf_op jit(solution)/shard_map/hidden/pallas_call | solution.py:182
  63.1 4.4 %collective-permute-done.17.mod_ref = bf16[2,3,2048]{2,1,0:T(4,128)(2,1)S(1)} collective-permute-done((bf16[2,3,2048]{2,1,0:T(4,128)(2,1)S(1)}, bf16[2,3,2048]{2,1,0:T(4,128)(2,1)S(1)}, u32[]{:S(2)}, u32[]{:S(2)}) %collective-permute-start.17) | collective-permute-done | bytes 24608 | tf_op jit(solution)/shard_map/ppermute | solution.py:26
  67.5 1.6 %hidden.3.hid_hbm = bf16[512,2048]{1,0:T(8,128)(2,1)S(1)} custom-call(bf16[512,512]{1,0:T(8,128)(2,1)S(1)} %pad_maximum_fusion.3.a_ref, bf16[512,512]{1,0:T(8,128)(2,1)S(1)} %collective-permute-done.15.b_ref, bf16[512,512]{1,0:T(8,128)(2,1)S(1)} %collective-permute-done.9.c_ref, bf16[512,512]{1,0:T(8,128)(2,1)S(1)} %collective-permute-done.16.d_ref, ...), custom_call_target="tpu_custom_call" | custom-call | flops 8388608 | bytes 4194304 | tf_op jit(solution)/shard_map/hidden/pallas_call | solution.py:182
  69.2 1.4 copy-done.1
  70.5 5.5 %all-gather.3.cloned.1.call-done = bf16[224,32,256]{2,1,0:T(8,128)(2,1)} async-done(((bf16[28,32,256]{2,1,0:T(8,128)(2,1)}), bf16[224,32,256]{2,1,0:T(8,128)(2,1)}) %all-gather.3.cloned.1.call-update) | async-done | bytes 3670032 | tf_op jit(solution)/shard_map/all_gather | solution.py:414
  77.1 1.6 %collective-permute-start.7 = (bf16[8,4,32,256]{3,2,1,0:T(8,128)(2,1)S(1)}, bf16[8,4,32,256]{3,2,1,0:T(8,128)(2,1)S(1)}, u32[]{:S(2)}, u32[]{:S(2)}) collective-permute-start(bf16[8,4,32,256]{3,2,1,0:T(8,128)(2,1)S(1)} %slice.116.o0), channel_id=1, source_target_pairs={{0,32},{32,0},{64,96},{96,64},{1,33},{33,1},{65,97},{97,65},{2,34}... | collective-permute-start | bytes 1572872 | tf_op jit(solution)/shard_map/ppermute | solution.py:26
  78.7 2.1 %collective-permute-start.8 = (bf16[8,4,32,256]{3,2,1,0:T(8,128)(2,1)S(1)}, bf16[8,4,32,256]{3,2,1,0:T(8,128)(2,1)S(1)}, u32[]{:S(2)}, u32[]{:S(2)}) collective-permute-start(bf16[8,4,32,256]{3,2,1,0:T(8,128)(2,1)S(1)} %slice.116.o0), channel_id=1, source_target_pairs={{0,96},{32,64},{64,32},{96,0},{1,97},{33,65},{65,33},{97,1},{2,98}... | collective-permute-start | bytes 1572872 | tf_op jit(solution)/shard_map/ppermute | solution.py:26
  80.7 4.8 %attend.2 = bf16[512,256]{1,0:T(8,128)(2,1)} custom-call(bf16[512,2048]{1,0:T(8,128)(2,1)} %copy-done.1, bf16[8,28,32,256]{3,2,1,0:T(8,128)(2,1)} %bitcast.30), custom_call_target="tpu_custom_call" | custom-call | flops 3489660928 | bytes 6291456 | tf_op jit(solution)/shard_map/attend/pallas_call | solution.py:248
  87.0 4.8 %attend.3.a_ref = bf16[512,256]{1,0:T(8,128)(2,1)} custom-call(bf16[512,2048]{1,0:T(8,128)(2,1)} %copy-done, bf16[8,28,32,256]{3,2,1,0:T(8,128)(2,1)} %bitcast.31), custom_call_target="tpu_custom_call" | custom-call | flops 3489660928 | bytes 6291456 | tf_op jit(solution)/shard_map/attend/pallas_call | solution.py:248
  91.8 2.7 %collective-permute-done.18.d_ref = bf16[512,256]{1,0:T(8,128)(2,1)S(1)} collective-permute-done((bf16[512,256]{1,0:T(8,128)(2,1)}, bf16[512,256]{1,0:T(8,128)(2,1)S(1)}, u32[]{:S(2)}, u32[]{:S(2)}) %collective-permute-start.18) | collective-permute-done | bytes 262176 | tf_op jit(solution)/shard_map/ppermute | solution.py:26
  96.4 1.9 %collective-permute-start.21 = (bf16[512,256]{1,0:T(8,128)(2,1)S(1)}, bf16[512,256]{1,0:T(8,128)(2,1)S(1)}, u32[]{:S(2)}, u32[]{:S(2)}) collective-permute-start(bf16[512,256]{1,0:T(8,128)(2,1)S(1)} %collective-permute-done.19), channel_id=1, source_target_pairs={{0,130},{2,128},{128,2},{130,0},{1,131},{3,129},{129,3},{131,1},{4... | collective-permute-start | bytes 786440 | tf_op jit(solution)/shard_map/ppermute | solution.py:26
  98.3 2.9 %collective-permute-done.22 = bf16[4,4,32,256]{3,2,1,0:T(8,128)(2,1)S(1)} collective-permute-done((bf16[4,4,32,256]{3,2,1,0:T(8,128)(2,1)S(1)}, bf16[4,4,32,256]{3,2,1,0:T(8,128)(2,1)S(1)}, u32[]{:S(2)}, u32[]{:S(2)}) %collective-permute-start.22) | collective-permute-done | bytes 262176 | tf_op jit(solution)/shard_map/ppermute | solution.py:26
  101.2 1.7 %collective-permute-done.23 = bf16[4,4,32,256]{3,2,1,0:T(8,128)(2,1)S(1)} collective-permute-done((bf16[4,4,32,256]{3,2,1,0:T(8,128)(2,1)S(1)}, bf16[4,4,32,256]{3,2,1,0:T(8,128)(2,1)S(1)}, u32[]{:S(2)}, u32[]{:S(2)}) %collective-permute-start.23) | collective-permute-done | bytes 262176 | tf_op jit(solution)/shard_map/ppermute | solution.py:26
  104.0 1.6 %project.1 = (f32[512,512]{1,0:T(8,128)S(1)}, bf16[512,512]{1,0:T(8,128)(2,1)S(1)}) custom-call(bf16[512,256]{1,0:T(8,128)(2,1)S(1)} %copy-done.8, bf16[512,256]{1,0:T(8,128)(2,1)S(1)} %collective-permute-done.20.b_ref, bf16[512,256]{1,0:T(8,128)(2,1)S(1)} %collective-permute-done.21.c_ref, bf16[512,256]{1,0:T(8,128)(2,1)S(1)} %collective-permute-done.18.d_ref, ...), custom_call_target="tpu_custom_call" | custom-call | flops 1073741824 | bytes 4194304 | tf_op jit(solution)/shard_map/project/pallas_call | solution.py:294
  105.7 1.8 %collective-permute-done.24 = bf16[512,512]{1,0:T(8,128)(2,1)S(1)} collective-permute-done((bf16[512,512]{1,0:T(8,128)(2,1)S(1)}, bf16[512,512]{1,0:T(8,128)(2,1)S(1)}, u32[]{:S(2)}, u32[]{:S(2)}) %collective-permute-start.24) | collective-permute-done | bytes 524320 | tf_op jit(solution)/shard_map/ppermute | solution.py:26
  108.4 8.0 %collective-permute-start.25 = (bf16[156,512]{1,0:T(8,128)(2,1)S(1)}, bf16[156,512]{1,0:T(8,128)(2,1)S(1)}, u32[]{:S(2)}, u32[]{:S(2)}) collective-permute-start(bf16[156,512]{1,0:T(8,128)(2,1)S(1)} %select_n.126), channel_id=1, source_target_pairs={{16,32},{20,36},{24,40},{28,44},{32,16},{36,20},{40,24},{44,28},{4... | collective-permute-start | bytes 479240 | tf_op jit(solution)/shard_map/ppermute | solution.py:40
  117.2 11.7 %collective-permute-done.25 = bf16[156,512]{1,0:T(8,128)(2,1)S(1)} collective-permute-done((bf16[156,512]{1,0:T(8,128)(2,1)S(1)}, bf16[156,512]{1,0:T(8,128)(2,1)S(1)}, u32[]{:S(2)}, u32[]{:S(2)}) %collective-permute-start.25) | collective-permute-done | bytes 159776 | tf_op jit(solution)/shard_map/ppermute | solution.py:40
  129.5 3.3 %collective-permute-start.29 = (bf16[416,512]{1,0:T(8,128)(2,1)S(1)}, bf16[416,512]{1,0:T(8,128)(2,1)S(1)}, u32[]{:S(2)}, u32[]{:S(2)}) collective-permute-start(bf16[416,512]{1,0:T(8,128)(2,1)S(1)} %reshape.56), channel_id=1, source_target_pairs={{0,4},{4,0},{8,12},{12,8},{16,20},{20,16},{24,28},{28,24},{1,5},{5... | collective-permute-start | bytes 1277960 | tf_op jit(solution)/shard_map/ppermute | solution.py:26
  134.8 7.8 %collective-permute-done.28 = bf16[96,512]{1,0:T(8,128)(2,1)S(1)} collective-permute-done((bf16[96,512]{1,0:T(8,128)(2,1)S(1)}, bf16[96,512]{1,0:T(8,128)(2,1)S(1)}, u32[]{:S(2)}, u32[]{:S(2)}) %collective-permute-start.28) | collective-permute-done | bytes 98336 | tf_op jit(solution)/shard_map/ppermute | solution.py:450
  142.6 1.6 %collective-permute-done.29 = bf16[416,512]{1,0:T(8,128)(2,1)S(1)} collective-permute-done((bf16[416,512]{1,0:T(8,128)(2,1)S(1)}, bf16[416,512]{1,0:T(8,128)(2,1)S(1)}, u32[]{:S(2)}, u32[]{:S(2)}) %collective-permute-start.29) | collective-permute-done | bytes 426016 | tf_op jit(solution)/shard_map/ppermute | solution.py:26
  145.7 1.5 place.1
  (109 shorter events, 24.6 us)
Async XLA Ops:
  6.5 30.4 %copy-start.7 = (s32[64]{0:T(128)S(1)}, s32[64]{0:T(128)}, u32[]{:S(2)}) copy-start(s32[64]{0:T(128)} %counts_ref.5) | copy-start | bytes 772
  6.5 69.5 %all-gather.3.cloned.1.call-start = ((), (), s32[]{:S(2)}) async-start(), calls=%async_computation | async-start | bytes 4128768 | tf_op jit(solution)/shard_map/all_gather | solution.py:414
  8.2 6.0 %collective-permute-start = (bf16[5,32,256]{2,1,0:T(8,128)(2,1)S(1)}, bf16[5,32,256]{2,1,0:T(8,128)(2,1)S(1)}, u32[]{:S(2)}, u32[]{:S(2)}) collective-permute-start(bf16[5,32,256]{2,1,0:T(8,128)(2,1)S(1)} %get-tuple-element.39), channel_id=1, source_target_pairs={{0,128},{128,0},{1,129},{129,1},{2,130},{130,2},{3,131},{131,3},{4... | collective-permute-start | bytes 245768 | tf_op jit(solution)/shard_map/ppermute | solution.py:26
  14.3 8.2 %collective-permute-start.3 = (bf16[6,32,256]{2,1,0:T(8,128)(2,1)S(1)}, bf16[6,32,256]{2,1,0:T(8,128)(2,1)S(1)}, u32[]{:S(2)}, u32[]{:S(2)}) collective-permute-start(bf16[6,32,256]{2,1,0:T(8,128)(2,1)S(1)} %pad_maximum_fusion.9), channel_id=1, source_target_pairs={{0,64},{32,96},{64,0},{96,32},{1,65},{33,97},{65,1},{97,33},{2,66}... | collective-permute-start | bytes 294920 | tf_op jit(solution)/shard_map/ppermute | solution.py:26
  17.4 5.1 %collective-permute-start.4 = (bf16[6,32,256]{2,1,0:T(8,128)(2,1)S(1)}, bf16[6,32,256]{2,1,0:T(8,128)(2,1)S(1)}, u32[]{:S(2)}, u32[]{:S(2)}) collective-permute-start(bf16[6,32,256]{2,1,0:T(8,128)(2,1)S(1)} %pad_maximum_fusion.9), channel_id=1, source_target_pairs={{0,32},{32,0},{64,96},{96,64},{1,33},{33,1},{65,97},{97,65},{2,34}... | collective-permute-start | bytes 294920 | tf_op jit(solution)/shard_map/ppermute | solution.py:26
  18.0 5.8 %collective-permute-start.5 = (bf16[6,32,256]{2,1,0:T(8,128)(2,1)S(1)}, bf16[6,32,256]{2,1,0:T(8,128)(2,1)S(1)}, u32[]{:S(2)}, u32[]{:S(2)}) collective-permute-start(bf16[6,32,256]{2,1,0:T(8,128)(2,1)S(1)} %pad_maximum_fusion.9), channel_id=1, source_target_pairs={{0,96},{32,64},{64,32},{96,0},{1,97},{33,65},{65,33},{97,1},{2,98}... | collective-permute-start | bytes 294920 | tf_op jit(solution)/shard_map/ppermute | solution.py:26
  18.5 3.9 %collective-permute-start.6 = (bf16[2,32,256]{2,1,0:T(8,128)(2,1)S(1)}, bf16[2,32,256]{2,1,0:T(8,128)(2,1)S(1)}, u32[]{:S(2)}, u32[]{:S(2)}) collective-permute-start(bf16[2,32,256]{2,1,0:T(8,128)(2,1)S(1)} %broadcast_select_fusion.4), channel_id=1, source_target_pairs={{0,2},{2,0},{1,3},{3,1},{4,6},{6,4},{5,7},{7,5},{8,10},{10,8},{9,1... | collective-permute-start | bytes 98312 | tf_op jit(solution)/shard_map/ppermute | solution.py:26
  24.7 12.2 %collective-permute-start.1 = (bf16[2,256,512]{2,1,0:T(8,128)(2,1)S(1)}, bf16[2,256,512]{2,1,0:T(8,128)(2,1)S(1)}, u32[]{:S(2)}, u32[]{:S(2)}) collective-permute-start(bf16[2,256,512]{2,1,0:T(8,128)(2,1)S(1)} %get-tuple-element.43), channel_id=1, source_target_pairs={{0,4},{4,0},{8,12},{12,8},{16,20},{20,16},{24,28},{28,24},{1,5},{5... | collective-permute-start | bytes 1572872 | tf_op jit(solution)/shard_map/ppermute | solution.py:26
  26.7 10.2 %collective-permute-start.2 = (bf16[1,3,2048]{2,1,0:T(4,128)(2,1)S(1)}, bf16[1,3,2048]{2,1,0:T(4,128)(2,1)S(1)}, u32[]{:S(2)}, u32[]{:S(2)}) collective-permute-start(bf16[1,3,2048]{2,1,0:T(4,128)(2,1)S(1)} %copy-done.5), channel_id=1, source_target_pairs={{0,4},{4,0},{8,12},{12,8},{16,20},{20,16},{24,28},{28,24},{1,5},{5... | collective-permute-start | bytes 36872 | tf_op jit(solution)/shard_map/ppermute | solution.py:26
  37.5 10.9 %collective-permute-start.11 = (bf16[512,512]{1,0:T(8,128)(2,1)S(1)}, bf16[512,512]{1,0:T(8,128)(2,1)S(1)}, u32[]{:S(2)}, u32[]{:S(2)}) collective-permute-start(bf16[512,512]{1,0:T(8,128)(2,1)S(1)} %bitcast.14), channel_id=1, source_target_pairs={{0,2},{2,0},{128,130},{130,128},{1,3},{3,1},{129,131},{131,129},{4... | collective-permute-start | bytes 1572872 | tf_op jit(solution)/shard_map/ppermute | solution.py:26
  38.4 11.8 %collective-permute-start.9 = (bf16[512,512]{1,0:T(8,128)(2,1)S(1)}, bf16[512,512]{1,0:T(8,128)(2,1)S(1)}, u32[]{:S(2)}, u32[]{:S(2)}) collective-permute-start(bf16[512,512]{1,0:T(8,128)(2,1)S(1)} %bitcast.15), channel_id=1, source_target_pairs={{0,130},{2,128},{128,2},{130,0},{1,131},{3,129},{129,3},{131,1},{4... | collective-permute-start | bytes 1572872 | tf_op jit(solution)/shard_map/ppermute | solution.py:26
  39.4 19.7 %collective-permute-start.13 = (bf16[512,512]{1,0:T(8,128)(2,1)S(1)}, bf16[512,512]{1,0:T(8,128)(2,1)S(1)}, u32[]{:S(2)}, u32[]{:S(2)}) collective-permute-start(bf16[512,512]{1,0:T(8,128)(2,1)S(1)} %bitcast.16), channel_id=1, source_target_pairs={{0,1},{1,0},{2,3},{3,2},{4,5},{5,4},{6,7},{7,6},{8,9},{9,8},{10,11... | collective-permute-start | bytes 1572872 | tf_op jit(solution)/shard_map/ppermute | solution.py:26
  48.5 10.7 %collective-permute-start.14 = (bf16[512,512]{1,0:T(8,128)(2,1)S(1)}, bf16[512,512]{1,0:T(8,128)(2,1)S(1)}, u32[]{:S(2)}, u32[]{:S(2)}) collective-permute-start(bf16[512,512]{1,0:T(8,128)(2,1)S(1)} %collective-permute-done.11.c_ref), channel_id=1, source_target_pairs={{0,1},{1,0},{2,3},{3,2},{4,5},{5,4},{6,7},{7,6},{8,9},{9,8},{10,11... | collective-permute-start | bytes 1572872 | tf_op jit(solution)/shard_map/ppermute | solution.py:26
  50.1 7.1 %collective-permute-start.10 = (bf16[256,512]{1,0:T(8,128)(2,1)S(1)}, bf16[256,512]{1,0:T(8,128)(2,1)S(1)}, u32[]{:S(2)}, u32[]{:S(2)}) collective-permute-start(bf16[256,512]{1,0:T(8,128)(2,1)S(1)} %slice.117), channel_id=1, source_target_pairs={{0,2},{2,0},{128,130},{130,128},{1,3},{3,1},{129,131},{131,129},{4... | collective-permute-start | bytes 786440 | tf_op jit(solution)/shard_map/ppermute | solution.py:26
  50.3 8.7 %collective-permute-start.12 = (bf16[256,512]{1,0:T(8,128)(2,1)S(1)}, bf16[256,512]{1,0:T(8,128)(2,1)S(1)}, u32[]{:S(2)}, u32[]{:S(2)}) collective-permute-start(bf16[256,512]{1,0:T(8,128)(2,1)S(1)} %slice.118), channel_id=1, source_target_pairs={{0,130},{2,128},{128,2},{130,0},{1,131},{3,129},{129,3},{131,1},{4... | collective-permute-start | bytes 786440 | tf_op jit(solution)/shard_map/ppermute | solution.py:26
  51.9 15.6 %collective-permute-start.16 = (bf16[512,512]{1,0:T(8,128)(2,1)S(1)}, bf16[512,512]{1,0:T(8,128)(2,1)S(1)}, u32[]{:S(2)}, u32[]{:S(2)}) collective-permute-start(bf16[512,512]{1,0:T(8,128)(2,1)S(1)} %collective-permute-done.9.c_ref), channel_id=1, source_target_pairs={{0,1},{1,0},{2,3},{3,2},{4,5},{5,4},{6,7},{7,6},{8,9},{9,8},{10,11... | collective-permute-start | bytes 1572872 | tf_op jit(solution)/shard_map/ppermute | solution.py:26
  62.1 5.4 %collective-permute-start.15 = (bf16[512,512]{1,0:T(8,128)(2,1)S(1)}, bf16[512,512]{1,0:T(8,128)(2,1)S(1)}, u32[]{:S(2)}, u32[]{:S(2)}) collective-permute-start(bf16[512,512]{1,0:T(8,128)(2,1)S(1)} %pad_maximum_fusion.3.a_ref), channel_id=1, source_target_pairs={{0,1},{1,0},{2,3},{3,2},{4,5},{5,4},{6,7},{7,6},{8,9},{9,8},{10,11... | collective-permute-start | bytes 1572872 | tf_op jit(solution)/shard_map/ppermute | solution.py:26
  62.1 5.4 %collective-permute-start.17 = (bf16[2,3,2048]{2,1,0:T(4,128)(2,1)S(1)}, bf16[2,3,2048]{2,1,0:T(4,128)(2,1)S(1)}, u32[]{:S(2)}, u32[]{:S(2)}) collective-permute-start(bf16[2,3,2048]{2,1,0:T(4,128)(2,1)S(1)} %get-tuple-element.54.mod_ref), channel_id=1, source_target_pairs={{0,128},{128,0},{1,129},{129,1},{2,130},{130,2},{3,131},{131,3},{4... | collective-permute-start | bytes 73736 | tf_op jit(solution)/shard_map/ppermute | solution.py:26
  77.1 17.4 %collective-permute-start.7 = (bf16[8,4,32,256]{3,2,1,0:T(8,128)(2,1)S(1)}, bf16[8,4,32,256]{3,2,1,0:T(8,128)(2,1)S(1)}, u32[]{:S(2)}, u32[]{:S(2)}) collective-permute-start(bf16[8,4,32,256]{3,2,1,0:T(8,128)(2,1)S(1)} %slice.116.o0), channel_id=1, source_target_pairs={{0,32},{32,0},{64,96},{96,64},{1,33},{33,1},{65,97},{97,65},{2,34}... | collective-permute-start | bytes 1572872 | tf_op jit(solution)/shard_map/ppermute | solution.py:26
  78.7 15.9 %collective-permute-start.8 = (bf16[8,4,32,256]{3,2,1,0:T(8,128)(2,1)S(1)}, bf16[8,4,32,256]{3,2,1,0:T(8,128)(2,1)S(1)}, u32[]{:S(2)}, u32[]{:S(2)}) collective-permute-start(bf16[8,4,32,256]{3,2,1,0:T(8,128)(2,1)S(1)} %slice.116.o0), channel_id=1, source_target_pairs={{0,96},{32,64},{64,32},{96,0},{1,97},{33,65},{65,33},{97,1},{2,98}... | collective-permute-start | bytes 1572872 | tf_op jit(solution)/shard_map/ppermute | solution.py:26
  85.5 9.0 %collective-permute-start.18 = (bf16[512,256]{1,0:T(8,128)(2,1)}, bf16[512,256]{1,0:T(8,128)(2,1)S(1)}, u32[]{:S(2)}, u32[]{:S(2)}) collective-permute-start(bf16[512,256]{1,0:T(8,128)(2,1)} %attend.2), channel_id=1, source_target_pairs={{0,130},{2,128},{128,2},{130,0},{1,131},{3,129},{129,3},{131,1},{4... | collective-permute-start | bytes 786440 | tf_op jit(solution)/shard_map/ppermute | solution.py:26
  86.1 8.4 %collective-permute-start.19 = (bf16[512,256]{1,0:T(8,128)(2,1)}, bf16[512,256]{1,0:T(8,128)(2,1)S(1)}, u32[]{:S(2)}, u32[]{:S(2)}) collective-permute-start(bf16[512,256]{1,0:T(8,128)(2,1)} %attend.2), channel_id=1, source_target_pairs={{0,2},{2,0},{128,130},{130,128},{1,3},{3,1},{129,131},{131,129},{4... | collective-permute-start | bytes 786440 | tf_op jit(solution)/shard_map/ppermute | solution.py:26
  94.6 6.7 %collective-permute-start.22 = (bf16[4,4,32,256]{3,2,1,0:T(8,128)(2,1)S(1)}, bf16[4,4,32,256]{3,2,1,0:T(8,128)(2,1)S(1)}, u32[]{:S(2)}, u32[]{:S(2)}) collective-permute-start(bf16[4,4,32,256]{3,2,1,0:T(8,128)(2,1)S(1)} %slice.95), channel_id=1, source_target_pairs={{0,32},{32,0},{64,96},{96,64},{1,33},{33,1},{65,97},{97,65},{2,34}... | collective-permute-start | bytes 786440 | tf_op jit(solution)/shard_map/ppermute | solution.py:26
  95.3 7.7 %collective-permute-start.23 = (bf16[4,4,32,256]{3,2,1,0:T(8,128)(2,1)S(1)}, bf16[4,4,32,256]{3,2,1,0:T(8,128)(2,1)S(1)}, u32[]{:S(2)}, u32[]{:S(2)}) collective-permute-start(bf16[4,4,32,256]{3,2,1,0:T(8,128)(2,1)S(1)} %slice.96), channel_id=1, source_target_pairs={{0,96},{32,64},{64,32},{96,0},{1,97},{33,65},{65,33},{97,1},{2,98}... | collective-permute-start | bytes 786440 | tf_op jit(solution)/shard_map/ppermute | solution.py:26
  96.2 6.8 %collective-permute-start.20 = (bf16[512,256]{1,0:T(8,128)(2,1)}, bf16[512,256]{1,0:T(8,128)(2,1)S(1)}, u32[]{:S(2)}, u32[]{:S(2)}) collective-permute-start(bf16[512,256]{1,0:T(8,128)(2,1)} %attend.3.a_ref), channel_id=1, source_target_pairs={{0,2},{2,0},{128,130},{130,128},{1,3},{3,1},{129,131},{131,129},{4... | collective-permute-start | bytes 786440 | tf_op jit(solution)/shard_map/ppermute | solution.py:26
  96.4 7.6 %collective-permute-start.21 = (bf16[512,256]{1,0:T(8,128)(2,1)S(1)}, bf16[512,256]{1,0:T(8,128)(2,1)S(1)}, u32[]{:S(2)}, u32[]{:S(2)}) collective-permute-start(bf16[512,256]{1,0:T(8,128)(2,1)S(1)} %collective-permute-done.19), channel_id=1, source_target_pairs={{0,130},{2,128},{128,2},{130,0},{1,131},{3,129},{129,3},{131,1},{4... | collective-permute-start | bytes 786440 | tf_op jit(solution)/shard_map/ppermute | solution.py:26
  105.6 2.0 %collective-permute-start.24 = (bf16[512,512]{1,0:T(8,128)(2,1)S(1)}, bf16[512,512]{1,0:T(8,128)(2,1)S(1)}, u32[]{:S(2)}, u32[]{:S(2)}) collective-permute-start(bf16[512,512]{1,0:T(8,128)(2,1)S(1)} %get-tuple-element.67), channel_id=1, source_target_pairs={{0,1},{1,0},{2,3},{3,2},{4,5},{5,4},{6,7},{7,6},{8,9},{9,8},{10,11... | collective-permute-start | bytes 1572872 | tf_op jit(solution)/shard_map/ppermute | solution.py:26
  108.4 20.5 %collective-permute-start.25 = (bf16[156,512]{1,0:T(8,128)(2,1)S(1)}, bf16[156,512]{1,0:T(8,128)(2,1)S(1)}, u32[]{:S(2)}, u32[]{:S(2)}) collective-permute-start(bf16[156,512]{1,0:T(8,128)(2,1)S(1)} %select_n.126), channel_id=1, source_target_pairs={{16,32},{20,36},{24,40},{28,44},{32,16},{36,20},{40,24},{44,28},{4... | collective-permute-start | bytes 479240 | tf_op jit(solution)/shard_map/ppermute | solution.py:40
  116.5 12.4 %collective-permute-start.26 = (bf16[156,512]{1,0:T(8,128)(2,1)S(1)}, bf16[156,512]{1,0:T(8,128)(2,1)S(1)}, u32[]{:S(2)}, u32[]{:S(2)}) collective-permute-start(bf16[156,512]{1,0:T(8,128)(2,1)S(1)} %select_n.128), channel_id=1, source_target_pairs={{0,16},{4,20},{8,24},{12,28},{16,0},{20,4},{24,8},{28,12},{32,48},... | collective-permute-start | bytes 479240 | tf_op jit(solution)/shard_map/ppermute | solution.py:40
  129.5 14.7 %collective-permute-start.29 = (bf16[416,512]{1,0:T(8,128)(2,1)S(1)}, bf16[416,512]{1,0:T(8,128)(2,1)S(1)}, u32[]{:S(2)}, u32[]{:S(2)}) collective-permute-start(bf16[416,512]{1,0:T(8,128)(2,1)S(1)} %reshape.56), channel_id=1, source_target_pairs={{0,4},{4,0},{8,12},{12,8},{16,20},{20,16},{24,28},{28,24},{1,5},{5... | collective-permute-start | bytes 1277960 | tf_op jit(solution)/shard_map/ppermute | solution.py:26
  132.8 2.0 %collective-permute-start.27 = (bf16[96,512]{1,0:T(8,128)(2,1)S(1)}, bf16[96,512]{1,0:T(8,128)(2,1)S(1)}, u32[]{:S(2)}, u32[]{:S(2)}) collective-permute-start(bf16[96,512]{1,0:T(8,128)(2,1)S(1)} %reshape.55), channel_id=1, source_target_pairs={{4,8},{8,4},{20,24},{24,20},{36,40},{40,36},{52,56},{56,52},{68,72... | collective-permute-start | bytes 294920 | tf_op jit(solution)/shard_map/ppermute | solution.py:447
  133.5 9.1 %collective-permute-start.28 = (bf16[96,512]{1,0:T(8,128)(2,1)S(1)}, bf16[96,512]{1,0:T(8,128)(2,1)S(1)}, u32[]{:S(2)}, u32[]{:S(2)}) collective-permute-start(bf16[96,512]{1,0:T(8,128)(2,1)S(1)} %reshape.55), channel_id=1, source_target_pairs={{4,12},{8,0},{20,28},{24,16},{36,44},{40,32},{52,60},{56,48},{68,7... | collective-permute-start | bytes 294920 | tf_op jit(solution)/shard_map/ppermute | solution.py:450
  (10 other events, 40.4 us)
Sparse Core Ops, SparseCore 0:
  24.8 51.1 all-gather.2

commit v7 on v6

--- a/solution.py
+++ b/solution.py
@@ -418,7 +418,7 @@
     _, near, across, side = ring_of_four(mine, ring, 0)
     mods_across = xor_swap(mods, "h", 1)
     hid_own = hidden_of((mine, xor_swap(mine, "c", 1), near, xor_swap(near, "c", 1)), mods)
-    across, hid_own = lax.optimization_barrier((across, hid_own))
+    across, hid_own, mods_across = lax.optimization_barrier((across, hid_own, mods_across))
     hid_other = hidden_of(
         (across, xor_swap(across, "c", 1), side, xor_swap(side, "c", 1)), mods_across
     )
@@ -450,7 +450,7 @@
     beyond = lax.ppermute(
         edge, REGION, [(i, i ^ 2) for i in range(64) if i % 4 in (1, 2)]
     )
-    beside, beyond, other = lax.optimization_barrier((beside, beyond, other))
+    other, beside, beyond = lax.optimization_barrier((other, beside, beyond))
     edge = jnp.where((region % 4 == 1) | (region % 4 == 2), beside, beyond).reshape(S, W, NARROW)
     joined = join_pair(strip, other.reshape(strip.shape), edge, region, blend_weights)
     return place_tiles(tile_counts, joined.reshape(4, TOK, NARROW))

time: 157 us -> 157 us (level)
  starting transfers between devices: 35.9 us -> 37.5 us
    ppermute x26, waiting for transfers between devices: 50.8 us -> 46.5 us  [xor_swap(): return lax.ppermute(block, axis, [(i, i ^ bit) for i in range(size)])]
    all_gather x1, waiting for transfers between devices: 5.5 us -> 8.31 us  [on_device(): gathered = lax.all_gather(block, 'z', axis=0)]
where the time goes in v7:
time: 157 us; the launch traced here: 154 us
  waiting for transfers between devices  74.3 us (47%)
  starting transfers between devices  37.5 us (24%)
  Pallas kernels  17.2 us (11%)
  between operations  13.9 us (9%)
  local copies, waits for them, and re-layouts  9.16 us (6%)
  other arithmetic  2.01 us (1%)
    ppermute x26, waiting for transfers between devices, xor_swap(): return lax.ppermute(block, axis, [(i, i ^ bit) for i in range(size)])  46.5 us
    ppermute x26, starting transfers between devices, xor_swap(): return lax.ppermute(block, axis, [(i, i ^ bit) for i in range(size)])  26.7 us
    ppermute x2, waiting for transfers between devices, trade(): return lax.ppermute(block, REGION, route)  11.7 us
    pallas_call x2, Pallas kernels, attended_of(): pl.pallas_call(attend_kernel, in_specs=[HBM] * 2, out_specs=VMEM, out_sha...  9.58 us
    ppermute x2, starting transfers between devices, trade(): return lax.ppermute(block, REGION, route)  8.76 us
    all_gather x1, waiting for transfers between devices, on_device(): gathered = lax.all_gather(block, 'z', axis=0)  8.31 us
    ppermute x1, waiting for transfers between devices, on_device(): lax.ppermute(edge, REGION, [(i, i ^ 2) for i in range(64) if i % 4 in (1,...  7.8 us
    unnamed x27, local copies, waits for them, and re-layouts  7.06 us
  transfers between devices with their start and end apart: 31, of which 18 were waited for; matrix products, arithmetic and copies ran while one was open for 0% of the time, Pallas kernels for 9%

profile of v7, /device:TPU:24, one launch (start us, length us, event | category | flops | bytes accessed | tf_op | source)
XLA Modules:
  0.0 154.1 jit_solution(1971247771559112447)
XLA Ops:
  12.1 2.2 %collective-permute-done = bf16[5,32,256]{2,1,0:T(8,128)(2,1)S(1)} collective-permute-done((bf16[5,32,256]{2,1,0:T(8,128)(2,1)S(1)}, bf16[5,32,256]{2,1,0:T(8,128)(2,1)S(1)}, u32[]{:S(2)}, u32[]{:S(2)}) %collective-permute-start) | collective-permute-done | bytes 81952 | tf_op jit(solution)/shard_map/ppermute | solution.py:26
  14.3 3.1 %collective-permute-start.3 = (bf16[6,32,256]{2,1,0:T(8,128)(2,1)S(1)}, bf16[6,32,256]{2,1,0:T(8,128)(2,1)S(1)}, u32[]{:S(2)}, u32[]{:S(2)}) collective-permute-start(bf16[6,32,256]{2,1,0:T(8,128)(2,1)S(1)} %pad_maximum_fusion.9), channel_id=1, source_target_pairs={{0,64},{32,96},{64,0},{96,32},{1,65},{33,97},{65,1},{97,33},{2,66}... | collective-permute-start | bytes 294920 | tf_op jit(solution)/shard_map/ppermute | solution.py:26
  19.3 3.2 %collective-permute-done.6 = bf16[2,32,256]{2,1,0:T(8,128)(2,1)S(1)} collective-permute-done((bf16[2,32,256]{2,1,0:T(8,128)(2,1)S(1)}, bf16[2,32,256]{2,1,0:T(8,128)(2,1)S(1)}, u32[]{:S(2)}, u32[]{:S(2)}) %collective-permute-start.6) | collective-permute-done | bytes 32800 | tf_op jit(solution)/shard_map/ppermute | solution.py:26
  24.7 2.0 %collective-permute-start.1 = (bf16[2,256,512]{2,1,0:T(8,128)(2,1)S(1)}, bf16[2,256,512]{2,1,0:T(8,128)(2,1)S(1)}, u32[]{:S(2)}, u32[]{:S(2)}) collective-permute-start(bf16[2,256,512]{2,1,0:T(8,128)(2,1)S(1)} %get-tuple-element.44), channel_id=1, source_target_pairs={{0,4},{4,0},{8,12},{12,8},{16,20},{20,16},{24,28},{28,24},{1,5},{5... | collective-permute-start | bytes 1572872 | tf_op jit(solution)/shard_map/ppermute | solution.py:26
  26.8 10.1 %collective-permute-done.2.other_mod = bf16[1,3,2048]{2,1,0:T(4,128)(2,1)S(1)} collective-permute-done((bf16[1,3,2048]{2,1,0:T(4,128)(2,1)S(1)}, bf16[1,3,2048]{2,1,0:T(4,128)(2,1)S(1)}, u32[]{:S(2)}, u32[]{:S(2)}) %collective-permute-start.2) | collective-permute-done | bytes 12320 | tf_op jit(solution)/shard_map/ppermute | solution.py:26
  39.4 9.0 %collective-permute-done.11.c_ref = bf16[512,512]{1,0:T(8,128)(2,1)S(1)} collective-permute-done((bf16[512,512]{1,0:T(8,128)(2,1)S(1)}, bf16[512,512]{1,0:T(8,128)(2,1)S(1)}, u32[]{:S(2)}, u32[]{:S(2)}) %collective-permute-start.11) | collective-permute-done | bytes 524320 | tf_op jit(solution)/shard_map/ppermute | solution.py:26
  48.5 1.7 %collective-permute-done.9.c_ref = bf16[512,512]{1,0:T(8,128)(2,1)S(1)} collective-permute-done((bf16[512,512]{1,0:T(8,128)(2,1)S(1)}, bf16[512,512]{1,0:T(8,128)(2,1)S(1)}, u32[]{:S(2)}, u32[]{:S(2)}) %collective-permute-start.9) | collective-permute-done | bytes 524320 | tf_op jit(solution)/shard_map/ppermute | solution.py:26
  50.3 1.6 %collective-permute-start.12 = (bf16[256,512]{1,0:T(8,128)(2,1)S(1)}, bf16[256,512]{1,0:T(8,128)(2,1)S(1)}, u32[]{:S(2)}, u32[]{:S(2)}) collective-permute-start(bf16[256,512]{1,0:T(8,128)(2,1)S(1)} %slice.118), channel_id=1, source_target_pairs={{0,130},{2,128},{128,2},{130,0},{1,131},{3,129},{129,3},{131,1},{4... | collective-permute-start | bytes 786440 | tf_op jit(solution)/shard_map/ppermute | solution.py:26
  51.9 2.5 %collective-permute-start.15 = (bf16[2,3,2048]{2,1,0:T(4,128)(2,1)S(1)}, bf16[2,3,2048]{2,1,0:T(4,128)(2,1)S(1)}, u32[]{:S(2)}, u32[]{:S(2)}) collective-permute-start(bf16[2,3,2048]{2,1,0:T(4,128)(2,1)S(1)} %get-tuple-element.55.mod_ref), channel_id=1, source_target_pairs={{0,128},{128,0},{1,129},{129,1},{2,130},{130,2},{3,131},{131,3},{4... | collective-permute-start | bytes 73736 | tf_op jit(solution)/shard_map/ppermute | solution.py:26
  54.4 3.2 %collective-permute-done.10 = bf16[256,512]{1,0:T(8,128)(2,1)S(1)} collective-permute-done((bf16[256,512]{1,0:T(8,128)(2,1)S(1)}, bf16[256,512]{1,0:T(8,128)(2,1)S(1)}, u32[]{:S(2)}, u32[]{:S(2)}) %collective-permute-start.10) | collective-permute-done | bytes 262176 | tf_op jit(solution)/shard_map/ppermute | solution.py:26
  57.6 2.1 %collective-permute-done.12 = bf16[256,512]{1,0:T(8,128)(2,1)S(1)} collective-permute-done((bf16[256,512]{1,0:T(8,128)(2,1)S(1)}, bf16[256,512]{1,0:T(8,128)(2,1)S(1)}, u32[]{:S(2)}, u32[]{:S(2)}) %collective-permute-start.12) | collective-permute-done | bytes 262176 | tf_op jit(solution)/shard_map/ppermute | solution.py:26
  59.8 1.6 %hidden.2.hid_hbm = bf16[512,2048]{1,0:T(8,128)(2,1)S(1)} custom-call(bf16[512,512]{1,0:T(8,128)(2,1)S(1)} %bitcast.17, bf16[512,512]{1,0:T(8,128)(2,1)S(1)} %collective-permute-done.13.b_ref, bf16[512,512]{1,0:T(8,128)(2,1)S(1)} %collective-permute-done.11.c_ref, bf16[512,512]{1,0:T(8,128)(2,1)S(1)} %collective-permute-done.14.d_ref, ...), custom_call_target="tpu_custom_call" | custom-call | flops 8388608 | bytes 4194304 | tf_op jit(solution)/shard_map/hidden/pallas_call | solution.py:182
  62.8 1.9 %collective-permute-done.16.b_ref = bf16[512,512]{1,0:T(8,128)(2,1)S(1)} collective-permute-done((bf16[512,512]{1,0:T(8,128)(2,1)S(1)}, bf16[512,512]{1,0:T(8,128)(2,1)S(1)}, u32[]{:S(2)}, u32[]{:S(2)}) %collective-permute-start.16) | collective-permute-done | bytes 524320 | tf_op jit(solution)/shard_map/ppermute | solution.py:26
  64.7 1.6 %hidden.3.hid_hbm = bf16[512,2048]{1,0:T(8,128)(2,1)S(1)} custom-call(bf16[512,512]{1,0:T(8,128)(2,1)S(1)} %pad_maximum_fusion.3.a_ref, bf16[512,512]{1,0:T(8,128)(2,1)S(1)} %collective-permute-done.16.b_ref, bf16[512,512]{1,0:T(8,128)(2,1)S(1)} %collective-permute-done.9.c_ref, bf16[512,512]{1,0:T(8,128)(2,1)S(1)} %collective-permute-done.17.d_ref, ...), custom_call_target="tpu_custom_call" | custom-call | flops 8388608 | bytes 4194304 | tf_op jit(solution)/shard_map/hidden/pallas_call | solution.py:182
  66.4 1.4 copy-done.1
  67.7 8.3 %all-gather.3.cloned.1.call-done = bf16[224,32,256]{2,1,0:T(8,128)(2,1)} async-done(((bf16[28,32,256]{2,1,0:T(8,128)(2,1)}), bf16[224,32,256]{2,1,0:T(8,128)(2,1)}) %all-gather.3.cloned.1.call-update) | async-done | bytes 3670032 | tf_op jit(solution)/shard_map/all_gather | solution.py:414
  77.1 1.6 %collective-permute-start.7 = (bf16[8,4,32,256]{3,2,1,0:T(8,128)(2,1)S(1)}, bf16[8,4,32,256]{3,2,1,0:T(8,128)(2,1)S(1)}, u32[]{:S(2)}, u32[]{:S(2)}) collective-permute-start(bf16[8,4,32,256]{3,2,1,0:T(8,128)(2,1)S(1)} %slice.116.o0), channel_id=1, source_target_pairs={{0,32},{32,0},{64,96},{96,64},{1,33},{33,1},{65,97},{97,65},{2,34}... | collective-permute-start | bytes 1572872 | tf_op jit(solution)/shard_map/ppermute | solution.py:26
  78.7 2.1 %collective-permute-start.8 = (bf16[8,4,32,256]{3,2,1,0:T(8,128)(2,1)S(1)}, bf16[8,4,32,256]{3,2,1,0:T(8,128)(2,1)S(1)}, u32[]{:S(2)}, u32[]{:S(2)}) collective-permute-start(bf16[8,4,32,256]{3,2,1,0:T(8,128)(2,1)S(1)} %slice.116.o0), channel_id=1, source_target_pairs={{0,96},{32,64},{64,32},{96,0},{1,97},{33,65},{65,33},{97,1},{2,98}... | collective-permute-start | bytes 1572872 | tf_op jit(solution)/shard_map/ppermute | solution.py:26
  80.7 4.8 %attend.2 = bf16[512,256]{1,0:T(8,128)(2,1)} custom-call(bf16[512,2048]{1,0:T(8,128)(2,1)} %copy-done.1, bf16[8,28,32,256]{3,2,1,0:T(8,128)(2,1)} %bitcast.30), custom_call_target="tpu_custom_call" | custom-call | flops 3489660928 | bytes 6291456 | tf_op jit(solution)/shard_map/attend/pallas_call | solution.py:248
  87.0 4.8 %attend.3.a_ref = bf16[512,256]{1,0:T(8,128)(2,1)} custom-call(bf16[512,2048]{1,0:T(8,128)(2,1)} %copy-done, bf16[8,28,32,256]{3,2,1,0:T(8,128)(2,1)} %bitcast.31), custom_call_target="tpu_custom_call" | custom-call | flops 3489660928 | bytes 6291456 | tf_op jit(solution)/shard_map/attend/pallas_call | solution.py:248
  91.8 2.7 %collective-permute-done.18.d_ref = bf16[512,256]{1,0:T(8,128)(2,1)S(1)} collective-permute-done((bf16[512,256]{1,0:T(8,128)(2,1)}, bf16[512,256]{1,0:T(8,128)(2,1)S(1)}, u32[]{:S(2)}, u32[]{:S(2)}) %collective-permute-start.18) | collective-permute-done | bytes 262176 | tf_op jit(solution)/shard_map/ppermute | solution.py:26
  96.4 1.9 %collective-permute-start.21 = (bf16[512,256]{1,0:T(8,128)(2,1)S(1)}, bf16[512,256]{1,0:T(8,128)(2,1)S(1)}, u32[]{:S(2)}, u32[]{:S(2)}) collective-permute-start(bf16[512,256]{1,0:T(8,128)(2,1)S(1)} %collective-permute-done.19), channel_id=1, source_target_pairs={{0,130},{2,128},{128,2},{130,0},{1,131},{3,129},{129,3},{131,1},{4... | collective-permute-start | bytes 786440 | tf_op jit(solution)/shard_map/ppermute | solution.py:26
  98.3 2.9 %collective-permute-done.22 = bf16[4,4,32,256]{3,2,1,0:T(8,128)(2,1)S(1)} collective-permute-done((bf16[4,4,32,256]{3,2,1,0:T(8,128)(2,1)S(1)}, bf16[4,4,32,256]{3,2,1,0:T(8,128)(2,1)S(1)}, u32[]{:S(2)}, u32[]{:S(2)}) %collective-permute-start.22) | collective-permute-done | bytes 262176 | tf_op jit(solution)/shard_map/ppermute | solution.py:26
  101.2 1.7 %collective-permute-done.23 = bf16[4,4,32,256]{3,2,1,0:T(8,128)(2,1)S(1)} collective-permute-done((bf16[4,4,32,256]{3,2,1,0:T(8,128)(2,1)S(1)}, bf16[4,4,32,256]{3,2,1,0:T(8,128)(2,1)S(1)}, u32[]{:S(2)}, u32[]{:S(2)}) %collective-permute-start.23) | collective-permute-done | bytes 262176 | tf_op jit(solution)/shard_map/ppermute | solution.py:26
  104.0 1.6 %project.1 = (f32[512,512]{1,0:T(8,128)S(1)}, bf16[512,512]{1,0:T(8,128)(2,1)S(1)}) custom-call(bf16[512,256]{1,0:T(8,128)(2,1)S(1)} %copy-done.8, bf16[512,256]{1,0:T(8,128)(2,1)S(1)} %collective-permute-done.20.b_ref, bf16[512,256]{1,0:T(8,128)(2,1)S(1)} %collective-permute-done.21.c_ref, bf16[512,256]{1,0:T(8,128)(2,1)S(1)} %collective-permute-done.18.d_ref, ...), custom_call_target="tpu_custom_call" | custom-call | flops 1073741824 | bytes 4194304 | tf_op jit(solution)/shard_map/project/pallas_call | solution.py:294
  105.7 1.8 %collective-permute-done.24 = bf16[512,512]{1,0:T(8,128)(2,1)S(1)} collective-permute-done((bf16[512,512]{1,0:T(8,128)(2,1)S(1)}, bf16[512,512]{1,0:T(8,128)(2,1)S(1)}, u32[]{:S(2)}, u32[]{:S(2)}) %collective-permute-start.24) | collective-permute-done | bytes 524320 | tf_op jit(solution)/shard_map/ppermute | solution.py:26
  108.4 8.0 %collective-permute-start.25 = (bf16[156,512]{1,0:T(8,128)(2,1)S(1)}, bf16[156,512]{1,0:T(8,128)(2,1)S(1)}, u32[]{:S(2)}, u32[]{:S(2)}) collective-permute-start(bf16[156,512]{1,0:T(8,128)(2,1)S(1)} %select_n.125), channel_id=1, source_target_pairs={{16,32},{20,36},{24,40},{28,44},{32,16},{36,20},{40,24},{44,28},{4... | collective-permute-start | bytes 479240 | tf_op jit(solution)/shard_map/ppermute | solution.py:40
  117.2 11.7 %collective-permute-done.25 = bf16[156,512]{1,0:T(8,128)(2,1)S(1)} collective-permute-done((bf16[156,512]{1,0:T(8,128)(2,1)S(1)}, bf16[156,512]{1,0:T(8,128)(2,1)S(1)}, u32[]{:S(2)}, u32[]{:S(2)}) %collective-permute-start.25) | collective-permute-done | bytes 159776 | tf_op jit(solution)/shard_map/ppermute | solution.py:40
  129.5 3.3 %collective-permute-start.27 = (bf16[416,512]{1,0:T(8,128)(2,1)S(1)}, bf16[416,512]{1,0:T(8,128)(2,1)S(1)}, u32[]{:S(2)}, u32[]{:S(2)}) collective-permute-start(bf16[416,512]{1,0:T(8,128)(2,1)S(1)} %reshape.55), channel_id=1, source_target_pairs={{0,4},{4,0},{8,12},{12,8},{16,20},{20,16},{24,28},{28,24},{1,5},{5... | collective-permute-start | bytes 1277960 | tf_op jit(solution)/shard_map/ppermute | solution.py:26
  134.8 7.8 %collective-permute-done.29 = bf16[96,512]{1,0:T(8,128)(2,1)S(1)} collective-permute-done((bf16[96,512]{1,0:T(8,128)(2,1)S(1)}, bf16[96,512]{1,0:T(8,128)(2,1)S(1)}, u32[]{:S(2)}, u32[]{:S(2)}) %collective-permute-start.29) | collective-permute-done | bytes 98336 | tf_op jit(solution)/shard_map/ppermute | solution.py:450
  142.6 1.6 %collective-permute-done.27 = bf16[416,512]{1,0:T(8,128)(2,1)S(1)} collective-permute-done((bf16[416,512]{1,0:T(8,128)(2,1)S(1)}, bf16[416,512]{1,0:T(8,128)(2,1)S(1)}, u32[]{:S(2)}, u32[]{:S(2)}) %collective-permute-start.27) | collective-permute-done | bytes 426016 | tf_op jit(solution)/shard_map/ppermute | solution.py:26
  145.7 1.5 place.1
  (109 shorter events, 24.9 us)
Async XLA Ops:
  6.5 30.4 %copy-start.7 = (s32[64]{0:T(128)S(1)}, s32[64]{0:T(128)}, u32[]{:S(2)}) copy-start(s32[64]{0:T(128)} %counts_ref.5) | copy-start | bytes 772
  6.5 69.5 %all-gather.3.cloned.1.call-start = ((), (), s32[]{:S(2)}) async-start(), calls=%async_computation | async-start | bytes 4128768 | tf_op jit(solution)/shard_map/all_gather | solution.py:414
  8.2 6.0 %collective-permute-start = (bf16[5,32,256]{2,1,0:T(8,128)(2,1)S(1)}, bf16[5,32,256]{2,1,0:T(8,128)(2,1)S(1)}, u32[]{:S(2)}, u32[]{:S(2)}) collective-permute-start(bf16[5,32,256]{2,1,0:T(8,128)(2,1)S(1)} %get-tuple-element.40), channel_id=1, source_target_pairs={{0,128},{128,0},{1,129},{129,1},{2,130},{130,2},{3,131},{131,3},{4... | collective-permute-start | bytes 245768 | tf_op jit(solution)/shard_map/ppermute | solution.py:26
  14.3 8.2 %collective-permute-start.3 = (bf16[6,32,256]{2,1,0:T(8,128)(2,1)S(1)}, bf16[6,32,256]{2,1,0:T(8,128)(2,1)S(1)}, u32[]{:S(2)}, u32[]{:S(2)}) collective-permute-start(bf16[6,32,256]{2,1,0:T(8,128)(2,1)S(1)} %pad_maximum_fusion.9), channel_id=1, source_target_pairs={{0,64},{32,96},{64,0},{96,32},{1,65},{33,97},{65,1},{97,33},{2,66}... | collective-permute-start | bytes 294920 | tf_op jit(solution)/shard_map/ppermute | solution.py:26
  17.4 5.1 %collective-permute-start.4 = (bf16[6,32,256]{2,1,0:T(8,128)(2,1)S(1)}, bf16[6,32,256]{2,1,0:T(8,128)(2,1)S(1)}, u32[]{:S(2)}, u32[]{:S(2)}) collective-permute-start(bf16[6,32,256]{2,1,0:T(8,128)(2,1)S(1)} %pad_maximum_fusion.9), channel_id=1, source_target_pairs={{0,32},{32,0},{64,96},{96,64},{1,33},{33,1},{65,97},{97,65},{2,34}... | collective-permute-start | bytes 294920 | tf_op jit(solution)/shard_map/ppermute | solution.py:26
  18.0 5.8 %collective-permute-start.5 = (bf16[6,32,256]{2,1,0:T(8,128)(2,1)S(1)}, bf16[6,32,256]{2,1,0:T(8,128)(2,1)S(1)}, u32[]{:S(2)}, u32[]{:S(2)}) collective-permute-start(bf16[6,32,256]{2,1,0:T(8,128)(2,1)S(1)} %pad_maximum_fusion.9), channel_id=1, source_target_pairs={{0,96},{32,64},{64,32},{96,0},{1,97},{33,65},{65,33},{97,1},{2,98}... | collective-permute-start | bytes 294920 | tf_op jit(solution)/shard_map/ppermute | solution.py:26
  18.5 3.9 %collective-permute-start.6 = (bf16[2,32,256]{2,1,0:T(8,128)(2,1)S(1)}, bf16[2,32,256]{2,1,0:T(8,128)(2,1)S(1)}, u32[]{:S(2)}, u32[]{:S(2)}) collective-permute-start(bf16[2,32,256]{2,1,0:T(8,128)(2,1)S(1)} %broadcast_select_fusion.4), channel_id=1, source_target_pairs={{0,2},{2,0},{1,3},{3,1},{4,6},{6,4},{5,7},{7,5},{8,10},{10,8},{9,1... | collective-permute-start | bytes 98312 | tf_op jit(solution)/shard_map/ppermute | solution.py:26
  24.7 12.2 %collective-permute-start.1 = (bf16[2,256,512]{2,1,0:T(8,128)(2,1)S(1)}, bf16[2,256,512]{2,1,0:T(8,128)(2,1)S(1)}, u32[]{:S(2)}, u32[]{:S(2)}) collective-permute-start(bf16[2,256,512]{2,1,0:T(8,128)(2,1)S(1)} %get-tuple-element.44), channel_id=1, source_target_pairs={{0,4},{4,0},{8,12},{12,8},{16,20},{20,16},{24,28},{28,24},{1,5},{5... | collective-permute-start | bytes 1572872 | tf_op jit(solution)/shard_map/ppermute | solution.py:26
  26.7 10.2 %collective-permute-start.2 = (bf16[1,3,2048]{2,1,0:T(4,128)(2,1)S(1)}, bf16[1,3,2048]{2,1,0:T(4,128)(2,1)S(1)}, u32[]{:S(2)}, u32[]{:S(2)}) collective-permute-start(bf16[1,3,2048]{2,1,0:T(4,128)(2,1)S(1)} %copy-done.5), channel_id=1, source_target_pairs={{0,4},{4,0},{8,12},{12,8},{16,20},{20,16},{24,28},{28,24},{1,5},{5... | collective-permute-start | bytes 36872 | tf_op jit(solution)/shard_map/ppermute | solution.py:26
  37.5 10.9 %collective-permute-start.11 = (bf16[512,512]{1,0:T(8,128)(2,1)S(1)}, bf16[512,512]{1,0:T(8,128)(2,1)S(1)}, u32[]{:S(2)}, u32[]{:S(2)}) collective-permute-start(bf16[512,512]{1,0:T(8,128)(2,1)S(1)} %bitcast.14), channel_id=1, source_target_pairs={{0,2},{2,0},{128,130},{130,128},{1,3},{3,1},{129,131},{131,129},{4... | collective-permute-start | bytes 1572872 | tf_op jit(solution)/shard_map/ppermute | solution.py:26
  38.4 11.8 %collective-permute-start.9 = (bf16[512,512]{1,0:T(8,128)(2,1)S(1)}, bf16[512,512]{1,0:T(8,128)(2,1)S(1)}, u32[]{:S(2)}, u32[]{:S(2)}) collective-permute-start(bf16[512,512]{1,0:T(8,128)(2,1)S(1)} %bitcast.15), channel_id=1, source_target_pairs={{0,130},{2,128},{128,2},{130,0},{1,131},{3,129},{129,3},{131,1},{4... | collective-permute-start | bytes 1572872 | tf_op jit(solution)/shard_map/ppermute | solution.py:26
  39.4 20.4 %collective-permute-start.13 = (bf16[512,512]{1,0:T(8,128)(2,1)S(1)}, bf16[512,512]{1,0:T(8,128)(2,1)S(1)}, u32[]{:S(2)}, u32[]{:S(2)}) collective-permute-start(bf16[512,512]{1,0:T(8,128)(2,1)S(1)} %bitcast.16), channel_id=1, source_target_pairs={{0,1},{1,0},{2,3},{3,2},{4,5},{5,4},{6,7},{7,6},{8,9},{9,8},{10,11... | collective-permute-start | bytes 1572872 | tf_op jit(solution)/shard_map/ppermute | solution.py:26
  48.5 11.4 %collective-permute-start.14 = (bf16[512,512]{1,0:T(8,128)(2,1)S(1)}, bf16[512,512]{1,0:T(8,128)(2,1)S(1)}, u32[]{:S(2)}, u32[]{:S(2)}) collective-permute-start(bf16[512,512]{1,0:T(8,128)(2,1)S(1)} %collective-permute-done.11.c_ref), channel_id=1, source_target_pairs={{0,1},{1,0},{2,3},{3,2},{4,5},{5,4},{6,7},{7,6},{8,9},{9,8},{10,11... | collective-permute-start | bytes 1572872 | tf_op jit(solution)/shard_map/ppermute | solution.py:26
  50.1 7.5 %collective-permute-start.10 = (bf16[256,512]{1,0:T(8,128)(2,1)S(1)}, bf16[256,512]{1,0:T(8,128)(2,1)S(1)}, u32[]{:S(2)}, u32[]{:S(2)}) collective-permute-start(bf16[256,512]{1,0:T(8,128)(2,1)S(1)} %slice.117), channel_id=1, source_target_pairs={{0,2},{2,0},{128,130},{130,128},{1,3},{3,1},{129,131},{131,129},{4... | collective-permute-start | bytes 786440 | tf_op jit(solution)/shard_map/ppermute | solution.py:26
  50.3 9.4 %collective-permute-start.12 = (bf16[256,512]{1,0:T(8,128)(2,1)S(1)}, bf16[256,512]{1,0:T(8,128)(2,1)S(1)}, u32[]{:S(2)}, u32[]{:S(2)}) collective-permute-start(bf16[256,512]{1,0:T(8,128)(2,1)S(1)} %slice.118), channel_id=1, source_target_pairs={{0,130},{2,128},{128,2},{130,0},{1,131},{3,129},{129,3},{131,1},{4... | collective-permute-start | bytes 786440 | tf_op jit(solution)/shard_map/ppermute | solution.py:26
  51.9 10.9 %collective-permute-start.15 = (bf16[2,3,2048]{2,1,0:T(4,128)(2,1)S(1)}, bf16[2,3,2048]{2,1,0:T(4,128)(2,1)S(1)}, u32[]{:S(2)}, u32[]{:S(2)}) collective-permute-start(bf16[2,3,2048]{2,1,0:T(4,128)(2,1)S(1)} %get-tuple-element.55.mod_ref), channel_id=1, source_target_pairs={{0,128},{128,0},{1,129},{129,1},{2,130},{130,2},{3,131},{131,3},{4... | collective-permute-start | bytes 73736 | tf_op jit(solution)/shard_map/ppermute | solution.py:26
  57.6 5.2 %collective-permute-start.17 = (bf16[512,512]{1,0:T(8,128)(2,1)S(1)}, bf16[512,512]{1,0:T(8,128)(2,1)S(1)}, u32[]{:S(2)}, u32[]{:S(2)}) collective-permute-start(bf16[512,512]{1,0:T(8,128)(2,1)S(1)} %collective-permute-done.9.c_ref), channel_id=1, source_target_pairs={{0,1},{1,0},{2,3},{3,2},{4,5},{5,4},{6,7},{7,6},{8,9},{9,8},{10,11... | collective-permute-start | bytes 1572872 | tf_op jit(solution)/shard_map/ppermute | solution.py:26
  62.8 1.9 %collective-permute-start.16 = (bf16[512,512]{1,0:T(8,128)(2,1)S(1)}, bf16[512,512]{1,0:T(8,128)(2,1)S(1)}, u32[]{:S(2)}, u32[]{:S(2)}) collective-permute-start(bf16[512,512]{1,0:T(8,128)(2,1)S(1)} %pad_maximum_fusion.3.a_ref), channel_id=1, source_target_pairs={{0,1},{1,0},{2,3},{3,2},{4,5},{5,4},{6,7},{7,6},{8,9},{9,8},{10,11... | collective-permute-start | bytes 1572872 | tf_op jit(solution)/shard_map/ppermute | solution.py:26
  77.1 17.4 %collective-permute-start.7 = (bf16[8,4,32,256]{3,2,1,0:T(8,128)(2,1)S(1)}, bf16[8,4,32,256]{3,2,1,0:T(8,128)(2,1)S(1)}, u32[]{:S(2)}, u32[]{:S(2)}) collective-permute-start(bf16[8,4,32,256]{3,2,1,0:T(8,128)(2,1)S(1)} %slice.116.o0), channel_id=1, source_target_pairs={{0,32},{32,0},{64,96},{96,64},{1,33},{33,1},{65,97},{97,65},{2,34}... | collective-permute-start | bytes 1572872 | tf_op jit(solution)/shard_map/ppermute | solution.py:26
  78.7 15.9 %collective-permute-start.8 = (bf16[8,4,32,256]{3,2,1,0:T(8,128)(2,1)S(1)}, bf16[8,4,32,256]{3,2,1,0:T(8,128)(2,1)S(1)}, u32[]{:S(2)}, u32[]{:S(2)}) collective-permute-start(bf16[8,4,32,256]{3,2,1,0:T(8,128)(2,1)S(1)} %slice.116.o0), channel_id=1, source_target_pairs={{0,96},{32,64},{64,32},{96,0},{1,97},{33,65},{65,33},{97,1},{2,98}... | collective-permute-start | bytes 1572872 | tf_op jit(solution)/shard_map/ppermute | solution.py:26
  85.5 9.0 %collective-permute-start.18 = (bf16[512,256]{1,0:T(8,128)(2,1)}, bf16[512,256]{1,0:T(8,128)(2,1)S(1)}, u32[]{:S(2)}, u32[]{:S(2)}) collective-permute-start(bf16[512,256]{1,0:T(8,128)(2,1)} %attend.2), channel_id=1, source_target_pairs={{0,130},{2,128},{128,2},{130,0},{1,131},{3,129},{129,3},{131,1},{4... | collective-permute-start | bytes 786440 | tf_op jit(solution)/shard_map/ppermute | solution.py:26
  86.1 8.4 %collective-permute-start.19 = (bf16[512,256]{1,0:T(8,128)(2,1)}, bf16[512,256]{1,0:T(8,128)(2,1)S(1)}, u32[]{:S(2)}, u32[]{:S(2)}) collective-permute-start(bf16[512,256]{1,0:T(8,128)(2,1)} %attend.2), channel_id=1, source_target_pairs={{0,2},{2,0},{128,130},{130,128},{1,3},{3,1},{129,131},{131,129},{4... | collective-permute-start | bytes 786440 | tf_op jit(solution)/shard_map/ppermute | solution.py:26
  94.6 6.7 %collective-permute-start.22 = (bf16[4,4,32,256]{3,2,1,0:T(8,128)(2,1)S(1)}, bf16[4,4,32,256]{3,2,1,0:T(8,128)(2,1)S(1)}, u32[]{:S(2)}, u32[]{:S(2)}) collective-permute-start(bf16[4,4,32,256]{3,2,1,0:T(8,128)(2,1)S(1)} %slice.95), channel_id=1, source_target_pairs={{0,32},{32,0},{64,96},{96,64},{1,33},{33,1},{65,97},{97,65},{2,34}... | collective-permute-start | bytes 786440 | tf_op jit(solution)/shard_map/ppermute | solution.py:26
  95.3 7.7 %collective-permute-start.23 = (bf16[4,4,32,256]{3,2,1,0:T(8,128)(2,1)S(1)}, bf16[4,4,32,256]{3,2,1,0:T(8,128)(2,1)S(1)}, u32[]{:S(2)}, u32[]{:S(2)}) collective-permute-start(bf16[4,4,32,256]{3,2,1,0:T(8,128)(2,1)S(1)} %slice.96), channel_id=1, source_target_pairs={{0,96},{32,64},{64,32},{96,0},{1,97},{33,65},{65,33},{97,1},{2,98}... | collective-permute-start | bytes 786440 | tf_op jit(solution)/shard_map/ppermute | solution.py:26
  96.2 6.8 %collective-permute-start.20 = (bf16[512,256]{1,0:T(8,128)(2,1)}, bf16[512,256]{1,0:T(8,128)(2,1)S(1)}, u32[]{:S(2)}, u32[]{:S(2)}) collective-permute-start(bf16[512,256]{1,0:T(8,128)(2,1)} %attend.3.a_ref), channel_id=1, source_target_pairs={{0,2},{2,0},{128,130},{130,128},{1,3},{3,1},{129,131},{131,129},{4... | collective-permute-start | bytes 786440 | tf_op jit(solution)/shard_map/ppermute | solution.py:26
  96.4 7.6 %collective-permute-start.21 = (bf16[512,256]{1,0:T(8,128)(2,1)S(1)}, bf16[512,256]{1,0:T(8,128)(2,1)S(1)}, u32[]{:S(2)}, u32[]{:S(2)}) collective-permute-start(bf16[512,256]{1,0:T(8,128)(2,1)S(1)} %collective-permute-done.19), channel_id=1, source_target_pairs={{0,130},{2,128},{128,2},{130,0},{1,131},{3,129},{129,3},{131,1},{4... | collective-permute-start | bytes 786440 | tf_op jit(solution)/shard_map/ppermute | solution.py:26
  105.6 2.0 %collective-permute-start.24 = (bf16[512,512]{1,0:T(8,128)(2,1)S(1)}, bf16[512,512]{1,0:T(8,128)(2,1)S(1)}, u32[]{:S(2)}, u32[]{:S(2)}) collective-permute-start(bf16[512,512]{1,0:T(8,128)(2,1)S(1)} %get-tuple-element.69), channel_id=1, source_target_pairs={{0,1},{1,0},{2,3},{3,2},{4,5},{5,4},{6,7},{7,6},{8,9},{9,8},{10,11... | collective-permute-start | bytes 1572872 | tf_op jit(solution)/shard_map/ppermute | solution.py:26
  108.4 20.5 %collective-permute-start.25 = (bf16[156,512]{1,0:T(8,128)(2,1)S(1)}, bf16[156,512]{1,0:T(8,128)(2,1)S(1)}, u32[]{:S(2)}, u32[]{:S(2)}) collective-permute-start(bf16[156,512]{1,0:T(8,128)(2,1)S(1)} %select_n.125), channel_id=1, source_target_pairs={{16,32},{20,36},{24,40},{28,44},{32,16},{36,20},{40,24},{44,28},{4... | collective-permute-start | bytes 479240 | tf_op jit(solution)/shard_map/ppermute | solution.py:40
  116.5 12.4 %collective-permute-start.26 = (bf16[156,512]{1,0:T(8,128)(2,1)S(1)}, bf16[156,512]{1,0:T(8,128)(2,1)S(1)}, u32[]{:S(2)}, u32[]{:S(2)}) collective-permute-start(bf16[156,512]{1,0:T(8,128)(2,1)S(1)} %select_n.127), channel_id=1, source_target_pairs={{0,16},{4,20},{8,24},{12,28},{16,0},{20,4},{24,8},{28,12},{32,48},... | collective-permute-start | bytes 479240 | tf_op jit(solution)/shard_map/ppermute | solution.py:40
  129.5 14.7 %collective-permute-start.27 = (bf16[416,512]{1,0:T(8,128)(2,1)S(1)}, bf16[416,512]{1,0:T(8,128)(2,1)S(1)}, u32[]{:S(2)}, u32[]{:S(2)}) collective-permute-start(bf16[416,512]{1,0:T(8,128)(2,1)S(1)} %reshape.55), channel_id=1, source_target_pairs={{0,4},{4,0},{8,12},{12,8},{16,20},{20,16},{24,28},{28,24},{1,5},{5... | collective-permute-start | bytes 1277960 | tf_op jit(solution)/shard_map/ppermute | solution.py:26
  132.8 2.0 %collective-permute-start.28 = (bf16[96,512]{1,0:T(8,128)(2,1)S(1)}, bf16[96,512]{1,0:T(8,128)(2,1)S(1)}, u32[]{:S(2)}, u32[]{:S(2)}) collective-permute-start(bf16[96,512]{1,0:T(8,128)(2,1)S(1)} %reshape.56), channel_id=1, source_target_pairs={{4,8},{8,4},{20,24},{24,20},{36,40},{40,36},{52,56},{56,52},{68,72... | collective-permute-start | bytes 294920 | tf_op jit(solution)/shard_map/ppermute | solution.py:447
  133.5 9.1 %collective-permute-start.29 = (bf16[96,512]{1,0:T(8,128)(2,1)S(1)}, bf16[96,512]{1,0:T(8,128)(2,1)S(1)}, u32[]{:S(2)}, u32[]{:S(2)}) collective-permute-start(bf16[96,512]{1,0:T(8,128)(2,1)S(1)} %reshape.56), channel_id=1, source_target_pairs={{4,12},{8,0},{20,28},{24,16},{36,44},{40,32},{52,60},{56,48},{68,7... | collective-permute-start | bytes 294920 | tf_op jit(solution)/shard_map/ppermute | solution.py:450
  (10 other events, 40.5 us)
Sparse Core Ops, SparseCore 0:
  24.8 51.1 all-gather.2

commit v8 on v7

--- a/solution.py
+++ b/solution.py
@@ -264,44 +264,46 @@
     )(hidden, gathered)
 
 
-def project_kernel(a_ref, b_ref, c_ref, d_ref, o0, o1, o2, o3, keep_ref, send_ref, w_ref, sem):
+def project_kernel(far, a_ref, b_ref, c_ref, d_ref, o0, o1, o2, o3, out_ref, w_ref, sem):
     h, x, _, _, c = where_am_i()
-    copies = []
-    for xr, piece in enumerate((o0, o1, o2, o3)):
-        px = x ^ xr
-        slot = ((px // 2) ^ c) * 2 + px % 2
+    first = ((x // 2) ^ c) == far
+    waits = []
+    for k in range(2):
+        for pair, use in (((o0, o1), first), ((o2, o3), jnp.logical_not(first))):
+
+            @pl.when(use)
+            def _():
+                for j in range(4):
+                    block = (j % 2) * 2 + (h ^ (j // 2))
+                    pltpu.make_async_copy(
+                        pair[k].at[:, block], w_ref.at[(x ^ k) % 2, :, :, pl.ds(j * HALF, HALF)], sem
+                    ).start()
+
         for j in range(4):
-            block = (j % 2) * 2 + (h ^ (j // 2))
-            copies.append(
+            waits.append(
                 pltpu.make_async_copy(
-                    piece.at[:, block], w_ref.at[slot, :, :, pl.ds(j * HALF, HALF)], sem
+                    o0.at[:, j], w_ref.at[(x ^ k) % 2, :, :, pl.ds(j * HALF, HALF)], sem
                 )
             )
-    for copy in copies:
-        copy.start()
-    for copy in copies:
-        copy.wait()
+    for wait in waits:
+        wait.wait()
     attended = jnp.concatenate([r[...] for r in (a_ref, b_ref, c_ref, d_ref)], axis=1)
-    for b, out_ref in ((1, send_ref), (0, keep_ref)):
-        weight = w_ref[2 * b : 2 * b + 2].reshape(NARROW, 4 * HALF)
-        total = lax.dot_general(
-            attended, weight, (((1,), (1,)), ((), ())), preferred_element_type=F32
-        )
-        out_ref[...] = total.astype(out_ref.dtype)
-
-
-def partial_of(attended, os):
-    return pl.pallas_call(
-        project_kernel,
+    weight = w_ref[...].reshape(NARROW, 4 * HALF)
+    total = lax.dot_general(
+        attended, weight, (((1,), (1,)), ((), ())), preferred_element_type=F32
+    )
+    out_ref[...] = total.astype(out_ref.dtype)
+
+
+def partial_of(far, attended, os):
+    return pl.pallas_call(
+        functools.partial(project_kernel, far),
         in_specs=[VMEM] * 4 + [HBM] * 4,
-        out_specs=[VMEM] * 2,
-        out_shape=[
-            jax.ShapeDtypeStruct((512, NARROW), F32),
-            jax.ShapeDtypeStruct((512, NARROW), BF),
-        ],
-        scratch_shapes=[pltpu.VMEM((4, 8, 32, 4 * HALF), BF), pltpu.SemaphoreType.DMA],
+        out_specs=VMEM,
+        out_shape=jax.ShapeDtypeStruct((512, NARROW), BF if far else F32),
+        scratch_shapes=[pltpu.VMEM((2, 8, 32, 4 * HALF), BF), pltpu.SemaphoreType.DMA],
         compiler_params=pltpu.CompilerParams(vmem_limit_bytes=16 * 2**20),
-        cost_estimate=cost(2 * 512 * 1024 * 1024, 4 * 2**20),
+        cost_estimate=cost(512 * 1024 * 1024, 2 * 2**20),
         name="project",
     )(*attended, *os)
 
@@ -436,8 +438,9 @@
     att_near, att_across = xor_swap(att_own, ring, 1), xor_swap(att_relay, ring, 3)
     o_all = (o_block, o_near, opposite(o_near, o_side, "x", 0), o_side)
 
-    keep, send = partial_of((att_own, att_near, att_across, att_side), o_all)
-    summed = keep + xor_swap(send, "c", 1).astype(F32)
+    attended = (att_own, att_near, att_across, att_side)
+    send = partial_of(1, attended, o_all)
+    summed = partial_of(0, attended, o_all) + xor_swap(send, "c", 1).astype(F32)
     updated = tiles.astype(F32) + gate * summed.reshape(2, TOK, NARROW)
     updated = updated.astype(BF).reshape(2, S, S, NARROW)
     strip = join_tiles(updated, region, blend_weights)

time: 157 us -> 159 us (1.013)
  local copies, waits for them, and re-layouts: 9.16 us -> 10.8 us
    unnamed x27 -> x32, local copies, waits for them, and re-layouts: 7.06 us -> 8.71 us
  transfers between devices with their start and end apart: 31 -> 31, of which waited for: 18 -> 18; matrix products, arithmetic and copies ran while one was open for 0% -> 0% of each run, Pallas kernels for 9% -> 10%
where the time goes in v8:
time: 159 us; the launch traced here: 156 us
  waiting for transfers between devices  72.8 us (46%)
  starting transfers between devices  37.4 us (24%)
  Pallas kernels  18.2 us (11%)
  between operations  13.9 us (9%)
  local copies, waits for them, and re-layouts  10.8 us (7%)
  other arithmetic  2.98 us (2%)
    ppermute x26, waiting for transfers between devices, xor_swap(): return lax.ppermute(block, axis, [(i, i ^ bit) for i in range(size)])  45 us
    ppermute x26, starting transfers between devices, xor_swap(): return lax.ppermute(block, axis, [(i, i ^ bit) for i in range(size)])  26.6 us
    ppermute x2, waiting for transfers between devices, trade(): return lax.ppermute(block, REGION, route)  11.7 us
    pallas_call x2, Pallas kernels, attended_of(): pl.pallas_call(attend_kernel, in_specs=[HBM] * 2, out_specs=VMEM, out_sha...  9.58 us
    ppermute x2, starting transfers between devices, trade(): return lax.ppermute(block, REGION, route)  8.77 us
    unnamed x32, local copies, waits for them, and re-layouts  8.71 us
    all_gather x1, waiting for transfers between devices, on_device(): gathered = lax.all_gather(block, 'z', axis=0)  8.32 us
    ppermute x1, waiting for transfers between devices, on_device(): lax.ppermute(edge, REGION, [(i, i ^ 2) for i in range(64) if i % 4 in (1,...  7.81 us
  transfers between devices with their start and end apart: 31, of which 18 were waited for; matrix products, arithmetic and copies ran while one was open for 0% of the time, Pallas kernels for 10%

profile of v8, /device:TPU:24, one launch (start us, length us, event | category | flops | bytes accessed | tf_op | source)
XLA Modules:
  0.0 156.1 jit_solution(8758280144575117037)
XLA Ops:
  12.1 2.2 %collective-permute-done = bf16[5,32,256]{2,1,0:T(8,128)(2,1)S(1)} collective-permute-done((bf16[5,32,256]{2,1,0:T(8,128)(2,1)S(1)}, bf16[5,32,256]{2,1,0:T(8,128)(2,1)S(1)}, u32[]{:S(2)}, u32[]{:S(2)}) %collective-permute-start) | collective-permute-done | bytes 81952 | tf_op jit(solution)/shard_map/ppermute | solution.py:26
  14.3 3.1 %collective-permute-start.3 = (bf16[6,32,256]{2,1,0:T(8,128)(2,1)S(1)}, bf16[6,32,256]{2,1,0:T(8,128)(2,1)S(1)}, u32[]{:S(2)}, u32[]{:S(2)}) collective-permute-start(bf16[6,32,256]{2,1,0:T(8,128)(2,1)S(1)} %pad_maximum_fusion.8), channel_id=1, source_target_pairs={{0,64},{32,96},{64,0},{96,32},{1,65},{33,97},{65,1},{97,33},{2,66}... | collective-permute-start | bytes 294920 | tf_op jit(solution)/shard_map/ppermute | solution.py:26
  19.3 3.2 %collective-permute-done.6 = bf16[2,32,256]{2,1,0:T(8,128)(2,1)S(1)} collective-permute-done((bf16[2,32,256]{2,1,0:T(8,128)(2,1)S(1)}, bf16[2,32,256]{2,1,0:T(8,128)(2,1)S(1)}, u32[]{:S(2)}, u32[]{:S(2)}) %collective-permute-start.6) | collective-permute-done | bytes 32800 | tf_op jit(solution)/shard_map/ppermute | solution.py:26
  22.5 1.4 collective-permute-done.5
  24.7 2.0 %collective-permute-start.1 = (bf16[2,256,512]{2,1,0:T(8,128)(2,1)S(1)}, bf16[2,256,512]{2,1,0:T(8,128)(2,1)S(1)}, u32[]{:S(2)}, u32[]{:S(2)}) collective-permute-start(bf16[2,256,512]{2,1,0:T(8,128)(2,1)S(1)} %get-tuple-element.42), channel_id=1, source_target_pairs={{0,4},{4,0},{8,12},{12,8},{16,20},{20,16},{24,28},{28,24},{1,5},{5... | collective-permute-start | bytes 1572872 | tf_op jit(solution)/shard_map/ppermute | solution.py:26
  26.8 10.1 %collective-permute-done.2.other_mod = bf16[1,3,2048]{2,1,0:T(4,128)(2,1)S(1)} collective-permute-done((bf16[1,3,2048]{2,1,0:T(4,128)(2,1)S(1)}, bf16[1,3,2048]{2,1,0:T(4,128)(2,1)S(1)}, u32[]{:S(2)}, u32[]{:S(2)}) %collective-permute-start.2) | collective-permute-done | bytes 12320 | tf_op jit(solution)/shard_map/ppermute | solution.py:26
  39.4 9.0 %collective-permute-done.11.c_ref = bf16[512,512]{1,0:T(8,128)(2,1)S(1)} collective-permute-done((bf16[512,512]{1,0:T(8,128)(2,1)S(1)}, bf16[512,512]{1,0:T(8,128)(2,1)S(1)}, u32[]{:S(2)}, u32[]{:S(2)}) %collective-permute-start.11) | collective-permute-done | bytes 524320 | tf_op jit(solution)/shard_map/ppermute | solution.py:26
  48.5 1.7 %collective-permute-done.9.c_ref = bf16[512,512]{1,0:T(8,128)(2,1)S(1)} collective-permute-done((bf16[512,512]{1,0:T(8,128)(2,1)S(1)}, bf16[512,512]{1,0:T(8,128)(2,1)S(1)}, u32[]{:S(2)}, u32[]{:S(2)}) %collective-permute-start.9) | collective-permute-done | bytes 524320 | tf_op jit(solution)/shard_map/ppermute | solution.py:26
  50.3 1.6 %collective-permute-start.12 = (bf16[256,512]{1,0:T(8,128)(2,1)S(1)}, bf16[256,512]{1,0:T(8,128)(2,1)S(1)}, u32[]{:S(2)}, u32[]{:S(2)}) collective-permute-start(bf16[256,512]{1,0:T(8,128)(2,1)S(1)} %slice.118), channel_id=1, source_target_pairs={{0,130},{2,128},{128,2},{130,0},{1,131},{3,129},{129,3},{131,1},{4... | collective-permute-start | bytes 786440 | tf_op jit(solution)/shard_map/ppermute | solution.py:26
  51.9 2.5 %collective-permute-start.15 = (bf16[2,3,2048]{2,1,0:T(4,128)(2,1)S(1)}, bf16[2,3,2048]{2,1,0:T(4,128)(2,1)S(1)}, u32[]{:S(2)}, u32[]{:S(2)}) collective-permute-start(bf16[2,3,2048]{2,1,0:T(4,128)(2,1)S(1)} %get-tuple-element.53.mod_ref), channel_id=1, source_target_pairs={{0,128},{128,0},{1,129},{129,1},{2,130},{130,2},{3,131},{131,3},{4... | collective-permute-start | bytes 73736 | tf_op jit(solution)/shard_map/ppermute | solution.py:26
  54.4 3.2 %collective-permute-done.10 = bf16[256,512]{1,0:T(8,128)(2,1)S(1)} collective-permute-done((bf16[256,512]{1,0:T(8,128)(2,1)S(1)}, bf16[256,512]{1,0:T(8,128)(2,1)S(1)}, u32[]{:S(2)}, u32[]{:S(2)}) %collective-permute-start.10) | collective-permute-done | bytes 262176 | tf_op jit(solution)/shard_map/ppermute | solution.py:26
  57.6 2.1 %collective-permute-done.12 = bf16[256,512]{1,0:T(8,128)(2,1)S(1)} collective-permute-done((bf16[256,512]{1,0:T(8,128)(2,1)S(1)}, bf16[256,512]{1,0:T(8,128)(2,1)S(1)}, u32[]{:S(2)}, u32[]{:S(2)}) %collective-permute-start.12) | collective-permute-done | bytes 262176 | tf_op jit(solution)/shard_map/ppermute | solution.py:26
  59.8 1.6 %hidden.2.hid_hbm = bf16[512,2048]{1,0:T(8,128)(2,1)S(1)} custom-call(bf16[512,512]{1,0:T(8,128)(2,1)S(1)} %bitcast.17, bf16[512,512]{1,0:T(8,128)(2,1)S(1)} %collective-permute-done.13.b_ref, bf16[512,512]{1,0:T(8,128)(2,1)S(1)} %collective-permute-done.11.c_ref, bf16[512,512]{1,0:T(8,128)(2,1)S(1)} %collective-permute-done.14.d_ref, ...), custom_call_target="tpu_custom_call" | custom-call | flops 8388608 | bytes 4194304 | tf_op jit(solution)/shard_map/hidden/pallas_call | solution.py:182
  62.8 1.9 %collective-permute-done.16.b_ref = bf16[512,512]{1,0:T(8,128)(2,1)S(1)} collective-permute-done((bf16[512,512]{1,0:T(8,128)(2,1)S(1)}, bf16[512,512]{1,0:T(8,128)(2,1)S(1)}, u32[]{:S(2)}, u32[]{:S(2)}) %collective-permute-start.16) | collective-permute-done | bytes 524320 | tf_op jit(solution)/shard_map/ppermute | solution.py:26
  64.7 1.6 %hidden.3.hid_hbm = bf16[512,2048]{1,0:T(8,128)(2,1)S(1)} custom-call(bf16[512,512]{1,0:T(8,128)(2,1)S(1)} %pad_maximum_fusion.3.a_ref, bf16[512,512]{1,0:T(8,128)(2,1)S(1)} %collective-permute-done.16.b_ref, bf16[512,512]{1,0:T(8,128)(2,1)S(1)} %collective-permute-done.9.c_ref, bf16[512,512]{1,0:T(8,128)(2,1)S(1)} %collective-permute-done.17.d_ref, ...), custom_call_target="tpu_custom_call" | custom-call | flops 8388608 | bytes 4194304 | tf_op jit(solution)/shard_map/hidden/pallas_call | solution.py:182
  66.3 1.4 copy-done.1
  67.7 8.3 %all-gather.3.cloned.1.call-done = bf16[224,32,256]{2,1,0:T(8,128)(2,1)} async-done(((bf16[28,32,256]{2,1,0:T(8,128)(2,1)}), bf16[224,32,256]{2,1,0:T(8,128)(2,1)}) %all-gather.3.cloned.1.call-update) | async-done | bytes 3670032 | tf_op jit(solution)/shard_map/all_gather | solution.py:416
  77.1 1.6 collective-permute-start.7
  78.7 2.1 %collective-permute-start.8 = (bf16[8,4,32,256]{3,2,1,0:T(8,128)(2,1)S(1)}, bf16[8,4,32,256]{3,2,1,0:T(8,128)(2,1)S(1)}, u32[]{:S(2)}, u32[]{:S(2)}) collective-permute-start(bf16[8,4,32,256]{3,2,1,0:T(8,128)(2,1)S(1)} %slice.116.o0), channel_id=1, source_target_pairs={{0,96},{32,64},{64,32},{96,0},{1,97},{33,65},{65,33},{97,1},{2,98}... | collective-permute-start | bytes 1572872 | tf_op jit(solution)/shard_map/ppermute | solution.py:26
  80.7 4.8 %attend.2 = bf16[512,256]{1,0:T(8,128)(2,1)} custom-call(bf16[512,2048]{1,0:T(8,128)(2,1)} %copy-done.1, bf16[8,28,32,256]{3,2,1,0:T(8,128)(2,1)} %bitcast.30), custom_call_target="tpu_custom_call" | custom-call | flops 3489660928 | bytes 6291456 | tf_op jit(solution)/shard_map/attend/pallas_call | solution.py:248
  87.0 4.8 %attend.3.a_ref = bf16[512,256]{1,0:T(8,128)(2,1)} custom-call(bf16[512,2048]{1,0:T(8,128)(2,1)} %copy-done, bf16[8,28,32,256]{3,2,1,0:T(8,128)(2,1)} %bitcast.31), custom_call_target="tpu_custom_call" | custom-call | flops 3489660928 | bytes 6291456 | tf_op jit(solution)/shard_map/attend/pallas_call | solution.py:248
  91.8 2.7 %collective-permute-done.18.d_ref = bf16[512,256]{1,0:T(8,128)(2,1)S(1)} collective-permute-done((bf16[512,256]{1,0:T(8,128)(2,1)}, bf16[512,256]{1,0:T(8,128)(2,1)S(1)}, u32[]{:S(2)}, u32[]{:S(2)}) %collective-permute-start.18) | collective-permute-done | bytes 262176 | tf_op jit(solution)/shard_map/ppermute | solution.py:26
  96.4 1.9 %collective-permute-start.21 = (bf16[512,256]{1,0:T(8,128)(2,1)S(1)}, bf16[512,256]{1,0:T(8,128)(2,1)S(1)}, u32[]{:S(2)}, u32[]{:S(2)}) collective-permute-start(bf16[512,256]{1,0:T(8,128)(2,1)S(1)} %collective-permute-done.19), channel_id=1, source_target_pairs={{0,130},{2,128},{128,2},{130,0},{1,131},{3,129},{129,3},{131,1},{4... | collective-permute-start | bytes 786440 | tf_op jit(solution)/shard_map/ppermute | solution.py:26
  98.3 2.9 %collective-permute-done.22 = bf16[4,4,32,256]{3,2,1,0:T(8,128)(2,1)S(1)} collective-permute-done((bf16[4,4,32,256]{3,2,1,0:T(8,128)(2,1)S(1)}, bf16[4,4,32,256]{3,2,1,0:T(8,128)(2,1)S(1)}, u32[]{:S(2)}, u32[]{:S(2)}) %collective-permute-start.22) | collective-permute-done | bytes 262176 | tf_op jit(solution)/shard_map/ppermute | solution.py:26
  101.3 1.7 %collective-permute-done.23 = bf16[4,4,32,256]{3,2,1,0:T(8,128)(2,1)S(1)} collective-permute-done((bf16[4,4,32,256]{3,2,1,0:T(8,128)(2,1)S(1)}, bf16[4,4,32,256]{3,2,1,0:T(8,128)(2,1)S(1)}, u32[]{:S(2)}, u32[]{:S(2)}) %collective-permute-start.23) | collective-permute-done | bytes 262176 | tf_op jit(solution)/shard_map/ppermute | solution.py:26
  104.0 1.7 %project.3 = bf16[512,512]{1,0:T(8,128)(2,1)} custom-call(bf16[512,256]{1,0:T(8,128)(2,1)S(1)} %copy-done.2, bf16[512,256]{1,0:T(8,128)(2,1)S(1)} %collective-permute-done.20.b_ref, bf16[512,256]{1,0:T(8,128)(2,1)S(1)} %collective-permute-done.21.c_ref, bf16[512,256]{1,0:T(8,128)(2,1)S(1)} %collective-permute-done.18.d_ref, ...), custom_call_target="tpu_custom_call" | custom-call | flops 536870912 | bytes 2097152 | tf_op jit(solution)/shard_map/project/pallas_call | solution.py:299
  110.5 8.0 %collective-permute-start.25 = (bf16[156,512]{1,0:T(8,128)(2,1)S(1)}, bf16[156,512]{1,0:T(8,128)(2,1)S(1)}, u32[]{:S(2)}, u32[]{:S(2)}) collective-permute-start(bf16[156,512]{1,0:T(8,128)(2,1)S(1)} %select_n.125), channel_id=1, source_target_pairs={{16,32},{20,36},{24,40},{28,44},{32,16},{36,20},{40,24},{44,28},{4... | collective-permute-start | bytes 479240 | tf_op jit(solution)/shard_map/ppermute | solution.py:40
  119.3 11.7 %collective-permute-done.25 = bf16[156,512]{1,0:T(8,128)(2,1)S(1)} collective-permute-done((bf16[156,512]{1,0:T(8,128)(2,1)S(1)}, bf16[156,512]{1,0:T(8,128)(2,1)S(1)}, u32[]{:S(2)}, u32[]{:S(2)}) %collective-permute-start.25) | collective-permute-done | bytes 159776 | tf_op jit(solution)/shard_map/ppermute | solution.py:40
  131.6 3.3 %collective-permute-start.27 = (bf16[416,512]{1,0:T(8,128)(2,1)S(1)}, bf16[416,512]{1,0:T(8,128)(2,1)S(1)}, u32[]{:S(2)}, u32[]{:S(2)}) collective-permute-start(bf16[416,512]{1,0:T(8,128)(2,1)S(1)} %reshape.55), channel_id=1, source_target_pairs={{0,4},{4,0},{8,12},{12,8},{16,20},{20,16},{24,28},{28,24},{1,5},{5... | collective-permute-start | bytes 1277960 | tf_op jit(solution)/shard_map/ppermute | solution.py:26
  136.9 7.8 %collective-permute-done.29 = bf16[96,512]{1,0:T(8,128)(2,1)S(1)} collective-permute-done((bf16[96,512]{1,0:T(8,128)(2,1)S(1)}, bf16[96,512]{1,0:T(8,128)(2,1)S(1)}, u32[]{:S(2)}, u32[]{:S(2)}) %collective-permute-start.29) | collective-permute-done | bytes 98336 | tf_op jit(solution)/shard_map/ppermute | solution.py:453
  144.7 1.5 collective-permute-done.27
  147.7 1.5 place.1
  (115 shorter events, 27.5 us)
Async XLA Ops:
  6.5 30.4 %copy-start.10 = (s32[64]{0:T(128)S(1)}, s32[64]{0:T(128)}, u32[]{:S(2)}) copy-start(s32[64]{0:T(128)} %counts_ref.5) | copy-start | bytes 772
  6.5 69.5 %all-gather.3.cloned.1.call-start = ((), (), s32[]{:S(2)}) async-start(), calls=%async_computation | async-start | bytes 4128768 | tf_op jit(solution)/shard_map/all_gather | solution.py:416
  8.2 6.0 %collective-permute-start = (bf16[5,32,256]{2,1,0:T(8,128)(2,1)S(1)}, bf16[5,32,256]{2,1,0:T(8,128)(2,1)S(1)}, u32[]{:S(2)}, u32[]{:S(2)}) collective-permute-start(bf16[5,32,256]{2,1,0:T(8,128)(2,1)S(1)} %get-tuple-element.38), channel_id=1, source_target_pairs={{0,128},{128,0},{1,129},{129,1},{2,130},{130,2},{3,131},{131,3},{4... | collective-permute-start | bytes 245768 | tf_op jit(solution)/shard_map/ppermute | solution.py:26
  14.3 8.2 %collective-permute-start.3 = (bf16[6,32,256]{2,1,0:T(8,128)(2,1)S(1)}, bf16[6,32,256]{2,1,0:T(8,128)(2,1)S(1)}, u32[]{:S(2)}, u32[]{:S(2)}) collective-permute-start(bf16[6,32,256]{2,1,0:T(8,128)(2,1)S(1)} %pad_maximum_fusion.8), channel_id=1, source_target_pairs={{0,64},{32,96},{64,0},{96,32},{1,65},{33,97},{65,1},{97,33},{2,66}... | collective-permute-start | bytes 294920 | tf_op jit(solution)/shard_map/ppermute | solution.py:26
  17.4 5.1 %collective-permute-start.4 = (bf16[6,32,256]{2,1,0:T(8,128)(2,1)S(1)}, bf16[6,32,256]{2,1,0:T(8,128)(2,1)S(1)}, u32[]{:S(2)}, u32[]{:S(2)}) collective-permute-start(bf16[6,32,256]{2,1,0:T(8,128)(2,1)S(1)} %pad_maximum_fusion.8), channel_id=1, source_target_pairs={{0,32},{32,0},{64,96},{96,64},{1,33},{33,1},{65,97},{97,65},{2,34}... | collective-permute-start | bytes 294920 | tf_op jit(solution)/shard_map/ppermute | solution.py:26
  18.0 5.8 %collective-permute-start.5 = (bf16[6,32,256]{2,1,0:T(8,128)(2,1)S(1)}, bf16[6,32,256]{2,1,0:T(8,128)(2,1)S(1)}, u32[]{:S(2)}, u32[]{:S(2)}) collective-permute-start(bf16[6,32,256]{2,1,0:T(8,128)(2,1)S(1)} %pad_maximum_fusion.8), channel_id=1, source_target_pairs={{0,96},{32,64},{64,32},{96,0},{1,97},{33,65},{65,33},{97,1},{2,98}... | collective-permute-start | bytes 294920 | tf_op jit(solution)/shard_map/ppermute | solution.py:26
  18.5 3.9 %collective-permute-start.6 = (bf16[2,32,256]{2,1,0:T(8,128)(2,1)S(1)}, bf16[2,32,256]{2,1,0:T(8,128)(2,1)S(1)}, u32[]{:S(2)}, u32[]{:S(2)}) collective-permute-start(bf16[2,32,256]{2,1,0:T(8,128)(2,1)S(1)} %broadcast_select_fusion.4), channel_id=1, source_target_pairs={{0,2},{2,0},{1,3},{3,1},{4,6},{6,4},{5,7},{7,5},{8,10},{10,8},{9,1... | collective-permute-start | bytes 98312 | tf_op jit(solution)/shard_map/ppermute | solution.py:26
  24.7 12.2 %collective-permute-start.1 = (bf16[2,256,512]{2,1,0:T(8,128)(2,1)S(1)}, bf16[2,256,512]{2,1,0:T(8,128)(2,1)S(1)}, u32[]{:S(2)}, u32[]{:S(2)}) collective-permute-start(bf16[2,256,512]{2,1,0:T(8,128)(2,1)S(1)} %get-tuple-element.42), channel_id=1, source_target_pairs={{0,4},{4,0},{8,12},{12,8},{16,20},{20,16},{24,28},{28,24},{1,5},{5... | collective-permute-start | bytes 1572872 | tf_op jit(solution)/shard_map/ppermute | solution.py:26
  26.7 10.2 %collective-permute-start.2 = (bf16[1,3,2048]{2,1,0:T(4,128)(2,1)S(1)}, bf16[1,3,2048]{2,1,0:T(4,128)(2,1)S(1)}, u32[]{:S(2)}, u32[]{:S(2)}) collective-permute-start(bf16[1,3,2048]{2,1,0:T(4,128)(2,1)S(1)} %copy-done.8), channel_id=1, source_target_pairs={{0,4},{4,0},{8,12},{12,8},{16,20},{20,16},{24,28},{28,24},{1,5},{5... | collective-permute-start | bytes 36872 | tf_op jit(solution)/shard_map/ppermute | solution.py:26
  37.5 10.9 %collective-permute-start.11 = (bf16[512,512]{1,0:T(8,128)(2,1)S(1)}, bf16[512,512]{1,0:T(8,128)(2,1)S(1)}, u32[]{:S(2)}, u32[]{:S(2)}) collective-permute-start(bf16[512,512]{1,0:T(8,128)(2,1)S(1)} %bitcast.14), channel_id=1, source_target_pairs={{0,2},{2,0},{128,130},{130,128},{1,3},{3,1},{129,131},{131,129},{4... | collective-permute-start | bytes 1572872 | tf_op jit(solution)/shard_map/ppermute | solution.py:26
  38.4 11.8 %collective-permute-start.9 = (bf16[512,512]{1,0:T(8,128)(2,1)S(1)}, bf16[512,512]{1,0:T(8,128)(2,1)S(1)}, u32[]{:S(2)}, u32[]{:S(2)}) collective-permute-start(bf16[512,512]{1,0:T(8,128)(2,1)S(1)} %bitcast.15), channel_id=1, source_target_pairs={{0,130},{2,128},{128,2},{130,0},{1,131},{3,129},{129,3},{131,1},{4... | collective-permute-start | bytes 1572872 | tf_op jit(solution)/shard_map/ppermute | solution.py:26
  39.4 20.4 %collective-permute-start.13 = (bf16[512,512]{1,0:T(8,128)(2,1)S(1)}, bf16[512,512]{1,0:T(8,128)(2,1)S(1)}, u32[]{:S(2)}, u32[]{:S(2)}) collective-permute-start(bf16[512,512]{1,0:T(8,128)(2,1)S(1)} %bitcast.16), channel_id=1, source_target_pairs={{0,1},{1,0},{2,3},{3,2},{4,5},{5,4},{6,7},{7,6},{8,9},{9,8},{10,11... | collective-permute-start | bytes 1572872 | tf_op jit(solution)/shard_map/ppermute | solution.py:26
  48.5 11.4 %collective-permute-start.14 = (bf16[512,512]{1,0:T(8,128)(2,1)S(1)}, bf16[512,512]{1,0:T(8,128)(2,1)S(1)}, u32[]{:S(2)}, u32[]{:S(2)}) collective-permute-start(bf16[512,512]{1,0:T(8,128)(2,1)S(1)} %collective-permute-done.11.c_ref), channel_id=1, source_target_pairs={{0,1},{1,0},{2,3},{3,2},{4,5},{5,4},{6,7},{7,6},{8,9},{9,8},{10,11... | collective-permute-start | bytes 1572872 | tf_op jit(solution)/shard_map/ppermute | solution.py:26
  50.1 7.5 %collective-permute-start.10 = (bf16[256,512]{1,0:T(8,128)(2,1)S(1)}, bf16[256,512]{1,0:T(8,128)(2,1)S(1)}, u32[]{:S(2)}, u32[]{:S(2)}) collective-permute-start(bf16[256,512]{1,0:T(8,128)(2,1)S(1)} %slice.117), channel_id=1, source_target_pairs={{0,2},{2,0},{128,130},{130,128},{1,3},{3,1},{129,131},{131,129},{4... | collective-permute-start | bytes 786440 | tf_op jit(solution)/shard_map/ppermute | solution.py:26
  50.3 9.4 %collective-permute-start.12 = (bf16[256,512]{1,0:T(8,128)(2,1)S(1)}, bf16[256,512]{1,0:T(8,128)(2,1)S(1)}, u32[]{:S(2)}, u32[]{:S(2)}) collective-permute-start(bf16[256,512]{1,0:T(8,128)(2,1)S(1)} %slice.118), channel_id=1, source_target_pairs={{0,130},{2,128},{128,2},{130,0},{1,131},{3,129},{129,3},{131,1},{4... | collective-permute-start | bytes 786440 | tf_op jit(solution)/shard_map/ppermute | solution.py:26
  51.9 10.9 %collective-permute-start.15 = (bf16[2,3,2048]{2,1,0:T(4,128)(2,1)S(1)}, bf16[2,3,2048]{2,1,0:T(4,128)(2,1)S(1)}, u32[]{:S(2)}, u32[]{:S(2)}) collective-permute-start(bf16[2,3,2048]{2,1,0:T(4,128)(2,1)S(1)} %get-tuple-element.53.mod_ref), channel_id=1, source_target_pairs={{0,128},{128,0},{1,129},{129,1},{2,130},{130,2},{3,131},{131,3},{4... | collective-permute-start | bytes 73736 | tf_op jit(solution)/shard_map/ppermute | solution.py:26
  57.6 5.2 %collective-permute-start.17 = (bf16[512,512]{1,0:T(8,128)(2,1)S(1)}, bf16[512,512]{1,0:T(8,128)(2,1)S(1)}, u32[]{:S(2)}, u32[]{:S(2)}) collective-permute-start(bf16[512,512]{1,0:T(8,128)(2,1)S(1)} %collective-permute-done.9.c_ref), channel_id=1, source_target_pairs={{0,1},{1,0},{2,3},{3,2},{4,5},{5,4},{6,7},{7,6},{8,9},{9,8},{10,11... | collective-permute-start | bytes 1572872 | tf_op jit(solution)/shard_map/ppermute | solution.py:26
  62.8 1.9 %collective-permute-start.16 = (bf16[512,512]{1,0:T(8,128)(2,1)S(1)}, bf16[512,512]{1,0:T(8,128)(2,1)S(1)}, u32[]{:S(2)}, u32[]{:S(2)}) collective-permute-start(bf16[512,512]{1,0:T(8,128)(2,1)S(1)} %pad_maximum_fusion.3.a_ref), channel_id=1, source_target_pairs={{0,1},{1,0},{2,3},{3,2},{4,5},{5,4},{6,7},{7,6},{8,9},{9,8},{10,11... | collective-permute-start | bytes 1572872 | tf_op jit(solution)/shard_map/ppermute | solution.py:26
  77.1 17.4 %collective-permute-start.7 = (bf16[8,4,32,256]{3,2,1,0:T(8,128)(2,1)S(1)}, bf16[8,4,32,256]{3,2,1,0:T(8,128)(2,1)S(1)}, u32[]{:S(2)}, u32[]{:S(2)}) collective-permute-start(bf16[8,4,32,256]{3,2,1,0:T(8,128)(2,1)S(1)} %slice.116.o0), channel_id=1, source_target_pairs={{0,32},{32,0},{64,96},{96,64},{1,33},{33,1},{65,97},{97,65},{2,34}... | collective-permute-start | bytes 1572872 | tf_op jit(solution)/shard_map/ppermute | solution.py:26
  78.7 15.9 %collective-permute-start.8 = (bf16[8,4,32,256]{3,2,1,0:T(8,128)(2,1)S(1)}, bf16[8,4,32,256]{3,2,1,0:T(8,128)(2,1)S(1)}, u32[]{:S(2)}, u32[]{:S(2)}) collective-permute-start(bf16[8,4,32,256]{3,2,1,0:T(8,128)(2,1)S(1)} %slice.116.o0), channel_id=1, source_target_pairs={{0,96},{32,64},{64,32},{96,0},{1,97},{33,65},{65,33},{97,1},{2,98}... | collective-permute-start | bytes 1572872 | tf_op jit(solution)/shard_map/ppermute | solution.py:26
  85.5 9.0 %collective-permute-start.18 = (bf16[512,256]{1,0:T(8,128)(2,1)}, bf16[512,256]{1,0:T(8,128)(2,1)S(1)}, u32[]{:S(2)}, u32[]{:S(2)}) collective-permute-start(bf16[512,256]{1,0:T(8,128)(2,1)} %attend.2), channel_id=1, source_target_pairs={{0,130},{2,128},{128,2},{130,0},{1,131},{3,129},{129,3},{131,1},{4... | collective-permute-start | bytes 786440 | tf_op jit(solution)/shard_map/ppermute | solution.py:26
  86.1 8.4 %collective-permute-start.19 = (bf16[512,256]{1,0:T(8,128)(2,1)}, bf16[512,256]{1,0:T(8,128)(2,1)S(1)}, u32[]{:S(2)}, u32[]{:S(2)}) collective-permute-start(bf16[512,256]{1,0:T(8,128)(2,1)} %attend.2), channel_id=1, source_target_pairs={{0,2},{2,0},{128,130},{130,128},{1,3},{3,1},{129,131},{131,129},{4... | collective-permute-start | bytes 786440 | tf_op jit(solution)/shard_map/ppermute | solution.py:26
  94.6 6.7 %collective-permute-start.22 = (bf16[4,4,32,256]{3,2,1,0:T(8,128)(2,1)S(1)}, bf16[4,4,32,256]{3,2,1,0:T(8,128)(2,1)S(1)}, u32[]{:S(2)}, u32[]{:S(2)}) collective-permute-start(bf16[4,4,32,256]{3,2,1,0:T(8,128)(2,1)S(1)} %slice.95), channel_id=1, source_target_pairs={{0,32},{32,0},{64,96},{96,64},{1,33},{33,1},{65,97},{97,65},{2,34}... | collective-permute-start | bytes 786440 | tf_op jit(solution)/shard_map/ppermute | solution.py:26
  95.3 7.7 %collective-permute-start.23 = (bf16[4,4,32,256]{3,2,1,0:T(8,128)(2,1)S(1)}, bf16[4,4,32,256]{3,2,1,0:T(8,128)(2,1)S(1)}, u32[]{:S(2)}, u32[]{:S(2)}) collective-permute-start(bf16[4,4,32,256]{3,2,1,0:T(8,128)(2,1)S(1)} %slice.96), channel_id=1, source_target_pairs={{0,96},{32,64},{64,32},{96,0},{1,97},{33,65},{65,33},{97,1},{2,98}... | collective-permute-start | bytes 786440 | tf_op jit(solution)/shard_map/ppermute | solution.py:26
  96.2 6.7 %collective-permute-start.20 = (bf16[512,256]{1,0:T(8,128)(2,1)}, bf16[512,256]{1,0:T(8,128)(2,1)S(1)}, u32[]{:S(2)}, u32[]{:S(2)}) collective-permute-start(bf16[512,256]{1,0:T(8,128)(2,1)} %attend.3.a_ref), channel_id=1, source_target_pairs={{0,2},{2,0},{128,130},{130,128},{1,3},{3,1},{129,131},{131,129},{4... | collective-permute-start | bytes 786440 | tf_op jit(solution)/shard_map/ppermute | solution.py:26
  96.4 7.6 %collective-permute-start.21 = (bf16[512,256]{1,0:T(8,128)(2,1)S(1)}, bf16[512,256]{1,0:T(8,128)(2,1)S(1)}, u32[]{:S(2)}, u32[]{:S(2)}) collective-permute-start(bf16[512,256]{1,0:T(8,128)(2,1)S(1)} %collective-permute-done.19), channel_id=1, source_target_pairs={{0,130},{2,128},{128,2},{130,0},{1,131},{3,129},{129,3},{131,1},{4... | collective-permute-start | bytes 786440 | tf_op jit(solution)/shard_map/ppermute | solution.py:26
  106.4 2.3 %collective-permute-start.24 = (bf16[512,512]{1,0:T(8,128)(2,1)}, bf16[512,512]{1,0:T(8,128)(2,1)}, u32[]{:S(2)}, u32[]{:S(2)}) collective-permute-start(bf16[512,512]{1,0:T(8,128)(2,1)} %project.3), channel_id=1, source_target_pairs={{0,1},{1,0},{2,3},{3,2},{4,5},{5,4},{6,7},{7,6},{8,9},{9,8},{10,11... | collective-permute-start | bytes 1572872 | tf_op jit(solution)/shard_map/ppermute | solution.py:26
  110.5 20.5 %collective-permute-start.25 = (bf16[156,512]{1,0:T(8,128)(2,1)S(1)}, bf16[156,512]{1,0:T(8,128)(2,1)S(1)}, u32[]{:S(2)}, u32[]{:S(2)}) collective-permute-start(bf16[156,512]{1,0:T(8,128)(2,1)S(1)} %select_n.125), channel_id=1, source_target_pairs={{16,32},{20,36},{24,40},{28,44},{32,16},{36,20},{40,24},{44,28},{4... | collective-permute-start | bytes 479240 | tf_op jit(solution)/shard_map/ppermute | solution.py:40
  118.5 12.4 %collective-permute-start.26 = (bf16[156,512]{1,0:T(8,128)(2,1)S(1)}, bf16[156,512]{1,0:T(8,128)(2,1)S(1)}, u32[]{:S(2)}, u32[]{:S(2)}) collective-permute-start(bf16[156,512]{1,0:T(8,128)(2,1)S(1)} %select_n.127), channel_id=1, source_target_pairs={{0,16},{4,20},{8,24},{12,28},{16,0},{20,4},{24,8},{28,12},{32,48},... | collective-permute-start | bytes 479240 | tf_op jit(solution)/shard_map/ppermute | solution.py:40
  131.6 14.7 %collective-permute-start.27 = (bf16[416,512]{1,0:T(8,128)(2,1)S(1)}, bf16[416,512]{1,0:T(8,128)(2,1)S(1)}, u32[]{:S(2)}, u32[]{:S(2)}) collective-permute-start(bf16[416,512]{1,0:T(8,128)(2,1)S(1)} %reshape.55), channel_id=1, source_target_pairs={{0,4},{4,0},{8,12},{12,8},{16,20},{20,16},{24,28},{28,24},{1,5},{5... | collective-permute-start | bytes 1277960 | tf_op jit(solution)/shard_map/ppermute | solution.py:26
  134.9 2.0 %collective-permute-start.28 = (bf16[96,512]{1,0:T(8,128)(2,1)S(1)}, bf16[96,512]{1,0:T(8,128)(2,1)S(1)}, u32[]{:S(2)}, u32[]{:S(2)}) collective-permute-start(bf16[96,512]{1,0:T(8,128)(2,1)S(1)} %reshape.56), channel_id=1, source_target_pairs={{4,8},{8,4},{20,24},{24,20},{36,40},{40,36},{52,56},{56,52},{68,72... | collective-permute-start | bytes 294920 | tf_op jit(solution)/shard_map/ppermute | solution.py:450
  135.6 9.1 %collective-permute-start.29 = (bf16[96,512]{1,0:T(8,128)(2,1)S(1)}, bf16[96,512]{1,0:T(8,128)(2,1)S(1)}, u32[]{:S(2)}, u32[]{:S(2)}) collective-permute-start(bf16[96,512]{1,0:T(8,128)(2,1)S(1)} %reshape.56), channel_id=1, source_target_pairs={{4,12},{8,0},{20,28},{24,16},{36,44},{40,32},{52,60},{56,48},{68,7... | collective-permute-start | bytes 294920 | tf_op jit(solution)/shard_map/ppermute | solution.py:453
  (12 other events, 44.5 us)
Sparse Core Ops, SparseCore 0:
  24.8 51.1 all-gather.2

commit v9 on v7

--- a/solution.py
+++ b/solution.py
@@ -430,8 +430,8 @@
     o_near, o_side = xor_swap(o_block, "x", 1), xor_swap(o_block, "x", 3)
     att_side, att_relay = xor_swap(att_sent, ring, 3), xor_swap(att_sent, ring, 1)
     att_own = attended_of(hid_own, gathered)
-    o_near, o_side, att_side, att_relay, att_own = lax.optimization_barrier(
-        (o_near, o_side, att_side, att_relay, att_own)
+    o_near, o_side, att_relay, att_side, att_own = lax.optimization_barrier(
+        (o_near, o_side, att_relay, att_side, att_own)
     )
     att_near, att_across = xor_swap(att_own, ring, 1), xor_swap(att_relay, ring, 3)
     o_all = (o_block, o_near, opposite(o_near, o_side, "x", 0), o_side)

time: 157 us -> 157 us (level)
  the two profiles are of different devices: /device:TPU:24 before, /device:TPU:6 now
where the time goes in v9:
time: 157 us
  waiting for transfers between devices  73.8 us (47%)
  starting transfers between devices  40.6 us (26%)
  Pallas kernels  17.2 us (11%)
  between operations  14 us (9%)
  local copies, waits for them, and re-layouts  9.16 us (6%)
  other arithmetic  2.01 us (1%)
    ppermute x26, waiting for transfers between devices, xor_swap(): return lax.ppermute(block, axis, [(i, i ^ bit) for i in range(size)])  41.6 us
    ppermute x26, starting transfers between devices, xor_swap(): return lax.ppermute(block, axis, [(i, i ^ bit) for i in range(size)])  28.6 us
    ppermute x2, waiting for transfers between devices, trade(): return lax.ppermute(block, REGION, route)  13.3 us
    all_gather x1, waiting for transfers between devices, on_device(): gathered = lax.all_gather(block, 'z', axis=0)  10.2 us
    ppermute x2, starting transfers between devices, trade(): return lax.ppermute(block, REGION, route)  10 us
    pallas_call x2, Pallas kernels, attended_of(): pl.pallas_call(attend_kernel, in_specs=[HBM] * 2, out_specs=VMEM, out_sha...  9.58 us
    ppermute x1, waiting for transfers between devices, on_device(): lax.ppermute(edge, REGION, [(i, i ^ 2) for i in range(64) if i % 4 in (1,...  8.77 us
    unnamed x27, local copies, waits for them, and re-layouts  7.06 us
  transfers between devices with their start and end apart: 31, of which 20 were waited for; matrix products, arithmetic and copies ran while one was open for 0% of the time, Pallas kernels for 9%

profile of v9, /device:TPU:6, one launch (start us, length us, event | category | flops | bytes accessed | tf_op | source)
XLA Modules:
  0.0 156.8 jit_solution(3725092308381166792)
XLA Ops:
  8.2 3.3 %collective-permute-start = (bf16[5,32,256]{2,1,0:T(8,128)(2,1)S(1)}, bf16[5,32,256]{2,1,0:T(8,128)(2,1)S(1)}, u32[]{:S(2)}, u32[]{:S(2)}) collective-permute-start(bf16[5,32,256]{2,1,0:T(8,128)(2,1)S(1)} %get-tuple-element.40), channel_id=1, source_target_pairs={{0,128},{128,0},{1,129},{129,1},{2,130},{130,2},{3,131},{131,3},{4... | collective-permute-start | bytes 245768 | tf_op jit(solution)/shard_map/ppermute | solution.py:26
  15.8 1.7 %collective-permute-start.4 = (bf16[6,32,256]{2,1,0:T(8,128)(2,1)S(1)}, bf16[6,32,256]{2,1,0:T(8,128)(2,1)S(1)}, u32[]{:S(2)}, u32[]{:S(2)}) collective-permute-start(bf16[6,32,256]{2,1,0:T(8,128)(2,1)S(1)} %pad_maximum_fusion.9), channel_id=1, source_target_pairs={{0,32},{32,0},{64,96},{96,64},{1,33},{33,1},{65,97},{97,65},{2,34}... | collective-permute-start | bytes 294920 | tf_op jit(solution)/shard_map/ppermute | solution.py:26
  18.5 1.6 %collective-permute-start.6 = (bf16[2,32,256]{2,1,0:T(8,128)(2,1)S(1)}, bf16[2,32,256]{2,1,0:T(8,128)(2,1)S(1)}, u32[]{:S(2)}, u32[]{:S(2)}) collective-permute-start(bf16[2,32,256]{2,1,0:T(8,128)(2,1)S(1)} %broadcast_select_fusion.4), channel_id=1, source_target_pairs={{0,2},{2,0},{1,3},{3,1},{4,6},{6,4},{5,7},{7,5},{8,10},{10,8},{9,1... | collective-permute-start | bytes 98312 | tf_op jit(solution)/shard_map/ppermute | solution.py:26
  20.1 2.3 %collective-permute-done.6 = bf16[2,32,256]{2,1,0:T(8,128)(2,1)S(1)} collective-permute-done((bf16[2,32,256]{2,1,0:T(8,128)(2,1)S(1)}, bf16[2,32,256]{2,1,0:T(8,128)(2,1)S(1)}, u32[]{:S(2)}, u32[]{:S(2)}) %collective-permute-start.6) | collective-permute-done | bytes 32800 | tf_op jit(solution)/shard_map/ppermute | solution.py:26
  26.3 9.7 %collective-permute-done.2.other_mod = bf16[1,3,2048]{2,1,0:T(4,128)(2,1)S(1)} collective-permute-done((bf16[1,3,2048]{2,1,0:T(4,128)(2,1)S(1)}, bf16[1,3,2048]{2,1,0:T(4,128)(2,1)S(1)}, u32[]{:S(2)}, u32[]{:S(2)}) %collective-permute-start.2) | collective-permute-done | bytes 12320 | tf_op jit(solution)/shard_map/ppermute | solution.py:26
  36.7 2.2 %collective-permute-start.9 = (bf16[512,512]{1,0:T(8,128)(2,1)S(1)}, bf16[512,512]{1,0:T(8,128)(2,1)S(1)}, u32[]{:S(2)}, u32[]{:S(2)}) collective-permute-start(bf16[512,512]{1,0:T(8,128)(2,1)S(1)} %bitcast.15), channel_id=1, source_target_pairs={{0,130},{2,128},{128,2},{130,0},{1,131},{3,129},{129,3},{131,1},{4... | collective-permute-start | bytes 1572872 | tf_op jit(solution)/shard_map/ppermute | solution.py:26
  38.9 8.3 %collective-permute-done.11.c_ref = bf16[512,512]{1,0:T(8,128)(2,1)S(1)} collective-permute-done((bf16[512,512]{1,0:T(8,128)(2,1)S(1)}, bf16[512,512]{1,0:T(8,128)(2,1)S(1)}, u32[]{:S(2)}, u32[]{:S(2)}) %collective-permute-start.11) | collective-permute-done | bytes 524320 | tf_op jit(solution)/shard_map/ppermute | solution.py:26
  50.1 2.8 %collective-permute-start.15 = (bf16[2,3,2048]{2,1,0:T(4,128)(2,1)S(1)}, bf16[2,3,2048]{2,1,0:T(4,128)(2,1)S(1)}, u32[]{:S(2)}, u32[]{:S(2)}) collective-permute-start(bf16[2,3,2048]{2,1,0:T(4,128)(2,1)S(1)} %get-tuple-element.55.mod_ref), channel_id=1, source_target_pairs={{0,128},{128,0},{1,129},{129,1},{2,130},{130,2},{3,131},{131,3},{4... | collective-permute-start | bytes 73736 | tf_op jit(solution)/shard_map/ppermute | solution.py:26
  52.8 3.6 %collective-permute-done.10 = bf16[256,512]{1,0:T(8,128)(2,1)S(1)} collective-permute-done((bf16[256,512]{1,0:T(8,128)(2,1)S(1)}, bf16[256,512]{1,0:T(8,128)(2,1)S(1)}, u32[]{:S(2)}, u32[]{:S(2)}) %collective-permute-start.10) | collective-permute-done | bytes 262176 | tf_op jit(solution)/shard_map/ppermute | solution.py:26
  56.4 1.7 %collective-permute-done.12 = bf16[256,512]{1,0:T(8,128)(2,1)S(1)} collective-permute-done((bf16[256,512]{1,0:T(8,128)(2,1)S(1)}, bf16[256,512]{1,0:T(8,128)(2,1)S(1)}, u32[]{:S(2)}, u32[]{:S(2)}) %collective-permute-start.12) | collective-permute-done | bytes 262176 | tf_op jit(solution)/shard_map/ppermute | solution.py:26
  58.1 1.6 %hidden.2.hid_hbm = bf16[512,2048]{1,0:T(8,128)(2,1)S(1)} custom-call(bf16[512,512]{1,0:T(8,128)(2,1)S(1)} %bitcast.17, bf16[512,512]{1,0:T(8,128)(2,1)S(1)} %collective-permute-done.13.b_ref, bf16[512,512]{1,0:T(8,128)(2,1)S(1)} %collective-permute-done.11.c_ref, bf16[512,512]{1,0:T(8,128)(2,1)S(1)} %collective-permute-done.14.d_ref, ...), custom_call_target="tpu_custom_call" | custom-call | flops 8388608 | bytes 4194304 | tf_op jit(solution)/shard_map/hidden/pallas_call | solution.py:182
  61.1 1.9 %collective-permute-done.16.b_ref = bf16[512,512]{1,0:T(8,128)(2,1)S(1)} collective-permute-done((bf16[512,512]{1,0:T(8,128)(2,1)S(1)}, bf16[512,512]{1,0:T(8,128)(2,1)S(1)}, u32[]{:S(2)}, u32[]{:S(2)}) %collective-permute-start.16) | collective-permute-done | bytes 524320 | tf_op jit(solution)/shard_map/ppermute | solution.py:26
  63.0 1.6 %hidden.3.hid_hbm = bf16[512,2048]{1,0:T(8,128)(2,1)S(1)} custom-call(bf16[512,512]{1,0:T(8,128)(2,1)S(1)} %pad_maximum_fusion.3.a_ref, bf16[512,512]{1,0:T(8,128)(2,1)S(1)} %collective-permute-done.16.b_ref, bf16[512,512]{1,0:T(8,128)(2,1)S(1)} %collective-permute-done.9.c_ref, bf16[512,512]{1,0:T(8,128)(2,1)S(1)} %collective-permute-done.17.d_ref, ...), custom_call_target="tpu_custom_call" | custom-call | flops 8388608 | bytes 4194304 | tf_op jit(solution)/shard_map/hidden/pallas_call | solution.py:182
  66.0 10.2 %all-gather.3.cloned.1.call-done = bf16[224,32,256]{2,1,0:T(8,128)(2,1)} async-done(((bf16[28,32,256]{2,1,0:T(8,128)(2,1)}), bf16[224,32,256]{2,1,0:T(8,128)(2,1)}) %all-gather.3.cloned.1.call-update) | async-done | bytes 3670032 | tf_op jit(solution)/shard_map/all_gather | solution.py:414
  79.4 4.8 %attend.2 = bf16[512,256]{1,0:T(8,128)(2,1)} custom-call(bf16[512,2048]{1,0:T(8,128)(2,1)} %copy-done.1, bf16[8,28,32,256]{3,2,1,0:T(8,128)(2,1)} %bitcast.30), custom_call_target="tpu_custom_call" | custom-call | flops 3489660928 | bytes 6291456 | tf_op jit(solution)/shard_map/attend/pallas_call | solution.py:248
  84.2 1.6 %collective-permute-start.18 = (bf16[512,256]{1,0:T(8,128)(2,1)}, bf16[512,256]{1,0:T(8,128)(2,1)S(1)}, u32[]{:S(2)}, u32[]{:S(2)}) collective-permute-start(bf16[512,256]{1,0:T(8,128)(2,1)} %attend.2), channel_id=1, source_target_pairs={{0,2},{2,0},{128,130},{130,128},{1,3},{3,1},{129,131},{131,129},{4... | collective-permute-start | bytes 786440 | tf_op jit(solution)/shard_map/ppermute | solution.py:26
  85.8 2.2 %collective-permute-start.19 = (bf16[512,256]{1,0:T(8,128)(2,1)}, bf16[512,256]{1,0:T(8,128)(2,1)S(1)}, u32[]{:S(2)}, u32[]{:S(2)}) collective-permute-start(bf16[512,256]{1,0:T(8,128)(2,1)} %attend.2), channel_id=1, source_target_pairs={{0,130},{2,128},{128,2},{130,0},{1,131},{3,129},{129,3},{131,1},{4... | collective-permute-start | bytes 786440 | tf_op jit(solution)/shard_map/ppermute | solution.py:26
  88.0 4.8 %attend.3.a_ref = bf16[512,256]{1,0:T(8,128)(2,1)} custom-call(bf16[512,2048]{1,0:T(8,128)(2,1)} %copy-done, bf16[8,28,32,256]{3,2,1,0:T(8,128)(2,1)} %bitcast.31), custom_call_target="tpu_custom_call" | custom-call | flops 3489660928 | bytes 6291456 | tf_op jit(solution)/shard_map/attend/pallas_call | solution.py:248
  92.8 1.6 %collective-permute-done.19.d_ref = bf16[512,256]{1,0:T(8,128)(2,1)S(1)} collective-permute-done((bf16[512,256]{1,0:T(8,128)(2,1)}, bf16[512,256]{1,0:T(8,128)(2,1)S(1)}, u32[]{:S(2)}, u32[]{:S(2)}) %collective-permute-start.19) | collective-permute-done | bytes 262176 | tf_op jit(solution)/shard_map/ppermute | solution.py:26
  94.9 2.4 %collective-permute-start.23 = (bf16[4,4,32,256]{3,2,1,0:T(8,128)(2,1)S(1)}, bf16[4,4,32,256]{3,2,1,0:T(8,128)(2,1)S(1)}, u32[]{:S(2)}, u32[]{:S(2)}) collective-permute-start(bf16[4,4,32,256]{3,2,1,0:T(8,128)(2,1)S(1)} %slice.96), channel_id=1, source_target_pairs={{0,96},{32,64},{64,32},{96,0},{1,97},{33,65},{65,33},{97,1},{2,98}... | collective-permute-start | bytes 786440 | tf_op jit(solution)/shard_map/ppermute | solution.py:26
  97.3 2.1 %collective-permute-start.21 = (bf16[512,256]{1,0:T(8,128)(2,1)S(1)}, bf16[512,256]{1,0:T(8,128)(2,1)S(1)}, u32[]{:S(2)}, u32[]{:S(2)}) collective-permute-start(bf16[512,256]{1,0:T(8,128)(2,1)S(1)} %collective-permute-done.18), channel_id=1, source_target_pairs={{0,130},{2,128},{128,2},{130,0},{1,131},{3,129},{129,3},{131,1},{4... | collective-permute-start | bytes 786440 | tf_op jit(solution)/shard_map/ppermute | solution.py:26
  99.4 1.5 collective-permute-done.22
  100.9 1.6 %collective-permute-done.23 = bf16[4,4,32,256]{3,2,1,0:T(8,128)(2,1)S(1)} collective-permute-done((bf16[4,4,32,256]{3,2,1,0:T(8,128)(2,1)S(1)}, bf16[4,4,32,256]{3,2,1,0:T(8,128)(2,1)S(1)}, u32[]{:S(2)}, u32[]{:S(2)}) %collective-permute-start.23) | collective-permute-done | bytes 262176 | tf_op jit(solution)/shard_map/ppermute | solution.py:26
  104.9 1.6 %project.1 = (f32[512,512]{1,0:T(8,128)S(1)}, bf16[512,512]{1,0:T(8,128)(2,1)S(1)}) custom-call(bf16[512,256]{1,0:T(8,128)(2,1)S(1)} %copy-done.8, bf16[512,256]{1,0:T(8,128)(2,1)S(1)} %collective-permute-done.20.b_ref, bf16[512,256]{1,0:T(8,128)(2,1)S(1)} %collective-permute-done.21.c_ref, bf16[512,256]{1,0:T(8,128)(2,1)S(1)} %collective-permute-done.19.d_ref, ...), custom_call_target="tpu_custom_call" | custom-call | flops 1073741824 | bytes 4194304 | tf_op jit(solution)/shard_map/project/pallas_call | solution.py:294
  106.6 1.8 %collective-permute-done.24 = bf16[512,512]{1,0:T(8,128)(2,1)S(1)} collective-permute-done((bf16[512,512]{1,0:T(8,128)(2,1)S(1)}, bf16[512,512]{1,0:T(8,128)(2,1)S(1)}, u32[]{:S(2)}, u32[]{:S(2)}) %collective-permute-start.24) | collective-permute-done | bytes 524320 | tf_op jit(solution)/shard_map/ppermute | solution.py:26
  109.3 5.2 %collective-permute-start.25 = (bf16[156,512]{1,0:T(8,128)(2,1)S(1)}, bf16[156,512]{1,0:T(8,128)(2,1)S(1)}, u32[]{:S(2)}, u32[]{:S(2)}) collective-permute-start(bf16[156,512]{1,0:T(8,128)(2,1)S(1)} %select_n.125), channel_id=1, source_target_pairs={{16,32},{20,36},{24,40},{28,44},{32,16},{36,20},{40,24},{44,28},{4... | collective-permute-start | bytes 479240 | tf_op jit(solution)/shard_map/ppermute | solution.py:40
  114.6 4.8 %collective-permute-start.26 = (bf16[156,512]{1,0:T(8,128)(2,1)S(1)}, bf16[156,512]{1,0:T(8,128)(2,1)S(1)}, u32[]{:S(2)}, u32[]{:S(2)}) collective-permute-start(bf16[156,512]{1,0:T(8,128)(2,1)S(1)} %select_n.127), channel_id=1, source_target_pairs={{0,16},{4,20},{8,24},{12,28},{16,0},{20,4},{24,8},{28,12},{32,48},... | collective-permute-start | bytes 479240 | tf_op jit(solution)/shard_map/ppermute | solution.py:40
  119.4 7.5 %collective-permute-done.25 = bf16[156,512]{1,0:T(8,128)(2,1)S(1)} collective-permute-done((bf16[156,512]{1,0:T(8,128)(2,1)S(1)}, bf16[156,512]{1,0:T(8,128)(2,1)S(1)}, u32[]{:S(2)}, u32[]{:S(2)}) %collective-permute-start.25) | collective-permute-done | bytes 159776 | tf_op jit(solution)/shard_map/ppermute | solution.py:40
  126.8 5.8 %collective-permute-done.26 = bf16[156,512]{1,0:T(8,128)(2,1)S(1)} collective-permute-done((bf16[156,512]{1,0:T(8,128)(2,1)S(1)}, bf16[156,512]{1,0:T(8,128)(2,1)S(1)}, u32[]{:S(2)}, u32[]{:S(2)}) %collective-permute-start.26) | collective-permute-done | bytes 159776 | tf_op jit(solution)/shard_map/ppermute | solution.py:40
  135.4 8.8 %collective-permute-done.29 = bf16[96,512]{1,0:T(8,128)(2,1)S(1)} collective-permute-done((bf16[96,512]{1,0:T(8,128)(2,1)S(1)}, bf16[96,512]{1,0:T(8,128)(2,1)S(1)}, u32[]{:S(2)}, u32[]{:S(2)}) %collective-permute-start.29) | collective-permute-done | bytes 98336 | tf_op jit(solution)/shard_map/ppermute | solution.py:450
  144.2 2.8 %collective-permute-done.27 = bf16[416,512]{1,0:T(8,128)(2,1)S(1)} collective-permute-done((bf16[416,512]{1,0:T(8,128)(2,1)S(1)}, bf16[416,512]{1,0:T(8,128)(2,1)S(1)}, u32[]{:S(2)}, u32[]{:S(2)}) %collective-permute-start.27) | collective-permute-done | bytes 426016 | tf_op jit(solution)/shard_map/ppermute | solution.py:26
  148.4 1.5 place.1
  (109 shorter events, 28.0 us)
Async XLA Ops:
  6.5 29.5 %copy-start.7 = (s32[64]{0:T(128)S(1)}, s32[64]{0:T(128)}, u32[]{:S(2)}) copy-start(s32[64]{0:T(128)} %counts_ref.5) | copy-start | bytes 772
  6.5 69.7 %all-gather.3.cloned.1.call-start = ((), (), s32[]{:S(2)}) async-start(), calls=%async_computation | async-start | bytes 4128768 | tf_op jit(solution)/shard_map/all_gather | solution.py:414
  8.2 6.0 %collective-permute-start = (bf16[5,32,256]{2,1,0:T(8,128)(2,1)S(1)}, bf16[5,32,256]{2,1,0:T(8,128)(2,1)S(1)}, u32[]{:S(2)}, u32[]{:S(2)}) collective-permute-start(bf16[5,32,256]{2,1,0:T(8,128)(2,1)S(1)} %get-tuple-element.40), channel_id=1, source_target_pairs={{0,128},{128,0},{1,129},{129,1},{2,130},{130,2},{3,131},{131,3},{4... | collective-permute-start | bytes 245768 | tf_op jit(solution)/shard_map/ppermute | solution.py:26
  14.3 8.1 %collective-permute-start.3 = (bf16[6,32,256]{2,1,0:T(8,128)(2,1)S(1)}, bf16[6,32,256]{2,1,0:T(8,128)(2,1)S(1)}, u32[]{:S(2)}, u32[]{:S(2)}) collective-permute-start(bf16[6,32,256]{2,1,0:T(8,128)(2,1)S(1)} %pad_maximum_fusion.9), channel_id=1, source_target_pairs={{0,64},{32,96},{64,0},{96,32},{1,65},{33,97},{65,1},{97,33},{2,66}... | collective-permute-start | bytes 294920 | tf_op jit(solution)/shard_map/ppermute | solution.py:26
  15.8 6.6 %collective-permute-start.4 = (bf16[6,32,256]{2,1,0:T(8,128)(2,1)S(1)}, bf16[6,32,256]{2,1,0:T(8,128)(2,1)S(1)}, u32[]{:S(2)}, u32[]{:S(2)}) collective-permute-start(bf16[6,32,256]{2,1,0:T(8,128)(2,1)S(1)} %pad_maximum_fusion.9), channel_id=1, source_target_pairs={{0,32},{32,0},{64,96},{96,64},{1,33},{33,1},{65,97},{97,65},{2,34}... | collective-permute-start | bytes 294920 | tf_op jit(solution)/shard_map/ppermute | solution.py:26
  17.4 5.8 %collective-permute-start.5 = (bf16[6,32,256]{2,1,0:T(8,128)(2,1)S(1)}, bf16[6,32,256]{2,1,0:T(8,128)(2,1)S(1)}, u32[]{:S(2)}, u32[]{:S(2)}) collective-permute-start(bf16[6,32,256]{2,1,0:T(8,128)(2,1)S(1)} %pad_maximum_fusion.9), channel_id=1, source_target_pairs={{0,96},{32,64},{64,32},{96,0},{1,97},{33,65},{65,33},{97,1},{2,98}... | collective-permute-start | bytes 294920 | tf_op jit(solution)/shard_map/ppermute | solution.py:26
  18.5 3.9 %collective-permute-start.6 = (bf16[2,32,256]{2,1,0:T(8,128)(2,1)S(1)}, bf16[2,32,256]{2,1,0:T(8,128)(2,1)S(1)}, u32[]{:S(2)}, u32[]{:S(2)}) collective-permute-start(bf16[2,32,256]{2,1,0:T(8,128)(2,1)S(1)} %broadcast_select_fusion.4), channel_id=1, source_target_pairs={{0,2},{2,0},{1,3},{3,1},{4,6},{6,4},{5,7},{7,5},{8,10},{10,8},{9,1... | collective-permute-start | bytes 98312 | tf_op jit(solution)/shard_map/ppermute | solution.py:26
  24.1 11.8 %collective-permute-start.1 = (bf16[2,256,512]{2,1,0:T(8,128)(2,1)S(1)}, bf16[2,256,512]{2,1,0:T(8,128)(2,1)S(1)}, u32[]{:S(2)}, u32[]{:S(2)}) collective-permute-start(bf16[2,256,512]{2,1,0:T(8,128)(2,1)S(1)} %get-tuple-element.44), channel_id=1, source_target_pairs={{0,4},{4,0},{8,12},{12,8},{16,20},{20,16},{24,28},{28,24},{1,5},{5... | collective-permute-start | bytes 1572872 | tf_op jit(solution)/shard_map/ppermute | solution.py:26
  25.3 10.7 %collective-permute-start.2 = (bf16[1,3,2048]{2,1,0:T(4,128)(2,1)S(1)}, bf16[1,3,2048]{2,1,0:T(4,128)(2,1)S(1)}, u32[]{:S(2)}, u32[]{:S(2)}) collective-permute-start(bf16[1,3,2048]{2,1,0:T(4,128)(2,1)S(1)} %copy-done.5), channel_id=1, source_target_pairs={{0,4},{4,0},{8,12},{12,8},{16,20},{20,16},{24,28},{28,24},{1,5},{5... | collective-permute-start | bytes 36872 | tf_op jit(solution)/shard_map/ppermute | solution.py:26
  36.6 10.6 %collective-permute-start.11 = (bf16[512,512]{1,0:T(8,128)(2,1)S(1)}, bf16[512,512]{1,0:T(8,128)(2,1)S(1)}, u32[]{:S(2)}, u32[]{:S(2)}) collective-permute-start(bf16[512,512]{1,0:T(8,128)(2,1)S(1)} %bitcast.14), channel_id=1, source_target_pairs={{0,2},{2,0},{128,130},{130,128},{1,3},{3,1},{129,131},{131,129},{4... | collective-permute-start | bytes 1572872 | tf_op jit(solution)/shard_map/ppermute | solution.py:26
  36.7 11.8 %collective-permute-start.9 = (bf16[512,512]{1,0:T(8,128)(2,1)S(1)}, bf16[512,512]{1,0:T(8,128)(2,1)S(1)}, u32[]{:S(2)}, u32[]{:S(2)}) collective-permute-start(bf16[512,512]{1,0:T(8,128)(2,1)S(1)} %bitcast.15), channel_id=1, source_target_pairs={{0,130},{2,128},{128,2},{130,0},{1,131},{3,129},{129,3},{131,1},{4... | collective-permute-start | bytes 1572872 | tf_op jit(solution)/shard_map/ppermute | solution.py:26
  38.9 19.2 %collective-permute-start.13 = (bf16[512,512]{1,0:T(8,128)(2,1)S(1)}, bf16[512,512]{1,0:T(8,128)(2,1)S(1)}, u32[]{:S(2)}, u32[]{:S(2)}) collective-permute-start(bf16[512,512]{1,0:T(8,128)(2,1)S(1)} %bitcast.16), channel_id=1, source_target_pairs={{0,1},{1,0},{2,3},{3,2},{4,5},{5,4},{6,7},{7,6},{8,9},{9,8},{10,11... | collective-permute-start | bytes 1572872 | tf_op jit(solution)/shard_map/ppermute | solution.py:26
  47.2 10.9 %collective-permute-start.14 = (bf16[512,512]{1,0:T(8,128)(2,1)S(1)}, bf16[512,512]{1,0:T(8,128)(2,1)S(1)}, u32[]{:S(2)}, u32[]{:S(2)}) collective-permute-start(bf16[512,512]{1,0:T(8,128)(2,1)S(1)} %collective-permute-done.11.c_ref), channel_id=1, source_target_pairs={{0,1},{1,0},{2,3},{3,2},{4,5},{5,4},{6,7},{7,6},{8,9},{9,8},{10,11... | collective-permute-start | bytes 1572872 | tf_op jit(solution)/shard_map/ppermute | solution.py:26
  48.5 7.9 %collective-permute-start.10 = (bf16[256,512]{1,0:T(8,128)(2,1)S(1)}, bf16[256,512]{1,0:T(8,128)(2,1)S(1)}, u32[]{:S(2)}, u32[]{:S(2)}) collective-permute-start(bf16[256,512]{1,0:T(8,128)(2,1)S(1)} %slice.117), channel_id=1, source_target_pairs={{0,2},{2,0},{128,130},{130,128},{1,3},{3,1},{129,131},{131,129},{4... | collective-permute-start | bytes 786440 | tf_op jit(solution)/shard_map/ppermute | solution.py:26
  49.1 9.0 %collective-permute-start.12 = (bf16[256,512]{1,0:T(8,128)(2,1)S(1)}, bf16[256,512]{1,0:T(8,128)(2,1)S(1)}, u32[]{:S(2)}, u32[]{:S(2)}) collective-permute-start(bf16[256,512]{1,0:T(8,128)(2,1)S(1)} %slice.118), channel_id=1, source_target_pairs={{0,130},{2,128},{128,2},{130,0},{1,131},{3,129},{129,3},{131,1},{4... | collective-permute-start | bytes 786440 | tf_op jit(solution)/shard_map/ppermute | solution.py:26
  50.1 11.1 %collective-permute-start.15 = (bf16[2,3,2048]{2,1,0:T(4,128)(2,1)S(1)}, bf16[2,3,2048]{2,1,0:T(4,128)(2,1)S(1)}, u32[]{:S(2)}, u32[]{:S(2)}) collective-permute-start(bf16[2,3,2048]{2,1,0:T(4,128)(2,1)S(1)} %get-tuple-element.55.mod_ref), channel_id=1, source_target_pairs={{0,128},{128,0},{1,129},{129,1},{2,130},{130,2},{3,131},{131,3},{4... | collective-permute-start | bytes 73736 | tf_op jit(solution)/shard_map/ppermute | solution.py:26
  56.4 4.7 %collective-permute-start.17 = (bf16[512,512]{1,0:T(8,128)(2,1)S(1)}, bf16[512,512]{1,0:T(8,128)(2,1)S(1)}, u32[]{:S(2)}, u32[]{:S(2)}) collective-permute-start(bf16[512,512]{1,0:T(8,128)(2,1)S(1)} %collective-permute-done.9.c_ref), channel_id=1, source_target_pairs={{0,1},{1,0},{2,3},{3,2},{4,5},{5,4},{6,7},{7,6},{8,9},{9,8},{10,11... | collective-permute-start | bytes 1572872 | tf_op jit(solution)/shard_map/ppermute | solution.py:26
  61.1 1.9 %collective-permute-start.16 = (bf16[512,512]{1,0:T(8,128)(2,1)S(1)}, bf16[512,512]{1,0:T(8,128)(2,1)S(1)}, u32[]{:S(2)}, u32[]{:S(2)}) collective-permute-start(bf16[512,512]{1,0:T(8,128)(2,1)S(1)} %pad_maximum_fusion.3.a_ref), channel_id=1, source_target_pairs={{0,1},{1,0},{2,3},{3,2},{4,5},{5,4},{6,7},{7,6},{8,9},{9,8},{10,11... | collective-permute-start | bytes 1572872 | tf_op jit(solution)/shard_map/ppermute | solution.py:26
  77.3 17.1 %collective-permute-start.7 = (bf16[8,4,32,256]{3,2,1,0:T(8,128)(2,1)S(1)}, bf16[8,4,32,256]{3,2,1,0:T(8,128)(2,1)S(1)}, u32[]{:S(2)}, u32[]{:S(2)}) collective-permute-start(bf16[8,4,32,256]{3,2,1,0:T(8,128)(2,1)S(1)} %slice.116.o0), channel_id=1, source_target_pairs={{0,32},{32,0},{64,96},{96,64},{1,33},{33,1},{65,97},{97,65},{2,34}... | collective-permute-start | bytes 1572872 | tf_op jit(solution)/shard_map/ppermute | solution.py:26
  78.3 16.2 %collective-permute-start.8 = (bf16[8,4,32,256]{3,2,1,0:T(8,128)(2,1)S(1)}, bf16[8,4,32,256]{3,2,1,0:T(8,128)(2,1)S(1)}, u32[]{:S(2)}, u32[]{:S(2)}) collective-permute-start(bf16[8,4,32,256]{3,2,1,0:T(8,128)(2,1)S(1)} %slice.116.o0), channel_id=1, source_target_pairs={{0,96},{32,64},{64,32},{96,0},{1,97},{33,65},{65,33},{97,1},{2,98}... | collective-permute-start | bytes 1572872 | tf_op jit(solution)/shard_map/ppermute | solution.py:26
  84.2 8.6 %collective-permute-start.18 = (bf16[512,256]{1,0:T(8,128)(2,1)}, bf16[512,256]{1,0:T(8,128)(2,1)S(1)}, u32[]{:S(2)}, u32[]{:S(2)}) collective-permute-start(bf16[512,256]{1,0:T(8,128)(2,1)} %attend.2), channel_id=1, source_target_pairs={{0,2},{2,0},{128,130},{130,128},{1,3},{3,1},{129,131},{131,129},{4... | collective-permute-start | bytes 786440 | tf_op jit(solution)/shard_map/ppermute | solution.py:26
  85.8 8.6 %collective-permute-start.19 = (bf16[512,256]{1,0:T(8,128)(2,1)}, bf16[512,256]{1,0:T(8,128)(2,1)S(1)}, u32[]{:S(2)}, u32[]{:S(2)}) collective-permute-start(bf16[512,256]{1,0:T(8,128)(2,1)} %attend.2), channel_id=1, source_target_pairs={{0,130},{2,128},{128,2},{130,0},{1,131},{3,129},{129,3},{131,1},{4... | collective-permute-start | bytes 786440 | tf_op jit(solution)/shard_map/ppermute | solution.py:26
  94.5 6.5 %collective-permute-start.22 = (bf16[4,4,32,256]{3,2,1,0:T(8,128)(2,1)S(1)}, bf16[4,4,32,256]{3,2,1,0:T(8,128)(2,1)S(1)}, u32[]{:S(2)}, u32[]{:S(2)}) collective-permute-start(bf16[4,4,32,256]{3,2,1,0:T(8,128)(2,1)S(1)} %slice.95), channel_id=1, source_target_pairs={{0,32},{32,0},{64,96},{96,64},{1,33},{33,1},{65,97},{97,65},{2,34}... | collective-permute-start | bytes 786440 | tf_op jit(solution)/shard_map/ppermute | solution.py:26
  94.9 7.7 %collective-permute-start.23 = (bf16[4,4,32,256]{3,2,1,0:T(8,128)(2,1)S(1)}, bf16[4,4,32,256]{3,2,1,0:T(8,128)(2,1)S(1)}, u32[]{:S(2)}, u32[]{:S(2)}) collective-permute-start(bf16[4,4,32,256]{3,2,1,0:T(8,128)(2,1)S(1)} %slice.96), channel_id=1, source_target_pairs={{0,96},{32,64},{64,32},{96,0},{1,97},{33,65},{65,33},{97,1},{2,98}... | collective-permute-start | bytes 786440 | tf_op jit(solution)/shard_map/ppermute | solution.py:26
  97.3 6.6 %collective-permute-start.20 = (bf16[512,256]{1,0:T(8,128)(2,1)}, bf16[512,256]{1,0:T(8,128)(2,1)S(1)}, u32[]{:S(2)}, u32[]{:S(2)}) collective-permute-start(bf16[512,256]{1,0:T(8,128)(2,1)} %attend.3.a_ref), channel_id=1, source_target_pairs={{0,2},{2,0},{128,130},{130,128},{1,3},{3,1},{129,131},{131,129},{4... | collective-permute-start | bytes 786440 | tf_op jit(solution)/shard_map/ppermute | solution.py:26
  97.3 7.6 %collective-permute-start.21 = (bf16[512,256]{1,0:T(8,128)(2,1)S(1)}, bf16[512,256]{1,0:T(8,128)(2,1)S(1)}, u32[]{:S(2)}, u32[]{:S(2)}) collective-permute-start(bf16[512,256]{1,0:T(8,128)(2,1)S(1)} %collective-permute-done.18), channel_id=1, source_target_pairs={{0,130},{2,128},{128,2},{130,0},{1,131},{3,129},{129,3},{131,1},{4... | collective-permute-start | bytes 786440 | tf_op jit(solution)/shard_map/ppermute | solution.py:26
  106.5 2.0 %collective-permute-start.24 = (bf16[512,512]{1,0:T(8,128)(2,1)S(1)}, bf16[512,512]{1,0:T(8,128)(2,1)S(1)}, u32[]{:S(2)}, u32[]{:S(2)}) collective-permute-start(bf16[512,512]{1,0:T(8,128)(2,1)S(1)} %get-tuple-element.69), channel_id=1, source_target_pairs={{0,1},{1,0},{2,3},{3,2},{4,5},{5,4},{6,7},{7,6},{8,9},{9,8},{10,11... | collective-permute-start | bytes 1572872 | tf_op jit(solution)/shard_map/ppermute | solution.py:26
  109.3 17.5 %collective-permute-start.25 = (bf16[156,512]{1,0:T(8,128)(2,1)S(1)}, bf16[156,512]{1,0:T(8,128)(2,1)S(1)}, u32[]{:S(2)}, u32[]{:S(2)}) collective-permute-start(bf16[156,512]{1,0:T(8,128)(2,1)S(1)} %select_n.125), channel_id=1, source_target_pairs={{16,32},{20,36},{24,40},{28,44},{32,16},{36,20},{40,24},{44,28},{4... | collective-permute-start | bytes 479240 | tf_op jit(solution)/shard_map/ppermute | solution.py:40
  114.6 18.0 %collective-permute-start.26 = (bf16[156,512]{1,0:T(8,128)(2,1)S(1)}, bf16[156,512]{1,0:T(8,128)(2,1)S(1)}, u32[]{:S(2)}, u32[]{:S(2)}) collective-permute-start(bf16[156,512]{1,0:T(8,128)(2,1)S(1)} %select_n.127), channel_id=1, source_target_pairs={{0,16},{4,20},{8,24},{12,28},{16,0},{20,4},{24,8},{28,12},{32,48},... | collective-permute-start | bytes 479240 | tf_op jit(solution)/shard_map/ppermute | solution.py:40
  133.2 13.8 %collective-permute-start.27 = (bf16[416,512]{1,0:T(8,128)(2,1)S(1)}, bf16[416,512]{1,0:T(8,128)(2,1)S(1)}, u32[]{:S(2)}, u32[]{:S(2)}) collective-permute-start(bf16[416,512]{1,0:T(8,128)(2,1)S(1)} %reshape.55), channel_id=1, source_target_pairs={{0,4},{4,0},{8,12},{12,8},{16,20},{20,16},{24,28},{28,24},{1,5},{5... | collective-permute-start | bytes 1277960 | tf_op jit(solution)/shard_map/ppermute | solution.py:26
  133.4 2.0 %collective-permute-start.28 = (bf16[96,512]{1,0:T(8,128)(2,1)S(1)}, bf16[96,512]{1,0:T(8,128)(2,1)S(1)}, u32[]{:S(2)}, u32[]{:S(2)}) collective-permute-start(bf16[96,512]{1,0:T(8,128)(2,1)S(1)} %reshape.56), channel_id=1, source_target_pairs={{4,8},{8,4},{20,24},{24,20},{36,40},{40,36},{52,56},{56,52},{68,72... | collective-permute-start | bytes 294920 | tf_op jit(solution)/shard_map/ppermute | solution.py:447
  134.1 10.1 %collective-permute-start.29 = (bf16[96,512]{1,0:T(8,128)(2,1)S(1)}, bf16[96,512]{1,0:T(8,128)(2,1)S(1)}, u32[]{:S(2)}, u32[]{:S(2)}) collective-permute-start(bf16[96,512]{1,0:T(8,128)(2,1)S(1)} %reshape.56), channel_id=1, source_target_pairs={{4,12},{8,0},{20,28},{24,16},{36,44},{40,32},{52,60},{56,48},{68,7... | collective-permute-start | bytes 294920 | tf_op jit(solution)/shard_map/ppermute | solution.py:450
  (10 other events, 40.3 us)
Sparse Core Ops, SparseCore 0:
  24.3 51.9 all-gather.2
